TPU v7x, 128 devices: a whole 4x4x4 slice. The times are simulated.
128 devices in a mesh: row: 16 (over y_lo, z, core), col: 8 (over y_hi, x).
Axes of the slice: x: 4, y: 4 (y_hi: 2, y_lo: 2; y = y_hi * 2 + y_lo), z: 4, core: 2. Of those that a mesh axis runs over, the one named last changes fastest.
Arguments:
- features: bfloat16 [65536, 512], P(('row', 'col')), may hold values from -6 to 6
- partition_of: int32 [65536], P(('row', 'col')), may hold values from 0 to 127, as said below
- weight: bfloat16 [512, 512], replicated, may hold values from -0.25 to 0.25
- tile_values: bfloat16 [16, 8, 192, 128, 128], P('row', 'col'), may hold values from -0.109375 to 0.109375
- tile_rows: int32 [16, 8, 192], P('row', 'col'), may hold values from 0 to 31
- tile_cols: int32 [16, 8, 192], P('row', 'col'), may hold values from 0 to 63
- tile_count: int32 [16, 8], P('row', 'col'), may hold values from 48 to 192, as said below
- out_cotangent: bfloat16 [65536, 512], P('row'), may hold values from -6 to 6
Outputs:
- activations: bfloat16 [65536, 512], P(('row', 'col'))
- weight_grad: float32 [512, 512], replicated
Inputs may be any that keep to these rules, and one draw needn't show every extreme that they name: `partition_of`: of the 512 regions of each device in detection order, exactly 4 go to each partition. `tile_count`: some grid position has all 192 slots live in every draw.
All inputs are finite; a program needn't handle non-finite values.
Results may differ from a plain program's by a relative error of at most 0.005.
Values may be sent and summed in bfloat16 or wider, within the bound.
No kernel may reach another device: no remote copies, remote signals or barrier semaphores. Data moves between devices by JAX's collectives and lax.ppermute only.
A program may use at most 192 MiB of HBM per device.

v0:
```python
import math

import jax
import jax.numpy as jnp
from jax import lax
from jax.sharding import PartitionSpec as P


def silu_slope(pre):
    sigmoid = jax.nn.sigmoid(pre)
    return sigmoid * (1.0 + pre * (1.0 - sigmoid))


def regroup(features, partition_of, n_row, n_col):
    slots, feature_width = features.shape
    per_peer = slots // (n_row * n_col)
    ordering = jnp.argsort(partition_of, stable=True)
    outgoing = features[ordering]
    shaped = outgoing.reshape(n_row * n_col, per_peer, feature_width)
    arrived = lax.all_to_all(shaped, ("row", "col"), split_axis=0, concat_axis=0, tiled=True)
    return arrived.reshape(slots, feature_width)


def tile_products(blocks, row_index, column_index, live_count, sources, out_tiles, forward):
    tile_size = blocks.shape[-1]
    feature_width = sources.shape[-1]
    source_tiles = sources.reshape(-1, tile_size, feature_width)
    empty = jnp.zeros((out_tiles, tile_size, feature_width), jnp.float32)
    block_total = (live_count + 31) // 32

    def one_block(block_step, totals):
        first_slot = block_step * 32
        tile_block = lax.dynamic_slice_in_dim(blocks, first_slot, 32, 0)
        row_part = lax.dynamic_slice_in_dim(row_index, first_slot, 32, 0)
        column_part = lax.dynamic_slice_in_dim(column_index, first_slot, 32, 0)
        is_live = first_slot + jnp.arange(32, dtype=jnp.int32) < live_count
        tile_block = jnp.where(is_live[:, None, None], tile_block, jnp.zeros_like(tile_block))
        if forward:
            picked = source_tiles[column_part]
            products = jnp.einsum(
                "tij,tjf->tif", tile_block, picked, preferred_element_type=jnp.float32
            )
            return totals.at[row_part].add(products)
        picked = source_tiles[row_part]
        products = jnp.einsum(
            "tij,tif->tjf", tile_block, picked, preferred_element_type=jnp.float32
        )
        return totals.at[column_part].add(products)

    totals = lax.fori_loop(0, block_total, one_block, empty)
    return totals.reshape(out_tiles * tile_size, feature_width)


def shards(
    features, partition_of, weight, tile_values, tile_rows, tile_cols, tile_count, out_cotangent
):
    n_row = lax.axis_size("row")
    n_col = lax.axis_size("col")
    regrouped = regroup(features, partition_of, n_row, n_col)
    slots, feature_width = regrouped.shape
    tile_size = tile_values.shape[-1]
    blocks = tile_values.reshape(-1, tile_size, tile_size)
    row_index = tile_rows.reshape(-1)
    column_index = tile_cols.reshape(-1)
    live_count = tile_count.reshape(())
    row_tiles = slots * n_col // tile_size
    column_tiles = slots * n_row // tile_size
    hidden = jnp.dot(regrouped, weight, preferred_element_type=jnp.float32).astype(jnp.bfloat16)
    hidden_columns = lax.all_gather(hidden, "row", axis=0, tiled=True)
    partial_value = tile_products(
        blocks, row_index, column_index, live_count, hidden_columns, row_tiles, True
    )
    position = lax.axis_index("col") * slots
    pre = lax.psum(partial_value, "col")
    own_pre = lax.dynamic_slice_in_dim(pre, position, slots, 0)
    activations = jax.nn.silu(own_pre).astype(jnp.bfloat16)
    slope = (out_cotangent.astype(jnp.float32) * silu_slope(pre)).astype(jnp.bfloat16)
    back_partial = tile_products(
        blocks, row_index, column_index, live_count, slope, column_tiles, False
    )
    hidden_grad = lax.psum_scatter(back_partial, "row", scatter_dimension=0, tiled=True)
    local_grad = jnp.dot(
        regrouped.astype(jnp.float32).T,
        hidden_grad,
        precision=lax.Precision.HIGHEST,
        preferred_element_type=jnp.float32,
    )
    weight_grad = lax.psum(local_grad, ("row", "col")) * (1.0 / math.sqrt(slots * n_row * n_col))
    return (activations, weight_grad)


def solution(mesh):
    placed = (
        P(("row", "col"), None),
        P(("row", "col")),
        P(),
        P("row", "col", None, None, None),
        P("row", "col", None),
        P("row", "col", None),
        P("row", "col"),
        P("row", None),
    )
    return jax.shard_map(
        shards,
        mesh=mesh,
        in_specs=placed,
        out_specs=(P(("row", "col"), None), P()),
        check_vma=False,
    )
```

profile of v0, /device:TPU:1, one launch (start us, length us, event | category | flops | bytes accessed | tf_op | source)
XLA Modules:
  0.0 937.7 jit_solution(18352285362092890931)
XLA Ops:
  7.2 4.5 sort.17
  11.8 2.0 gather_fusion.2
  13.9 23.8 %all_to_all.5 = bf16[128,4,512]{2,1,0:T(4,128)(2,1)S(1)} all-to-all(bf16[128,4,512]{2,1,0:T(4,128)(2,1)S(1)} %reshape.48), channel_id=1, replica_groups=mesh['row'=16,'col'=8] {'row','col'}, dimensions={0} | all-to-all | bytes 1048576 | tf_op jit(solution)/shard_map/all_to_all | solution.py:20
  37.9 2.5 convolution_convert_fusion
  41.1 49.4 %all-gather.2.cloned.1.call-done = bf16[8192,512]{1,0:T(8,128)(2,1)} async-done(((bf16[512,512]{1,0:T(8,128)(2,1)}), bf16[8192,512]{1,0:T(8,128)(2,1)}) %all-gather.2.cloned.1.call-update) | async-done | bytes 8388624 | tf_op jit(solution)/shard_map/all_gather | solution.py:69
  90.5 4.3 broadcast_in_dim.36
  94.8 195.6 %while.20 = (s32[]{:T(128)}, f32[32,128,512]{2,1,0:T(8,128)}, s32[]{:T(128)}, s32[192]{0:T(256)S(1)}, s32[]{:T(128)}, /*index=5*/bf16[192,128,128]{2,1,0:T(8,128...) while((s32[]{:T(128)}, f32[32,128,512]{2,1,0:T(8,128)}, ...), condition=%wide.region_3.4_spmd, body=%wide.region_1.3_spmd.sunk | while | flops 539493632 | bytes 47191152 | solution.py:50
  94.8 0.7 add_compare_fusion.4
  95.6 6.1 gather_fusion
  101.7 7.0 fusion.29
  108.7 18.6 %scatter_fusion = f32[32,128,512]{2,1,0:T(8,128)} fusion(f32[32,128,512]{2,1,0:T(8,128)} %get-tuple-element.257, s32[32]{0:T(128)S(1)} %get-tuple-element.232, f32[32,128,512]{2,1,0:T(8,128)} %fusion.29), kind=kCustom, calls=%fused_computation.3.clone.1 | custom fusion | flops 2097152 | bytes 25165952 | tf_op jit(solution)/shard_map/while/body/scatter-add | solution.py:43
  127.3 0.7 add_compare_fusion.4
  128.0 6.1 gather_fusion
  134.1 7.0 fusion.29
  141.1 18.7 %scatter_fusion = f32[32,128,512]{2,1,0:T(8,128)} fusion(f32[32,128,512]{2,1,0:T(8,128)} %get-tuple-element.257, s32[32]{0:T(128)S(1)} %get-tuple-element.232, f32[32,128,512]{2,1,0:T(8,128)} %fusion.29), kind=kCustom, calls=%fused_computation.3.clone.1 | custom fusion | flops 2097152 | bytes 25165952 | tf_op jit(solution)/shard_map/while/body/scatter-add | solution.py:43
  159.8 0.7 add_compare_fusion.4
  160.6 6.1 gather_fusion
  166.7 7.0 fusion.29
  173.7 18.5 %scatter_fusion = f32[32,128,512]{2,1,0:T(8,128)} fusion(f32[32,128,512]{2,1,0:T(8,128)} %get-tuple-element.257, s32[32]{0:T(128)S(1)} %get-tuple-element.232, f32[32,128,512]{2,1,0:T(8,128)} %fusion.29), kind=kCustom, calls=%fused_computation.3.clone.1 | custom fusion | flops 2097152 | bytes 25165952 | tf_op jit(solution)/shard_map/while/body/scatter-add | solution.py:43
  192.2 0.7 add_compare_fusion.4
  193.0 6.1 gather_fusion
  199.1 7.0 fusion.29
  206.1 18.8 %scatter_fusion = f32[32,128,512]{2,1,0:T(8,128)} fusion(f32[32,128,512]{2,1,0:T(8,128)} %get-tuple-element.257, s32[32]{0:T(128)S(1)} %get-tuple-element.232, f32[32,128,512]{2,1,0:T(8,128)} %fusion.29), kind=kCustom, calls=%fused_computation.3.clone.1 | custom fusion | flops 2097152 | bytes 25165952 | tf_op jit(solution)/shard_map/while/body/scatter-add | solution.py:43
  224.9 0.7 add_compare_fusion.4
  225.7 6.1 gather_fusion
  231.8 7.0 fusion.29
  238.8 18.7 %scatter_fusion = f32[32,128,512]{2,1,0:T(8,128)} fusion(f32[32,128,512]{2,1,0:T(8,128)} %get-tuple-element.257, s32[32]{0:T(128)S(1)} %get-tuple-element.232, f32[32,128,512]{2,1,0:T(8,128)} %fusion.29), kind=kCustom, calls=%fused_computation.3.clone.1 | custom fusion | flops 2097152 | bytes 25165952 | tf_op jit(solution)/shard_map/while/body/scatter-add | solution.py:43
  257.6 0.7 add_compare_fusion.4
  258.3 6.1 gather_fusion
  264.4 7.0 fusion.29
  271.5 18.9 %scatter_fusion = f32[32,128,512]{2,1,0:T(8,128)} fusion(f32[32,128,512]{2,1,0:T(8,128)} %get-tuple-element.257, s32[32]{0:T(128)S(1)} %get-tuple-element.232, f32[32,128,512]{2,1,0:T(8,128)} %fusion.29), kind=kCustom, calls=%fused_computation.3.clone.1 | custom fusion | flops 2097152 | bytes 25165952 | tf_op jit(solution)/shard_map/while/body/scatter-add | solution.py:43
  290.5 8.6 copy.10
  299.1 177.8 %all-reduce.3.cloned.1.call-done = f32[4096,512]{1,0:T(8,128)} async-done(((f32[4096,512]{1,0:T(8,128)}), f32[4096,512]{1,0:T(8,128)}) %all-reduce.3.cloned.1.call-update) | async-done | bytes 8388624 | tf_op jit(solution)/shard_map/psum | solution.py:74
  476.9 7.6 multiply_convert_fusion
  484.5 7.9 broadcast_in_dim.38
  492.3 189.8 %while.21 = (s32[]{:T(128)}, f32[64,128,512]{2,1,0:T(8,128)}, s32[]{:T(128)}, s32[192]{0:T(256)S(1)}, s32[]{:T(128)}, /*index=5*/bf16[192,128,128]{1,2,0:T(8,128...) while((s32[]{:T(128)}, f32[64,128,512]{2,1,0:T(8,128)}, ...), condition=%wide.region_7.8_spmd, body=%wide.region_5.7_spmd.sunk | while | flops 539493632 | bytes 47191152 | solution.py:50
  492.3 0.7 add_compare_fusion.5
  493.1 5.1 gather_fusion.1
  498.2 7.0 fusion.32
  505.2 18.9 %scatter_fusion.1 = f32[64,128,512]{2,1,0:T(8,128)} fusion(f32[64,128,512]{2,1,0:T(8,128)} %get-tuple-element.293, s32[32]{0:T(128)S(1)} %get-tuple-element.242, f32[32,128,512]{2,1,0:T(8,128)} %fusion.32), kind=kCustom, calls=%fused_computation.4.clone.1 | custom fusion | flops 2097152 | bytes 25165952 | tf_op jit(solution)/shard_map/while/body/scatter-add | solution.py:48
  524.1 0.7 add_compare_fusion.5
  524.8 5.1 gather_fusion.1
  529.9 7.0 fusion.32
  536.9 18.8 %scatter_fusion.1 = f32[64,128,512]{2,1,0:T(8,128)} fusion(f32[64,128,512]{2,1,0:T(8,128)} %get-tuple-element.293, s32[32]{0:T(128)S(1)} %get-tuple-element.242, f32[32,128,512]{2,1,0:T(8,128)} %fusion.32), kind=kCustom, calls=%fused_computation.4.clone.1 | custom fusion | flops 2097152 | bytes 25165952 | tf_op jit(solution)/shard_map/while/body/scatter-add | solution.py:48
  555.7 0.7 add_compare_fusion.5
  556.5 5.1 gather_fusion.1
  561.5 7.0 fusion.32
  568.6 18.8 %scatter_fusion.1 = f32[64,128,512]{2,1,0:T(8,128)} fusion(f32[64,128,512]{2,1,0:T(8,128)} %get-tuple-element.293, s32[32]{0:T(128)S(1)} %get-tuple-element.242, f32[32,128,512]{2,1,0:T(8,128)} %fusion.32), kind=kCustom, calls=%fused_computation.4.clone.1 | custom fusion | flops 2097152 | bytes 25165952 | tf_op jit(solution)/shard_map/while/body/scatter-add | solution.py:48
  587.4 0.7 add_compare_fusion.5
  588.1 5.1 gather_fusion.1
  593.2 7.0 fusion.32
  600.2 18.8 %scatter_fusion.1 = f32[64,128,512]{2,1,0:T(8,128)} fusion(f32[64,128,512]{2,1,0:T(8,128)} %get-tuple-element.293, s32[32]{0:T(128)S(1)} %get-tuple-element.242, f32[32,128,512]{2,1,0:T(8,128)} %fusion.32), kind=kCustom, calls=%fused_computation.4.clone.1 | custom fusion | flops 2097152 | bytes 25165952 | tf_op jit(solution)/shard_map/while/body/scatter-add | solution.py:48
  619.0 0.7 add_compare_fusion.5
  619.8 5.1 gather_fusion.1
  624.9 7.0 fusion.32
  631.9 18.7 %scatter_fusion.1 = f32[64,128,512]{2,1,0:T(8,128)} fusion(f32[64,128,512]{2,1,0:T(8,128)} %get-tuple-element.293, s32[32]{0:T(128)S(1)} %get-tuple-element.242, f32[32,128,512]{2,1,0:T(8,128)} %fusion.32), kind=kCustom, calls=%fused_computation.4.clone.1 | custom fusion | flops 2097152 | bytes 25165952 | tf_op jit(solution)/shard_map/while/body/scatter-add | solution.py:48
  651.4 5.1 gather_fusion.1
  656.5 7.0 fusion.32
  663.5 18.7 %scatter_fusion.1 = f32[64,128,512]{2,1,0:T(8,128)} fusion(f32[64,128,512]{2,1,0:T(8,128)} %get-tuple-element.293, s32[32]{0:T(128)S(1)} %get-tuple-element.242, f32[32,128,512]{2,1,0:T(8,128)} %fusion.32), kind=kCustom, calls=%fused_computation.4.clone.1 | custom fusion | flops 2097152 | bytes 25165952 | tf_op jit(solution)/shard_map/while/body/scatter-add | solution.py:48
  682.3 93.8 %reduce-scatter.2.cloned.1.call-done = f32[512,512]{1,0:T(8,128)} async-done(((f32[8192,512]{1,0:T(8,128)}), f32[512,512]{1,0:T(8,128)}) %reduce-scatter.2.cloned.1.call-update) | async-done | bytes 1048592 | tf_op jit(solution)/shard_map/reduce_scatter | solution.py:81
  776.1 3.3 fusion.14
  779.4 2.3 multiply_convert_fusion.1
  781.7 147.2 %all-reduce.5.cloned.1.call-done = f32[512,512]{1,0:T(8,128)} async-done(((f32[512,512]{1,0:T(8,128)}), f32[512,512]{1,0:T(8,128)}) %all-reduce.5.cloned.1.call-update) | async-done | bytes 1048592 | tf_op jit(solution)/shard_map/psum | solution.py:88
  928.9 2.3 broadcast_multiply_fusion
  (50 shorter events, 2.2 us)
Async XLA Ops:
  7.2 4.6 copy-start
  7.2 83.3 %all-gather.2.cloned.1.call-start = ((), (), s32[]{:S(2)}) async-start(), calls=%async_computation.2 | async-start | bytes 8912896 | tf_op jit(solution)/shard_map/all_gather | solution.py:69
  11.7 83.0 %copy-start.4 = (s32[1,1,192]{2,1,0:T(1,128)S(1)}, s32[1,1,192]{2,1,0:T(1,128)}, u32[]{:S(2)}) copy-start(s32[1,1,192]{2,1,0:T(1,128)} %param.16) | copy-start | bytes 2308
  11.8 83.0 %copy-start.5 = (s32[1,1,192]{2,1,0:T(1,128)S(1)}, s32[1,1,192]{2,1,0:T(1,128)}, u32[]{:S(2)}) copy-start(s32[1,1,192]{2,1,0:T(1,128)} %param.17) | copy-start | bytes 2308
  37.9 56.9 %copy-start.2 = (bf16[512,512]{1,0:T(8,128)(2,1)}, bf16[512,512]{1,0:T(8,128)(2,1)S(1)}, u32[]{:S(2)}) copy-start(bf16[512,512]{1,0:T(8,128)(2,1)S(1)} %reshape.49) | copy-start | bytes 1572868
  40.4 436.5 %all-reduce.3.cloned.1.call-start = ((), (), s32[]{:S(2)}) async-start(), calls=%async_computation.3 | async-start | bytes 16777216 | tf_op jit(solution)/shard_map/psum | solution.py:74
  290.4 485.6 %reduce-scatter.2.cloned.1.call-start = ((), (), s32[]{:S(2)}) async-start(), calls=%async_computation.4 | async-start | bytes 17825792 | tf_op jit(solution)/shard_map/reduce_scatter | solution.py:81
  682.2 249.0 %copy-start.1 = (bf16[512,512]{1,0:T(8,128)(2,1)S(1)}, bf16[512,512]{1,0:T(8,128)(2,1)}, u32[]{:S(2)}) copy-start(bf16[512,512]{1,0:T(8,128)(2,1)} %param.12) | copy-start | bytes 1572868
  682.2 93.9 %copy-start.3 = (bf16[512,512]{1,0:T(8,128)(2,1)S(1)}, bf16[512,512]{1,0:T(8,128)(2,1)}, u32[]{:S(2)}) copy-start(bf16[512,512]{1,0:T(8,128)(2,1)} %copy-done.2) | copy-start | bytes 1572868
  682.2 246.7 %all-reduce.5.cloned.1.call-start = ((), (), s32[]{:S(2)}) async-start(), calls=%async_computation.5 | async-start | bytes 2097152 | tf_op jit(solution)/shard_map/psum | solution.py:88
Sparse Core Ops, SparseCore 0:
  40.5 49.9 all-gather.1
  290.5 186.2 all-reduce.2
  682.3 93.6 reduce-scatter.1
  781.3 147.5 all-reduce.4
where the time goes:
time: 939 us; the launch traced here: 938 us
  waiting for transfers between devices  468 us (50%)
  other arithmetic  251 us (27%)
  local copies, waits for them, and re-layouts  90.3 us (10%)
  matrix products  89.9 us (10%)
  blocking collectives  23.8 us (3%)
  between operations  14.5 us (2%)
    psum x1, waiting for transfers between devices, shards(): pre = lax.psum(partial_value, 'col')  178 us
    psum x1, waiting for transfers between devices, shards(): lax.psum(local_grad, ('row', 'col'))  147 us
    scatter-add x6, other arithmetic, one_block(): return totals.at[column_part].add(products)  113 us
    scatter-add x6, other arithmetic, one_block(): return totals.at[row_part].add(products)  112 us
    reduce_scatter x1, waiting for transfers between devices, shards(): lax.psum_scatter(back_partial, 'row', scatter_dimension=0, tiled=True)  93.8 us
    all_gather x1, waiting for transfers between devices, shards(): hidden_columns = lax.all_gather(hidden, 'row', axis=0, tiled=True)  49.4 us
    dot_general x6, matrix products, one_block(): jnp.einsum('tij,tjf->tif', tile_block, picked, preferred_element_type=jnp...  42.1 us
    dot_general x6, matrix products, one_block(): jnp.einsum('tij,tif->tjf', tile_block, picked, preferred_element_type=jnp...  42.1 us
  transfers between devices with their start and end apart: 4, of which 4 were waited for; matrix products, arithmetic and copies ran while one was open for 1% of the time, Pallas kernels for 0%

commit v1 on v0

v1 whole, which is shorter than its diff:
```python
import jax
import jax.numpy as jnp
from jax import lax
from jax.experimental import pallas as pl
from jax.experimental.pallas import tpu as pltpu
from jax.sharding import PartitionSpec as P

N_ROW = 16
N_COL = 8
TILE = 128
SLOTS = 512
F = 512
PER_PEER = 4
BF16 = jnp.bfloat16
F32 = jnp.float32
VMEM_LIMIT = 56 * 1024 * 1024


def params():
    return pltpu.CompilerParams(vmem_limit_bytes=VMEM_LIMIT)


def selection(position, rows, columns):
    wanted = lax.broadcasted_iota(jnp.int32, (rows, columns), 0)
    return jnp.where(position == wanted, 1.0, 0.0).astype(BF16)


def group_kernel(part_ref, features_ref, out_ref):
    part = part_ref[...]
    devices = N_ROW * N_COL
    member = jnp.where(
        part == lax.broadcasted_iota(jnp.int32, (devices, SLOTS), 0), 1.0, 0.0
    )
    before = jnp.where(
        lax.broadcasted_iota(jnp.int32, (SLOTS, SLOTS), 0)
        < lax.broadcasted_iota(jnp.int32, (SLOTS, SLOTS), 1),
        1.0,
        0.0,
    ).astype(BF16)
    earlier = jnp.dot(member.astype(BF16), before, preferred_element_type=F32)
    rank = jnp.sum(member * earlier, axis=0, keepdims=True).astype(jnp.int32)
    place = ((part & (N_COL - 1)) * N_ROW + (part >> 3)) * PER_PEER + rank
    pick = selection(place, SLOTS, SLOTS)
    out_ref[...] = jnp.dot(pick, features_ref[...], preferred_element_type=F32).astype(BF16)


def interleave_kernel(arrived_ref, out_ref):
    source = lax.broadcasted_iota(jnp.int32, (1, SLOTS), 1)
    giver, inner = source >> 6, source & 63
    place = (inner >> 2) * (N_COL * PER_PEER) + giver * PER_PEER + (inner & 3)
    pick = selection(place, SLOTS, SLOTS)
    out_ref[...] = jnp.dot(pick, arrived_ref[...], preferred_element_type=F32).astype(BF16)


def tiles_kernel(count_ref, rows_ref, cols_ref, tiles_ref, source_ref, out_ref, total):
    total[...] = jnp.zeros_like(total)

    def one_slot(t, carry):
        r = rows_ref[t]
        u = cols_ref[t]
        block = source_ref[pl.ds((u & 3) * 4, 4), u >> 2].reshape(TILE, F)
        total[r] += jnp.dot(tiles_ref[t], block, preferred_element_type=F32)
        return carry

    lax.fori_loop(0, count_ref[0], one_slot, 0)
    out_ref[...] = total[...].astype(BF16)


def layer_kernel(parts_ref, weight_ref, cotangent_ref, act_ref, grad_ref):
    mixed = parts_ref[0].astype(F32)
    for k in range(1, N_COL):
        mixed = mixed + parts_ref[k].astype(F32)
    high = mixed.astype(BF16)
    low = (mixed - high.astype(F32)).astype(BF16)
    weight = weight_ref[...]
    pre = jnp.dot(high, weight, preferred_element_type=F32) + jnp.dot(
        low, weight, preferred_element_type=F32
    )
    sigmoid = jax.nn.sigmoid(pre)
    act_ref[...] = (pre * sigmoid).astype(BF16)
    slope = (
        cotangent_ref[...].astype(F32) * (sigmoid * (1.0 + pre * (1.0 - sigmoid)))
    ).astype(BF16)
    contract = (((0,), (0,)), ((), ()))
    grad = lax.dot_general(high, slope, contract, preferred_element_type=F32)
    grad = grad + lax.dot_general(low, slope, contract, preferred_element_type=F32)
    grad_ref[...] = grad * (1.0 / 256.0)


def row_moves(move):
    pairs = []
    for yl in range(2):
        for z in range(4):
            for c in range(2):
                a, b, d = move(yl, z, c)
                pairs.append(((yl * 4 + z) * 2 + c, (a * 4 + b) * 2 + d))
    return pairs


def all_moves_y(k):
    pairs = []
    for i in range(N_ROW):
        for j in range(N_COL):
            y = (j // 4) * 2 + i // 8
            to = (y + k) % 4
            pairs.append((i * N_COL + j, ((to % 2) * 8 + i % 8) * N_COL + (to // 2) * 4 + j % 4))
    return pairs


def x_moves(k):
    return [(yh * 4 + x, yh * 4 + (x + k) % 4) for yh in range(2) for x in range(4)]


def scatter4(total, me, axis, moves):
    quarter = total.shape[0] // 4
    parts = total.reshape(4, quarter, F)
    out = lax.dynamic_index_in_dim(parts, me, 0, False)
    got = []
    for k in (2, 1, 3):
        send = lax.dynamic_index_in_dim(parts, (me + k) % 4, 0, False)
        got.append(lax.ppermute(send, axis, moves(k)))
    return ((out + got[0]) + got[1]) + got[2]


def gather4(part, me, axis, moves):
    got = [part] + [lax.ppermute(part, axis, moves(k)) for k in (1, 2, 3)]
    stacked = jnp.stack(got)
    order = (me - jnp.arange(4, dtype=jnp.int32)) % 4
    return stacked[order[0]], stacked[order[1]], stacked[order[2]], stacked[order[3]]


def shards(
    features, partition_of, weight, tile_values, tile_rows, tile_cols, tile_count, out_cotangent
):
    row = lax.axis_index("row")
    col = lax.axis_index("col")
    core, z, yl = row % 2, (row // 2) % 4, row // 8
    x, yh = col % 4, col // 4
    y = yh * 2 + yl
    vmem = pl.BlockSpec(memory_space=pltpu.VMEM)
    smem = pl.BlockSpec(memory_space=pltpu.SMEM)

    grouped = pl.pallas_call(
        group_kernel,
        out_shape=jax.ShapeDtypeStruct((SLOTS, F), BF16),
        compiler_params=params(),
    )(partition_of.reshape(1, SLOTS), features)
    arrived = lax.all_to_all(grouped, "col", split_axis=0, concat_axis=0, tiled=True)
    mine = pl.pallas_call(
        interleave_kernel,
        out_shape=jax.ShapeDtypeStruct((SLOTS, F), BF16),
        compiler_params=params(),
    )(arrived)
    sources = lax.all_gather(mine, "row", axis=0, tiled=True)
    sources = sources.reshape(N_ROW, N_ROW, N_COL * PER_PEER, F)

    partial = pl.pallas_call(
        tiles_kernel,
        in_specs=[smem, smem, smem, vmem, vmem],
        out_specs=vmem,
        out_shape=jax.ShapeDtypeStruct((32, TILE, F), BF16),
        scratch_shapes=[pltpu.VMEM((32, TILE, F), F32)],
        compiler_params=params(),
    )(
        tile_count.reshape(1),
        tile_rows.reshape(-1),
        tile_cols.reshape(-1),
        tile_values.reshape(-1, TILE, TILE),
        sources,
    )
    parts = lax.all_to_all(
        partial.reshape(N_COL * SLOTS, F), "col", split_axis=0, concat_axis=0, tiled=True
    ).reshape(N_COL, SLOTS, F)
    cotangent = lax.dynamic_slice_in_dim(out_cotangent, col * SLOTS, SLOTS, 0)
    activations, grad = pl.pallas_call(
        layer_kernel,
        out_shape=(
            jax.ShapeDtypeStruct((SLOTS, F), BF16),
            jax.ShapeDtypeStruct((F, F), F32),
        ),
        compiler_params=params(),
    )(parts, weight, cotangent)

    z_moves = lambda k: row_moves(lambda yl, z, c: (yl, (z + k) % 4, c))
    swap = row_moves(lambda yl, z, c: (yl, z, 1 - c))
    halves = grad.reshape(2, F // 2, F)
    half = lax.dynamic_index_in_dim(halves, core, 0, False) + lax.ppermute(
        lax.dynamic_index_in_dim(halves, 1 - core, 0, False), "row", swap
    )
    eighth = scatter4(half, x, "col", x_moves)
    piece = scatter4(eighth, z, "row", z_moves)
    a, b, c, d = gather4(piece, y, ("row", "col"), all_moves_y)
    piece = (a + b) + (c + d)
    eighth = jnp.concatenate(gather4(piece, z, "row", z_moves))
    half = jnp.concatenate(gather4(eighth, x, "col", x_moves))
    other = lax.ppermute(half, "row", swap)
    first = jnp.where(core == 0, half, other)
    second = jnp.where(core == 0, other, half)
    return activations, jnp.concatenate([first, second])


def solution(mesh):
    placed = (
        P(("row", "col"), None),
        P(("row", "col")),
        P(),
        P("row", "col", None, None, None),
        P("row", "col", None),
        P("row", "col", None),
        P("row", "col"),
        P("row", None),
    )
    return jax.shard_map(
        shards,
        mesh=mesh,
        in_specs=placed,
        out_specs=(P(("row", "col"), None), P()),
        check_vma=False,
    )
```

time: 939 us -> 271 us (0.29)
  waiting for transfers between devices: 468 us -> 116 us
  other arithmetic: 251 us -> 2.49 us
  matrix products: 89.9 us -> 0 us
  local copies, waits for them, and re-layouts: 90.3 us -> 5.06 us
  Pallas kernels: 0 us -> 52.1 us
  starting transfers between devices: 0.16 us -> 36.1 us
  between operations: 14.5 us -> 37.1 us
    psum x2 -> x0, waiting for transfers between devices: 325 us -> none  [the longest x1 178 us: shards(): pre = lax.psum(partial_value, 'col')]
    scatter-add x12 -> x0, other arithmetic: 225 us -> none  [the longest x6 113 us: one_block(): return totals.at[column_part].add(products)]
    reduce_scatter x1 -> x0, waiting for transfers between devices: 93.8 us -> none  [shards(): lax.psum_scatter(back_partial, 'row', scatter_dimension=0, tiled=True)]
    dot_general x14 -> x0, matrix products: 89.9 us -> none  [the longest x6 42.1 us: one_block(): jnp.einsum('tij,tjf->tif', tile_block, picked, preferred_element_type=jnp...]
    gather x13 -> x0, local copies, waits for them, and re-layouts: 69.3 us -> none  [the longest x6 36.7 us: one_block(): picked = source_tiles[column_part]]
    pallas_call x0 -> x4, Pallas kernels: none -> 52.1 us  [the longest x1 42.1 us: shards(): pl.pallas_call(tiles_kernel, in_specs=[smem, smem, smem, vmem, vmem], out...]
    all_to_all x0 -> x1, waiting for transfers between devices: none -> 47.9 us  [shards(): lax.all_to_all(partial.reshape(N_COL * SLOTS, F), 'col', split_axis=0, co...]
    ppermute x0 -> x17, starting transfers between devices: none -> 31.2 us  [the longest x6 16.9 us: scatter4(): got.append(lax.ppermute(send, axis, moves(k)))]
  transfers between devices with their start and end apart: 4 -> 19, of which waited for: 4 -> 11; matrix products, arithmetic and copies ran while one was open for 1% -> 1% of each run, Pallas kernels for 0% -> 0%
where the time goes in v1:
time: 271 us; the launch traced here: 268 us
  waiting for transfers between devices  116 us (43%)
  Pallas kernels  52.1 us (19%)
  between operations  37.1 us (14%)
  starting transfers between devices  36.1 us (13%)
  blocking collectives  18.2 us (7%)
  local copies, waits for them, and re-layouts  5.06 us (2%)
    all_gather x1, waiting for transfers between devices, shards(): sources = lax.all_gather(mine, 'row', axis=0, tiled=True)  51.5 us
    all_to_all x1, waiting for transfers between devices, shards(): lax.all_to_all(partial.reshape(N_COL * SLOTS, F), 'col', split_axis=0, co...  47.9 us
    pallas_call x1, Pallas kernels, shards(): pl.pallas_call(tiles_kernel, in_specs=[smem, smem, smem, vmem, vmem], out...  42.1 us
    all_to_all x1, blocking collectives, shards(): lax.all_to_all(grouped, 'col', split_axis=0, concat_axis=0, tiled=True)  18.2 us
    ppermute x6, starting transfers between devices, scatter4(): got.append(lax.ppermute(send, axis, moves(k)))  16.9 us
    ppermute x6, waiting for transfers between devices, scatter4(): got.append(lax.ppermute(send, axis, moves(k)))  10.3 us
    ppermute x9, starting transfers between devices, gather4(): got = [part] + [lax.ppermute(part, axis, moves(k)) for k in (1, 2, 3)]  8.26 us
    ppermute x1, starting transfers between devices, shards(): other = lax.ppermute(half, 'row', swap)  5.67 us
  transfers between devices with their start and end apart: 19, of which 11 were waited for; matrix products, arithmetic and copies ran while one was open for 1% of the time, Pallas kernels for 0%

profile of v1, /device:TPU:1, one launch (start us, length us, event | category | flops | bytes accessed | tf_op | source)
XLA Modules:
  0.0 267.6 jit_solution(6023590336924556363)
XLA Ops:
  7.2 0.0 all-gather.2.cloned.1.call-start
  7.2 2.5 shard_map.95
  9.7 18.2 %all_to_all.20 = bf16[8,64,512]{2,1,0:T(8,128)(2,1)} all-to-all(bf16[8,64,512]{2,1,0:T(8,128)(2,1)} %bitcast.89), channel_id=1, replica_groups=mesh['row'=16,'col'=8] {'col'}, dimensions={0} | all-to-all | bytes 1048576 | tf_op jit(solution)/shard_map/all_to_all | solution.py:148
  28.0 2.3 shard_map.96
  30.2 0.0 all-gather.2.cloned.1.call-update
  30.9 51.5 %all-gather.2.cloned.1.call-done = bf16[8192,512]{1,0:T(8,128)(2,1)} async-done(((bf16[512,512]{1,0:T(8,128)(2,1)}), bf16[8192,512]{1,0:T(8,128)(2,1)}) %all-gather.2.cloned.1.call-update) | async-done | bytes 8388624 | tf_op jit(solution)/shard_map/all_gather | solution.py:154
  82.4 42.1 %shard_map.97 = bf16[32,128,512]{2,1,0:T(8,128)(2,1)} custom-call(s32[1]{0:T(128)} %bitcast.82.count_ref, s32[192]{0:T(256)} %bitcast.105, s32[192]{0:T(256)} %bitcast.106, bf16[192,128,128]{2,1,0:T(8,128)(2,1)} %bitcast.85, bf16[16,16,32,512]{3,2,1,0:T(8,128)(2,1)} %bitcast.84), custom_call_target="tpu_custom_call" | custom-call | tf_op jit(solution)/shard_map/pallas_call | solution.py:157
  124.5 4.9 %all-to-all-start.1 = ((bf16[8,512,512]{2,1,0:T(8,128)(2,1)}), bf16[8,512,512]{2,1,0:T(8,128)(2,1)}, u32[]{:S(2)}, u32[]{:S(2)}) async-start(bf16[8,512,512]{2,1,0:T(8,128)(2,1)} %bitcast.83), calls=%async_computation.1 | async-start | bytes 8388608 | tf_op jit(solution)/shard_map/all_to_all | solution.py:171
  129.4 1.9 constant_dynamic-slice_fusion.cotangent_ref
  131.3 47.9 %all-to-all-done.1.parts_ref = bf16[8,512,512]{2,1,0:T(8,128)(2,1)} async-done(((bf16[8,512,512]{2,1,0:T(8,128)(2,1)}), bf16[8,512,512]{2,1,0:T(8,128)(2,1)}, u32[]{:S(2)}, u32[]{:S(2)}) %all-to-all-start.1) | async-done | bytes 4194336 | tf_op jit(solution)/shard_map/all_to_all | solution.py:171
  179.3 5.2 %shard_map.98 = (bf16[512,512]{1,0:T(8,128)(2,1)}, f32[512,512]{1,0:T(8,128)}) custom-call(bf16[8,512,512]{2,1,0:T(8,128)(2,1)} %all-to-all-done.1.parts_ref, bf16[512,512]{1,0:T(8,128)(2,1)} %weight_ref.1, bf16[512,512]{1,0:T(8,128)(2,1)} %constant_dynamic-slice_fusion.cotangent_ref), custom_call_target="tpu_custom_call" | custom-call | tf_op jit(solution)/shard_map/pallas_call | solution.py:175
  184.5 1.1 dynamic-slice_bitcast_fusion
  185.6 0.3 collective-permute-start
  185.9 1.7 collective-permute-done
  187.6 1.1 bitcast_add_fusion
  188.7 13.2 %collective-permute-start.3 = (f32[64,512]{1,0:T(8,128)S(1)}, f32[64,512]{1,0:T(8,128)S(1)}, u32[]{:S(2)}, u32[]{:S(2)}) collective-permute-start(f32[64,512]{1,0:T(8,128)S(1)} %get-tuple-element.13), channel_id=1, source_target_pairs={{0,3},{1,0},{2,1},{3,2},{4,7},{5,4},{6,5},{7,6},{8,11},{9,8},{10,9... | collective-permute-start | bytes 393224 | tf_op jit(solution)/shard_map/ppermute | solution.py:121
  201.9 0.0 collective-permute-start.2
  201.9 1.3 collective-permute-start.1
  203.3 0.7 fusion.10
  203.9 0.5 collective-permute-done.3
  204.4 6.2 %collective-permute-done.2 = f32[64,512]{1,0:T(8,128)S(1)} collective-permute-done((f32[64,512]{1,0:T(8,128)S(1)}, f32[64,512]{1,0:T(8,128)S(1)}, u32[]{:S(2)}, u32[]{:S(2)}) %collective-permute-start.2) | collective-permute-done | bytes 131104 | tf_op jit(solution)/shard_map/ppermute | solution.py:121
  210.6 0.0 collective-permute-done.1
  210.6 1.0 collective-permute-start.6
  211.6 0.6 collective-permute-start.5
  212.2 1.0 collective-permute-start.4
  213.1 0.3 collective-permute-done.6
  213.5 2.1 collective-permute-done.5
  215.6 1.2 collective-permute-done.4
  216.8 2.5 collective-permute-start.9
  219.3 0.3 collective-permute-start.8
  219.6 0.8 collective-permute-start.7
  220.4 0.7 fusion.9
  235.9 0.0 collective-permute-done.9
  235.9 0.0 collective-permute-done.8
  235.9 0.0 collective-permute-done.7
  235.9 2.0 collective-permute-start.12
  237.9 0.6 collective-permute-start.11
  238.5 0.6 collective-permute-start.10
  239.1 0.0 collective-permute-done.12
  239.1 3.1 %collective-permute-done.11 = f32[16,512]{1,0:T(8,128)S(1)} collective-permute-done((f32[16,512]{1,0:T(8,128)S(1)}, f32[16,512]{1,0:T(8,128)S(1)}, u32[]{:S(2)}, u32[]{:S(2)}) %collective-permute-start.11) | collective-permute-done | bytes 32800 | tf_op jit(solution)/shard_map/ppermute | solution.py:126
  242.2 0.3 collective-permute-done.10
  242.6 0.1 collective-permute-start.15
  242.7 0.4 collective-permute-start.14
  243.1 1.0 collective-permute-start.13
  244.2 0.7 fusion.8
  252.2 0.0 collective-permute-done.15
  252.2 0.0 collective-permute-done.14
  252.2 0.0 collective-permute-done.13
  252.4 5.7 %collective-permute-start.16 = (f32[256,512]{1,0:T(8,128)S(1)}, f32[256,512]{1,0:T(8,128)S(1)}, u32[]{:S(2)}, u32[]{:S(2)}) collective-permute-start(f32[256,512]{1,0:T(8,128)S(1)} %pad_maximum_fusion.2), channel_id=1, source_target_pairs={{0,8},{8,0},{16,24},{24,16},{32,40},{40,32},{48,56},{56,48},{64,72... | collective-permute-start | bytes 1572872 | tf_op jit(solution)/shard_map/ppermute | solution.py:196
  258.0 1.5 collective-permute-done.16
  259.6 0.1 broadcast_select_fusion.1
  259.7 1.0 pad_maximum_fusion
  (15 shorter events, 0.3 us)
Async XLA Ops:
  7.2 75.2 %all-gather.2.cloned.1.call-start = ((), (), s32[]{:S(2)}) async-start(), calls=%async_computation.2 | async-start | bytes 8912896 | tf_op jit(solution)/shard_map/all_gather | solution.py:154
  124.5 54.8 %all-to-all-start.1 = ((bf16[8,512,512]{2,1,0:T(8,128)(2,1)}), bf16[8,512,512]{2,1,0:T(8,128)(2,1)}, u32[]{:S(2)}, u32[]{:S(2)}) async-start(bf16[8,512,512]{2,1,0:T(8,128)(2,1)} %bitcast.83), calls=%async_computation.1 | async-start | bytes 8388608 | tf_op jit(solution)/shard_map/all_to_all | solution.py:171
  185.6 2.0 collective-permute-start
  188.7 15.7 %collective-permute-start.3 = (f32[64,512]{1,0:T(8,128)S(1)}, f32[64,512]{1,0:T(8,128)S(1)}, u32[]{:S(2)}, u32[]{:S(2)}) collective-permute-start(f32[64,512]{1,0:T(8,128)S(1)} %get-tuple-element.13), channel_id=1, source_target_pairs={{0,3},{1,0},{2,1},{3,2},{4,7},{5,4},{6,5},{7,6},{8,11},{9,8},{10,9... | collective-permute-start | bytes 393224 | tf_op jit(solution)/shard_map/ppermute | solution.py:121
  201.9 8.7 %collective-permute-start.2 = (f32[64,512]{1,0:T(8,128)S(1)}, f32[64,512]{1,0:T(8,128)S(1)}, u32[]{:S(2)}, u32[]{:S(2)}) collective-permute-start(f32[64,512]{1,0:T(8,128)S(1)} %get-tuple-element.14), channel_id=1, source_target_pairs={{0,1},{1,2},{2,3},{3,0},{4,5},{5,6},{6,7},{7,4},{8,9},{9,10},{10,1... | collective-permute-start | bytes 393224 | tf_op jit(solution)/shard_map/ppermute | solution.py:121
  201.9 8.7 %collective-permute-start.1 = (f32[64,512]{1,0:T(8,128)S(1)}, f32[64,512]{1,0:T(8,128)S(1)}, u32[]{:S(2)}, u32[]{:S(2)}) collective-permute-start(f32[64,512]{1,0:T(8,128)S(1)} %get-tuple-element.12), channel_id=1, source_target_pairs={{0,2},{1,3},{2,0},{3,1},{4,6},{5,7},{6,4},{7,5},{8,10},{9,11},{10,... | collective-permute-start | bytes 393224 | tf_op jit(solution)/shard_map/ppermute | solution.py:121
  210.6 2.8 %collective-permute-start.6 = (f32[16,512]{1,0:T(8,128)S(1)}, f32[16,512]{1,0:T(8,128)S(1)}, u32[]{:S(2)}, u32[]{:S(2)}) collective-permute-start(f32[16,512]{1,0:T(8,128)S(1)} %get-tuple-element.22), channel_id=1, source_target_pairs={{0,48},{8,56},{16,0},{24,8},{32,16},{40,24},{48,32},{56,40},{64,11... | collective-permute-start | bytes 98312 | tf_op jit(solution)/shard_map/ppermute | solution.py:121
  211.6 4.0 %collective-permute-start.5 = (f32[16,512]{1,0:T(8,128)S(1)}, f32[16,512]{1,0:T(8,128)S(1)}, u32[]{:S(2)}, u32[]{:S(2)}) collective-permute-start(f32[16,512]{1,0:T(8,128)S(1)} %get-tuple-element.23), channel_id=1, source_target_pairs={{0,16},{8,24},{16,32},{24,40},{32,48},{40,56},{48,0},{56,8},{64,80... | collective-permute-start | bytes 98312 | tf_op jit(solution)/shard_map/ppermute | solution.py:121
  212.2 4.6 %collective-permute-start.4 = (f32[16,512]{1,0:T(8,128)S(1)}, f32[16,512]{1,0:T(8,128)S(1)}, u32[]{:S(2)}, u32[]{:S(2)}) collective-permute-start(f32[16,512]{1,0:T(8,128)S(1)} %get-tuple-element.21), channel_id=1, source_target_pairs={{0,32},{8,40},{16,48},{24,56},{32,0},{40,8},{48,16},{56,24},{64,96... | collective-permute-start | bytes 98312 | tf_op jit(solution)/shard_map/ppermute | solution.py:121
  216.8 19.1 %collective-permute-start.9 = (f32[16,512]{1,0:T(8,128)S(1)}, f32[16,512]{1,0:T(8,128)S(1)}, u32[]{:S(2)}, u32[]{:S(2)}) collective-permute-start(f32[16,512]{1,0:T(8,128)S(1)} %fusion.3), channel_id=1, source_target_pairs={{0,68},{1,69},{2,70},{3,71},{4,64},{5,65},{6,66},{7,67},{8,76},{9,... | collective-permute-start | bytes 98312 | tf_op jit(solution)/shard_map/ppermute | solution.py:126
  219.3 16.5 %collective-permute-start.8 = (f32[16,512]{1,0:T(8,128)S(1)}, f32[16,512]{1,0:T(8,128)S(1)}, u32[]{:S(2)}, u32[]{:S(2)}) collective-permute-start(f32[16,512]{1,0:T(8,128)S(1)} %fusion.3), channel_id=1, source_target_pairs={{0,4},{1,5},{2,6},{3,7},{4,0},{5,1},{6,2},{7,3},{8,12},{9,13},{10,... | collective-permute-start | bytes 98312 | tf_op jit(solution)/shard_map/ppermute | solution.py:126
  219.6 16.2 %collective-permute-start.7 = (f32[16,512]{1,0:T(8,128)S(1)}, f32[16,512]{1,0:T(8,128)S(1)}, u32[]{:S(2)}, u32[]{:S(2)}) collective-permute-start(f32[16,512]{1,0:T(8,128)S(1)} %fusion.3), channel_id=1, source_target_pairs={{0,64},{1,65},{2,66},{3,67},{4,68},{5,69},{6,70},{7,71},{8,72},{9,... | collective-permute-start | bytes 98312 | tf_op jit(solution)/shard_map/ppermute | solution.py:126
  235.9 3.1 %collective-permute-start.12 = (f32[16,512]{1,0:T(8,128)S(1)}, f32[16,512]{1,0:T(8,128)S(1)}, u32[]{:S(2)}, u32[]{:S(2)}) collective-permute-start(f32[16,512]{1,0:T(8,128)S(1)} %fusion.11), channel_id=1, source_target_pairs={{0,48},{8,56},{16,0},{24,8},{32,16},{40,24},{48,32},{56,40},{64,11... | collective-permute-start | bytes 98312 | tf_op jit(solution)/shard_map/ppermute | solution.py:126
  237.9 4.3 %collective-permute-start.11 = (f32[16,512]{1,0:T(8,128)S(1)}, f32[16,512]{1,0:T(8,128)S(1)}, u32[]{:S(2)}, u32[]{:S(2)}) collective-permute-start(f32[16,512]{1,0:T(8,128)S(1)} %fusion.11), channel_id=1, source_target_pairs={{0,32},{8,40},{16,48},{24,56},{32,0},{40,8},{48,16},{56,24},{64,96... | collective-permute-start | bytes 98312 | tf_op jit(solution)/shard_map/ppermute | solution.py:126
  238.5 4.1 %collective-permute-start.10 = (f32[16,512]{1,0:T(8,128)S(1)}, f32[16,512]{1,0:T(8,128)S(1)}, u32[]{:S(2)}, u32[]{:S(2)}) collective-permute-start(f32[16,512]{1,0:T(8,128)S(1)} %fusion.11), channel_id=1, source_target_pairs={{0,16},{8,24},{16,32},{24,40},{32,48},{40,56},{48,0},{56,8},{64,80... | collective-permute-start | bytes 98312 | tf_op jit(solution)/shard_map/ppermute | solution.py:126
  242.6 9.6 %collective-permute-start.15 = (f32[64,512]{1,0:T(8,128)S(1)}, f32[64,512]{1,0:T(8,128)S(1)}, u32[]{:S(2)}, u32[]{:S(2)}) collective-permute-start(f32[64,512]{1,0:T(8,128)S(1)} %get-tuple-element.16), channel_id=1, source_target_pairs={{0,3},{1,0},{2,1},{3,2},{4,7},{5,4},{6,5},{7,6},{8,11},{9,8},{10,9... | collective-permute-start | bytes 393224 | tf_op jit(solution)/shard_map/ppermute | solution.py:126
  242.7 9.5 %collective-permute-start.14 = (f32[64,512]{1,0:T(8,128)S(1)}, f32[64,512]{1,0:T(8,128)S(1)}, u32[]{:S(2)}, u32[]{:S(2)}) collective-permute-start(f32[64,512]{1,0:T(8,128)S(1)} %get-tuple-element.16), channel_id=1, source_target_pairs={{0,2},{1,3},{2,0},{3,1},{4,6},{5,7},{6,4},{7,5},{8,10},{9,11},{10,... | collective-permute-start | bytes 393224 | tf_op jit(solution)/shard_map/ppermute | solution.py:126
  243.1 9.1 %collective-permute-start.13 = (f32[64,512]{1,0:T(8,128)S(1)}, f32[64,512]{1,0:T(8,128)S(1)}, u32[]{:S(2)}, u32[]{:S(2)}) collective-permute-start(f32[64,512]{1,0:T(8,128)S(1)} %get-tuple-element.16), channel_id=1, source_target_pairs={{0,1},{1,2},{2,3},{3,0},{4,5},{5,6},{6,7},{7,4},{8,9},{9,10},{10,1... | collective-permute-start | bytes 393224 | tf_op jit(solution)/shard_map/ppermute | solution.py:126
  252.4 7.2 %collective-permute-start.16 = (f32[256,512]{1,0:T(8,128)S(1)}, f32[256,512]{1,0:T(8,128)S(1)}, u32[]{:S(2)}, u32[]{:S(2)}) collective-permute-start(f32[256,512]{1,0:T(8,128)S(1)} %pad_maximum_fusion.2), channel_id=1, source_target_pairs={{0,8},{8,0},{16,24},{24,16},{32,40},{40,32},{48,56},{56,48},{64,72... | collective-permute-start | bytes 1572872 | tf_op jit(solution)/shard_map/ppermute | solution.py:196
Sparse Core Ops, SparseCore 0:
  30.4 51.9 all-gather.1

commit v2 on v1

--- a/solution.py
+++ b/solution.py
@@ -11,6 +11,11 @@
 SLOTS = 512
 F = 512
 PER_PEER = 4
+SLOT_CAP = 192
+ROW_TILES = 32
+GROUP_BITS = 2
+GROUP = 1 << GROUP_BITS
+PLAN = SLOT_CAP + ROW_TILES * (GROUP - 1)
 BF16 = jnp.bfloat16
 F32 = jnp.float32
 VMEM_LIMIT = 56 * 1024 * 1024
@@ -52,17 +57,75 @@
     out_ref[...] = jnp.dot(pick, arrived_ref[...], preferred_element_type=F32).astype(BF16)
 
 
-def tiles_kernel(count_ref, rows_ref, cols_ref, tiles_ref, source_ref, out_ref, total):
+def plan_kernel(count_ref, rows_ref, cols_ref, plan_ref):
+    slot = lax.broadcasted_iota(jnp.int32, (1, SLOT_CAP), 1)
+    rows = rows_ref[...]
+    live = slot < count_ref[0]
+    kinds = lax.broadcasted_iota(jnp.int32, (ROW_TILES, SLOT_CAP), 0)
+    member = jnp.where(live & (rows == kinds), 1.0, 0.0)
+    before = jnp.where(
+        lax.broadcasted_iota(jnp.int32, (SLOT_CAP, SLOT_CAP), 0)
+        < lax.broadcasted_iota(jnp.int32, (SLOT_CAP, SLOT_CAP), 1),
+        1.0,
+        0.0,
+    ).astype(BF16)
+    earlier = jnp.dot(member.astype(BF16), before, preferred_element_type=F32)
+    number = jnp.sum(member, axis=1, keepdims=True).astype(jnp.int32)
+    groups = jnp.broadcast_to((number + (GROUP - 1)) >> GROUP_BITS, (ROW_TILES, TILE))
+    below = jnp.where(
+        lax.broadcasted_iota(jnp.int32, (ROW_TILES, ROW_TILES), 1)
+        < lax.broadcasted_iota(jnp.int32, (ROW_TILES, ROW_TILES), 0),
+        1.0,
+        0.0,
+    ).astype(BF16)
+    groups = groups.astype(F32)
+    start = jnp.dot(below, groups.astype(BF16), preferred_element_type=F32)[:, :1]
+    total = jnp.sum(groups, axis=0, keepdims=True)[:, :1]
+    place = jnp.sum(member * (GROUP * start + earlier + 1.0), axis=0, keepdims=True) - 1.0
+    taken = selection(place.astype(jnp.int32), PLAN, SLOT_CAP)
+    line = lax.broadcasted_iota(jnp.int32, (8, SLOT_CAP), 0)
+    values = jnp.where(line == 0, slot - SLOT_CAP, jnp.where(line == 1, cols_ref[...], rows))
+    found = lax.dot_general(
+        values.astype(F32).astype(BF16),
+        taken,
+        (((1,), (1,)), ((), ())),
+        preferred_element_type=F32,
+    )
+    line = lax.broadcasted_iota(jnp.int32, (8, PLAN), 0)
+    found = jnp.where(line == 0, found + SLOT_CAP, jnp.where(line == 3, total, found))
+    plan_ref[...] = found.astype(jnp.int32)
+
+
+def tiles_kernel(plan_ref, tiles_hbm, source_hbm, out_ref, tiles, source, total, sems):
+    tiles_copy = pltpu.make_async_copy(tiles_hbm, tiles.at[pl.ds(0, SLOT_CAP)], sems.at[0])
+    source_copy = pltpu.make_async_copy(source_hbm, source, sems.at[1])
+    tiles_copy.start()
+    source_copy.start()
+    tiles[SLOT_CAP] = jnp.zeros((TILE, TILE), BF16)
     total[...] = jnp.zeros_like(total)
-
-    def one_slot(t, carry):
-        r = rows_ref[t]
-        u = cols_ref[t]
-        block = source_ref[pl.ds((u & 3) * 4, 4), u >> 2].reshape(TILE, F)
-        total[r] += jnp.dot(tiles_ref[t], block, preferred_element_type=F32)
+    tiles_copy.wait()
+    source_copy.wait()
+
+    def product(g):
+        left, right = [], []
+        for e in range(GROUP):
+            u = plan_ref[1, g * GROUP + e]
+            left.append(tiles[plan_ref[0, g * GROUP + e]])
+            right.append(source[pl.ds((u & 3) * 4, 4), u >> 2].reshape(TILE, F))
+        return jnp.dot(
+            jnp.concatenate(left, axis=1),
+            jnp.concatenate(right, axis=0),
+            preferred_element_type=F32,
+        )
+
+    def two_groups(h, carry):
+        g = h * 2
+        first, second = product(g), product(g + 1)
+        total[plan_ref[2, g * GROUP]] += first
+        total[plan_ref[2, g * GROUP + GROUP]] += second
         return carry
 
-    lax.fori_loop(0, count_ref[0], one_slot, 0)
+    lax.fori_loop(0, (plan_ref[3, 0] + 1) >> 1, two_groups, 0)
     out_ref[...] = total[...].astype(BF16)
 
 
@@ -115,18 +178,15 @@
     quarter = total.shape[0] // 4
     parts = total.reshape(4, quarter, F)
     out = lax.dynamic_index_in_dim(parts, me, 0, False)
-    got = []
     for k in (2, 1, 3):
-        send = lax.dynamic_index_in_dim(parts, (me + k) % 4, 0, False)
-        got.append(lax.ppermute(send, axis, moves(k)))
-    return ((out + got[0]) + got[1]) + got[2]
-
-
-def gather4(part, me, axis, moves):
-    got = [part] + [lax.ppermute(part, axis, moves(k)) for k in (1, 2, 3)]
-    stacked = jnp.stack(got)
-    order = (me - jnp.arange(4, dtype=jnp.int32)) % 4
-    return stacked[order[0]], stacked[order[1]], stacked[order[2]], stacked[order[3]]
+        send = lax.dynamic_index_in_dim(parts, (me + k) % 4, 0, False).astype(BF16)
+        out = out + lax.ppermute(send, axis, moves(k)).astype(F32)
+    return out
+
+
+def by_giver(own, me, axis, moves):
+    got = jnp.stack([own] + [lax.ppermute(own, axis, moves(k)) for k in (1, 2, 3)])
+    return [got[(me - k) % 4] for k in range(4)]
 
 
 def shards(
@@ -140,6 +200,14 @@
     vmem = pl.BlockSpec(memory_space=pltpu.VMEM)
     smem = pl.BlockSpec(memory_space=pltpu.SMEM)
 
+    hbm = pl.BlockSpec(memory_space=pl.ANY)
+    plan = pl.pallas_call(
+        plan_kernel,
+        in_specs=[smem, vmem, vmem],
+        out_specs=vmem,
+        out_shape=jax.ShapeDtypeStruct((8, PLAN), jnp.int32),
+        compiler_params=params(),
+    )(tile_count.reshape(1), tile_rows.reshape(1, -1), tile_cols.reshape(1, -1))
     grouped = pl.pallas_call(
         group_kernel,
         out_shape=jax.ShapeDtypeStruct((SLOTS, F), BF16),
@@ -156,18 +224,17 @@
 
     partial = pl.pallas_call(
         tiles_kernel,
-        in_specs=[smem, smem, smem, vmem, vmem],
+        in_specs=[smem, hbm, hbm],
         out_specs=vmem,
-        out_shape=jax.ShapeDtypeStruct((32, TILE, F), BF16),
-        scratch_shapes=[pltpu.VMEM((32, TILE, F), F32)],
-        compiler_params=params(),
-    )(
-        tile_count.reshape(1),
-        tile_rows.reshape(-1),
-        tile_cols.reshape(-1),
-        tile_values.reshape(-1, TILE, TILE),
-        sources,
-    )
+        out_shape=jax.ShapeDtypeStruct((ROW_TILES, TILE, F), BF16),
+        scratch_shapes=[
+            pltpu.VMEM((SLOT_CAP + 1, TILE, TILE), BF16),
+            pltpu.VMEM((N_ROW, N_ROW, N_COL * PER_PEER, F), BF16),
+            pltpu.VMEM((ROW_TILES, TILE, F), F32),
+            pltpu.SemaphoreType.DMA((2,)),
+        ],
+        compiler_params=params(),
+    )(plan, tile_values.reshape(-1, TILE, TILE), sources)
     parts = lax.all_to_all(
         partial.reshape(N_COL * SLOTS, F), "col", split_axis=0, concat_axis=0, tiled=True
     ).reshape(N_COL, SLOTS, F)
@@ -188,14 +255,14 @@
         lax.dynamic_index_in_dim(halves, 1 - core, 0, False), "row", swap
     )
     eighth = scatter4(half, x, "col", x_moves)
-    piece = scatter4(eighth, z, "row", z_moves)
-    a, b, c, d = gather4(piece, y, ("row", "col"), all_moves_y)
-    piece = (a + b) + (c + d)
-    eighth = jnp.concatenate(gather4(piece, z, "row", z_moves))
-    half = jnp.concatenate(gather4(eighth, x, "col", x_moves))
+    a, b, c, d = by_giver(eighth, z, "row", z_moves)
+    eighth = (a + b) + (c + d)
+    a, b, c, d = by_giver(eighth, y, ("row", "col"), all_moves_y)
+    eighth = (a + b) + (c + d)
+    half = jnp.concatenate(by_giver(eighth.astype(BF16), x, "col", x_moves))
     other = lax.ppermute(half, "row", swap)
-    first = jnp.where(core == 0, half, other)
-    second = jnp.where(core == 0, other, half)
+    first = jnp.where(core == 0, half, other).astype(F32)
+    second = jnp.where(core == 0, other, half).astype(F32)
     return activations, jnp.concatenate([first, second])
 
 

time: 271 us -> 229 us (0.85); the launches traced: 268 us -> 229 us
  Pallas kernels: 52.1 us -> 26.2 us
  between operations: 37.1 us -> 14.8 us
  waiting for transfers between devices: 116 us -> 128 us
    pallas_call x1 -> x2, Pallas kernels: 42.1 us -> 16.1 us  [the longest x1 14.4 us: shards(): pl.pallas_call(tiles_kernel, in_specs=[smem, hbm, hbm], out_specs=vmem, o...]
    ppermute x15 -> x12, waiting for transfers between devices: 13.8 us -> 26.7 us  [the longest x9 21.7 us: by_giver(): lax.ppermute(own, axis, moves(k))]
    ppermute x1, starting transfers between devices: 5.67 us -> 1.49 us  [shards(): other = lax.ppermute(half, 'row', swap)]
    ppermute x15 -> x12, starting transfers between devices: 25.2 us -> 25.9 us  [the longest x9 19.6 us: by_giver(): lax.ppermute(own, axis, moves(k))]
  transfers between devices with their start and end apart: 19 -> 16, of which waited for: 11 -> 14; matrix products, arithmetic and copies ran while one was open for 1% -> 1% of each run, Pallas kernels for 0% -> 1%
where the time goes in v2:
time: 229 us
  waiting for transfers between devices  128 us (56%)
  starting transfers between devices  35.5 us (16%)
  Pallas kernels  26.2 us (11%)
  blocking collectives  18.2 us (8%)
  between operations  14.8 us (6%)
  local copies, waits for them, and re-layouts  3.02 us (1%)
  other arithmetic  2.64 us (1%)
    all_gather x1, waiting for transfers between devices, shards(): sources = lax.all_gather(mine, 'row', axis=0, tiled=True)  49.7 us
    all_to_all x1, waiting for transfers between devices, shards(): lax.all_to_all(partial.reshape(N_COL * SLOTS, F), 'col', split_axis=0, co...  49.2 us
    ppermute x9, waiting for transfers between devices, by_giver(): lax.ppermute(own, axis, moves(k))  21.7 us
    ppermute x9, starting transfers between devices, by_giver(): lax.ppermute(own, axis, moves(k))  19.6 us
    all_to_all x1, blocking collectives, shards(): lax.all_to_all(grouped, 'col', split_axis=0, concat_axis=0, tiled=True)  18.2 us
    pallas_call x1, Pallas kernels, shards(): pl.pallas_call(tiles_kernel, in_specs=[smem, hbm, hbm], out_specs=vmem, o...  14.4 us
    all_to_all x1, starting transfers between devices, shards(): lax.all_to_all(partial.reshape(N_COL * SLOTS, F), 'col', split_axis=0, co...  7.13 us
    ppermute x3, starting transfers between devices, scatter4(): out = out + lax.ppermute(send, axis, moves(k)).astype(F32)  6.33 us
  transfers between devices with their start and end apart: 16, of which 14 were waited for; matrix products, arithmetic and copies ran while one was open for 1% of the time, Pallas kernels for 1%

profile of v2, /device:TPU:1, one launch (start us, length us, event | category | flops | bytes accessed | tf_op | source)
XLA Modules:
  0.0 228.7 jit_solution(16059780823415857787)
XLA Ops:
  7.2 0.0 all-gather.2.cloned.1.call-start
  7.2 2.5 %shard_map.96 = bf16[512,512]{1,0:T(8,128)(2,1)} custom-call(s32[1,512]{1,0:T(1,128)} %bitcast.69, bf16[512,512]{1,0:T(8,128)(2,1)} %features_ref.1), custom_call_target="tpu_custom_call" | custom-call | tf_op jit(solution)/shard_map/pallas_call | solution.py:211
  9.7 18.2 %all_to_all.20 = bf16[8,64,512]{2,1,0:T(8,128)(2,1)} all-to-all(bf16[8,64,512]{2,1,0:T(8,128)(2,1)} %bitcast.54), channel_id=1, replica_groups=mesh['row'=16,'col'=8] {'col'}, dimensions={0} | all-to-all | bytes 1048576 | tf_op jit(solution)/shard_map/all_to_all | solution.py:216
  28.0 2.3 shard_map.97
  30.2 0.0 all-gather.2.cloned.1.call-update
  30.9 1.8 shard_map.95.plan_ref
  32.7 49.7 %all-gather.2.cloned.1.call-done = bf16[8192,512]{1,0:T(8,128)(2,1)} async-done(((bf16[512,512]{1,0:T(8,128)(2,1)}), bf16[8192,512]{1,0:T(8,128)(2,1)}) %all-gather.2.cloned.1.call-update) | async-done | bytes 8388624 | tf_op jit(solution)/shard_map/all_gather | solution.py:222
  82.4 14.4 %shard_map.98 = bf16[32,128,512]{2,1,0:T(8,128)(2,1)} custom-call(s32[8,288]{1,0:T(8,128)} %shard_map.95.plan_ref, bf16[192,128,128]{2,1,0:T(8,128)(2,1)} %bitcast.52, bf16[16,16,32,512]{3,2,1,0:T(8,128)(2,1)} %bitcast.51), custom_call_target="tpu_custom_call" | custom-call | tf_op jit(solution)/shard_map/pallas_call | solution.py:225
  96.8 7.1 %all-to-all-start.1 = ((bf16[8,512,512]{2,1,0:T(8,128)(2,1)}), bf16[8,512,512]{2,1,0:T(8,128)(2,1)}, u32[]{:S(2)}, u32[]{:S(2)}) async-start(bf16[8,512,512]{2,1,0:T(8,128)(2,1)} %bitcast.50), calls=%async_computation.1 | async-start | bytes 8388608 | tf_op jit(solution)/shard_map/all_to_all | solution.py:238
  103.9 1.9 constant_dynamic-slice_fusion.cotangent_ref
  105.8 49.2 %all-to-all-done.1.parts_ref = bf16[8,512,512]{2,1,0:T(8,128)(2,1)} async-done(((bf16[8,512,512]{2,1,0:T(8,128)(2,1)}), bf16[8,512,512]{2,1,0:T(8,128)(2,1)}, u32[]{:S(2)}, u32[]{:S(2)}) %all-to-all-start.1) | async-done | bytes 4194336 | tf_op jit(solution)/shard_map/all_to_all | solution.py:238
  155.0 5.3 %shard_map.99 = (bf16[512,512]{1,0:T(8,128)(2,1)}, f32[512,512]{1,0:T(8,128)}) custom-call(bf16[8,512,512]{2,1,0:T(8,128)(2,1)} %all-to-all-done.1.parts_ref, bf16[512,512]{1,0:T(8,128)(2,1)} %weight_ref.1, bf16[512,512]{1,0:T(8,128)(2,1)} %constant_dynamic-slice_fusion.cotangent_ref), custom_call_target="tpu_custom_call" | custom-call | tf_op jit(solution)/shard_map/pallas_call | solution.py:242
  160.3 1.1 dynamic-slice_bitcast_fusion
  161.3 0.9 collective-permute-start
  162.3 1.5 collective-permute-done
  163.8 1.1 bitcast_add_fusion
  165.0 5.1 %collective-permute-start.3 = (bf16[64,512]{1,0:T(8,128)(2,1)S(1)}, bf16[64,512]{1,0:T(8,128)(2,1)S(1)}, u32[]{:S(2)}, u32[]{:S(2)}) collective-permute-start(bf16[64,512]{1,0:T(8,128)(2,1)S(1)} %get-tuple-element.9), channel_id=1, source_target_pairs={{0,3},{1,0},{2,1},{3,2},{4,7},{5,4},{6,5},{7,6},{8,11},{9,8},{10,9... | collective-permute-start | bytes 196616 | tf_op jit(solution)/shard_map/ppermute | solution.py:183
  170.1 0.0 collective-permute-start.2
  170.1 1.3 collective-permute-start.1
  171.3 0.1 collective-permute-done.3
  171.4 5.0 %collective-permute-done.2 = bf16[64,512]{1,0:T(8,128)(2,1)S(1)} collective-permute-done((bf16[64,512]{1,0:T(8,128)(2,1)S(1)}, bf16[64,512]{1,0:T(8,128)(2,1)S(1)}, u32[]{:S(2)}, u32[]{:S(2)}) %collective-permute-start.2) | collective-permute-done | bytes 65568 | tf_op jit(solution)/shard_map/ppermute | solution.py:183
  176.4 0.0 collective-permute-done.1
  176.4 13.3 %collective-permute-start.6 = (f32[64,512]{1,0:T(8,128)S(1)}, f32[64,512]{1,0:T(8,128)S(1)}, u32[]{:S(2)}, u32[]{:S(2)}) collective-permute-start(f32[64,512]{1,0:T(8,128)S(1)} %fusion.1), channel_id=1, source_target_pairs={{0,48},{8,56},{16,0},{24,8},{32,16},{40,24},{48,32},{56,40},{64,11... | collective-permute-start | bytes 393224 | tf_op jit(solution)/shard_map/ppermute | solution.py:188
  189.7 0.0 collective-permute-start.5
  189.7 0.7 collective-permute-start.4
  190.4 4.9 %collective-permute-done.6 = f32[64,512]{1,0:T(8,128)S(1)} collective-permute-done((f32[64,512]{1,0:T(8,128)S(1)}, f32[64,512]{1,0:T(8,128)S(1)}, u32[]{:S(2)}, u32[]{:S(2)}) %collective-permute-start.6) | collective-permute-done | bytes 131104 | tf_op jit(solution)/shard_map/ppermute | solution.py:188
  195.3 0.0 collective-permute-done.5
  195.3 3.5 %collective-permute-done.4 = f32[64,512]{1,0:T(8,128)S(1)} collective-permute-done((f32[64,512]{1,0:T(8,128)S(1)}, f32[64,512]{1,0:T(8,128)S(1)}, u32[]{:S(2)}, u32[]{:S(2)}) %collective-permute-start.4) | collective-permute-done | bytes 131104 | tf_op jit(solution)/shard_map/ppermute | solution.py:188
  198.9 3.4 %collective-permute-start.9 = (f32[64,512]{1,0:T(8,128)S(1)}, f32[64,512]{1,0:T(8,128)S(1)}, u32[]{:S(2)}, u32[]{:S(2)}) collective-permute-start(f32[64,512]{1,0:T(8,128)S(1)} %fusion.6), channel_id=1, source_target_pairs={{0,68},{1,69},{2,70},{3,71},{4,64},{5,65},{6,66},{7,67},{8,76},{9,... | collective-permute-start | bytes 393224 | tf_op jit(solution)/shard_map/ppermute | solution.py:188
  202.3 0.0 collective-permute-start.8
  202.3 0.7 collective-permute-start.7
  203.0 4.5 %collective-permute-done.9 = f32[64,512]{1,0:T(8,128)S(1)} collective-permute-done((f32[64,512]{1,0:T(8,128)S(1)}, f32[64,512]{1,0:T(8,128)S(1)}, u32[]{:S(2)}, u32[]{:S(2)}) %collective-permute-start.9) | collective-permute-done | bytes 131104 | tf_op jit(solution)/shard_map/ppermute | solution.py:188
  207.5 0.5 collective-permute-done.8
  208.0 3.4 %collective-permute-done.7 = f32[64,512]{1,0:T(8,128)S(1)} collective-permute-done((f32[64,512]{1,0:T(8,128)S(1)}, f32[64,512]{1,0:T(8,128)S(1)}, u32[]{:S(2)}, u32[]{:S(2)}) %collective-permute-start.7) | collective-permute-done | bytes 131104 | tf_op jit(solution)/shard_map/ppermute | solution.py:188
  211.5 0.1 collective-permute-start.12
  211.6 0.1 collective-permute-start.11
  211.7 1.4 collective-permute-start.10
  213.1 1.6 collective-permute-done.12
  214.7 1.6 collective-permute-done.11
  216.3 1.6 collective-permute-done.10
  218.0 1.5 collective-permute-start.13
  219.5 1.2 collective-permute-done.13
  220.7 0.1 broadcast_select_fusion.1
  220.8 1.1 maximum_convert_fusion
  (11 shorter events, 0.4 us)
Async XLA Ops:
  7.2 75.2 %all-gather.2.cloned.1.call-start = ((), (), s32[]{:S(2)}) async-start(), calls=%async_computation.2 | async-start | bytes 8912896 | tf_op jit(solution)/shard_map/all_gather | solution.py:222
  96.8 58.2 %all-to-all-start.1 = ((bf16[8,512,512]{2,1,0:T(8,128)(2,1)}), bf16[8,512,512]{2,1,0:T(8,128)(2,1)}, u32[]{:S(2)}, u32[]{:S(2)}) async-start(bf16[8,512,512]{2,1,0:T(8,128)(2,1)} %bitcast.50), calls=%async_computation.1 | async-start | bytes 8388608 | tf_op jit(solution)/shard_map/all_to_all | solution.py:238
  161.3 2.5 %collective-permute-start = (f32[256,512]{1,0:T(8,128)S(1)}, f32[256,512]{1,0:T(8,128)S(1)}, u32[]{:S(2)}, u32[]{:S(2)}) collective-permute-start(f32[256,512]{1,0:T(8,128)S(1)} %dynamic-slice_bitcast_fusion), channel_id=1, source_target_pairs={{0,8},{8,0},{16,24},{24,16},{32,40},{40,32},{48,56},{56,48},{64,72... | collective-permute-start | bytes 1572872 | tf_op jit(solution)/shard_map/ppermute | solution.py:254
  165.0 6.4 %collective-permute-start.3 = (bf16[64,512]{1,0:T(8,128)(2,1)S(1)}, bf16[64,512]{1,0:T(8,128)(2,1)S(1)}, u32[]{:S(2)}, u32[]{:S(2)}) collective-permute-start(bf16[64,512]{1,0:T(8,128)(2,1)S(1)} %get-tuple-element.9), channel_id=1, source_target_pairs={{0,3},{1,0},{2,1},{3,2},{4,7},{5,4},{6,5},{7,6},{8,11},{9,8},{10,9... | collective-permute-start | bytes 196616 | tf_op jit(solution)/shard_map/ppermute | solution.py:183
  170.1 6.3 %collective-permute-start.2 = (bf16[64,512]{1,0:T(8,128)(2,1)S(1)}, bf16[64,512]{1,0:T(8,128)(2,1)S(1)}, u32[]{:S(2)}, u32[]{:S(2)}) collective-permute-start(bf16[64,512]{1,0:T(8,128)(2,1)S(1)} %get-tuple-element.10), channel_id=1, source_target_pairs={{0,1},{1,2},{2,3},{3,0},{4,5},{5,6},{6,7},{7,4},{8,9},{9,10},{10,1... | collective-permute-start | bytes 196616 | tf_op jit(solution)/shard_map/ppermute | solution.py:183
  170.1 6.3 %collective-permute-start.1 = (bf16[64,512]{1,0:T(8,128)(2,1)S(1)}, bf16[64,512]{1,0:T(8,128)(2,1)S(1)}, u32[]{:S(2)}, u32[]{:S(2)}) collective-permute-start(bf16[64,512]{1,0:T(8,128)(2,1)S(1)} %get-tuple-element.8), channel_id=1, source_target_pairs={{0,2},{1,3},{2,0},{3,1},{4,6},{5,7},{6,4},{7,5},{8,10},{9,11},{10,... | collective-permute-start | bytes 196616 | tf_op jit(solution)/shard_map/ppermute | solution.py:183
  176.4 18.9 %collective-permute-start.6 = (f32[64,512]{1,0:T(8,128)S(1)}, f32[64,512]{1,0:T(8,128)S(1)}, u32[]{:S(2)}, u32[]{:S(2)}) collective-permute-start(f32[64,512]{1,0:T(8,128)S(1)} %fusion.1), channel_id=1, source_target_pairs={{0,48},{8,56},{16,0},{24,8},{32,16},{40,24},{48,32},{56,40},{64,11... | collective-permute-start | bytes 393224 | tf_op jit(solution)/shard_map/ppermute | solution.py:188
  189.7 5.6 %collective-permute-start.5 = (f32[64,512]{1,0:T(8,128)S(1)}, f32[64,512]{1,0:T(8,128)S(1)}, u32[]{:S(2)}, u32[]{:S(2)}) collective-permute-start(f32[64,512]{1,0:T(8,128)S(1)} %fusion.1), channel_id=1, source_target_pairs={{0,32},{8,40},{16,48},{24,56},{32,0},{40,8},{48,16},{56,24},{64,96... | collective-permute-start | bytes 393224 | tf_op jit(solution)/shard_map/ppermute | solution.py:188
  189.7 9.1 %collective-permute-start.4 = (f32[64,512]{1,0:T(8,128)S(1)}, f32[64,512]{1,0:T(8,128)S(1)}, u32[]{:S(2)}, u32[]{:S(2)}) collective-permute-start(f32[64,512]{1,0:T(8,128)S(1)} %fusion.1), channel_id=1, source_target_pairs={{0,16},{8,24},{16,32},{24,40},{32,48},{40,56},{48,0},{56,8},{64,80... | collective-permute-start | bytes 393224 | tf_op jit(solution)/shard_map/ppermute | solution.py:188
  198.9 8.6 %collective-permute-start.9 = (f32[64,512]{1,0:T(8,128)S(1)}, f32[64,512]{1,0:T(8,128)S(1)}, u32[]{:S(2)}, u32[]{:S(2)}) collective-permute-start(f32[64,512]{1,0:T(8,128)S(1)} %fusion.6), channel_id=1, source_target_pairs={{0,68},{1,69},{2,70},{3,71},{4,64},{5,65},{6,66},{7,67},{8,76},{9,... | collective-permute-start | bytes 393224 | tf_op jit(solution)/shard_map/ppermute | solution.py:188
  202.3 5.7 %collective-permute-start.8 = (f32[64,512]{1,0:T(8,128)S(1)}, f32[64,512]{1,0:T(8,128)S(1)}, u32[]{:S(2)}, u32[]{:S(2)}) collective-permute-start(f32[64,512]{1,0:T(8,128)S(1)} %fusion.6), channel_id=1, source_target_pairs={{0,4},{1,5},{2,6},{3,7},{4,0},{5,1},{6,2},{7,3},{8,12},{9,13},{10,... | collective-permute-start | bytes 393224 | tf_op jit(solution)/shard_map/ppermute | solution.py:188
  202.3 9.1 %collective-permute-start.7 = (f32[64,512]{1,0:T(8,128)S(1)}, f32[64,512]{1,0:T(8,128)S(1)}, u32[]{:S(2)}, u32[]{:S(2)}) collective-permute-start(f32[64,512]{1,0:T(8,128)S(1)} %fusion.6), channel_id=1, source_target_pairs={{0,64},{1,65},{2,66},{3,67},{4,68},{5,69},{6,70},{7,71},{8,72},{9,... | collective-permute-start | bytes 393224 | tf_op jit(solution)/shard_map/ppermute | solution.py:188
  211.5 3.2 %collective-permute-start.12 = (bf16[64,512]{1,0:T(8,128)(2,1)S(1)}, bf16[64,512]{1,0:T(8,128)(2,1)S(1)}, u32[]{:S(2)}, u32[]{:S(2)}) collective-permute-start(bf16[64,512]{1,0:T(8,128)(2,1)S(1)} %fusion.5), channel_id=1, source_target_pairs={{0,3},{1,0},{2,1},{3,2},{4,7},{5,4},{6,5},{7,6},{8,11},{9,8},{10,9... | collective-permute-start | bytes 196616 | tf_op jit(solution)/shard_map/ppermute | solution.py:188
  211.6 4.7 %collective-permute-start.11 = (bf16[64,512]{1,0:T(8,128)(2,1)S(1)}, bf16[64,512]{1,0:T(8,128)(2,1)S(1)}, u32[]{:S(2)}, u32[]{:S(2)}) collective-permute-start(bf16[64,512]{1,0:T(8,128)(2,1)S(1)} %fusion.5), channel_id=1, source_target_pairs={{0,2},{1,3},{2,0},{3,1},{4,6},{5,7},{6,4},{7,5},{8,10},{9,11},{10,... | collective-permute-start | bytes 196616 | tf_op jit(solution)/shard_map/ppermute | solution.py:188
  211.7 6.3 %collective-permute-start.10 = (bf16[64,512]{1,0:T(8,128)(2,1)S(1)}, bf16[64,512]{1,0:T(8,128)(2,1)S(1)}, u32[]{:S(2)}, u32[]{:S(2)}) collective-permute-start(bf16[64,512]{1,0:T(8,128)(2,1)S(1)} %fusion.5), channel_id=1, source_target_pairs={{0,1},{1,2},{2,3},{3,0},{4,5},{5,6},{6,7},{7,4},{8,9},{9,10},{10,1... | collective-permute-start | bytes 196616 | tf_op jit(solution)/shard_map/ppermute | solution.py:188
  218.0 2.7 %collective-permute-start.13 = (bf16[256,512]{1,0:T(8,128)(2,1)S(1)}, bf16[256,512]{1,0:T(8,128)(2,1)S(1)}, u32[]{:S(2)}, u32[]{:S(2)}) collective-permute-start(bf16[256,512]{1,0:T(8,128)(2,1)S(1)} %pad_maximum_fusion.3), channel_id=1, source_target_pairs={{0,8},{8,0},{16,24},{24,16},{32,40},{40,32},{48,56},{56,48},{64,72... | collective-permute-start | bytes 786440 | tf_op jit(solution)/shard_map/ppermute | solution.py:263
Sparse Core Ops, SparseCore 0:
  30.4 51.9 all-gather.1

commit v3 on v2

--- a/solution.py
+++ b/solution.py
@@ -11,6 +11,8 @@
 SLOTS = 512
 F = 512
 PER_PEER = 4
+HALF = 256
+CHIPS = 8
 SLOT_CAP = 192
 ROW_TILES = 32
 GROUP_BITS = 2
@@ -30,23 +32,30 @@
     return jnp.where(position == wanted, 1.0, 0.0).astype(BF16)
 
 
-def group_kernel(part_ref, features_ref, out_ref):
-    part = part_ref[...]
+def group_kernel(meta_ref, part_ref, features_ref, other_part_ref, other_ref, out_ref):
+    core = meta_ref[0]
     devices = N_ROW * N_COL
-    member = jnp.where(
-        part == lax.broadcasted_iota(jnp.int32, (devices, SLOTS), 0), 1.0, 0.0
-    )
     before = jnp.where(
         lax.broadcasted_iota(jnp.int32, (SLOTS, SLOTS), 0)
         < lax.broadcasted_iota(jnp.int32, (SLOTS, SLOTS), 1),
         1.0,
         0.0,
     ).astype(BF16)
-    earlier = jnp.dot(member.astype(BF16), before, preferred_element_type=F32)
-    rank = jnp.sum(member * earlier, axis=0, keepdims=True).astype(jnp.int32)
-    place = ((part & (N_COL - 1)) * N_ROW + (part >> 3)) * PER_PEER + rank
-    pick = selection(place, SLOTS, SLOTS)
-    out_ref[...] = jnp.dot(pick, features_ref[...], preferred_element_type=F32).astype(BF16)
+
+    def grouped(part, rows):
+        member = jnp.where(
+            part == lax.broadcasted_iota(jnp.int32, (devices, SLOTS), 0), 1.0, 0.0
+        )
+        earlier = jnp.dot(member.astype(BF16), before, preferred_element_type=F32)
+        rank = jnp.sum(member * earlier, axis=0, keepdims=True).astype(jnp.int32)
+        place = ((part & (N_COL - 1)) * N_ROW + (part >> 3)) * PER_PEER + rank
+        pick = selection(place, SLOTS, SLOTS)
+        wanted = jnp.where(core == 0, rows[:, :HALF], rows[:, HALF:])
+        picked = jnp.dot(pick, wanted, preferred_element_type=F32).astype(BF16)
+        return picked.reshape(N_COL, 1, SLOTS // N_COL, HALF)
+
+    out_ref[:, pl.ds(core, 1)] = grouped(part_ref[...], features_ref[...])
+    out_ref[:, pl.ds(1 - core, 1)] = grouped(other_part_ref[...], other_ref[...])
 
 
 def interleave_kernel(arrived_ref, out_ref):
@@ -54,7 +63,9 @@
     giver, inner = source >> 6, source & 63
     place = (inner >> 2) * (N_COL * PER_PEER) + giver * PER_PEER + (inner & 3)
     pick = selection(place, SLOTS, SLOTS)
-    out_ref[...] = jnp.dot(pick, arrived_ref[...], preferred_element_type=F32).astype(BF16)
+    for c in range(2):
+        rows = arrived_ref[:, c].reshape(SLOTS, HALF)
+        out_ref[c] = jnp.dot(pick, rows, preferred_element_type=F32).astype(BF16)
 
 
 def plan_kernel(count_ref, rows_ref, cols_ref, plan_ref):
@@ -96,22 +107,40 @@
     plan_ref[...] = found.astype(jnp.int32)
 
 
-def tiles_kernel(plan_ref, tiles_hbm, source_hbm, out_ref, tiles, source, total, sems):
-    tiles_copy = pltpu.make_async_copy(tiles_hbm, tiles.at[pl.ds(0, SLOT_CAP)], sems.at[0])
-    source_copy = pltpu.make_async_copy(source_hbm, source, sems.at[1])
-    tiles_copy.start()
-    source_copy.start()
+def tiles_kernel(part, meta_ref, plan_ref, own_hbm, other_hbm, *refs):
+    blocks, outs = refs[:CHIPS], refs[CHIPS:-6]
+    tiles, source, total, narrow, sems, out_sems = refs[-6:]
+    core, x, yh = meta_ref[0], meta_ref[1], meta_ref[2]
+    live = tiles.at[pl.ds(0, SLOT_CAP)]
+    own_copy = pltpu.make_async_copy(own_hbm, live, sems.at[CHIPS])
+    other_copy = pltpu.make_async_copy(other_hbm, live, sems.at[CHIPS])
+
+    @pl.when(core == part)
+    def _():
+        own_copy.start()
+
+    @pl.when(core != part)
+    def _():
+        other_copy.start()
+
+    copies = [
+        pltpu.make_async_copy(blocks[k], source.at[meta_ref[4 + k]], sems.at[k])
+        for k in range(CHIPS)
+    ]
+    for copy in copies:
+        copy.start()
     tiles[SLOT_CAP] = jnp.zeros((TILE, TILE), BF16)
     total[...] = jnp.zeros_like(total)
-    tiles_copy.wait()
-    source_copy.wait()
+    own_copy.wait()
+    for copy in copies:
+        copy.wait()
 
     def product(g):
         left, right = [], []
         for e in range(GROUP):
             u = plan_ref[1, g * GROUP + e]
             left.append(tiles[plan_ref[0, g * GROUP + e]])
-            right.append(source[pl.ds((u & 3) * 4, 4), u >> 2].reshape(TILE, F))
+            right.append(source[pl.ds((u & 3) * 2, 2), :, u >> 2].reshape(TILE, HALF))
         return jnp.dot(
             jnp.concatenate(left, axis=1),
             jnp.concatenate(right, axis=0),
@@ -126,27 +155,79 @@
         return carry
 
     lax.fori_loop(0, (plan_ref[3, 0] + 1) >> 1, two_groups, 0)
-    out_ref[...] = total[...].astype(BF16)
-
-
-def layer_kernel(parts_ref, weight_ref, cotangent_ref, act_ref, grad_ref):
-    mixed = parts_ref[0].astype(F32)
-    for k in range(1, N_COL):
-        mixed = mixed + parts_ref[k].astype(F32)
-    high = mixed.astype(BF16)
-    low = (mixed - high.astype(F32)).astype(BF16)
-    weight = weight_ref[...]
-    pre = jnp.dot(high, weight, preferred_element_type=F32) + jnp.dot(
-        low, weight, preferred_element_type=F32
-    )
+    narrow[...] = total[...].astype(BF16).reshape(narrow.shape)
+    if part == 0:
+        given = [narrow.at[:, (x + k) & 3] for k in range(4)]
+    else:
+        given = [narrow.at[yh], narrow.at[1 - yh]]
+    copies = [
+        pltpu.make_async_copy(piece, out, out_sems.at[k])
+        for k, (piece, out) in enumerate(zip(given, outs))
+    ]
+    for copy in copies:
+        copy.start()
+    for copy in copies:
+        copy.wait()
+
+
+def x_summed_kernel(meta_ref, own_ref, a_ref, b_ref, c_ref, keep_ref, send_ref):
+    yh = meta_ref[2]
+
+    def summed(k):
+        pair = own_ref[k].astype(F32) + a_ref[k].astype(F32)
+        return pair + (b_ref[k].astype(F32) + c_ref[k].astype(F32))
+
+    keep_ref[...] = summed(yh)
+    send_ref[...] = summed(1 - yh).astype(BF16)
+
+
+def y_summed_kernel(meta_ref, own_ref, got_ref, keep_ref, a_ref, b_ref, c_ref):
+    x = meta_ref[1]
+
+    def summed(k):
+        return own_ref[k].astype(F32) + got_ref[k].astype(F32)
+
+    keep_ref[...] = summed(x)
+    for k, out in ((1, a_ref), (2, b_ref), (3, c_ref)):
+        out[...] = summed((x + k) & 3).astype(BF16)
+
+
+def sums_kernel(meta_ref, keep0, got0, keep1, a_ref, b_ref, c_ref, mine_ref, send_ref):
+    core = meta_ref[0]
+    first = keep0[...] + got0[...].astype(F32)
+    second = keep1[...] + a_ref[...].astype(F32)
+    second = second + (b_ref[...].astype(F32) + c_ref[...].astype(F32))
+    mine_ref[...] = jnp.where(core == 0, first, second)
+    send_ref[...] = jnp.where(core == 0, second, first)
+
+
+def two_parts(value):
+    high = value.astype(BF16)
+    return high, (value - high.astype(F32)).astype(BF16)
+
+
+def layer_kernel(meta_ref, mine_ref, got_ref, weight_ref, cotangent_ref, act_ref, slope_ref):
+    core = meta_ref[0]
+    pre = jnp.zeros((SLOTS, F), F32)
+    for half, mixed in ((core, mine_ref[...]), (1 - core, got_ref[...])):
+        weight = weight_ref[pl.ds(pl.multiple_of(half * HALF, HALF), HALF), :]
+        for piece in two_parts(mixed):
+            pre = pre + jnp.dot(piece, weight, preferred_element_type=F32)
     sigmoid = jax.nn.sigmoid(pre)
     act_ref[...] = (pre * sigmoid).astype(BF16)
-    slope = (
+    slope_ref[...] = (
         cotangent_ref[...].astype(F32) * (sigmoid * (1.0 + pre * (1.0 - sigmoid)))
     ).astype(BF16)
+
+
+def gradient_kernel(mine_ref, other_ref, slope_ref, other_slope_ref, grad_ref):
     contract = (((0,), (0,)), ((), ()))
-    grad = lax.dot_general(high, slope, contract, preferred_element_type=F32)
-    grad = grad + lax.dot_general(low, slope, contract, preferred_element_type=F32)
+    grad = jnp.zeros((HALF, F), F32)
+    for mixed, slope in ((mine_ref, slope_ref), (other_ref, other_slope_ref)):
+        for piece in two_parts(mixed[...]):
+            grad = grad + lax.dot_general(
+                piece, slope[...], contract, preferred_element_type=F32
+            )
     grad_ref[...] = grad * (1.0 / 256.0)
 
 
@@ -174,6 +255,10 @@
     return [(yh * 4 + x, yh * 4 + (x + k) % 4) for yh in range(2) for x in range(4)]
 
 
+def y_moves():
+    return [(yh * 4 + x, (1 - yh) * 4 + x) for yh in range(2) for x in range(4)]
+
+
 def scatter4(total, me, axis, moves):
     quarter = total.shape[0] // 4
     parts = total.reshape(4, quarter, F)
@@ -187,6 +272,21 @@
 def by_giver(own, me, axis, moves):
     got = jnp.stack([own] + [lax.ppermute(own, axis, moves(k)) for k in (1, 2, 3)])
     return [got[(me - k) % 4] for k in range(4)]
+
+
+def call(kernel, in_specs, outs, scratch=()):
+    return pl.pallas_call(
+        kernel,
+        in_specs=in_specs,
+        out_specs=jax.tree.map(lambda _: pl.BlockSpec(memory_space=pltpu.VMEM), outs),
+        out_shape=outs,
+        scratch_shapes=list(scratch),
+        compiler_params=params(),
+    )
+
+
+def array(*shape, dtype=BF16):
+    return jax.ShapeDtypeStruct(shape, dtype)
 
 
 def shards(
@@ -199,61 +299,110 @@
     y = yh * 2 + yl
     vmem = pl.BlockSpec(memory_space=pltpu.VMEM)
     smem = pl.BlockSpec(memory_space=pltpu.SMEM)
-
     hbm = pl.BlockSpec(memory_space=pl.ANY)
-    plan = pl.pallas_call(
-        plan_kernel,
-        in_specs=[smem, vmem, vmem],
-        out_specs=vmem,
-        out_shape=jax.ShapeDtypeStruct((8, PLAN), jnp.int32),
-        compiler_params=params(),
-    )(tile_count.reshape(1), tile_rows.reshape(1, -1), tile_cols.reshape(1, -1))
-    grouped = pl.pallas_call(
+
+    here, there = yl * 4, (1 - yl) * 4
+    near = [here + (z - k) % 4 for k in range(4)]
+    far = [there + (z - k) % 4 for k in range(4)]
+    first = core == 0
+    places = [
+        near[0],
+        jnp.where(first, near[1], far[0]),
+        jnp.where(first, near[3], near[1]),
+        jnp.where(first, near[2], near[3]),
+        jnp.where(first, far[0], near[2]),
+        far[1],
+        far[3],
+        far[2],
+    ]
+    meta = jnp.stack([core, x, yh, z] + places).astype(jnp.int32)
+
+    swap = row_moves(lambda yl, z, c: (yl, z, 1 - c))
+    tiles = tile_values.reshape(-1, TILE, TILE)
+    part = partition_of.reshape(1, SLOTS)
+    other_part = lax.ppermute(part, "row", swap)
+    other_features = lax.ppermute(features, "row", swap)
+    other_tiles = lax.ppermute(tiles, "row", swap)
+    grouped = call(
         group_kernel,
-        out_shape=jax.ShapeDtypeStruct((SLOTS, F), BF16),
-        compiler_params=params(),
-    )(partition_of.reshape(1, SLOTS), features)
+        [smem, vmem, vmem, vmem, vmem],
+        array(N_COL, 2, SLOTS // N_COL, HALF),
+    )(meta, part, features, other_part, other_features)
     arrived = lax.all_to_all(grouped, "col", split_axis=0, concat_axis=0, tiled=True)
-    mine = pl.pallas_call(
-        interleave_kernel,
-        out_shape=jax.ShapeDtypeStruct((SLOTS, F), BF16),
-        compiler_params=params(),
-    )(arrived)
-    sources = lax.all_gather(mine, "row", axis=0, tiled=True)
-    sources = sources.reshape(N_ROW, N_ROW, N_COL * PER_PEER, F)
-
-    partial = pl.pallas_call(
-        tiles_kernel,
-        in_specs=[smem, hbm, hbm],
-        out_specs=vmem,
-        out_shape=jax.ShapeDtypeStruct((ROW_TILES, TILE, F), BF16),
-        scratch_shapes=[
-            pltpu.VMEM((SLOT_CAP + 1, TILE, TILE), BF16),
-            pltpu.VMEM((N_ROW, N_ROW, N_COL * PER_PEER, F), BF16),
-            pltpu.VMEM((ROW_TILES, TILE, F), F32),
-            pltpu.SemaphoreType.DMA((2,)),
-        ],
-        compiler_params=params(),
-    )(plan, tile_values.reshape(-1, TILE, TILE), sources)
-    parts = lax.all_to_all(
-        partial.reshape(N_COL * SLOTS, F), "col", split_axis=0, concat_axis=0, tiled=True
-    ).reshape(N_COL, SLOTS, F)
+    plan = call(plan_kernel, [smem, vmem, vmem], array(8, PLAN, dtype=jnp.int32))(
+        tile_count.reshape(1), tile_rows.reshape(1, -1), tile_cols.reshape(1, -1)
+    )
+    other_plan = lax.ppermute(plan, "row", swap)
+    own = call(interleave_kernel, [vmem], array(2, SLOTS, HALF))(arrived)
+
+    def hop(block, move0, move1):
+        def move(yl, z, c):
+            dy, dz = move1 if c else move0
+            return (yl + dy) % 2, (z + dz) % 4, c
+
+        return lax.ppermute(block, "row", row_moves(move))
+
+    r1 = hop(own, (0, 1), (1, 0))
+    r2 = hop(own, (0, 3), (0, 1))
+    r3 = hop(own, (0, 2), (0, 3))
+    r4 = hop(own, (1, 0), (0, 2))
+    s1 = hop(r1, (1, 0), (0, 1))
+    s2 = hop(jnp.where(first, r2, r1), (1, 0), (0, 3))
+    s3 = hop(jnp.where(first, r3, r1), (1, 0), (0, 2))
+    blocks = [
+        b.reshape(2, N_ROW, N_COL * PER_PEER, HALF) for b in (own, r1, r2, r3, r4, s1, s2, s3)
+    ]
+
+    def tile_sums(part, outs):
+        return pl.pallas_call(
+            lambda *refs: tiles_kernel(part, *refs),
+            in_specs=[smem, smem] + [hbm] * (2 + CHIPS),
+            out_specs=[hbm] * len(outs),
+            out_shape=outs,
+            scratch_shapes=[
+                pltpu.VMEM((SLOT_CAP + 1, TILE, TILE), BF16),
+                pltpu.VMEM((CHIPS, 2, N_ROW, N_COL * PER_PEER, HALF), BF16),
+                pltpu.VMEM((ROW_TILES, TILE, HALF), F32),
+                pltpu.VMEM((2, 4, SLOTS, HALF), BF16),
+                pltpu.SemaphoreType.DMA((CHIPS + 1,)),
+                pltpu.SemaphoreType.DMA((4,)),
+            ],
+            compiler_params=params(),
+        )(
+            meta,
+            jnp.where(core == part, plan, other_plan),
+            tiles,
+            other_tiles,
+            *blocks,
+        )
+
+    row0 = tile_sums(0, [array(2, SLOTS, HALF)] * 4)
+    got0 = [lax.ppermute(row0[k], "col", x_moves(k)) for k in (1, 2, 3)]
+    keep1, send1 = tile_sums(1, [array(4, SLOTS, HALF)] * 2)
+    got1 = lax.ppermute(send1, "col", y_moves())
+    wide, narrow = array(SLOTS, HALF, dtype=F32), array(SLOTS, HALF)
+    keep0, send0 = call(x_summed_kernel, [smem] + [vmem] * 4, [wide, narrow])(
+        meta, row0[0], *got0
+    )
+    got0 = lax.ppermute(send0, "col", y_moves())
+    keep1, *send1 = call(y_summed_kernel, [smem] + [vmem] * 2, [wide] + [narrow] * 3)(
+        meta, keep1, got1
+    )
+    got1 = [lax.ppermute(send1[k - 1], "col", x_moves(k)) for k in (1, 2, 3)]
+    mine, others = call(sums_kernel, [smem] + [vmem] * 6, [wide] * 2)(
+        meta, keep0, got0, keep1, *got1
+    )
+    theirs = lax.ppermute(others, "row", swap)
     cotangent = lax.dynamic_slice_in_dim(out_cotangent, col * SLOTS, SLOTS, 0)
-    activations, grad = pl.pallas_call(
-        layer_kernel,
-        out_shape=(
-            jax.ShapeDtypeStruct((SLOTS, F), BF16),
-            jax.ShapeDtypeStruct((F, F), F32),
-        ),
-        compiler_params=params(),
-    )(parts, weight, cotangent)
+    activations, slope = call(layer_kernel, [smem] + [vmem] * 4, [array(SLOTS, F)] * 2)(
+        meta, mine, theirs, weight, cotangent
+    )
+    other_slope = lax.ppermute(slope, "row", swap)
+    half = call(gradient_kernel, [vmem] * 4, array(HALF, F, dtype=F32))(
+        mine, others, slope, other_slope
+    )
 
     z_moves = lambda k: row_moves(lambda yl, z, c: (yl, (z + k) % 4, c))
-    swap = row_moves(lambda yl, z, c: (yl, z, 1 - c))
-    halves = grad.reshape(2, F // 2, F)
-    half = lax.dynamic_index_in_dim(halves, core, 0, False) + lax.ppermute(
-        lax.dynamic_index_in_dim(halves, 1 - core, 0, False), "row", swap
-    )
     eighth = scatter4(half, x, "col", x_moves)
     a, b, c, d = by_giver(eighth, z, "row", z_moves)
     eighth = (a + b) + (c + d)

time: 229 us -> 216 us (0.943)
  waiting for transfers between devices: 128 us -> 78.4 us
  starting transfers between devices: 35.5 us -> 56.1 us
  Pallas kernels: 26.2 us -> 46.2 us
  between operations: 14.8 us -> 1.49 us
  local copies, waits for them, and re-layouts: 3.02 us -> 9.22 us
  other arithmetic: 2.64 us -> 4.97 us
    ppermute x1 -> x21, waiting for transfers between devices: 1.54 us -> 53.1 us  [the longest x7 21.4 us: hop(): return lax.ppermute(block, 'row', row_moves(move))]
    all_gather x1 -> x0, waiting for transfers between devices: 49.7 us -> none  [shards(): sources = lax.all_gather(mine, 'row', axis=0, tiled=True)]
    all_to_all x1 -> x0, waiting for transfers between devices: 49.2 us -> none  [shards(): lax.all_to_all(partial.reshape(N_COL * SLOTS, F), 'col', split_axis=0, co...]
    ppermute x1 -> x21, starting transfers between devices: 0.93 us -> 41.5 us  [the longest x1 11.7 us: shards(): theirs = lax.ppermute(others, 'row', swap)]
    pallas_call x5 -> x10, Pallas kernels: 26.2 us -> 46.2 us  [the longest x2 24.9 us: tile_sums(): pl.pallas_call(lambda *refs: tiles_kernel(part, *refs), in_specs=[smem, s...]
    ppermute x9, starting transfers between devices: 19.6 us -> 8.05 us  [by_giver(): lax.ppermute(own, axis, moves(k))]
    all_to_all x1 -> x0, starting transfers between devices: 7.13 us -> none  [shards(): lax.all_to_all(partial.reshape(N_COL * SLOTS, F), 'col', split_axis=0, co...]
    unnamed x0 -> x36, local copies, waits for them, and re-layouts: none -> 5.64 us
  transfers between devices with their start and end apart: 16 -> 34, of which waited for: 14 -> 24; matrix products, arithmetic and copies ran while one was open for 1% -> 2% of each run, Pallas kernels for 1% -> 11%
where the time goes in v3:
time: 216 us; the launch traced here: 215 us
  waiting for transfers between devices  78.4 us (36%)
  starting transfers between devices  56.1 us (26%)
  Pallas kernels  46.2 us (21%)
  blocking collectives  18.6 us (9%)
  local copies, waits for them, and re-layouts  9.22 us (4%)
  other arithmetic  4.97 us (2%)
    pallas_call x2, Pallas kernels, tile_sums(): pl.pallas_call(lambda *refs: tiles_kernel(part, *refs), in_specs=[smem, s...  24.9 us
    ppermute x7, waiting for transfers between devices, hop(): return lax.ppermute(block, 'row', row_moves(move))  21.4 us
    ppermute x9, waiting for transfers between devices, by_giver(): lax.ppermute(own, axis, moves(k))  19.1 us
    all_to_all x1, blocking collectives, shards(): lax.all_to_all(grouped, 'col', split_axis=0, concat_axis=0, tiled=True)  18.6 us
    ppermute x3, waiting for transfers between devices, shards(): got0 = [lax.ppermute(row0[k], 'col', x_moves(k)) for k in (1, 2, 3)]  17.4 us
    ppermute x1, starting transfers between devices, shards(): theirs = lax.ppermute(others, 'row', swap)  11.7 us
    ppermute x7, starting transfers between devices, hop(): return lax.ppermute(block, 'row', row_moves(move))  11.4 us
    ppermute x9, starting transfers between devices, by_giver(): lax.ppermute(own, axis, moves(k))  8.05 us
  transfers between devices with their start and end apart: 34, of which 24 were waited for; matrix products, arithmetic and copies ran while one was open for 2% of the time, Pallas kernels for 11%

profile of v3, /device:TPU:1, one launch (start us, length us, event | category | flops | bytes accessed | tf_op | source)
XLA Modules:
  0.0 215.0 jit_solution(10925413079401272336)
XLA Ops:
  0.6 1.5 collective-permute-start.1
  3.2 6.3 %collective-permute-done.2.other_part_ref = s32[1,512]{1,0:T(1,128)S(1)} collective-permute-done((s32[1,512]{1,0:T(1,128)}, s32[1,512]{1,0:T(1,128)S(1)}, u32[]{:S(2)}, u32[]{:S(2)}) %collective-permute-start.2) | collective-permute-done | bytes 2080 | tf_op jit(solution)/shard_map/ppermute | solution.py:323
  10.9 2.7 %shard_map.96 = bf16[8,2,64,256]{3,2,1,0:T(8,128)(2,1)} custom-call(s32[12]{0:T(128)} %stack.92.meta_ref.refs_0_, s32[1,512]{1,0:T(1,128)} %bitcast.91, bf16[512,512]{1,0:T(8,128)(2,1)} %features_ref.1, s32[1,512]{1,0:T(1,128)} %copy-done.17, bf16[512,512]{1,0:T(8,128)(2,1)} %copy-done.12), custom_call_target="tpu_custom_call" | custom-call | tf_op jit(solution)/shard_map/pallas_call | solution.py:326
  13.6 18.6 %all_to_all.5.arrived_ref = bf16[8,2,64,256]{3,2,1,0:T(8,128)(2,1)} all-to-all(bf16[8,2,64,256]{3,2,1,0:T(8,128)(2,1)} %shard_map.96), channel_id=1, replica_groups=mesh['row'=16,'col'=8] {'col'}, dimensions={0} | all-to-all | bytes 1048576 | tf_op jit(solution)/shard_map/all_to_all | solution.py:331
  32.2 2.3 %shard_map.97 = bf16[2,512,256]{2,1,0:T(8,128)(2,1)} custom-call(bf16[8,2,64,256]{3,2,1,0:T(8,128)(2,1)} %all_to_all.5.arrived_ref), custom_call_target="tpu_custom_call" | custom-call | tf_op jit(solution)/shard_map/pallas_call | solution.py:336
  34.9 1.6 collective-permute-start.5
  36.5 2.1 collective-permute-start.6
  39.3 1.8 shard_map.95
  41.1 2.6 %collective-permute-start = (s32[8,288]{1,0:T(8,128)}, s32[8,288]{1,0:T(8,128)S(1)}, u32[]{:S(2)}, u32[]{:S(2)}) collective-permute-start(s32[8,288]{1,0:T(8,128)} %shard_map.95), channel_id=1, source_target_pairs={{0,8},{8,0},{16,24},{24,16},{32,40},{40,32},{48,56},{56,48},{64,72... | collective-permute-start | bytes 27656 | tf_op jit(solution)/shard_map/ppermute | solution.py:335
  43.6 3.0 %collective-permute-start.7 = (bf16[2,512,256]{2,1,0:T(8,128)(2,1)}, bf16[2,512,256]{2,1,0:T(8,128)(2,1)S(1)}, u32[]{:S(2)}, u32[]{:S(2)}) collective-permute-start(bf16[2,512,256]{2,1,0:T(8,128)(2,1)} %shard_map.97), channel_id=1, source_target_pairs={{0,64},{8,40},{16,80},{24,56},{32,96},{40,8},{48,112},{56,24},{64,... | collective-permute-start | bytes 1572872 | tf_op jit(solution)/shard_map/ppermute | solution.py:343
  46.6 4.2 %collective-permute-done.5 = bf16[2,512,256]{2,1,0:T(8,128)(2,1)S(1)} collective-permute-done((bf16[2,512,256]{2,1,0:T(8,128)(2,1)}, bf16[2,512,256]{2,1,0:T(8,128)(2,1)S(1)}, u32[]{:S(2)}, u32[]{:S(2)}) %collective-permute-start.5) | collective-permute-done | bytes 524320 | tf_op jit(solution)/shard_map/ppermute | solution.py:343
  50.9 1.2 broadcast_select_fusion
  52.1 3.0 %collective-permute-start.9 = (bf16[2,512,256]{2,1,0:T(8,128)(2,1)}, bf16[2,512,256]{2,1,0:T(8,128)(2,1)S(1)}, u32[]{:S(2)}, u32[]{:S(2)}) collective-permute-start(bf16[2,512,256]{2,1,0:T(8,128)(2,1)} %get-tuple-element.40), channel_id=1, source_target_pairs={{0,64},{8,56},{16,80},{24,8},{32,96},{40,24},{48,112},{56,40},{64,... | collective-permute-start | bytes 1572872 | tf_op jit(solution)/shard_map/ppermute | solution.py:343
  55.1 1.2 collective-permute-start.10
  56.3 1.3 broadcast_select_fusion.4
  57.6 5.3 %collective-permute-done.7 = bf16[2,512,256]{2,1,0:T(8,128)(2,1)S(1)} collective-permute-done((bf16[2,512,256]{2,1,0:T(8,128)(2,1)}, bf16[2,512,256]{2,1,0:T(8,128)(2,1)S(1)}, u32[]{:S(2)}, u32[]{:S(2)}) %collective-permute-start.7) | collective-permute-done | bytes 524320 | tf_op jit(solution)/shard_map/ppermute | solution.py:343
  62.9 6.1 %collective-permute-done.8 = bf16[2,512,256]{2,1,0:T(8,128)(2,1)S(1)} collective-permute-done((bf16[2,512,256]{2,1,0:T(8,128)(2,1)S(1)}, bf16[2,512,256]{2,1,0:T(8,128)(2,1)S(1)}, u32[]{:S(2)}, u32[]{:S(2)}) %collective-permute-start.8) | collective-permute-done | bytes 524320 | tf_op jit(solution)/shard_map/ppermute | solution.py:343
  69.1 4.1 %collective-permute-done.9 = bf16[2,512,256]{2,1,0:T(8,128)(2,1)S(1)} collective-permute-done((bf16[2,512,256]{2,1,0:T(8,128)(2,1)}, bf16[2,512,256]{2,1,0:T(8,128)(2,1)S(1)}, u32[]{:S(2)}, u32[]{:S(2)}) %collective-permute-start.9) | collective-permute-done | bytes 524320 | tf_op jit(solution)/shard_map/ppermute | solution.py:343
  73.2 1.6 collective-permute-done.10
  74.9 14.3 %shard_map.100 = (bf16[4,512,256]{2,1,0:T(8,128)(2,1)}, bf16[4,512,256]{2,1,0:T(8,128)(2,1)}) custom-call(s32[12]{0:T(128)} %stack.92.meta_ref.refs_0_, s32[8,288]{1,0:T(8,128)} %get-tuple-element.45.refs_1_, bf16[192,128,128]{2,1,0:T(8,128)(2,1)} %bitcast.62, bf16[192,128,128]{2,1,0:T(8,128)(2,1)} %collective-permute-done.1.refs_3_, ...), custom_call_target="tpu_custom_call" | custom-call | tf_op jit(solution)/shard_map/pallas_call | solution.py:357
  89.2 3.4 %collective-permute-start.15 = (bf16[4,512,256]{2,1,0:T(8,128)(2,1)}, bf16[4,512,256]{2,1,0:T(8,128)(2,1)S(1)}, u32[]{:S(2)}, u32[]{:S(2)}) collective-permute-start(bf16[4,512,256]{2,1,0:T(8,128)(2,1)} %get-tuple-element.25), channel_id=1, source_target_pairs={{0,4},{1,5},{2,6},{3,7},{4,0},{5,1},{6,2},{7,3},{8,12},{9,13},{10,... | collective-permute-start | bytes 3145736 | tf_op jit(solution)/shard_map/ppermute | solution.py:382
  92.6 10.6 %shard_map.98 = (bf16[2,512,256]{2,1,0:T(8,128)(2,1)}, bf16[2,512,256]{2,1,0:T(8,128)(2,1)}, bf16[2,512,256]{2,1,0:T(8,128)(2,1)}, bf16[2,512,256]{2,1,0:T(8,128)(2,1)}) custom-call(s32[12]{0:T(128)} %stack.92.meta_ref.refs_0_, s32[8,288]{1,0:T(8,128)} %get-tuple-element.46.refs_1_, bf16[192,128,128]{2,1,0:T(8,128)(2,1)} %bitcast.63, ...), custom_call_target="tpu_custom_call" | custom-call | tf_op jit(solution)/shard_map/pallas_call | solution.py:357
  103.2 2.6 %collective-permute-start.12 = (bf16[2,512,256]{2,1,0:T(8,128)(2,1)}, bf16[2,512,256]{2,1,0:T(8,128)(2,1)S(1)}, u32[]{:S(2)}, u32[]{:S(2)}) collective-permute-start(bf16[2,512,256]{2,1,0:T(8,128)(2,1)} %get-tuple-element.20), channel_id=1, source_target_pairs={{0,2},{1,3},{2,0},{3,1},{4,6},{5,7},{6,4},{7,5},{8,10},{9,11},{10,... | collective-permute-start | bytes 1572872 | tf_op jit(solution)/shard_map/ppermute | solution.py:380
  105.8 2.0 collective-permute-start.13
  107.8 9.7 %collective-permute-done.11.a_ref = bf16[2,512,256]{2,1,0:T(8,128)(2,1)S(1)} collective-permute-done((bf16[2,512,256]{2,1,0:T(8,128)(2,1)}, bf16[2,512,256]{2,1,0:T(8,128)(2,1)S(1)}, u32[]{:S(2)}, u32[]{:S(2)}) %collective-permute-start.11) | collective-permute-done | bytes 524320 | tf_op jit(solution)/shard_map/ppermute | solution.py:380
  117.5 1.9 collective-permute-done.12.b_ref
  119.4 5.8 %collective-permute-done.13.c_ref = bf16[2,512,256]{2,1,0:T(8,128)(2,1)S(1)} collective-permute-done((bf16[2,512,256]{2,1,0:T(8,128)(2,1)}, bf16[2,512,256]{2,1,0:T(8,128)(2,1)S(1)}, u32[]{:S(2)}, u32[]{:S(2)}) %collective-permute-start.13) | collective-permute-done | bytes 524320 | tf_op jit(solution)/shard_map/ppermute | solution.py:380
  125.2 0.8 copy-done.11
  126.0 2.5 %shard_map.99 = (f32[512,256]{1,0:T(8,128)}, bf16[512,256]{1,0:T(8,128)(2,1)}) custom-call(s32[12]{0:T(128)} %stack.92.meta_ref.refs_0_, bf16[2,512,256]{2,1,0:T(8,128)(2,1)} %get-tuple-element.18.own_ref, bf16[2,512,256]{2,1,0:T(8,128)(2,1)} %copy-done.8, bf16[2,512,256]{2,1,0:T(8,128)(2,1)} %copy-done.9, bf16[2,512,256]{2,1,0:T(8,128)(2,1)} %copy-done.11), custom_call_target="tpu_custom_call" | custom-call | tf_op jit(solution)/shard_map/pallas_call | solution.py:384
  128.5 1.4 collective-permute-start.14
  129.9 1.0 copy-done.6
  131.0 2.8 %shard_map.101 = (f32[512,256]{1,0:T(8,128)}, bf16[512,256]{1,0:T(8,128)(2,1)}, bf16[512,256]{1,0:T(8,128)(2,1)}, bf16[512,256]{1,0:T(8,128)(2,1)}) custom-call(s32[12]{0:T(128)} %stack.92.meta_ref.refs_0_, bf16[4,512,256]{2,1,0:T(8,128)(2,1)} %get-tuple-element.24.own_ref, bf16[4,512,256]{2,1,0:T(8,128)(2,1)} %copy-done.6), custom_call_target="tpu_custom_call" | custom-call | tf_op jit(solution)/shard_map/pallas_call | solution.py:388
  133.7 1.9 collective-permute-start.16
  135.6 1.4 collective-permute-start.17
  137.0 1.0 collective-permute-start.18
  138.0 2.4 %collective-permute-done.16.a_ref = bf16[512,256]{1,0:T(8,128)(2,1)S(1)} collective-permute-done((bf16[512,256]{1,0:T(8,128)(2,1)}, bf16[512,256]{1,0:T(8,128)(2,1)S(1)}, u32[]{:S(2)}, u32[]{:S(2)}) %collective-permute-start.16) | collective-permute-done | bytes 262176 | tf_op jit(solution)/shard_map/ppermute | solution.py:391
  140.4 3.7 %collective-permute-done.17.b_ref = bf16[512,256]{1,0:T(8,128)(2,1)S(1)} collective-permute-done((bf16[512,256]{1,0:T(8,128)(2,1)}, bf16[512,256]{1,0:T(8,128)(2,1)S(1)}, u32[]{:S(2)}, u32[]{:S(2)}) %collective-permute-start.17) | collective-permute-done | bytes 262176 | tf_op jit(solution)/shard_map/ppermute | solution.py:391
  144.9 2.6 %shard_map.102 = (f32[512,256]{1,0:T(8,128)}, f32[512,256]{1,0:T(8,128)}) custom-call(s32[12]{0:T(128)} %stack.92.meta_ref.refs_0_, f32[512,256]{1,0:T(8,128)} %get-tuple-element.22.keep0, bf16[512,256]{1,0:T(8,128)(2,1)} %copy-done.13, f32[512,256]{1,0:T(8,128)} %get-tuple-element.26.keep1, bf16[512,256]{1,0:T(8,128)(2,1)} %copy-done.14, ...), custom_call_target="tpu_custom_call" | custom-call | tf_op jit(solution)/shard_map/pallas_call | solution.py:392
  147.5 11.7 %collective-permute-start.19 = (f32[512,256]{1,0:T(8,128)}, f32[512,256]{1,0:T(8,128)S(1)}, u32[]{:S(2)}, u32[]{:S(2)}) collective-permute-start(f32[512,256]{1,0:T(8,128)} %get-tuple-element.31.other_ref), channel_id=1, source_target_pairs={{0,8},{8,0},{16,24},{24,16},{32,40},{40,32},{48,56},{56,48},{64,72... | collective-permute-start | bytes 1572872 | tf_op jit(solution)/shard_map/ppermute | solution.py:395
  159.3 1.9 constant_dynamic-slice_fusion.cotangent_ref
  162.0 3.5 %shard_map.103 = (bf16[512,512]{1,0:T(8,128)(2,1)}, bf16[512,512]{1,0:T(8,128)(2,1)}) custom-call(s32[12]{0:T(128)} %stack.92.meta_ref.refs_0_, f32[512,256]{1,0:T(8,128)} %get-tuple-element.30.mine_ref, f32[512,256]{1,0:T(8,128)} %copy-done.10, bf16[512,512]{1,0:T(8,128)(2,1)} %weight_ref.1, bf16[512,512]{1,0:T(8,128)(2,1)} %constant_dynamic-slice_fusion.cotangent_ref), custom_call_target="tpu_custom_call" | custom-call | tf_op jit(solution)/shard_map/pallas_call | solution.py:397
  165.7 1.9 collective-permute-done.20.other_slope_ref
  168.4 3.1 %shard_map.104 = f32[256,512]{1,0:T(8,128)} custom-call(f32[512,256]{1,0:T(8,128)} %get-tuple-element.30.mine_ref, f32[512,256]{1,0:T(8,128)} %get-tuple-element.31.other_ref, bf16[512,512]{1,0:T(8,128)(2,1)} %get-tuple-element.33.slope_ref, bf16[512,512]{1,0:T(8,128)(2,1)} %copy-done.7), custom_call_target="tpu_custom_call" | custom-call | tf_op jit(solution)/shard_map/pallas_call | solution.py:401
  171.4 1.1 fusion.2
  172.5 2.2 %collective-permute-start.23 = (bf16[64,512]{1,0:T(8,128)(2,1)S(1)}, bf16[64,512]{1,0:T(8,128)(2,1)S(1)}, u32[]{:S(2)}, u32[]{:S(2)}) collective-permute-start(bf16[64,512]{1,0:T(8,128)(2,1)S(1)} %get-tuple-element.37), channel_id=1, source_target_pairs={{0,3},{1,0},{2,1},{3,2},{4,7},{5,4},{6,5},{7,6},{8,11},{9,8},{10,9... | collective-permute-start | bytes 196616 | tf_op jit(solution)/shard_map/ppermute | solution.py:268
  174.7 1.3 collective-permute-start.21
  176.0 5.0 %collective-permute-done.22 = bf16[64,512]{1,0:T(8,128)(2,1)S(1)} collective-permute-done((bf16[64,512]{1,0:T(8,128)(2,1)S(1)}, bf16[64,512]{1,0:T(8,128)(2,1)S(1)}, u32[]{:S(2)}, u32[]{:S(2)}) %collective-permute-start.22) | collective-permute-done | bytes 65568 | tf_op jit(solution)/shard_map/ppermute | solution.py:268
  181.0 0.9 fusion.1
  182.1 1.4 collective-permute-start.24
  183.5 2.8 %collective-permute-done.26 = f32[64,512]{1,0:T(8,128)S(1)} collective-permute-done((f32[64,512]{1,0:T(8,128)S(1)}, f32[64,512]{1,0:T(8,128)S(1)}, u32[]{:S(2)}, u32[]{:S(2)}) %collective-permute-start.26) | collective-permute-done | bytes 131104 | tf_op jit(solution)/shard_map/ppermute | solution.py:273
  186.2 1.6 collective-permute-done.25
  187.8 3.9 %collective-permute-done.24 = f32[64,512]{1,0:T(8,128)S(1)} collective-permute-done((f32[64,512]{1,0:T(8,128)S(1)}, f32[64,512]{1,0:T(8,128)S(1)}, u32[]{:S(2)}, u32[]{:S(2)}) %collective-permute-start.24) | collective-permute-done | bytes 131104 | tf_op jit(solution)/shard_map/ppermute | solution.py:273
  191.8 2.2 %collective-permute-start.29 = (f32[64,512]{1,0:T(8,128)S(1)}, f32[64,512]{1,0:T(8,128)S(1)}, u32[]{:S(2)}, u32[]{:S(2)}) collective-permute-start(f32[64,512]{1,0:T(8,128)S(1)} %fusion.6), channel_id=1, source_target_pairs={{0,68},{1,69},{2,70},{3,71},{4,64},{5,65},{6,66},{7,67},{8,76},{9,... | collective-permute-start | bytes 393224 | tf_op jit(solution)/shard_map/ppermute | solution.py:273
  194.0 2.8 %collective-permute-start.28 = (f32[64,512]{1,0:T(8,128)S(1)}, f32[64,512]{1,0:T(8,128)S(1)}, u32[]{:S(2)}, u32[]{:S(2)}) collective-permute-start(f32[64,512]{1,0:T(8,128)S(1)} %fusion.6), channel_id=1, source_target_pairs={{0,4},{1,5},{2,6},{3,7},{4,0},{5,1},{6,2},{7,3},{8,12},{9,13},{10,... | collective-permute-start | bytes 393224 | tf_op jit(solution)/shard_map/ppermute | solution.py:273
  196.9 1.5 collective-permute-done.29
  198.4 1.0 collective-permute-done.28
  199.3 4.4 %collective-permute-done.27 = f32[64,512]{1,0:T(8,128)S(1)} collective-permute-done((f32[64,512]{1,0:T(8,128)S(1)}, f32[64,512]{1,0:T(8,128)S(1)}, u32[]{:S(2)}, u32[]{:S(2)}) %collective-permute-start.27) | collective-permute-done | bytes 131104 | tf_op jit(solution)/shard_map/ppermute | solution.py:273
  204.0 1.4 collective-permute-start.30
  205.4 1.6 collective-permute-done.32
  207.0 1.6 collective-permute-done.31
  208.6 0.8 collective-permute-done.30
  209.5 3.1 %collective-permute-start.33 = (bf16[256,512]{1,0:T(8,128)(2,1)S(1)}, bf16[256,512]{1,0:T(8,128)(2,1)S(1)}, u32[]{:S(2)}, u32[]{:S(2)}) collective-permute-start(bf16[256,512]{1,0:T(8,128)(2,1)S(1)} %pad_maximum_fusion.3), channel_id=1, source_target_pairs={{0,8},{8,0},{16,24},{24,16},{32,40},{40,32},{48,56},{56,48},{64,72... | collective-permute-start | bytes 786440 | tf_op jit(solution)/shard_map/ppermute | solution.py:412
  212.6 1.2 collective-permute-done.33
  213.9 1.1 maximum_convert_fusion
  (68 shorter events, 6.5 us)
Async XLA Ops:
  0.6 74.2 %collective-permute-start.1 = (bf16[192,128,128]{2,1,0:T(8,128)(2,1)}, bf16[192,128,128]{2,1,0:T(8,128)(2,1)}, u32[]{:S(2)}, u32[]{:S(2)}) collective-permute-start(bf16[192,128,128]{2,1,0:T(8,128)(2,1)} %bitcast.61), channel_id=1, source_target_pairs={{0,8},{8,0},{16,24},{24,16},{32,40},{40,32},{48,56},{56,48},{64,72... | collective-permute-start | bytes 18874376 | tf_op jit(solution)/shard_map/ppermute | solution.py:325
  2.1 7.4 %collective-permute-start.3 = (bf16[512,512]{1,0:T(8,128)(2,1)}, bf16[512,512]{1,0:T(8,128)(2,1)S(1)}, u32[]{:S(2)}, u32[]{:S(2)}) collective-permute-start(bf16[512,512]{1,0:T(8,128)(2,1)} %features_ref.1), channel_id=1, source_target_pairs={{0,8},{8,0},{16,24},{24,16},{32,40},{40,32},{48,56},{56,48},{64,72... | collective-permute-start | bytes 1572872 | tf_op jit(solution)/shard_map/ppermute | solution.py:324
  2.2 7.3 %collective-permute-start.2 = (s32[1,512]{1,0:T(1,128)}, s32[1,512]{1,0:T(1,128)S(1)}, u32[]{:S(2)}, u32[]{:S(2)}) collective-permute-start(s32[1,512]{1,0:T(1,128)} %bitcast.90), channel_id=1, source_target_pairs={{0,8},{8,0},{16,24},{24,16},{32,40},{40,32},{48,56},{56,48},{64,72... | collective-permute-start | bytes 6152 | tf_op jit(solution)/shard_map/ppermute | solution.py:323
  9.5 0.6 copy-start.17
  10.1 0.8 copy-start.12
  34.5 9.1 %collective-permute-start.4 = (bf16[2,512,256]{2,1,0:T(8,128)(2,1)}, bf16[2,512,256]{2,1,0:T(8,128)(2,1)S(1)}, u32[]{:S(2)}, u32[]{:S(2)}) collective-permute-start(bf16[2,512,256]{2,1,0:T(8,128)(2,1)} %shard_map.97), channel_id=1, source_target_pairs={{0,16},{8,72},{16,32},{24,88},{32,48},{40,104},{48,0},{56,120},{64... | collective-permute-start | bytes 1572872 | tf_op jit(solution)/shard_map/ppermute | solution.py:343
  34.9 16.0 %collective-permute-start.5 = (bf16[2,512,256]{2,1,0:T(8,128)(2,1)}, bf16[2,512,256]{2,1,0:T(8,128)(2,1)S(1)}, u32[]{:S(2)}, u32[]{:S(2)}) collective-permute-start(bf16[2,512,256]{2,1,0:T(8,128)(2,1)} %shard_map.97), channel_id=1, source_target_pairs={{0,48},{8,24},{16,0},{24,40},{32,16},{40,56},{48,32},{56,8},{64,11... | collective-permute-start | bytes 1572872 | tf_op jit(solution)/shard_map/ppermute | solution.py:343
  36.5 14.4 %collective-permute-start.6 = (bf16[2,512,256]{2,1,0:T(8,128)(2,1)}, bf16[2,512,256]{2,1,0:T(8,128)(2,1)S(1)}, u32[]{:S(2)}, u32[]{:S(2)}) collective-permute-start(bf16[2,512,256]{2,1,0:T(8,128)(2,1)} %shard_map.97), channel_id=1, source_target_pairs={{0,32},{8,56},{16,48},{24,8},{32,0},{40,24},{48,16},{56,40},{64,96... | collective-permute-start | bytes 1572872 | tf_op jit(solution)/shard_map/ppermute | solution.py:343
  41.1 14.1 %collective-permute-start = (s32[8,288]{1,0:T(8,128)}, s32[8,288]{1,0:T(8,128)S(1)}, u32[]{:S(2)}, u32[]{:S(2)}) collective-permute-start(s32[8,288]{1,0:T(8,128)} %shard_map.95), channel_id=1, source_target_pairs={{0,8},{8,0},{16,24},{24,16},{32,40},{40,32},{48,56},{56,48},{64,72... | collective-permute-start | bytes 27656 | tf_op jit(solution)/shard_map/ppermute | solution.py:335
  43.6 31.2 %copy-start = (bf16[2,512,256]{2,1,0:T(8,128)(2,1)}, bf16[2,512,256]{2,1,0:T(8,128)(2,1)S(1)}, u32[]{:S(2)}) copy-start(bf16[2,512,256]{2,1,0:T(8,128)(2,1)S(1)} %collective-permute-done.4) | copy-start | bytes 1572868
  43.6 19.3 %collective-permute-start.7 = (bf16[2,512,256]{2,1,0:T(8,128)(2,1)}, bf16[2,512,256]{2,1,0:T(8,128)(2,1)S(1)}, u32[]{:S(2)}, u32[]{:S(2)}) collective-permute-start(bf16[2,512,256]{2,1,0:T(8,128)(2,1)} %shard_map.97), channel_id=1, source_target_pairs={{0,64},{8,40},{16,80},{24,56},{32,96},{40,8},{48,112},{56,24},{64,... | collective-permute-start | bytes 1572872 | tf_op jit(solution)/shard_map/ppermute | solution.py:343
  50.9 24.0 %copy-start.1 = (bf16[2,512,256]{2,1,0:T(8,128)(2,1)}, bf16[2,512,256]{2,1,0:T(8,128)(2,1)S(1)}, u32[]{:S(2)}) copy-start(bf16[2,512,256]{2,1,0:T(8,128)(2,1)S(1)} %collective-permute-done.5) | copy-start | bytes 1572868
  50.9 24.0 %copy-start.2 = (bf16[2,512,256]{2,1,0:T(8,128)(2,1)}, bf16[2,512,256]{2,1,0:T(8,128)(2,1)S(1)}, u32[]{:S(2)}) copy-start(bf16[2,512,256]{2,1,0:T(8,128)(2,1)S(1)} %collective-permute-done.6) | copy-start | bytes 1572868
  52.1 21.1 %collective-permute-start.9 = (bf16[2,512,256]{2,1,0:T(8,128)(2,1)}, bf16[2,512,256]{2,1,0:T(8,128)(2,1)S(1)}, u32[]{:S(2)}, u32[]{:S(2)}) collective-permute-start(bf16[2,512,256]{2,1,0:T(8,128)(2,1)} %get-tuple-element.40), channel_id=1, source_target_pairs={{0,64},{8,56},{16,80},{24,8},{32,96},{40,24},{48,112},{56,40},{64,... | collective-permute-start | bytes 1572872 | tf_op jit(solution)/shard_map/ppermute | solution.py:343
  55.1 13.9 %collective-permute-start.8 = (bf16[2,512,256]{2,1,0:T(8,128)(2,1)S(1)}, bf16[2,512,256]{2,1,0:T(8,128)(2,1)S(1)}, u32[]{:S(2)}, u32[]{:S(2)}) collective-permute-start(bf16[2,512,256]{2,1,0:T(8,128)(2,1)S(1)} %collective-permute-done.4), channel_id=1, source_target_pairs={{0,64},{8,24},{16,80},{24,40},{32,96},{40,56},{48,112},{56,8},{64,... | collective-permute-start | bytes 1572872 | tf_op jit(solution)/shard_map/ppermute | solution.py:343
  55.1 19.7 %collective-permute-start.10 = (bf16[2,512,256]{2,1,0:T(8,128)(2,1)}, bf16[2,512,256]{2,1,0:T(8,128)(2,1)}, u32[]{:S(2)}, u32[]{:S(2)}) collective-permute-start(bf16[2,512,256]{2,1,0:T(8,128)(2,1)} %get-tuple-element.39), channel_id=1, source_target_pairs={{0,64},{8,40},{16,80},{24,56},{32,96},{40,8},{48,112},{56,24},{64,... | collective-permute-start | bytes 1572872 | tf_op jit(solution)/shard_map/ppermute | solution.py:343
  62.9 11.9 %copy-start.3 = (bf16[2,512,256]{2,1,0:T(8,128)(2,1)}, bf16[2,512,256]{2,1,0:T(8,128)(2,1)S(1)}, u32[]{:S(2)}) copy-start(bf16[2,512,256]{2,1,0:T(8,128)(2,1)S(1)} %collective-permute-done.7) | copy-start | bytes 1572868
  69.1 5.8 %copy-start.5 = (bf16[2,512,256]{2,1,0:T(8,128)(2,1)}, bf16[2,512,256]{2,1,0:T(8,128)(2,1)S(1)}, u32[]{:S(2)}) copy-start(bf16[2,512,256]{2,1,0:T(8,128)(2,1)S(1)} %collective-permute-done.8) | copy-start | bytes 1572868
  73.2 1.7 copy-start.4
  89.2 40.7 %collective-permute-start.15 = (bf16[4,512,256]{2,1,0:T(8,128)(2,1)}, bf16[4,512,256]{2,1,0:T(8,128)(2,1)S(1)}, u32[]{:S(2)}, u32[]{:S(2)}) collective-permute-start(bf16[4,512,256]{2,1,0:T(8,128)(2,1)} %get-tuple-element.25), channel_id=1, source_target_pairs={{0,4},{1,5},{2,6},{3,7},{4,0},{5,1},{6,2},{7,3},{8,12},{9,13},{10,... | collective-permute-start | bytes 3145736 | tf_op jit(solution)/shard_map/ppermute | solution.py:382
  103.1 14.3 %collective-permute-start.11 = (bf16[2,512,256]{2,1,0:T(8,128)(2,1)}, bf16[2,512,256]{2,1,0:T(8,128)(2,1)S(1)}, u32[]{:S(2)}, u32[]{:S(2)}) collective-permute-start(bf16[2,512,256]{2,1,0:T(8,128)(2,1)} %get-tuple-element.19), channel_id=1, source_target_pairs={{0,1},{1,2},{2,3},{3,0},{4,5},{5,6},{6,7},{7,4},{8,9},{9,10},{10,1... | collective-permute-start | bytes 1572872 | tf_op jit(solution)/shard_map/ppermute | solution.py:380
  103.2 16.2 %collective-permute-start.12 = (bf16[2,512,256]{2,1,0:T(8,128)(2,1)}, bf16[2,512,256]{2,1,0:T(8,128)(2,1)S(1)}, u32[]{:S(2)}, u32[]{:S(2)}) collective-permute-start(bf16[2,512,256]{2,1,0:T(8,128)(2,1)} %get-tuple-element.20), channel_id=1, source_target_pairs={{0,2},{1,3},{2,0},{3,1},{4,6},{5,7},{6,4},{7,5},{8,10},{9,11},{10,... | collective-permute-start | bytes 1572872 | tf_op jit(solution)/shard_map/ppermute | solution.py:380
  105.8 19.4 %collective-permute-start.13 = (bf16[2,512,256]{2,1,0:T(8,128)(2,1)}, bf16[2,512,256]{2,1,0:T(8,128)(2,1)S(1)}, u32[]{:S(2)}, u32[]{:S(2)}) collective-permute-start(bf16[2,512,256]{2,1,0:T(8,128)(2,1)} %get-tuple-element.21), channel_id=1, source_target_pairs={{0,3},{1,0},{2,1},{3,2},{4,7},{5,4},{6,5},{7,6},{8,11},{9,8},{10,9... | collective-permute-start | bytes 1572872 | tf_op jit(solution)/shard_map/ppermute | solution.py:380
  117.5 7.7 %copy-start.8 = (bf16[2,512,256]{2,1,0:T(8,128)(2,1)}, bf16[2,512,256]{2,1,0:T(8,128)(2,1)S(1)}, u32[]{:S(2)}) copy-start(bf16[2,512,256]{2,1,0:T(8,128)(2,1)S(1)} %collective-permute-done.11.a_ref) | copy-start | bytes 1572868
  119.4 5.8 %copy-start.9 = (bf16[2,512,256]{2,1,0:T(8,128)(2,1)}, bf16[2,512,256]{2,1,0:T(8,128)(2,1)S(1)}, u32[]{:S(2)}) copy-start(bf16[2,512,256]{2,1,0:T(8,128)(2,1)S(1)} %collective-permute-done.12.b_ref) | copy-start | bytes 1572868
  125.2 0.8 copy-start.11
  128.5 9.5 %collective-permute-start.14 = (bf16[512,256]{1,0:T(8,128)(2,1)}, bf16[512,256]{1,0:T(8,128)(2,1)S(1)}, u32[]{:S(2)}, u32[]{:S(2)}) collective-permute-start(bf16[512,256]{1,0:T(8,128)(2,1)} %get-tuple-element.23), channel_id=1, source_target_pairs={{0,4},{1,5},{2,6},{3,7},{4,0},{5,1},{6,2},{7,3},{8,12},{9,13},{10,... | collective-permute-start | bytes 786440 | tf_op jit(solution)/shard_map/ppermute | solution.py:387
  129.9 1.0 copy-start.6
  133.7 6.6 %collective-permute-start.16 = (bf16[512,256]{1,0:T(8,128)(2,1)}, bf16[512,256]{1,0:T(8,128)(2,1)S(1)}, u32[]{:S(2)}, u32[]{:S(2)}) collective-permute-start(bf16[512,256]{1,0:T(8,128)(2,1)} %get-tuple-element.27), channel_id=1, source_target_pairs={{0,1},{1,2},{2,3},{3,0},{4,5},{5,6},{6,7},{7,4},{8,9},{9,10},{10,1... | collective-permute-start | bytes 786440 | tf_op jit(solution)/shard_map/ppermute | solution.py:391
  135.6 8.5 %collective-permute-start.17 = (bf16[512,256]{1,0:T(8,128)(2,1)}, bf16[512,256]{1,0:T(8,128)(2,1)S(1)}, u32[]{:S(2)}, u32[]{:S(2)}) collective-permute-start(bf16[512,256]{1,0:T(8,128)(2,1)} %get-tuple-element.28), channel_id=1, source_target_pairs={{0,2},{1,3},{2,0},{3,1},{4,6},{5,7},{6,4},{7,5},{8,10},{9,11},{10,... | collective-permute-start | bytes 786440 | tf_op jit(solution)/shard_map/ppermute | solution.py:391
  137.0 7.1 %collective-permute-start.18 = (bf16[512,256]{1,0:T(8,128)(2,1)}, bf16[512,256]{1,0:T(8,128)(2,1)S(1)}, u32[]{:S(2)}, u32[]{:S(2)}) collective-permute-start(bf16[512,256]{1,0:T(8,128)(2,1)} %get-tuple-element.29), channel_id=1, source_target_pairs={{0,3},{1,0},{2,1},{3,2},{4,7},{5,4},{6,5},{7,6},{8,11},{9,8},{10,9... | collective-permute-start | bytes 786440 | tf_op jit(solution)/shard_map/ppermute | solution.py:391
  138.0 6.1 %copy-start.13 = (bf16[512,256]{1,0:T(8,128)(2,1)}, bf16[512,256]{1,0:T(8,128)(2,1)S(1)}, u32[]{:S(2)}) copy-start(bf16[512,256]{1,0:T(8,128)(2,1)S(1)} %collective-permute-done.14.got0) | copy-start | bytes 786436
  140.4 3.7 %copy-start.14 = (bf16[512,256]{1,0:T(8,128)(2,1)}, bf16[512,256]{1,0:T(8,128)(2,1)S(1)}, u32[]{:S(2)}) copy-start(bf16[512,256]{1,0:T(8,128)(2,1)S(1)} %collective-permute-done.16.a_ref) | copy-start | bytes 786436
  144.1 0.7 copy-start.15
  144.1 0.8 copy-start.16
  147.5 13.6 %collective-permute-start.19 = (f32[512,256]{1,0:T(8,128)}, f32[512,256]{1,0:T(8,128)S(1)}, u32[]{:S(2)}, u32[]{:S(2)}) collective-permute-start(f32[512,256]{1,0:T(8,128)} %get-tuple-element.31.other_ref), channel_id=1, source_target_pairs={{0,8},{8,0},{16,24},{24,16},{32,40},{40,32},{48,56},{56,48},{64,72... | collective-permute-start | bytes 1572872 | tf_op jit(solution)/shard_map/ppermute | solution.py:395
  161.2 0.8 copy-start.10
  165.5 2.1 collective-permute-start.20
  167.6 0.8 copy-start.7
  172.5 3.5 %collective-permute-start.23 = (bf16[64,512]{1,0:T(8,128)(2,1)S(1)}, bf16[64,512]{1,0:T(8,128)(2,1)S(1)}, u32[]{:S(2)}, u32[]{:S(2)}) collective-permute-start(bf16[64,512]{1,0:T(8,128)(2,1)S(1)} %get-tuple-element.37), channel_id=1, source_target_pairs={{0,3},{1,0},{2,1},{3,2},{4,7},{5,4},{6,5},{7,6},{8,11},{9,8},{10,9... | collective-permute-start | bytes 196616 | tf_op jit(solution)/shard_map/ppermute | solution.py:268
  174.7 6.3 %collective-permute-start.22 = (bf16[64,512]{1,0:T(8,128)(2,1)S(1)}, bf16[64,512]{1,0:T(8,128)(2,1)S(1)}, u32[]{:S(2)}, u32[]{:S(2)}) collective-permute-start(bf16[64,512]{1,0:T(8,128)(2,1)S(1)} %get-tuple-element.38), channel_id=1, source_target_pairs={{0,1},{1,2},{2,3},{3,0},{4,5},{5,6},{6,7},{7,4},{8,9},{9,10},{10,1... | collective-permute-start | bytes 196616 | tf_op jit(solution)/shard_map/ppermute | solution.py:268
  174.7 6.3 %collective-permute-start.21 = (bf16[64,512]{1,0:T(8,128)(2,1)S(1)}, bf16[64,512]{1,0:T(8,128)(2,1)S(1)}, u32[]{:S(2)}, u32[]{:S(2)}) collective-permute-start(bf16[64,512]{1,0:T(8,128)(2,1)S(1)} %get-tuple-element.36), channel_id=1, source_target_pairs={{0,2},{1,3},{2,0},{3,1},{4,6},{5,7},{6,4},{7,5},{8,10},{9,11},{10,... | collective-permute-start | bytes 196616 | tf_op jit(solution)/shard_map/ppermute | solution.py:268
  181.9 4.3 %collective-permute-start.26 = (f32[64,512]{1,0:T(8,128)S(1)}, f32[64,512]{1,0:T(8,128)S(1)}, u32[]{:S(2)}, u32[]{:S(2)}) collective-permute-start(f32[64,512]{1,0:T(8,128)S(1)} %fusion.1), channel_id=1, source_target_pairs={{0,48},{8,56},{16,0},{24,8},{32,16},{40,24},{48,32},{56,40},{64,11... | collective-permute-start | bytes 393224 | tf_op jit(solution)/shard_map/ppermute | solution.py:273
  182.0 5.8 %collective-permute-start.25 = (f32[64,512]{1,0:T(8,128)S(1)}, f32[64,512]{1,0:T(8,128)S(1)}, u32[]{:S(2)}, u32[]{:S(2)}) collective-permute-start(f32[64,512]{1,0:T(8,128)S(1)} %fusion.1), channel_id=1, source_target_pairs={{0,32},{8,40},{16,48},{24,56},{32,0},{40,8},{48,16},{56,24},{64,96... | collective-permute-start | bytes 393224 | tf_op jit(solution)/shard_map/ppermute | solution.py:273
  182.1 9.6 %collective-permute-start.24 = (f32[64,512]{1,0:T(8,128)S(1)}, f32[64,512]{1,0:T(8,128)S(1)}, u32[]{:S(2)}, u32[]{:S(2)}) collective-permute-start(f32[64,512]{1,0:T(8,128)S(1)} %fusion.1), channel_id=1, source_target_pairs={{0,16},{8,24},{16,32},{24,40},{32,48},{40,56},{48,0},{56,8},{64,80... | collective-permute-start | bytes 393224 | tf_op jit(solution)/shard_map/ppermute | solution.py:273
  191.8 6.5 %collective-permute-start.29 = (f32[64,512]{1,0:T(8,128)S(1)}, f32[64,512]{1,0:T(8,128)S(1)}, u32[]{:S(2)}, u32[]{:S(2)}) collective-permute-start(f32[64,512]{1,0:T(8,128)S(1)} %fusion.6), channel_id=1, source_target_pairs={{0,68},{1,69},{2,70},{3,71},{4,64},{5,65},{6,66},{7,67},{8,76},{9,... | collective-permute-start | bytes 393224 | tf_op jit(solution)/shard_map/ppermute | solution.py:273
  194.0 5.3 %collective-permute-start.28 = (f32[64,512]{1,0:T(8,128)S(1)}, f32[64,512]{1,0:T(8,128)S(1)}, u32[]{:S(2)}, u32[]{:S(2)}) collective-permute-start(f32[64,512]{1,0:T(8,128)S(1)} %fusion.6), channel_id=1, source_target_pairs={{0,4},{1,5},{2,6},{3,7},{4,0},{5,1},{6,2},{7,3},{8,12},{9,13},{10,... | collective-permute-start | bytes 393224 | tf_op jit(solution)/shard_map/ppermute | solution.py:273
  196.8 6.9 %collective-permute-start.27 = (f32[64,512]{1,0:T(8,128)S(1)}, f32[64,512]{1,0:T(8,128)S(1)}, u32[]{:S(2)}, u32[]{:S(2)}) collective-permute-start(f32[64,512]{1,0:T(8,128)S(1)} %fusion.6), channel_id=1, source_target_pairs={{0,64},{1,65},{2,66},{3,67},{4,68},{5,69},{6,70},{7,71},{8,72},{9,... | collective-permute-start | bytes 393224 | tf_op jit(solution)/shard_map/ppermute | solution.py:273
  203.8 3.2 %collective-permute-start.32 = (bf16[64,512]{1,0:T(8,128)(2,1)S(1)}, bf16[64,512]{1,0:T(8,128)(2,1)S(1)}, u32[]{:S(2)}, u32[]{:S(2)}) collective-permute-start(bf16[64,512]{1,0:T(8,128)(2,1)S(1)} %fusion.5), channel_id=1, source_target_pairs={{0,3},{1,0},{2,1},{3,2},{4,7},{5,4},{6,5},{7,6},{8,11},{9,8},{10,9... | collective-permute-start | bytes 196616 | tf_op jit(solution)/shard_map/ppermute | solution.py:273
  203.9 4.7 %collective-permute-start.31 = (bf16[64,512]{1,0:T(8,128)(2,1)S(1)}, bf16[64,512]{1,0:T(8,128)(2,1)S(1)}, u32[]{:S(2)}, u32[]{:S(2)}) collective-permute-start(bf16[64,512]{1,0:T(8,128)(2,1)S(1)} %fusion.5), channel_id=1, source_target_pairs={{0,2},{1,3},{2,0},{3,1},{4,6},{5,7},{6,4},{7,5},{8,10},{9,11},{10,... | collective-permute-start | bytes 196616 | tf_op jit(solution)/shard_map/ppermute | solution.py:273
  204.0 5.4 %collective-permute-start.30 = (bf16[64,512]{1,0:T(8,128)(2,1)S(1)}, bf16[64,512]{1,0:T(8,128)(2,1)S(1)}, u32[]{:S(2)}, u32[]{:S(2)}) collective-permute-start(bf16[64,512]{1,0:T(8,128)(2,1)S(1)} %fusion.5), channel_id=1, source_target_pairs={{0,1},{1,2},{2,3},{3,0},{4,5},{5,6},{6,7},{7,4},{8,9},{9,10},{10,1... | collective-permute-start | bytes 196616 | tf_op jit(solution)/shard_map/ppermute | solution.py:273
  209.5 4.3 %collective-permute-start.33 = (bf16[256,512]{1,0:T(8,128)(2,1)S(1)}, bf16[256,512]{1,0:T(8,128)(2,1)S(1)}, u32[]{:S(2)}, u32[]{:S(2)}) collective-permute-start(bf16[256,512]{1,0:T(8,128)(2,1)S(1)} %pad_maximum_fusion.3), channel_id=1, source_target_pairs={{0,8},{8,0},{16,24},{24,16},{32,40},{40,32},{48,56},{56,48},{64,72... | collective-permute-start | bytes 786440 | tf_op jit(solution)/shard_map/ppermute | solution.py:412

commit v4 on v3

--- a/solution.py
+++ b/solution.py
@@ -18,13 +18,14 @@
 GROUP_BITS = 2
 GROUP = 1 << GROUP_BITS
 PLAN = SLOT_CAP + ROW_TILES * (GROUP - 1)
+UNROLL_BITS = 2
+UNROLL = 1 << UNROLL_BITS
 BF16 = jnp.bfloat16
 F32 = jnp.float32
-VMEM_LIMIT = 56 * 1024 * 1024
-
-
-def params():
-    return pltpu.CompilerParams(vmem_limit_bytes=VMEM_LIMIT)
+
+
+def params(limit=16):
+    return pltpu.CompilerParams(vmem_limit_bytes=limit * 1024 * 1024)
 
 
 def selection(position, rows, columns):
@@ -107,33 +108,24 @@
     plan_ref[...] = found.astype(jnp.int32)
 
 
-def tiles_kernel(part, meta_ref, plan_ref, own_hbm, other_hbm, *refs):
-    blocks, outs = refs[:CHIPS], refs[CHIPS:-6]
-    tiles, source, total, narrow, sems, out_sems = refs[-6:]
-    core, x, yh = meta_ref[0], meta_ref[1], meta_ref[2]
-    live = tiles.at[pl.ds(0, SLOT_CAP)]
-    own_copy = pltpu.make_async_copy(own_hbm, live, sems.at[CHIPS])
-    other_copy = pltpu.make_async_copy(other_hbm, live, sems.at[CHIPS])
-
-    @pl.when(core == part)
-    def _():
-        own_copy.start()
-
-    @pl.when(core != part)
-    def _():
-        other_copy.start()
-
-    copies = [
-        pltpu.make_async_copy(blocks[k], source.at[meta_ref[4 + k]], sems.at[k])
-        for k in range(CHIPS)
-    ]
-    for copy in copies:
-        copy.start()
-    tiles[SLOT_CAP] = jnp.zeros((TILE, TILE), BF16)
+def stage_kernel(meta_ref, own_hbm, other_hbm, first_ref, second_ref, sems):
+    core = meta_ref[0]
+    refs = (first_ref, second_ref)
+    for out in refs:
+        out[SLOT_CAP] = jnp.zeros((TILE, TILE), BF16)
+    for c in range(2):
+
+        @pl.when(core == c)
+        def _():
+            for hbm, out, k in ((own_hbm, refs[c], 0), (other_hbm, refs[1 - c], 1)):
+                pltpu.make_async_copy(hbm, out.at[pl.ds(0, SLOT_CAP)], sems.at[k]).start()
+
+    for hbm, k in ((own_hbm, 0), (other_hbm, 1)):
+        pltpu.make_async_copy(hbm, refs[k].at[pl.ds(0, SLOT_CAP)], sems.at[k]).wait()
+
+
+def add_tiles(plan_ref, tiles, source, total):
     total[...] = jnp.zeros_like(total)
-    own_copy.wait()
-    for copy in copies:
-        copy.wait()
 
     def product(g):
         left, right = [], []
@@ -147,27 +139,48 @@
             preferred_element_type=F32,
         )
 
-    def two_groups(h, carry):
-        g = h * 2
-        first, second = product(g), product(g + 1)
-        total[plan_ref[2, g * GROUP]] += first
-        total[plan_ref[2, g * GROUP + GROUP]] += second
+    def some_groups(h, carry):
+        found = [
+            (plan_ref[2, (h * UNROLL + k) * GROUP], product(h * UNROLL + k))
+            for k in range(UNROLL)
+        ]
+        for place, value in found:
+            total[place] += value
         return carry
 
-    lax.fori_loop(0, (plan_ref[3, 0] + 1) >> 1, two_groups, 0)
-    narrow[...] = total[...].astype(BF16).reshape(narrow.shape)
-    if part == 0:
-        given = [narrow.at[:, (x + k) & 3] for k in range(4)]
-    else:
-        given = [narrow.at[yh], narrow.at[1 - yh]]
+    lax.fori_loop(0, (plan_ref[3, 0] + UNROLL - 1) >> UNROLL_BITS, some_groups, 0)
+
+
+def narrow_block(total, yh, x):
+    rows = total[pl.ds((yh * 4 + x) * 4, 4)].astype(BF16)
+    return rows.reshape(SLOTS, HALF)
+
+
+def tiles_y_kernel(meta_ref, plan_ref, tiles, *refs):
+    blocks, (keep_ref, send_ref, source) = refs[:CHIPS], refs[CHIPS : CHIPS + 3]
+    total, sems = refs[CHIPS + 3 :]
+    yh = meta_ref[2]
     copies = [
-        pltpu.make_async_copy(piece, out, out_sems.at[k])
-        for k, (piece, out) in enumerate(zip(given, outs))
+        pltpu.make_async_copy(blocks[k], source.at[meta_ref[4 + k]], sems.at[k])
+        for k in range(CHIPS)
     ]
     for copy in copies:
         copy.start()
     for copy in copies:
         copy.wait()
+    add_tiles(plan_ref, tiles, source, total)
+    for out, to in ((send_ref, 1 - yh), (keep_ref, yh)):
+        for x in range(4):
+            out[x] = narrow_block(total, to, x)
+
+
+def tiles_x_kernel(meta_ref, plan_ref, tiles, source, *refs):
+    outs, total = refs[:4], refs[4]
+    x = meta_ref[1]
+    add_tiles(plan_ref, tiles, source, total)
+    for k, out in enumerate(outs):
+        for yh in range(2):
+            out[yh] = narrow_block(total, yh, (x + k) & 3)
 
 
 def x_summed_kernel(meta_ref, own_ref, a_ref, b_ref, c_ref, keep_ref, send_ref):
@@ -274,19 +287,38 @@
     return [got[(me - k) % 4] for k in range(4)]
 
 
-def call(kernel, in_specs, outs, scratch=()):
-    return pl.pallas_call(
+def call(kernel, in_specs, outs, scratch=(), limit=16):
+    made = pl.pallas_call(
         kernel,
         in_specs=in_specs,
         out_specs=jax.tree.map(lambda _: pl.BlockSpec(memory_space=pltpu.VMEM), outs),
         out_shape=outs,
         scratch_shapes=list(scratch),
-        compiler_params=params(),
-    )
+        compiler_params=params(limit),
+    )
+
+    def run(*operands):
+        held = [
+            pltpu.with_memory_space_constraint(o, pltpu.VMEM)
+            if spec.memory_space == pltpu.VMEM
+            else o
+            for spec, o in zip(in_specs, operands)
+        ]
+        return made(*held)
+
+    return run
 
 
 def array(*shape, dtype=BF16):
     return jax.ShapeDtypeStruct(shape, dtype)
+
+
+def held(*shape, dtype=BF16):
+    return pltpu.VMEM(shape, dtype)
+
+
+def after(value, *others):
+    return lax.optimization_barrier((value, *others))[0]
 
 
 def shards(
@@ -322,18 +354,28 @@
     part = partition_of.reshape(1, SLOTS)
     other_part = lax.ppermute(part, "row", swap)
     other_features = lax.ppermute(features, "row", swap)
-    other_tiles = lax.ppermute(tiles, "row", swap)
+    plan = call(plan_kernel, [smem, vmem, vmem], array(8, PLAN, dtype=jnp.int32))(
+        tile_count.reshape(1), tile_rows.reshape(1, -1), tile_cols.reshape(1, -1)
+    )
+    other_plan = lax.ppermute(plan, "row", swap)
+    other_features = after(other_features, other_plan)
+    plans = [jnp.where(core == c, plan, other_plan) for c in range(2)]
+    other_tiles = lax.ppermute(after(tiles, other_features), "row", swap)
     grouped = call(
         group_kernel,
         [smem, vmem, vmem, vmem, vmem],
-        array(N_COL, 2, SLOTS // N_COL, HALF),
+        held(N_COL, 2, SLOTS // N_COL, HALF),
     )(meta, part, features, other_part, other_features)
     arrived = lax.all_to_all(grouped, "col", split_axis=0, concat_axis=0, tiled=True)
-    plan = call(plan_kernel, [smem, vmem, vmem], array(8, PLAN, dtype=jnp.int32))(
-        tile_count.reshape(1), tile_rows.reshape(1, -1), tile_cols.reshape(1, -1)
-    )
-    other_plan = lax.ppermute(plan, "row", swap)
     own = call(interleave_kernel, [vmem], array(2, SLOTS, HALF))(arrived)
+    own = after(own, other_tiles)
+
+    tiles0, tiles1 = call(
+        stage_kernel,
+        [smem, hbm, hbm],
+        [held(SLOT_CAP + 1, TILE, TILE)] * 2,
+        [pltpu.SemaphoreType.DMA((2,))],
+    )(meta, tiles, after(other_tiles, own))
 
     def hop(block, move0, move1):
         def move(yl, z, c):
@@ -353,52 +395,43 @@
         b.reshape(2, N_ROW, N_COL * PER_PEER, HALF) for b in (own, r1, r2, r3, r4, s1, s2, s3)
     ]
 
-    def tile_sums(part, outs):
-        return pl.pallas_call(
-            lambda *refs: tiles_kernel(part, *refs),
-            in_specs=[smem, smem] + [hbm] * (2 + CHIPS),
-            out_specs=[hbm] * len(outs),
-            out_shape=outs,
-            scratch_shapes=[
-                pltpu.VMEM((SLOT_CAP + 1, TILE, TILE), BF16),
-                pltpu.VMEM((CHIPS, 2, N_ROW, N_COL * PER_PEER, HALF), BF16),
-                pltpu.VMEM((ROW_TILES, TILE, HALF), F32),
-                pltpu.VMEM((2, 4, SLOTS, HALF), BF16),
-                pltpu.SemaphoreType.DMA((CHIPS + 1,)),
-                pltpu.SemaphoreType.DMA((4,)),
-            ],
-            compiler_params=params(),
-        )(
-            meta,
-            jnp.where(core == part, plan, other_plan),
-            tiles,
-            other_tiles,
-            *blocks,
-        )
-
-    row0 = tile_sums(0, [array(2, SLOTS, HALF)] * 4)
+    total = pltpu.VMEM((ROW_TILES, TILE, HALF), F32)
+    source = held(CHIPS, 2, N_ROW, N_COL * PER_PEER, HALF)
+    keep1, send1, source = call(
+        tiles_y_kernel,
+        [smem, smem, vmem] + [hbm] * CHIPS,
+        [held(4, SLOTS, HALF), held(4, SLOTS, HALF), source],
+        [total, pltpu.SemaphoreType.DMA((CHIPS,))],
+    )(meta, plans[1], tiles1, *blocks)
+    row0 = call(
+        tiles_x_kernel,
+        [smem, smem, vmem, vmem],
+        [held(2, SLOTS, HALF)] * 4,
+        [total],
+    )(meta, plans[0], tiles0, source)
     got0 = [lax.ppermute(row0[k], "col", x_moves(k)) for k in (1, 2, 3)]
-    keep1, send1 = tile_sums(1, [array(4, SLOTS, HALF)] * 2)
     got1 = lax.ppermute(send1, "col", y_moves())
-    wide, narrow = array(SLOTS, HALF, dtype=F32), array(SLOTS, HALF)
-    keep0, send0 = call(x_summed_kernel, [smem] + [vmem] * 4, [wide, narrow])(
-        meta, row0[0], *got0
-    )
-    got0 = lax.ppermute(send0, "col", y_moves())
+    wide, narrow = held(SLOTS, HALF, dtype=F32), held(SLOTS, HALF)
     keep1, *send1 = call(y_summed_kernel, [smem] + [vmem] * 2, [wide] + [narrow] * 3)(
         meta, keep1, got1
     )
+    keep0, send0 = call(x_summed_kernel, [smem] + [vmem] * 4, [wide, narrow])(
+        meta, after(row0[0], *send1), *got0
+    )
+    got0 = lax.ppermute(send0, "col", y_moves())
     got1 = [lax.ppermute(send1[k - 1], "col", x_moves(k)) for k in (1, 2, 3)]
     mine, others = call(sums_kernel, [smem] + [vmem] * 6, [wide] * 2)(
         meta, keep0, got0, keep1, *got1
     )
     theirs = lax.ppermute(others, "row", swap)
     cotangent = lax.dynamic_slice_in_dim(out_cotangent, col * SLOTS, SLOTS, 0)
-    activations, slope = call(layer_kernel, [smem] + [vmem] * 4, [array(SLOTS, F)] * 2)(
+    activations, slope = call(
+        layer_kernel, [smem] + [vmem] * 4, [array(SLOTS, F), held(SLOTS, F)]
+    )(
         meta, mine, theirs, weight, cotangent
     )
     other_slope = lax.ppermute(slope, "row", swap)
-    half = call(gradient_kernel, [vmem] * 4, array(HALF, F, dtype=F32))(
+    half = call(gradient_kernel, [vmem] * 4, held(HALF, F, dtype=F32))(
         mine, others, slope, other_slope
     )
 

time: 216 us -> 186 us (0.86)
  Pallas kernels: 46.2 us -> 21.1 us
  other arithmetic: 4.97 us -> 2.58 us
    pallas_call x10 -> x11, Pallas kernels: 46.2 us -> 21.1 us  [run(): return made(*held)]
    ppermute x3, waiting for transfers between devices: 17.4 us -> 5.59 us  [shards(): got0 = [lax.ppermute(row0[k], 'col', x_moves(k)) for k in (1, 2, 3)]]
    ppermute x1, starting transfers between devices: 11.7 us -> 19 us  [shards(): theirs = lax.ppermute(others, 'row', swap)]
    ppermute x1, waiting for transfers between devices: 0.01 us -> 4 us  [shards(): got1 = lax.ppermute(send1, 'col', y_moves())]
    ppermute x9, starting transfers between devices: 8.05 us -> 4.58 us  [by_giver(): lax.ppermute(own, axis, moves(k))]
    ppermute x1, starting transfers between devices: 2.55 us -> 0.04 us  [shards(): other_plan = lax.ppermute(plan, 'row', swap)]
    ppermute x3, waiting for transfers between devices: 6.06 us -> 8.34 us  [shards(): got1 = [lax.ppermute(send1[k - 1], 'col', x_moves(k)) for k in (1, 2, 3)]]
    ppermute x1, waiting for transfers between devices: 6.27 us -> 4.02 us  [shards(): other_part = lax.ppermute(part, 'row', swap)]
  transfers between devices with their start and end apart: 34 -> 34, of which waited for: 24 -> 26; matrix products, arithmetic and copies ran while one was open for 2% -> 1% of each run, Pallas kernels for 11% -> 6%
where the time goes in v4:
time: 186 us; the launch traced here: 185 us
  waiting for transfers between devices  77.2 us (42%)
  starting transfers between devices  57.7 us (31%)
  Pallas kernels  21.1 us (11%)
  blocking collectives  17.8 us (10%)
  local copies, waits for them, and re-layouts  7.09 us (4%)
  other arithmetic  2.58 us (1%)
    ppermute x7, waiting for transfers between devices, hop(): return lax.ppermute(block, 'row', row_moves(move))  23.1 us
    pallas_call x11, Pallas kernels, run(): return made(*held)  21.1 us
    ppermute x9, waiting for transfers between devices, by_giver(): lax.ppermute(own, axis, moves(k))  20.9 us
    ppermute x1, starting transfers between devices, shards(): theirs = lax.ppermute(others, 'row', swap)  19 us
    all_to_all x1, blocking collectives, shards(): lax.all_to_all(grouped, 'col', split_axis=0, concat_axis=0, tiled=True)  17.8 us
    ppermute x7, starting transfers between devices, hop(): return lax.ppermute(block, 'row', row_moves(move))  9.16 us
    ppermute x3, waiting for transfers between devices, shards(): got1 = [lax.ppermute(send1[k - 1], 'col', x_moves(k)) for k in (1, 2, 3)]  8.34 us
    ppermute x3, starting transfers between devices, shards(): got0 = [lax.ppermute(row0[k], 'col', x_moves(k)) for k in (1, 2, 3)]  6.06 us
  transfers between devices with their start and end apart: 34, of which 26 were waited for; matrix products, arithmetic and copies ran while one was open for 1% of the time, Pallas kernels for 6%

profile of v4, /device:TPU:1, one launch (start us, length us, event | category | flops | bytes accessed | tf_op | source)
XLA Modules:
  0.0 185.1 jit_solution(6517066665486713035)
XLA Ops:
  0.6 1.5 collective-permute-start.1
  2.8 0.7 copy-done.4
  3.5 0.7 copy-done.5
  4.6 1.2 collective-permute-done
  6.4 4.0 %collective-permute-done.3.other_part_ref = s32[1,512]{1,0:T(1,128)S(1)} collective-permute-done((s32[1,512]{1,0:T(1,128)}, s32[1,512]{1,0:T(1,128)S(1)}, u32[]{:S(2)}, u32[]{:S(2)}) %collective-permute-start.3) | collective-permute-done | bytes 2080 | tf_op jit(solution)/shard_map/ppermute | solution.py:355
  10.4 1.0 copy-done.2
  11.5 0.7 copy-done.3
  12.2 1.3 shard_map.96
  13.4 17.8 %all_to_all.5.arrived_ref = bf16[8,2,64,256]{3,2,1,0:T(8,128)(2,1)S(1)} all-to-all(bf16[8,2,64,256]{3,2,1,0:T(8,128)(2,1)S(1)} %shard_map.96), channel_id=1, replica_groups=mesh['row'=16,'col'=8] {'col'}, dimensions={0} | all-to-all | bytes 1048576 | tf_op jit(solution)/shard_map/all_to_all | solution.py:369
  31.7 0.5 collective-permute-start.4
  32.2 1.6 collective-permute-start.5
  33.8 1.8 collective-permute-start.6
  35.6 1.6 collective-permute-start.7
  37.2 2.9 %collective-permute-done.4 = bf16[2,512,256]{2,1,0:T(8,128)(2,1)S(1)} collective-permute-done((bf16[2,512,256]{2,1,0:T(8,128)(2,1)S(1)}, bf16[2,512,256]{2,1,0:T(8,128)(2,1)S(1)}, u32[]{:S(2)}, u32[]{:S(2)}) %collective-permute-start.4) | collective-permute-done | bytes 524320 | tf_op jit(solution)/shard_map/ppermute | solution.py:385
  40.1 6.6 %collective-permute-done.5 = bf16[2,512,256]{2,1,0:T(8,128)(2,1)S(1)} collective-permute-done((bf16[2,512,256]{2,1,0:T(8,128)(2,1)S(1)}, bf16[2,512,256]{2,1,0:T(8,128)(2,1)S(1)}, u32[]{:S(2)}, u32[]{:S(2)}) %collective-permute-start.5) | collective-permute-done | bytes 524320 | tf_op jit(solution)/shard_map/ppermute | solution.py:385
  46.7 1.1 broadcast_select_fusion
  47.8 2.4 %collective-permute-start.9 = (bf16[2,512,256]{2,1,0:T(8,128)(2,1)}, bf16[2,512,256]{2,1,0:T(8,128)(2,1)S(1)}, u32[]{:S(2)}, u32[]{:S(2)}) collective-permute-start(bf16[2,512,256]{2,1,0:T(8,128)(2,1)} %get-tuple-element.56), channel_id=1, source_target_pairs={{0,64},{8,56},{16,80},{24,8},{32,96},{40,24},{48,112},{56,40},{64,... | collective-permute-start | bytes 1572872 | tf_op jit(solution)/shard_map/ppermute | solution.py:385
  50.2 1.2 collective-permute-start.10
  51.4 2.8 %copy-done = bf16[1,1,192,128,128]{4,3,2,1,0:T(8,128)(2,1)S(1)} copy-done((bf16[1,1,192,128,128]{4,3,2,1,0:T(8,128)(2,1)S(1)}, bf16[1,1,192,128,128]{4,3,2,1,0:T(8,128)(2,1)}, u32[]{:S(2)}) %copy-start) | copy-done | bytes 6291480
  54.2 3.8 %shard_map.98 = (bf16[193,128,128]{2,1,0:T(8,128)(2,1)S(1)}, bf16[193,128,128]{2,1,0:T(8,128)(2,1)S(1)}) custom-call(s32[12]{0:T(128)S(1)} %stack.92.meta_ref, bf16[192,128,128]{2,1,0:T(8,128)(2,1)S(1)} %bitcast.62, bf16[192,128,128]{2,1,0:T(8,128)(2,1)} %collective-permute-done.2.other_hbm), custom_call_target="tpu_custom_call" | custom-call | tf_op jit(solution)/shard_map/pallas_call | solution.py:307
  58.0 0.9 collective-permute-done.7
  58.9 7.1 %collective-permute-done.8 = bf16[2,512,256]{2,1,0:T(8,128)(2,1)} collective-permute-done((bf16[2,512,256]{2,1,0:T(8,128)(2,1)S(1)}, bf16[2,512,256]{2,1,0:T(8,128)(2,1)}, u32[]{:S(2)}, u32[]{:S(2)}) %collective-permute-start.8) | collective-permute-done | bytes 524320 | tf_op jit(solution)/shard_map/ppermute | solution.py:385
  66.0 4.0 %collective-permute-done.9 = bf16[2,512,256]{2,1,0:T(8,128)(2,1)S(1)} collective-permute-done((bf16[2,512,256]{2,1,0:T(8,128)(2,1)}, bf16[2,512,256]{2,1,0:T(8,128)(2,1)S(1)}, u32[]{:S(2)}, u32[]{:S(2)}) %collective-permute-start.9) | collective-permute-done | bytes 524320 | tf_op jit(solution)/shard_map/ppermute | solution.py:385
  70.0 1.6 collective-permute-done.10
  71.6 5.3 %shard_map.99 = (bf16[4,512,256]{2,1,0:T(8,128)(2,1)S(1)}, bf16[4,512,256]{2,1,0:T(8,128)(2,1)S(1)}, bf16[8,2,16,32,256]{4,3,2,1,0:T(8,128)(2,1)S(1)}) custom-call(s32[12]{0:T(128)S(1)} %stack.92.meta_ref, s32[8,288]{1,0:T(8,128)S(1)} %get-tuple-element.61.plan_ref, bf16[193,128,128]{2,1,0:T(8,128)(2,1)S(1)} %get-tuple-element.31.tiles, ...), custom_call_target="tpu_custom_call" | custom-call | tf_op jit(solution)/shard_map/pallas_call | solution.py:307
  76.9 3.2 %collective-permute-start.11 = (bf16[4,512,256]{2,1,0:T(8,128)(2,1)S(1)}, bf16[4,512,256]{2,1,0:T(8,128)(2,1)S(1)}, u32[]{:S(2)}, u32[]{:S(2)}) collective-permute-start(bf16[4,512,256]{2,1,0:T(8,128)(2,1)S(1)} %get-tuple-element.35), channel_id=1, source_target_pairs={{0,4},{1,5},{2,6},{3,7},{4,0},{5,1},{6,2},{7,3},{8,12},{9,13},{10,... | collective-permute-start | bytes 3145736 | tf_op jit(solution)/shard_map/ppermute | solution.py:413
  80.1 4.5 %shard_map.100 = (bf16[2,512,256]{2,1,0:T(8,128)(2,1)S(1)}, bf16[2,512,256]{2,1,0:T(8,128)(2,1)S(1)}, bf16[2,512,256]{2,1,0:T(8,128)(2,1)S(1)}, bf16[2,512,256]{2,1,0:T(8,128)(2,1)S(1)}) custom-call(s32[12]{0:T(128)S(1)} %stack.92.meta_ref, s32[8,288]{1,0:T(8,128)S(1)} %get-tuple-element.62.plan_ref, bf16[193,128,128]{2,1,0:T(8,128)(2,1)S(1)} %get-tuple-element.30.tiles, ...), custom_call_target="tpu_custom_call" | custom-call | tf_op jit(solution)/shard_map/pallas_call | solution.py:307
  84.7 4.0 %collective-permute-start.13 = (bf16[2,512,256]{2,1,0:T(8,128)(2,1)S(1)}, bf16[2,512,256]{2,1,0:T(8,128)(2,1)S(1)}, u32[]{:S(2)}, u32[]{:S(2)}) collective-permute-start(bf16[2,512,256]{2,1,0:T(8,128)(2,1)S(1)} %get-tuple-element.41), channel_id=1, source_target_pairs={{0,2},{1,3},{2,0},{3,1},{4,6},{5,7},{6,4},{7,5},{8,10},{9,11},{10,... | collective-permute-start | bytes 1572872 | tf_op jit(solution)/shard_map/ppermute | solution.py:412
  88.7 2.0 %collective-permute-start.14 = (bf16[2,512,256]{2,1,0:T(8,128)(2,1)S(1)}, bf16[2,512,256]{2,1,0:T(8,128)(2,1)S(1)}, u32[]{:S(2)}, u32[]{:S(2)}) collective-permute-start(bf16[2,512,256]{2,1,0:T(8,128)(2,1)S(1)} %get-tuple-element.42), channel_id=1, source_target_pairs={{0,3},{1,0},{2,1},{3,2},{4,7},{5,4},{6,5},{7,6},{8,11},{9,8},{10,9... | collective-permute-start | bytes 1572872 | tf_op jit(solution)/shard_map/ppermute | solution.py:412
  90.7 4.0 %collective-permute-done.11.got_ref = bf16[4,512,256]{2,1,0:T(8,128)(2,1)S(1)} collective-permute-done((bf16[4,512,256]{2,1,0:T(8,128)(2,1)S(1)}, bf16[4,512,256]{2,1,0:T(8,128)(2,1)S(1)}, u32[]{:S(2)}, u32[]{:S(2)}) %collective-permute-start.11) | collective-permute-done | bytes 1048608 | tf_op jit(solution)/shard_map/ppermute | solution.py:413
  94.7 0.8 shard_map.101
  95.5 5.6 %collective-permute-done.13.b_ref = bf16[2,512,256]{2,1,0:T(8,128)(2,1)S(1)} collective-permute-done((bf16[2,512,256]{2,1,0:T(8,128)(2,1)S(1)}, bf16[2,512,256]{2,1,0:T(8,128)(2,1)S(1)}, u32[]{:S(2)}, u32[]{:S(2)}) %collective-permute-start.13) | collective-permute-done | bytes 524320 | tf_op jit(solution)/shard_map/ppermute | solution.py:412
  101.1 0.8 shard_map.102
  101.9 2.4 %collective-permute-start.15 = (bf16[512,256]{1,0:T(8,128)(2,1)S(1)}, bf16[512,256]{1,0:T(8,128)(2,1)S(1)}, u32[]{:S(2)}, u32[]{:S(2)}) collective-permute-start(bf16[512,256]{1,0:T(8,128)(2,1)S(1)} %get-tuple-element.44), channel_id=1, source_target_pairs={{0,4},{1,5},{2,6},{3,7},{4,0},{5,1},{6,2},{7,3},{8,12},{9,13},{10,... | collective-permute-start | bytes 786440 | tf_op jit(solution)/shard_map/ppermute | solution.py:421
  104.3 1.4 collective-permute-start.16
  105.8 2.2 %collective-permute-start.17 = (bf16[512,256]{1,0:T(8,128)(2,1)S(1)}, bf16[512,256]{1,0:T(8,128)(2,1)S(1)}, u32[]{:S(2)}, u32[]{:S(2)}) collective-permute-start(bf16[512,256]{1,0:T(8,128)(2,1)S(1)} %get-tuple-element.37), channel_id=1, source_target_pairs={{0,2},{1,3},{2,0},{3,1},{4,6},{5,7},{6,4},{7,5},{8,10},{9,11},{10,... | collective-permute-start | bytes 786440 | tf_op jit(solution)/shard_map/ppermute | solution.py:422
  107.9 2.1 %collective-permute-start.18 = (bf16[512,256]{1,0:T(8,128)(2,1)S(1)}, bf16[512,256]{1,0:T(8,128)(2,1)S(1)}, u32[]{:S(2)}, u32[]{:S(2)}) collective-permute-start(bf16[512,256]{1,0:T(8,128)(2,1)S(1)} %get-tuple-element.38), channel_id=1, source_target_pairs={{0,3},{1,0},{2,1},{3,2},{4,7},{5,4},{6,5},{7,6},{8,11},{9,8},{10,9... | collective-permute-start | bytes 786440 | tf_op jit(solution)/shard_map/ppermute | solution.py:422
  110.0 1.9 %collective-permute-done.15.got0 = bf16[512,256]{1,0:T(8,128)(2,1)S(1)} collective-permute-done((bf16[512,256]{1,0:T(8,128)(2,1)S(1)}, bf16[512,256]{1,0:T(8,128)(2,1)S(1)}, u32[]{:S(2)}, u32[]{:S(2)}) %collective-permute-start.15) | collective-permute-done | bytes 262176 | tf_op jit(solution)/shard_map/ppermute | solution.py:421
  111.9 8.3 %collective-permute-done.16.a_ref = bf16[512,256]{1,0:T(8,128)(2,1)S(1)} collective-permute-done((bf16[512,256]{1,0:T(8,128)(2,1)S(1)}, bf16[512,256]{1,0:T(8,128)(2,1)S(1)}, u32[]{:S(2)}, u32[]{:S(2)}) %collective-permute-start.16) | collective-permute-done | bytes 262176 | tf_op jit(solution)/shard_map/ppermute | solution.py:422
  120.2 0.8 shard_map.103
  121.0 19.0 %collective-permute-start.19 = (f32[512,256]{1,0:T(8,128)S(1)}, f32[512,256]{1,0:T(8,128)S(1)}, u32[]{:S(2)}, u32[]{:S(2)}) collective-permute-start(f32[512,256]{1,0:T(8,128)S(1)} %get-tuple-element.47.other_ref), channel_id=1, source_target_pairs={{0,8},{8,0},{16,24},{24,16},{32,40},{40,32},{48,56},{56,48},{64,72... | collective-permute-start | bytes 1572872 | tf_op jit(solution)/shard_map/ppermute | solution.py:426
  140.0 1.1 constant_dynamic-slice_fusion.cotangent_ref
  141.1 0.5 collective-permute-done.19.got_ref
  141.6 2.3 %shard_map.104 = (bf16[512,512]{1,0:T(8,128)(2,1)}, bf16[512,512]{1,0:T(8,128)(2,1)S(1)}) custom-call(s32[12]{0:T(128)S(1)} %stack.92.meta_ref, f32[512,256]{1,0:T(8,128)S(1)} %get-tuple-element.46.mine_ref, f32[512,256]{1,0:T(8,128)S(1)} %collective-permute-done.19.got_ref, bf16[512,512]{1,0:T(8,128)(2,1)S(1)} %copy-done.1, ...), custom_call_target="tpu_custom_call" | custom-call | tf_op jit(solution)/shard_map/pallas_call | solution.py:307
  144.3 1.5 collective-permute-done.20.other_slope_ref
  145.8 0.7 shard_map.105
  146.6 2.4 %collective-permute-start.23 = (bf16[64,512]{1,0:T(8,128)(2,1)S(1)}, bf16[64,512]{1,0:T(8,128)(2,1)S(1)}, u32[]{:S(2)}, u32[]{:S(2)}) collective-permute-start(bf16[64,512]{1,0:T(8,128)(2,1)S(1)} %get-tuple-element.53), channel_id=1, source_target_pairs={{0,3},{1,0},{2,1},{3,2},{4,7},{5,4},{6,5},{7,6},{8,11},{9,8},{10,9... | collective-permute-start | bytes 196616 | tf_op jit(solution)/shard_map/ppermute | solution.py:281
  149.0 1.3 collective-permute-start.21
  150.3 5.0 %collective-permute-done.22 = bf16[64,512]{1,0:T(8,128)(2,1)S(1)} collective-permute-done((bf16[64,512]{1,0:T(8,128)(2,1)S(1)}, bf16[64,512]{1,0:T(8,128)(2,1)S(1)}, u32[]{:S(2)}, u32[]{:S(2)}) %collective-permute-start.22) | collective-permute-done | bytes 65568 | tf_op jit(solution)/shard_map/ppermute | solution.py:281
  155.4 1.2 collective-permute-start.25
  156.9 2.7 %collective-permute-done.26 = f32[64,512]{1,0:T(8,128)S(1)} collective-permute-done((f32[64,512]{1,0:T(8,128)S(1)}, f32[64,512]{1,0:T(8,128)S(1)}, u32[]{:S(2)}, u32[]{:S(2)}) %collective-permute-start.26) | collective-permute-done | bytes 131104 | tf_op jit(solution)/shard_map/ppermute | solution.py:286
  159.6 1.6 collective-permute-done.25
  161.2 3.7 %collective-permute-done.24 = f32[64,512]{1,0:T(8,128)S(1)} collective-permute-done((f32[64,512]{1,0:T(8,128)S(1)}, f32[64,512]{1,0:T(8,128)S(1)}, u32[]{:S(2)}, u32[]{:S(2)}) %collective-permute-start.24) | collective-permute-done | bytes 131104 | tf_op jit(solution)/shard_map/ppermute | solution.py:286
  165.2 1.4 collective-permute-start.27
  166.6 2.7 %collective-permute-done.29 = f32[64,512]{1,0:T(8,128)S(1)} collective-permute-done((f32[64,512]{1,0:T(8,128)S(1)}, f32[64,512]{1,0:T(8,128)S(1)}, u32[]{:S(2)}, u32[]{:S(2)}) %collective-permute-start.29) | collective-permute-done | bytes 131104 | tf_op jit(solution)/shard_map/ppermute | solution.py:286
  169.2 1.6 collective-permute-done.28
  170.8 3.9 %collective-permute-done.27 = f32[64,512]{1,0:T(8,128)S(1)} collective-permute-done((f32[64,512]{1,0:T(8,128)S(1)}, f32[64,512]{1,0:T(8,128)S(1)}, u32[]{:S(2)}, u32[]{:S(2)}) %collective-permute-start.27) | collective-permute-done | bytes 131104 | tf_op jit(solution)/shard_map/ppermute | solution.py:286
  175.0 1.4 collective-permute-start.30
  176.4 1.6 collective-permute-done.32
  178.0 1.6 collective-permute-done.31
  179.6 1.5 collective-permute-done.30
  181.2 1.5 collective-permute-start.33
  182.7 1.2 collective-permute-done.33
  184.0 1.1 maximum_convert_fusion
  (45 shorter events, 3.2 us)
Async XLA Ops:
  0.6 5.2 %collective-permute-start.1 = (bf16[512,512]{1,0:T(8,128)(2,1)}, bf16[512,512]{1,0:T(8,128)(2,1)S(1)}, u32[]{:S(2)}, u32[]{:S(2)}) collective-permute-start(bf16[512,512]{1,0:T(8,128)(2,1)} %features_ref.1), channel_id=1, source_target_pairs={{0,8},{8,0},{16,24},{24,16},{32,40},{40,32},{48,56},{56,48},{64,72... | collective-permute-start | bytes 1572872 | tf_op jit(solution)/shard_map/ppermute | solution.py:356
  2.8 0.7 copy-start.4
  3.5 0.7 copy-start.5
  4.6 1.2 collective-permute-start
  5.8 25.9 %collective-permute-start.2 = (bf16[192,128,128]{2,1,0:T(8,128)(2,1)}, bf16[192,128,128]{2,1,0:T(8,128)(2,1)}, u32[]{:S(2)}, u32[]{:S(2)}) collective-permute-start(bf16[192,128,128]{2,1,0:T(8,128)(2,1)} %bitcast.61), channel_id=1, source_target_pairs={{0,8},{8,0},{16,24},{24,16},{32,40},{40,32},{48,56},{56,48},{64,72... | collective-permute-start | bytes 18874376 | tf_op jit(solution)/shard_map/ppermute | solution.py:363
  6.0 4.5 %collective-permute-start.3 = (s32[1,512]{1,0:T(1,128)}, s32[1,512]{1,0:T(1,128)S(1)}, u32[]{:S(2)}, u32[]{:S(2)}) collective-permute-start(s32[1,512]{1,0:T(1,128)} %bitcast.71), channel_id=1, source_target_pairs={{0,8},{8,0},{16,24},{24,16},{32,40},{40,32},{48,56},{56,48},{64,72... | collective-permute-start | bytes 6152 | tf_op jit(solution)/shard_map/ppermute | solution.py:355
  10.4 1.0 copy-start.2
  11.5 0.7 copy-start.3
  31.7 8.4 %collective-permute-start.4 = (bf16[2,512,256]{2,1,0:T(8,128)(2,1)S(1)}, bf16[2,512,256]{2,1,0:T(8,128)(2,1)S(1)}, u32[]{:S(2)}, u32[]{:S(2)}) collective-permute-start(bf16[2,512,256]{2,1,0:T(8,128)(2,1)S(1)} %shard_map.97), channel_id=1, source_target_pairs={{0,16},{8,72},{16,32},{24,88},{32,48},{40,104},{48,0},{56,120},{64... | collective-permute-start | bytes 1572872 | tf_op jit(solution)/shard_map/ppermute | solution.py:385
  32.2 14.5 %collective-permute-start.5 = (bf16[2,512,256]{2,1,0:T(8,128)(2,1)S(1)}, bf16[2,512,256]{2,1,0:T(8,128)(2,1)S(1)}, u32[]{:S(2)}, u32[]{:S(2)}) collective-permute-start(bf16[2,512,256]{2,1,0:T(8,128)(2,1)S(1)} %shard_map.97), channel_id=1, source_target_pairs={{0,48},{8,24},{16,0},{24,40},{32,16},{40,56},{48,32},{56,8},{64,11... | collective-permute-start | bytes 1572872 | tf_op jit(solution)/shard_map/ppermute | solution.py:385
  33.8 12.9 %collective-permute-start.6 = (bf16[2,512,256]{2,1,0:T(8,128)(2,1)S(1)}, bf16[2,512,256]{2,1,0:T(8,128)(2,1)S(1)}, u32[]{:S(2)}, u32[]{:S(2)}) collective-permute-start(bf16[2,512,256]{2,1,0:T(8,128)(2,1)S(1)} %shard_map.97), channel_id=1, source_target_pairs={{0,32},{8,56},{16,48},{24,8},{32,0},{40,24},{48,16},{56,40},{64,96... | collective-permute-start | bytes 1572872 | tf_op jit(solution)/shard_map/ppermute | solution.py:385
  35.6 23.3 %collective-permute-start.7 = (bf16[2,512,256]{2,1,0:T(8,128)(2,1)S(1)}, bf16[2,512,256]{2,1,0:T(8,128)(2,1)S(1)}, u32[]{:S(2)}, u32[]{:S(2)}) collective-permute-start(bf16[2,512,256]{2,1,0:T(8,128)(2,1)S(1)} %shard_map.97), channel_id=1, source_target_pairs={{0,64},{8,40},{16,80},{24,56},{32,96},{40,8},{48,112},{56,24},{64,... | collective-permute-start | bytes 1572872 | tf_op jit(solution)/shard_map/ppermute | solution.py:385
  47.8 22.2 %collective-permute-start.9 = (bf16[2,512,256]{2,1,0:T(8,128)(2,1)}, bf16[2,512,256]{2,1,0:T(8,128)(2,1)S(1)}, u32[]{:S(2)}, u32[]{:S(2)}) collective-permute-start(bf16[2,512,256]{2,1,0:T(8,128)(2,1)} %get-tuple-element.56), channel_id=1, source_target_pairs={{0,64},{8,56},{16,80},{24,8},{32,96},{40,24},{48,112},{56,40},{64,... | collective-permute-start | bytes 1572872 | tf_op jit(solution)/shard_map/ppermute | solution.py:385
  50.2 15.7 %collective-permute-start.8 = (bf16[2,512,256]{2,1,0:T(8,128)(2,1)S(1)}, bf16[2,512,256]{2,1,0:T(8,128)(2,1)}, u32[]{:S(2)}, u32[]{:S(2)}) collective-permute-start(bf16[2,512,256]{2,1,0:T(8,128)(2,1)S(1)} %collective-permute-done.4), channel_id=1, source_target_pairs={{0,64},{8,24},{16,80},{24,40},{32,96},{40,56},{48,112},{56,8},{64,... | collective-permute-start | bytes 1572872 | tf_op jit(solution)/shard_map/ppermute | solution.py:385
  50.2 21.4 %collective-permute-start.10 = (bf16[2,512,256]{2,1,0:T(8,128)(2,1)}, bf16[2,512,256]{2,1,0:T(8,128)(2,1)}, u32[]{:S(2)}, u32[]{:S(2)}) collective-permute-start(bf16[2,512,256]{2,1,0:T(8,128)(2,1)} %get-tuple-element.55), channel_id=1, source_target_pairs={{0,64},{8,40},{16,80},{24,56},{32,96},{40,8},{48,112},{56,24},{64,... | collective-permute-start | bytes 1572872 | tf_op jit(solution)/shard_map/ppermute | solution.py:385
  51.4 2.8 %copy-start = (bf16[1,1,192,128,128]{4,3,2,1,0:T(8,128)(2,1)S(1)}, bf16[1,1,192,128,128]{4,3,2,1,0:T(8,128)(2,1)}, u32[]{:S(2)}) copy-start(bf16[1,1,192,128,128]{4,3,2,1,0:T(8,128)(2,1)} %param.11) | copy-start | bytes 18874372
  76.9 17.8 %collective-permute-start.11 = (bf16[4,512,256]{2,1,0:T(8,128)(2,1)S(1)}, bf16[4,512,256]{2,1,0:T(8,128)(2,1)S(1)}, u32[]{:S(2)}, u32[]{:S(2)}) collective-permute-start(bf16[4,512,256]{2,1,0:T(8,128)(2,1)S(1)} %get-tuple-element.35), channel_id=1, source_target_pairs={{0,4},{1,5},{2,6},{3,7},{4,0},{5,1},{6,2},{7,3},{8,12},{9,13},{10,... | collective-permute-start | bytes 3145736 | tf_op jit(solution)/shard_map/ppermute | solution.py:413
  84.6 57.0 %copy-start.1 = (bf16[512,512]{1,0:T(8,128)(2,1)S(1)}, bf16[512,512]{1,0:T(8,128)(2,1)}, u32[]{:S(2)}) copy-start(bf16[512,512]{1,0:T(8,128)(2,1)} %weight_ref.1) | copy-start | bytes 1572868
  84.6 10.9 %collective-permute-start.12 = (bf16[2,512,256]{2,1,0:T(8,128)(2,1)S(1)}, bf16[2,512,256]{2,1,0:T(8,128)(2,1)S(1)}, u32[]{:S(2)}, u32[]{:S(2)}) collective-permute-start(bf16[2,512,256]{2,1,0:T(8,128)(2,1)S(1)} %get-tuple-element.40), channel_id=1, source_target_pairs={{0,1},{1,2},{2,3},{3,0},{4,5},{5,6},{6,7},{7,4},{8,9},{9,10},{10,1... | collective-permute-start | bytes 1572872 | tf_op jit(solution)/shard_map/ppermute | solution.py:412
  84.7 16.4 %collective-permute-start.13 = (bf16[2,512,256]{2,1,0:T(8,128)(2,1)S(1)}, bf16[2,512,256]{2,1,0:T(8,128)(2,1)S(1)}, u32[]{:S(2)}, u32[]{:S(2)}) collective-permute-start(bf16[2,512,256]{2,1,0:T(8,128)(2,1)S(1)} %get-tuple-element.41), channel_id=1, source_target_pairs={{0,2},{1,3},{2,0},{3,1},{4,6},{5,7},{6,4},{7,5},{8,10},{9,11},{10,... | collective-permute-start | bytes 1572872 | tf_op jit(solution)/shard_map/ppermute | solution.py:412
  88.7 12.4 %collective-permute-start.14 = (bf16[2,512,256]{2,1,0:T(8,128)(2,1)S(1)}, bf16[2,512,256]{2,1,0:T(8,128)(2,1)S(1)}, u32[]{:S(2)}, u32[]{:S(2)}) collective-permute-start(bf16[2,512,256]{2,1,0:T(8,128)(2,1)S(1)} %get-tuple-element.42), channel_id=1, source_target_pairs={{0,3},{1,0},{2,1},{3,2},{4,7},{5,4},{6,5},{7,6},{8,11},{9,8},{10,9... | collective-permute-start | bytes 1572872 | tf_op jit(solution)/shard_map/ppermute | solution.py:412
  101.9 10.0 %collective-permute-start.15 = (bf16[512,256]{1,0:T(8,128)(2,1)S(1)}, bf16[512,256]{1,0:T(8,128)(2,1)S(1)}, u32[]{:S(2)}, u32[]{:S(2)}) collective-permute-start(bf16[512,256]{1,0:T(8,128)(2,1)S(1)} %get-tuple-element.44), channel_id=1, source_target_pairs={{0,4},{1,5},{2,6},{3,7},{4,0},{5,1},{6,2},{7,3},{8,12},{9,13},{10,... | collective-permute-start | bytes 786440 | tf_op jit(solution)/shard_map/ppermute | solution.py:421
  104.3 15.9 %collective-permute-start.16 = (bf16[512,256]{1,0:T(8,128)(2,1)S(1)}, bf16[512,256]{1,0:T(8,128)(2,1)S(1)}, u32[]{:S(2)}, u32[]{:S(2)}) collective-permute-start(bf16[512,256]{1,0:T(8,128)(2,1)S(1)} %get-tuple-element.36), channel_id=1, source_target_pairs={{0,1},{1,2},{2,3},{3,0},{4,5},{5,6},{6,7},{7,4},{8,9},{9,10},{10,1... | collective-permute-start | bytes 786440 | tf_op jit(solution)/shard_map/ppermute | solution.py:422
  105.8 14.5 %collective-permute-start.17 = (bf16[512,256]{1,0:T(8,128)(2,1)S(1)}, bf16[512,256]{1,0:T(8,128)(2,1)S(1)}, u32[]{:S(2)}, u32[]{:S(2)}) collective-permute-start(bf16[512,256]{1,0:T(8,128)(2,1)S(1)} %get-tuple-element.37), channel_id=1, source_target_pairs={{0,2},{1,3},{2,0},{3,1},{4,6},{5,7},{6,4},{7,5},{8,10},{9,11},{10,... | collective-permute-start | bytes 786440 | tf_op jit(solution)/shard_map/ppermute | solution.py:422
  107.9 12.3 %collective-permute-start.18 = (bf16[512,256]{1,0:T(8,128)(2,1)S(1)}, bf16[512,256]{1,0:T(8,128)(2,1)S(1)}, u32[]{:S(2)}, u32[]{:S(2)}) collective-permute-start(bf16[512,256]{1,0:T(8,128)(2,1)S(1)} %get-tuple-element.38), channel_id=1, source_target_pairs={{0,3},{1,0},{2,1},{3,2},{4,7},{5,4},{6,5},{7,6},{8,11},{9,8},{10,9... | collective-permute-start | bytes 786440 | tf_op jit(solution)/shard_map/ppermute | solution.py:422
  121.0 20.6 %collective-permute-start.19 = (f32[512,256]{1,0:T(8,128)S(1)}, f32[512,256]{1,0:T(8,128)S(1)}, u32[]{:S(2)}, u32[]{:S(2)}) collective-permute-start(f32[512,256]{1,0:T(8,128)S(1)} %get-tuple-element.47.other_ref), channel_id=1, source_target_pairs={{0,8},{8,0},{16,24},{24,16},{32,40},{40,32},{48,56},{56,48},{64,72... | collective-permute-start | bytes 1572872 | tf_op jit(solution)/shard_map/ppermute | solution.py:426
  143.9 1.9 %collective-permute-start.20 = (bf16[512,512]{1,0:T(8,128)(2,1)S(1)}, bf16[512,512]{1,0:T(8,128)(2,1)S(1)}, u32[]{:S(2)}, u32[]{:S(2)}) collective-permute-start(bf16[512,512]{1,0:T(8,128)(2,1)S(1)} %get-tuple-element.49.slope_ref), channel_id=1, source_target_pairs={{0,8},{8,0},{16,24},{24,16},{32,40},{40,32},{48,56},{56,48},{64,72... | collective-permute-start | bytes 1572872 | tf_op jit(solution)/shard_map/ppermute | solution.py:433
  146.6 3.7 %collective-permute-start.23 = (bf16[64,512]{1,0:T(8,128)(2,1)S(1)}, bf16[64,512]{1,0:T(8,128)(2,1)S(1)}, u32[]{:S(2)}, u32[]{:S(2)}) collective-permute-start(bf16[64,512]{1,0:T(8,128)(2,1)S(1)} %get-tuple-element.53), channel_id=1, source_target_pairs={{0,3},{1,0},{2,1},{3,2},{4,7},{5,4},{6,5},{7,6},{8,11},{9,8},{10,9... | collective-permute-start | bytes 196616 | tf_op jit(solution)/shard_map/ppermute | solution.py:281
  149.0 6.3 %collective-permute-start.22 = (bf16[64,512]{1,0:T(8,128)(2,1)S(1)}, bf16[64,512]{1,0:T(8,128)(2,1)S(1)}, u32[]{:S(2)}, u32[]{:S(2)}) collective-permute-start(bf16[64,512]{1,0:T(8,128)(2,1)S(1)} %get-tuple-element.54), channel_id=1, source_target_pairs={{0,1},{1,2},{2,3},{3,0},{4,5},{5,6},{6,7},{7,4},{8,9},{9,10},{10,1... | collective-permute-start | bytes 196616 | tf_op jit(solution)/shard_map/ppermute | solution.py:281
  149.0 6.3 %collective-permute-start.21 = (bf16[64,512]{1,0:T(8,128)(2,1)S(1)}, bf16[64,512]{1,0:T(8,128)(2,1)S(1)}, u32[]{:S(2)}, u32[]{:S(2)}) collective-permute-start(bf16[64,512]{1,0:T(8,128)(2,1)S(1)} %get-tuple-element.52), channel_id=1, source_target_pairs={{0,2},{1,3},{2,0},{3,1},{4,6},{5,7},{6,4},{7,5},{8,10},{9,11},{10,... | collective-permute-start | bytes 196616 | tf_op jit(solution)/shard_map/ppermute | solution.py:281
  155.3 4.3 %collective-permute-start.26 = (f32[64,512]{1,0:T(8,128)S(1)}, f32[64,512]{1,0:T(8,128)S(1)}, u32[]{:S(2)}, u32[]{:S(2)}) collective-permute-start(f32[64,512]{1,0:T(8,128)S(1)} %fusion.1), channel_id=1, source_target_pairs={{0,48},{8,56},{16,0},{24,8},{32,16},{40,24},{48,32},{56,40},{64,11... | collective-permute-start | bytes 393224 | tf_op jit(solution)/shard_map/ppermute | solution.py:286
  155.4 5.8 %collective-permute-start.25 = (f32[64,512]{1,0:T(8,128)S(1)}, f32[64,512]{1,0:T(8,128)S(1)}, u32[]{:S(2)}, u32[]{:S(2)}) collective-permute-start(f32[64,512]{1,0:T(8,128)S(1)} %fusion.1), channel_id=1, source_target_pairs={{0,32},{8,40},{16,48},{24,56},{32,0},{40,8},{48,16},{56,24},{64,96... | collective-permute-start | bytes 393224 | tf_op jit(solution)/shard_map/ppermute | solution.py:286
  156.7 8.2 %collective-permute-start.24 = (f32[64,512]{1,0:T(8,128)S(1)}, f32[64,512]{1,0:T(8,128)S(1)}, u32[]{:S(2)}, u32[]{:S(2)}) collective-permute-start(f32[64,512]{1,0:T(8,128)S(1)} %fusion.1), channel_id=1, source_target_pairs={{0,16},{8,24},{16,32},{24,40},{32,48},{40,56},{48,0},{56,8},{64,80... | collective-permute-start | bytes 393224 | tf_op jit(solution)/shard_map/ppermute | solution.py:286
  165.0 4.2 %collective-permute-start.29 = (f32[64,512]{1,0:T(8,128)S(1)}, f32[64,512]{1,0:T(8,128)S(1)}, u32[]{:S(2)}, u32[]{:S(2)}) collective-permute-start(f32[64,512]{1,0:T(8,128)S(1)} %fusion.6), channel_id=1, source_target_pairs={{0,68},{1,69},{2,70},{3,71},{4,64},{5,65},{6,66},{7,67},{8,76},{9,... | collective-permute-start | bytes 393224 | tf_op jit(solution)/shard_map/ppermute | solution.py:286
  165.1 5.8 %collective-permute-start.28 = (f32[64,512]{1,0:T(8,128)S(1)}, f32[64,512]{1,0:T(8,128)S(1)}, u32[]{:S(2)}, u32[]{:S(2)}) collective-permute-start(f32[64,512]{1,0:T(8,128)S(1)} %fusion.6), channel_id=1, source_target_pairs={{0,4},{1,5},{2,6},{3,7},{4,0},{5,1},{6,2},{7,3},{8,12},{9,13},{10,... | collective-permute-start | bytes 393224 | tf_op jit(solution)/shard_map/ppermute | solution.py:286
  165.2 9.6 %collective-permute-start.27 = (f32[64,512]{1,0:T(8,128)S(1)}, f32[64,512]{1,0:T(8,128)S(1)}, u32[]{:S(2)}, u32[]{:S(2)}) collective-permute-start(f32[64,512]{1,0:T(8,128)S(1)} %fusion.6), channel_id=1, source_target_pairs={{0,64},{1,65},{2,66},{3,67},{4,68},{5,69},{6,70},{7,71},{8,72},{9,... | collective-permute-start | bytes 393224 | tf_op jit(solution)/shard_map/ppermute | solution.py:286
  174.8 3.2 %collective-permute-start.32 = (bf16[64,512]{1,0:T(8,128)(2,1)S(1)}, bf16[64,512]{1,0:T(8,128)(2,1)S(1)}, u32[]{:S(2)}, u32[]{:S(2)}) collective-permute-start(bf16[64,512]{1,0:T(8,128)(2,1)S(1)} %fusion.5), channel_id=1, source_target_pairs={{0,3},{1,0},{2,1},{3,2},{4,7},{5,4},{6,5},{7,6},{8,11},{9,8},{10,9... | collective-permute-start | bytes 196616 | tf_op jit(solution)/shard_map/ppermute | solution.py:286
  174.9 4.7 %collective-permute-start.31 = (bf16[64,512]{1,0:T(8,128)(2,1)S(1)}, bf16[64,512]{1,0:T(8,128)(2,1)S(1)}, u32[]{:S(2)}, u32[]{:S(2)}) collective-permute-start(bf16[64,512]{1,0:T(8,128)(2,1)S(1)} %fusion.5), channel_id=1, source_target_pairs={{0,2},{1,3},{2,0},{3,1},{4,6},{5,7},{6,4},{7,5},{8,10},{9,11},{10,... | collective-permute-start | bytes 196616 | tf_op jit(solution)/shard_map/ppermute | solution.py:286
  175.0 6.1 %collective-permute-start.30 = (bf16[64,512]{1,0:T(8,128)(2,1)S(1)}, bf16[64,512]{1,0:T(8,128)(2,1)S(1)}, u32[]{:S(2)}, u32[]{:S(2)}) collective-permute-start(bf16[64,512]{1,0:T(8,128)(2,1)S(1)} %fusion.5), channel_id=1, source_target_pairs={{0,1},{1,2},{2,3},{3,0},{4,5},{5,6},{6,7},{7,4},{8,9},{9,10},{10,1... | collective-permute-start | bytes 196616 | tf_op jit(solution)/shard_map/ppermute | solution.py:286
  181.2 2.6 %collective-permute-start.33 = (bf16[256,512]{1,0:T(8,128)(2,1)S(1)}, bf16[256,512]{1,0:T(8,128)(2,1)S(1)}, u32[]{:S(2)}, u32[]{:S(2)}) collective-permute-start(bf16[256,512]{1,0:T(8,128)(2,1)S(1)} %pad_maximum_fusion.3), channel_id=1, source_target_pairs={{0,8},{8,0},{16,24},{24,16},{32,40},{40,32},{48,56},{56,48},{64,72... | collective-permute-start | bytes 786440 | tf_op jit(solution)/shard_map/ppermute | solution.py:445

commit v5 on v4

--- a/solution.py
+++ b/solution.py
@@ -13,6 +13,7 @@
 PER_PEER = 4
 HALF = 256
 CHIPS = 8
+BLOCKS = CHIPS + 2
 SLOT_CAP = 192
 ROW_TILES = 32
 GROUP_BITS = 2
@@ -33,7 +34,11 @@
     return jnp.where(position == wanted, 1.0, 0.0).astype(BF16)
 
 
-def group_kernel(meta_ref, part_ref, features_ref, other_part_ref, other_ref, out_ref):
+def group_kernel(
+    meta_ref, part_ref, features_hbm, other_part_ref, other_ref, out_ref, features_ref, sem
+):
+    copy = pltpu.make_async_copy(features_hbm, features_ref, sem)
+    copy.start()
     core = meta_ref[0]
     devices = N_ROW * N_COL
     before = jnp.where(
@@ -55,8 +60,9 @@
         picked = jnp.dot(pick, wanted, preferred_element_type=F32).astype(BF16)
         return picked.reshape(N_COL, 1, SLOTS // N_COL, HALF)
 
+    out_ref[:, pl.ds(1 - core, 1)] = grouped(other_part_ref[...], other_ref[...])
+    copy.wait()
     out_ref[:, pl.ds(core, 1)] = grouped(part_ref[...], features_ref[...])
-    out_ref[:, pl.ds(1 - core, 1)] = grouped(other_part_ref[...], other_ref[...])
 
 
 def interleave_kernel(arrived_ref, out_ref):
@@ -157,12 +163,12 @@
 
 
 def tiles_y_kernel(meta_ref, plan_ref, tiles, *refs):
-    blocks, (keep_ref, send_ref, source) = refs[:CHIPS], refs[CHIPS : CHIPS + 3]
-    total, sems = refs[CHIPS + 3 :]
+    blocks, (keep_ref, send_ref, source) = refs[:BLOCKS], refs[BLOCKS : BLOCKS + 3]
+    total, sems = refs[BLOCKS + 3 :]
     yh = meta_ref[2]
     copies = [
         pltpu.make_async_copy(blocks[k], source.at[meta_ref[4 + k]], sems.at[k])
-        for k in range(CHIPS)
+        for k in range(BLOCKS)
     ]
     for copy in copies:
         copy.start()
@@ -241,7 +247,7 @@
             grad = grad + lax.dot_general(
                 piece, slope[...], contract, preferred_element_type=F32
             )
-    grad_ref[...] = grad * (1.0 / 256.0)
+    grad_ref[...] = (grad * (1.0 / 256.0)).astype(BF16)
 
 
 def row_moves(move):
@@ -249,18 +255,10 @@
     for yl in range(2):
         for z in range(4):
             for c in range(2):
-                a, b, d = move(yl, z, c)
-                pairs.append(((yl * 4 + z) * 2 + c, (a * 4 + b) * 2 + d))
-    return pairs
-
-
-def all_moves_y(k):
-    pairs = []
-    for i in range(N_ROW):
-        for j in range(N_COL):
-            y = (j // 4) * 2 + i // 8
-            to = (y + k) % 4
-            pairs.append((i * N_COL + j, ((to % 2) * 8 + i % 8) * N_COL + (to // 2) * 4 + j % 4))
+                to = move(yl, z, c)
+                if to is not None:
+                    a, b, d = to
+                    pairs.append(((yl * 4 + z) * 2 + c, (a * 4 + b) * 2 + d))
     return pairs
 
 
@@ -272,19 +270,16 @@
     return [(yh * 4 + x, (1 - yh) * 4 + x) for yh in range(2) for x in range(4)]
 
 
-def scatter4(total, me, axis, moves):
-    quarter = total.shape[0] // 4
-    parts = total.reshape(4, quarter, F)
-    out = lax.dynamic_index_in_dim(parts, me, 0, False)
-    for k in (2, 1, 3):
-        send = lax.dynamic_index_in_dim(parts, (me + k) % 4, 0, False).astype(BF16)
-        out = out + lax.ppermute(send, axis, moves(k)).astype(F32)
-    return out
-
-
-def by_giver(own, me, axis, moves):
-    got = jnp.stack([own] + [lax.ppermute(own, axis, moves(k)) for k in (1, 2, 3)])
-    return [got[(me - k) % 4] for k in range(4)]
+def exchange(parts, axis, groups=None):
+    return lax.all_to_all(
+        parts, axis, split_axis=0, concat_axis=0, axis_index_groups=groups, tiled=True
+    )
+
+
+def added(parts):
+    parts = parts.astype(F32)
+    a = (parts[0] + parts[1]) + (parts[2] + parts[3])
+    return a + ((parts[4] + parts[5]) + (parts[6] + parts[7]))
 
 
 def call(kernel, in_specs, outs, scratch=(), limit=16):
@@ -299,8 +294,8 @@
 
     def run(*operands):
         held = [
-            pltpu.with_memory_space_constraint(o, pltpu.VMEM)
-            if spec.memory_space == pltpu.VMEM
+            pltpu.with_memory_space_constraint(o, spec.memory_space)
+            if spec.memory_space in (pltpu.VMEM, pltpu.MemorySpace.HBM)
             else o
             for spec, o in zip(in_specs, operands)
         ]
@@ -328,10 +323,10 @@
     col = lax.axis_index("col")
     core, z, yl = row % 2, (row // 2) % 4, row // 8
     x, yh = col % 4, col // 4
-    y = yh * 2 + yl
     vmem = pl.BlockSpec(memory_space=pltpu.VMEM)
     smem = pl.BlockSpec(memory_space=pltpu.SMEM)
     hbm = pl.BlockSpec(memory_space=pl.ANY)
+    pinned = pl.BlockSpec(memory_space=pltpu.MemorySpace.HBM)
 
     here, there = yl * 4, (1 - yl) * 4
     near = [here + (z - k) % 4 for k in range(4)]
@@ -340,12 +335,14 @@
     places = [
         near[0],
         jnp.where(first, near[1], far[0]),
-        jnp.where(first, near[3], near[1]),
-        jnp.where(first, near[2], near[3]),
-        jnp.where(first, far[0], near[2]),
+        jnp.where(first, near[3], CHIPS),
+        jnp.where(first, near[2], CHIPS + 1),
+        jnp.where(first, far[0], near[1]),
         far[1],
-        far[3],
-        far[2],
+        jnp.where(first, far[3], near[3]),
+        jnp.where(first, far[2], near[2]),
+        jnp.where(first, CHIPS, far[3]),
+        jnp.where(first, CHIPS + 1, far[2]),
     ]
     meta = jnp.stack([core, x, yh, z] + places).astype(jnp.int32)
 
@@ -358,50 +355,55 @@
         tile_count.reshape(1), tile_rows.reshape(1, -1), tile_cols.reshape(1, -1)
     )
     other_plan = lax.ppermute(plan, "row", swap)
-    other_features = after(other_features, other_plan)
     plans = [jnp.where(core == c, plan, other_plan) for c in range(2)]
-    other_tiles = lax.ppermute(after(tiles, other_features), "row", swap)
+    other_tiles = lax.ppermute(after(tiles, other_features, other_part), "row", swap)
     grouped = call(
         group_kernel,
-        [smem, vmem, vmem, vmem, vmem],
+        [smem, vmem, pinned, vmem, vmem],
         held(N_COL, 2, SLOTS // N_COL, HALF),
+        [pltpu.VMEM((SLOTS, F), BF16), pltpu.SemaphoreType.DMA],
     )(meta, part, features, other_part, other_features)
     arrived = lax.all_to_all(grouped, "col", split_axis=0, concat_axis=0, tiled=True)
     own = call(interleave_kernel, [vmem], array(2, SLOTS, HALF))(arrived)
-    own = after(own, other_tiles)
+    own = after(own, other_tiles, other_plan)
 
     tiles0, tiles1 = call(
         stage_kernel,
-        [smem, hbm, hbm],
+        [smem, pinned, pinned],
         [held(SLOT_CAP + 1, TILE, TILE)] * 2,
         [pltpu.SemaphoreType.DMA((2,))],
     )(meta, tiles, after(other_tiles, own))
 
-    def hop(block, move0, move1):
+    def hop(block, *moves):
         def move(yl, z, c):
-            dy, dz = move1 if c else move0
-            return (yl + dy) % 2, (z + dz) % 4, c
+            if moves[c] is None:
+                return None
+            return (yl + moves[c][0]) % 2, (z + moves[c][1]) % 4, c
 
         return lax.ppermute(block, "row", row_moves(move))
 
     r1 = hop(own, (0, 1), (1, 0))
-    r2 = hop(own, (0, 3), (0, 1))
-    r3 = hop(own, (0, 2), (0, 3))
-    r4 = hop(own, (1, 0), (0, 2))
+    r2 = hop(own, (0, 3), None)
+    r3 = hop(own, (0, 2), None)
+    r4 = hop(own, (1, 0), (0, 1))
     s1 = hop(r1, (1, 0), (0, 1))
-    s2 = hop(jnp.where(first, r2, r1), (1, 0), (0, 3))
-    s3 = hop(jnp.where(first, r3, r1), (1, 0), (0, 2))
+    second = jnp.where(first, after(r2, r1), own)
+    s2 = hop(second, (1, 0), (0, 3))
+    s3 = hop(jnp.where(first, after(r3, second), own), (1, 0), (0, 2))
+    s4 = hop(r1, None, (0, 3))
+    s5 = hop(r1, None, (0, 2))
     blocks = [
-        b.reshape(2, N_ROW, N_COL * PER_PEER, HALF) for b in (own, r1, r2, r3, r4, s1, s2, s3)
+        b.reshape(2, N_ROW, N_COL * PER_PEER, HALF)
+        for b in (own, r1, r2, r3, r4, s1, s2, s3, s4, s5)
     ]
 
     total = pltpu.VMEM((ROW_TILES, TILE, HALF), F32)
-    source = held(CHIPS, 2, N_ROW, N_COL * PER_PEER, HALF)
+    source = held(BLOCKS, 2, N_ROW, N_COL * PER_PEER, HALF)
     keep1, send1, source = call(
         tiles_y_kernel,
-        [smem, smem, vmem] + [hbm] * CHIPS,
+        [smem, smem, vmem] + [hbm] * BLOCKS,
         [held(4, SLOTS, HALF), held(4, SLOTS, HALF), source],
-        [total, pltpu.SemaphoreType.DMA((CHIPS,))],
+        [total, pltpu.SemaphoreType.DMA((BLOCKS,))],
     )(meta, plans[1], tiles1, *blocks)
     row0 = call(
         tiles_x_kernel,
@@ -431,17 +433,16 @@
         meta, mine, theirs, weight, cotangent
     )
     other_slope = lax.ppermute(slope, "row", swap)
-    half = call(gradient_kernel, [vmem] * 4, held(HALF, F, dtype=F32))(
+    half = call(gradient_kernel, [vmem] * 4, held(HALF, F))(
         mine, others, slope, other_slope
     )
 
-    z_moves = lambda k: row_moves(lambda yl, z, c: (yl, (z + k) % 4, c))
-    eighth = scatter4(half, x, "col", x_moves)
-    a, b, c, d = by_giver(eighth, z, "row", z_moves)
-    eighth = (a + b) + (c + d)
-    a, b, c, d = by_giver(eighth, y, ("row", "col"), all_moves_y)
-    eighth = (a + b) + (c + d)
-    half = jnp.concatenate(by_giver(eighth.astype(BF16), x, "col", x_moves))
+    same_core = [[chip * 2 + c for chip in range(CHIPS)] for c in range(2)]
+    shape = (CHIPS, HALF // CHIPS, F)
+    piece = added(exchange(half.reshape(shape), "row", same_core))
+    piece = added(exchange(jnp.broadcast_to(piece, shape), "col"))
+    half = exchange(jnp.broadcast_to(piece.astype(BF16), shape), "row", same_core)
+    half = half.reshape(HALF, F)
     other = lax.ppermute(half, "row", swap)
     first = jnp.where(core == 0, half, other).astype(F32)
     second = jnp.where(core == 0, other, half).astype(F32)

time: 186 us -> 177 us (0.952)
  blocking collectives: 17.8 us -> 33.7 us
  starting transfers between devices: 57.7 us -> 42.5 us
  waiting for transfers between devices: 77.2 us -> 65.1 us
  Pallas kernels: 21.1 us -> 25.9 us
  local copies, waits for them, and re-layouts: 7.09 us -> 3.27 us
    ppermute x13 -> x1, waiting for transfers between devices: 25.9 us -> 0.01 us  [shards(): lax.ppermute(after(tiles, other_features, other_part), 'row', swap)]
    ppermute x1, starting transfers between devices: 19 us -> 1.74 us  [shards(): theirs = lax.ppermute(others, 'row', swap)]
    all_to_all x1 -> x3, blocking collectives: 17.8 us -> 33.7 us  [exchange(): lax.all_to_all(parts, axis, split_axis=0, concat_axis=0, axis_index_group...]
    all_to_all x0 -> x1, waiting for transfers between devices: none -> 8.83 us  [shards(): lax.all_to_all(grouped, 'col', split_axis=0, concat_axis=0, tiled=True)]
    ppermute x13 -> x1, starting transfers between devices: 8.42 us -> 0.37 us  [shards(): lax.ppermute(after(tiles, other_features, other_part), 'row', swap)]
    ppermute x7 -> x9, starting transfers between devices: 9.16 us -> 16.2 us  [hop(): return lax.ppermute(block, 'row', row_moves(move))]
    all_to_all x0 -> x1, starting transfers between devices: none -> 6.74 us  [shards(): lax.all_to_all(grouped, 'col', split_axis=0, concat_axis=0, tiled=True)]
    ppermute x1, waiting for transfers between devices: 4 us -> 10.6 us  [shards(): got1 = lax.ppermute(send1, 'col', y_moves())]
  transfers between devices with their start and end apart: 34 -> 25, of which waited for: 26 -> 16; matrix products, arithmetic and copies ran while one was open for 1% -> 2% of each run, Pallas kernels for 6% -> 9%
where the time goes in v5:
time: 177 us; the launch traced here: 175 us
  waiting for transfers between devices  65.1 us (37%)
  starting transfers between devices  42.5 us (24%)
  blocking collectives  33.7 us (19%)
  Pallas kernels  25.9 us (15%)
  local copies, waits for them, and re-layouts  3.27 us (2%)
  other arithmetic  3.02 us (2%)
    all_to_all x3, blocking collectives, exchange(): lax.all_to_all(parts, axis, split_axis=0, concat_axis=0, axis_index_group...  33.7 us
    pallas_call x11, Pallas kernels, run(): return made(*held)  25.9 us
    ppermute x9, waiting for transfers between devices, hop(): return lax.ppermute(block, 'row', row_moves(move))  18.5 us
    ppermute x9, starting transfers between devices, hop(): return lax.ppermute(block, 'row', row_moves(move))  16.2 us
    ppermute x3, waiting for transfers between devices, shards(): got0 = [lax.ppermute(row0[k], 'col', x_moves(k)) for k in (1, 2, 3)]  11.1 us
    ppermute x1, waiting for transfers between devices, shards(): got1 = lax.ppermute(send1, 'col', y_moves())  10.6 us
    ppermute x3, waiting for transfers between devices, shards(): got1 = [lax.ppermute(send1[k - 1], 'col', x_moves(k)) for k in (1, 2, 3)]  9.05 us
    all_to_all x1, waiting for transfers between devices, shards(): lax.all_to_all(grouped, 'col', split_axis=0, concat_axis=0, tiled=True)  8.83 us
  transfers between devices with their start and end apart: 25, of which 16 were waited for; matrix products, arithmetic and copies ran while one was open for 2% of the time, Pallas kernels for 9%

profile of v5, /device:TPU:1, one launch (start us, length us, event | category | flops | bytes accessed | tf_op | source)
XLA Modules:
  0.0 175.0 jit_solution(15357529613094366543)
XLA Ops:
  0.6 1.5 collective-permute-start.1
  2.1 0.1 collective-permute-start.2
  2.2 1.7 collective-permute-done.2.other_part_ref
  3.9 0.4 collective-permute-start.3
  4.3 0.1 stack.59.meta_ref
  4.4 0.7 copy-done.1
  5.0 3.0 %shard_map.96 = bf16[8,2,64,256]{3,2,1,0:T(8,128)(2,1)} custom-call(s32[14]{0:T(128)S(1)} %stack.59.meta_ref, s32[1,512]{1,0:T(1,128)S(1)} %bitcast.46, bf16[512,512]{1,0:T(8,128)(2,1)} %features_hbm.1, s32[1,512]{1,0:T(1,128)S(1)} %collective-permute-done.2.other_part_ref, bf16[512,512]{1,0:T(8,128)(2,1)S(1)} %collective-permute-done.1.other_ref), custom_call_target="tpu_custom_call" | custom-call | tf_op jit(solution)/shard_map/pallas_call | solution.py:302
  8.1 6.7 %all-to-all-start = ((bf16[8,2,64,256]{3,2,1,0:T(8,128)(2,1)}), bf16[8,2,64,256]{3,2,1,0:T(8,128)(2,1)S(1)}, u32[]{:S(2)}, u32[]{:S(2)}) async-start(bf16[8,2,64,256]{3,2,1,0:T(8,128)(2,1)} %shard_map.96), calls=%async_computation | async-start | bytes 1048576 | tf_op jit(solution)/shard_map/all_to_all | solution.py:366
  15.5 0.0 copy-start.2
  15.5 0.7 copy-done.2
  16.1 0.7 copy-done.3
  16.8 0.5 shard_map.95
  17.3 0.5 collective-permute-start
  17.7 8.8 %all-to-all-done.arrived_ref = bf16[8,2,64,256]{3,2,1,0:T(8,128)(2,1)S(1)} async-done(((bf16[8,2,64,256]{3,2,1,0:T(8,128)(2,1)}), bf16[8,2,64,256]{3,2,1,0:T(8,128)(2,1)S(1)}, u32[]{:S(2)}, u32[]{:S(2)}) %all-to-all-start) | async-done | bytes 524320 | tf_op jit(solution)/shard_map/all_to_all | solution.py:366
  26.6 0.4 shard_map.97
  27.0 0.5 collective-permute-start.4
  27.5 0.7 collective-permute-start.5
  28.2 0.7 collective-permute-start.6
  28.9 1.7 collective-permute-start.7
  30.6 4.8 %collective-permute-done.4 = bf16[2,512,256]{2,1,0:T(8,128)(2,1)S(1)} collective-permute-done((bf16[2,512,256]{2,1,0:T(8,128)(2,1)S(1)}, bf16[2,512,256]{2,1,0:T(8,128)(2,1)S(1)}, u32[]{:S(2)}, u32[]{:S(2)}) %collective-permute-start.4) | collective-permute-done | bytes 524320 | tf_op jit(solution)/shard_map/ppermute | solution.py:383
  35.4 0.9 broadcast_select_fusion.1
  36.3 3.8 %collective-permute-start.9 = (bf16[2,512,256]{2,1,0:T(8,128)(2,1)}, bf16[2,512,256]{2,1,0:T(8,128)(2,1)S(1)}, u32[]{:S(2)}, u32[]{:S(2)}) collective-permute-start(bf16[2,512,256]{2,1,0:T(8,128)(2,1)} %broadcast_select_fusion.1), channel_id=1, source_target_pairs={{0,64},{8,56},{16,80},{24,8},{32,96},{40,24},{48,112},{56,40},{64,... | collective-permute-start | bytes 1572872 | tf_op jit(solution)/shard_map/ppermute | solution.py:383
  40.1 0.9 broadcast_select_fusion
  40.9 1.3 collective-permute-start.10
  42.2 3.3 %collective-permute-start.11 = (bf16[2,512,256]{2,1,0:T(8,128)(2,1)S(1)}, bf16[2,512,256]{2,1,0:T(8,128)(2,1)}, u32[]{:S(2)}, u32[]{:S(2)}) collective-permute-start(bf16[2,512,256]{2,1,0:T(8,128)(2,1)S(1)} %collective-permute-done.4), channel_id=1, source_target_pairs={{8,56},{24,8},{40,24},{56,40},{72,120},{88,72},{104,88},{120,104},... | collective-permute-start | bytes 1572872 | tf_op jit(solution)/shard_map/ppermute | solution.py:383
  45.5 4.3 %collective-permute-start.12 = (bf16[2,512,256]{2,1,0:T(8,128)(2,1)S(1)}, bf16[2,512,256]{2,1,0:T(8,128)(2,1)}, u32[]{:S(2)}, u32[]{:S(2)}) collective-permute-start(bf16[2,512,256]{2,1,0:T(8,128)(2,1)S(1)} %collective-permute-done.4), channel_id=1, source_target_pairs={{8,40},{24,56},{40,8},{56,24},{72,104},{88,120},{104,72},{120,88},... | collective-permute-start | bytes 1572872 | tf_op jit(solution)/shard_map/ppermute | solution.py:383
  49.8 5.2 %shard_map.98 = (bf16[193,128,128]{2,1,0:T(8,128)(2,1)S(1)}, bf16[193,128,128]{2,1,0:T(8,128)(2,1)S(1)}) custom-call(s32[14]{0:T(128)S(1)} %stack.59.meta_ref, bf16[192,128,128]{2,1,0:T(8,128)(2,1)} %bitcast.50, bf16[192,128,128]{2,1,0:T(8,128)(2,1)} %collective-permute-done.3.other_hbm), custom_call_target="tpu_custom_call" | custom-call | tf_op jit(solution)/shard_map/pallas_call | solution.py:302
  55.0 0.7 collective-permute-done.8
  55.7 1.9 %collective-permute-done.9 = bf16[2,512,256]{2,1,0:T(8,128)(2,1)S(1)} collective-permute-done((bf16[2,512,256]{2,1,0:T(8,128)(2,1)}, bf16[2,512,256]{2,1,0:T(8,128)(2,1)S(1)}, u32[]{:S(2)}, u32[]{:S(2)}) %collective-permute-start.9) | collective-permute-done | bytes 524320 | tf_op jit(solution)/shard_map/ppermute | solution.py:383
  57.6 4.8 %collective-permute-done.10 = bf16[2,512,256]{2,1,0:T(8,128)(2,1)} collective-permute-done((bf16[2,512,256]{2,1,0:T(8,128)(2,1)}, bf16[2,512,256]{2,1,0:T(8,128)(2,1)}, u32[]{:S(2)}, u32[]{:S(2)}) %collective-permute-start.10) | collective-permute-done | bytes 524320 | tf_op jit(solution)/shard_map/ppermute | solution.py:383
  62.4 6.3 %collective-permute-done.11 = bf16[2,512,256]{2,1,0:T(8,128)(2,1)} collective-permute-done((bf16[2,512,256]{2,1,0:T(8,128)(2,1)S(1)}, bf16[2,512,256]{2,1,0:T(8,128)(2,1)}, u32[]{:S(2)}, u32[]{:S(2)}) %collective-permute-start.11) | collective-permute-done | bytes 524320 | tf_op jit(solution)/shard_map/ppermute | solution.py:383
  68.7 4.9 %shard_map.99 = (bf16[4,512,256]{2,1,0:T(8,128)(2,1)S(1)}, bf16[4,512,256]{2,1,0:T(8,128)(2,1)S(1)}, bf16[10,2,16,32,256]{4,3,2,1,0:T(8,128)(2,1)S(1)}) custom-call(s32[14]{0:T(128)S(1)} %stack.59.meta_ref, s32[8,288]{1,0:T(8,128)S(1)} %get-tuple-element.54.plan_ref, bf16[193,128,128]{2,1,0:T(8,128)(2,1)S(1)} %get-tuple-element.31.tiles, ...), custom_call_target="tpu_custom_call" | custom-call | tf_op jit(solution)/shard_map/pallas_call | solution.py:302
  73.7 3.6 %collective-permute-start.13 = (bf16[4,512,256]{2,1,0:T(8,128)(2,1)S(1)}, bf16[4,512,256]{2,1,0:T(8,128)(2,1)S(1)}, u32[]{:S(2)}, u32[]{:S(2)}) collective-permute-start(bf16[4,512,256]{2,1,0:T(8,128)(2,1)S(1)} %get-tuple-element.37), channel_id=1, source_target_pairs={{0,4},{1,5},{2,6},{3,7},{4,0},{5,1},{6,2},{7,3},{8,12},{9,13},{10,... | collective-permute-start | bytes 3145736 | tf_op jit(solution)/shard_map/ppermute | solution.py:415
  77.2 6.5 %shard_map.100 = (bf16[2,512,256]{2,1,0:T(8,128)(2,1)S(1)}, bf16[2,512,256]{2,1,0:T(8,128)(2,1)S(1)}, bf16[2,512,256]{2,1,0:T(8,128)(2,1)S(1)}, bf16[2,512,256]{2,1,0:T(8,128)(2,1)S(1)}) custom-call(s32[14]{0:T(128)S(1)} %stack.59.meta_ref, s32[8,288]{1,0:T(8,128)S(1)} %get-tuple-element.55.plan_ref, bf16[193,128,128]{2,1,0:T(8,128)(2,1)S(1)} %get-tuple-element.30.tiles, ...), custom_call_target="tpu_custom_call" | custom-call | tf_op jit(solution)/shard_map/pallas_call | solution.py:302
  83.7 0.1 collective-permute-start.14
  83.8 0.3 collective-permute-start.15
  84.1 2.3 %collective-permute-start.16 = (bf16[2,512,256]{2,1,0:T(8,128)(2,1)S(1)}, bf16[2,512,256]{2,1,0:T(8,128)(2,1)S(1)}, u32[]{:S(2)}, u32[]{:S(2)}) collective-permute-start(bf16[2,512,256]{2,1,0:T(8,128)(2,1)S(1)} %get-tuple-element.44), channel_id=1, source_target_pairs={{0,3},{1,0},{2,1},{3,2},{4,7},{5,4},{6,5},{7,6},{8,11},{9,8},{10,9... | collective-permute-start | bytes 1572872 | tf_op jit(solution)/shard_map/ppermute | solution.py:414
  86.5 10.6 %collective-permute-done.13.got_ref = bf16[4,512,256]{2,1,0:T(8,128)(2,1)S(1)} collective-permute-done((bf16[4,512,256]{2,1,0:T(8,128)(2,1)S(1)}, bf16[4,512,256]{2,1,0:T(8,128)(2,1)S(1)}, u32[]{:S(2)}, u32[]{:S(2)}) %collective-permute-start.13) | collective-permute-done | bytes 1048608 | tf_op jit(solution)/shard_map/ppermute | solution.py:415
  97.1 0.8 shard_map.101
  97.9 5.8 %collective-permute-done.15.b_ref = bf16[2,512,256]{2,1,0:T(8,128)(2,1)S(1)} collective-permute-done((bf16[2,512,256]{2,1,0:T(8,128)(2,1)S(1)}, bf16[2,512,256]{2,1,0:T(8,128)(2,1)S(1)}, u32[]{:S(2)}, u32[]{:S(2)}) %collective-permute-start.15) | collective-permute-done | bytes 524320 | tf_op jit(solution)/shard_map/ppermute | solution.py:414
  103.7 5.3 %collective-permute-done.16.c_ref = bf16[2,512,256]{2,1,0:T(8,128)(2,1)S(1)} collective-permute-done((bf16[2,512,256]{2,1,0:T(8,128)(2,1)S(1)}, bf16[2,512,256]{2,1,0:T(8,128)(2,1)S(1)}, u32[]{:S(2)}, u32[]{:S(2)}) %collective-permute-start.16) | collective-permute-done | bytes 524320 | tf_op jit(solution)/shard_map/ppermute | solution.py:414
  109.0 0.8 shard_map.102
  109.8 0.4 collective-permute-start.17
  110.2 2.0 %collective-permute-start.18 = (bf16[512,256]{1,0:T(8,128)(2,1)S(1)}, bf16[512,256]{1,0:T(8,128)(2,1)S(1)}, u32[]{:S(2)}, u32[]{:S(2)}) collective-permute-start(bf16[512,256]{1,0:T(8,128)(2,1)S(1)} %get-tuple-element.38), channel_id=1, source_target_pairs={{0,1},{1,2},{2,3},{3,0},{4,5},{5,6},{6,7},{7,4},{8,9},{9,10},{10,1... | collective-permute-start | bytes 786440 | tf_op jit(solution)/shard_map/ppermute | solution.py:424
  112.2 2.6 %collective-permute-start.19 = (bf16[512,256]{1,0:T(8,128)(2,1)S(1)}, bf16[512,256]{1,0:T(8,128)(2,1)S(1)}, u32[]{:S(2)}, u32[]{:S(2)}) collective-permute-start(bf16[512,256]{1,0:T(8,128)(2,1)S(1)} %get-tuple-element.39), channel_id=1, source_target_pairs={{0,2},{1,3},{2,0},{3,1},{4,6},{5,7},{6,4},{7,5},{8,10},{9,11},{10,... | collective-permute-start | bytes 786440 | tf_op jit(solution)/shard_map/ppermute | solution.py:424
  114.8 2.2 %collective-permute-done.17.got0 = bf16[512,256]{1,0:T(8,128)(2,1)S(1)} collective-permute-done((bf16[512,256]{1,0:T(8,128)(2,1)S(1)}, bf16[512,256]{1,0:T(8,128)(2,1)S(1)}, u32[]{:S(2)}, u32[]{:S(2)}) %collective-permute-start.17) | collective-permute-done | bytes 262176 | tf_op jit(solution)/shard_map/ppermute | solution.py:423
  117.0 1.8 %collective-permute-done.18.a_ref = bf16[512,256]{1,0:T(8,128)(2,1)S(1)} collective-permute-done((bf16[512,256]{1,0:T(8,128)(2,1)S(1)}, bf16[512,256]{1,0:T(8,128)(2,1)S(1)}, u32[]{:S(2)}, u32[]{:S(2)}) %collective-permute-start.18) | collective-permute-done | bytes 262176 | tf_op jit(solution)/shard_map/ppermute | solution.py:424
  118.8 7.3 %collective-permute-done.19.b_ref = bf16[512,256]{1,0:T(8,128)(2,1)S(1)} collective-permute-done((bf16[512,256]{1,0:T(8,128)(2,1)S(1)}, bf16[512,256]{1,0:T(8,128)(2,1)S(1)}, u32[]{:S(2)}, u32[]{:S(2)}) %collective-permute-start.19) | collective-permute-done | bytes 262176 | tf_op jit(solution)/shard_map/ppermute | solution.py:424
  126.0 0.8 shard_map.103
  126.8 1.7 collective-permute-start.21
  128.5 1.1 constant_dynamic-slice_fusion.cotangent_ref
  129.6 0.5 collective-permute-done.21.got_ref
  130.1 2.3 %shard_map.104 = (bf16[512,512]{1,0:T(8,128)(2,1)}, bf16[512,512]{1,0:T(8,128)(2,1)S(1)}) custom-call(s32[14]{0:T(128)S(1)} %stack.59.meta_ref, f32[512,256]{1,0:T(8,128)S(1)} %get-tuple-element.48.mine_ref, f32[512,256]{1,0:T(8,128)S(1)} %collective-permute-done.21.got_ref, bf16[512,512]{1,0:T(8,128)(2,1)S(1)} %copy-done, ...), custom_call_target="tpu_custom_call" | custom-call | tf_op jit(solution)/shard_map/pallas_call | solution.py:302
  132.4 0.4 collective-permute-start.22
  132.8 1.5 collective-permute-done.22.other_slope_ref
  134.3 0.7 shard_map.105
  135.0 10.9 %all_to_all.20 = bf16[8,32,512]{2,1,0:T(8,128)(2,1)S(1)} all-to-all(bf16[8,32,512]{2,1,0:T(8,128)(2,1)S(1)} %bitcast.41), channel_id=1, replica_groups={{0,16,32,48,64,80,96,112},{8,24,40,56,72,88,104,120},{1,17,33,49,65,81,..., dimensions={0} | all-to-all | bytes 524288 | tf_op jit(solution)/shard_map/all_to_all | solution.py:274
  146.1 0.1 broadcast_in_dim.6
  146.1 12.8 %all_to_all.21 = f32[8,32,512]{2,1,0:T(8,128)S(1)} all-to-all(f32[8,32,512]{2,1,0:T(8,128)S(1)} %broadcast_in_dim.6), channel_id=1, replica_groups=mesh['row'=16,'col'=8] {'col'}, dimensions={0} | all-to-all | bytes 1048576 | tf_op jit(solution)/shard_map/all_to_all | solution.py:274
  159.0 9.9 %all_to_all.22 = bf16[8,32,512]{2,1,0:T(8,128)(2,1)S(1)} all-to-all(bf16[8,32,512]{2,1,0:T(8,128)(2,1)S(1)} %broadcast_in_dim.7), channel_id=1, replica_groups={{0,16,32,48,64,80,96,112},{8,24,40,56,72,88,104,120},{1,17,33,49,65,81,..., dimensions={0} | all-to-all | bytes 524288 | tf_op jit(solution)/shard_map/all_to_all | solution.py:274
  169.0 3.7 %collective-permute-start.23 = (bf16[256,512]{1,0:T(8,128)(2,1)S(1)}, bf16[256,512]{1,0:T(8,128)(2,1)S(1)}, u32[]{:S(2)}, u32[]{:S(2)}) collective-permute-start(bf16[256,512]{1,0:T(8,128)(2,1)S(1)} %bitcast.51), channel_id=1, source_target_pairs={{0,8},{8,0},{16,24},{24,16},{32,40},{40,32},{48,56},{56,48},{64,72... | collective-permute-start | bytes 786440 | tf_op jit(solution)/shard_map/ppermute | solution.py:446
  172.7 1.2 collective-permute-done.23
  173.8 0.1 broadcast_select_fusion.3
  173.9 1.1 maximum_convert_fusion
  (20 shorter events, 0.2 us)
Async XLA Ops:
  0.6 3.3 %collective-permute-start.1 = (bf16[512,512]{1,0:T(8,128)(2,1)}, bf16[512,512]{1,0:T(8,128)(2,1)S(1)}, u32[]{:S(2)}, u32[]{:S(2)}) collective-permute-start(bf16[512,512]{1,0:T(8,128)(2,1)} %features_hbm.1), channel_id=1, source_target_pairs={{0,8},{8,0},{16,24},{24,16},{32,40},{40,32},{48,56},{56,48},{64,72... | collective-permute-start | bytes 1572872 | tf_op jit(solution)/shard_map/ppermute | solution.py:353
  2.1 1.8 %collective-permute-start.2 = (s32[1,512]{1,0:T(1,128)}, s32[1,512]{1,0:T(1,128)S(1)}, u32[]{:S(2)}, u32[]{:S(2)}) collective-permute-start(s32[1,512]{1,0:T(1,128)} %bitcast.45), channel_id=1, source_target_pairs={{0,8},{8,0},{16,24},{24,16},{32,40},{40,32},{48,56},{56,48},{64,72... | collective-permute-start | bytes 6152 | tf_op jit(solution)/shard_map/ppermute | solution.py:352
  3.9 23.2 %collective-permute-start.3 = (bf16[192,128,128]{2,1,0:T(8,128)(2,1)}, bf16[192,128,128]{2,1,0:T(8,128)(2,1)}, u32[]{:S(2)}, u32[]{:S(2)}) collective-permute-start(bf16[192,128,128]{2,1,0:T(8,128)(2,1)} %bitcast.49), channel_id=1, source_target_pairs={{0,8},{8,0},{16,24},{24,16},{32,40},{40,32},{48,56},{56,48},{64,72... | collective-permute-start | bytes 18874376 | tf_op jit(solution)/shard_map/ppermute | solution.py:359
  4.3 0.7 copy-start.1
  8.1 18.5 %all-to-all-start = ((bf16[8,2,64,256]{3,2,1,0:T(8,128)(2,1)}), bf16[8,2,64,256]{3,2,1,0:T(8,128)(2,1)S(1)}, u32[]{:S(2)}, u32[]{:S(2)}) async-start(bf16[8,2,64,256]{3,2,1,0:T(8,128)(2,1)} %shard_map.96), calls=%async_computation | async-start | bytes 1048576 | tf_op jit(solution)/shard_map/all_to_all | solution.py:366
  15.5 0.7 copy-start.2
  16.1 0.7 copy-start.3
  17.3 9.8 %collective-permute-start = (s32[8,288]{1,0:T(8,128)S(1)}, s32[8,288]{1,0:T(8,128)S(1)}, u32[]{:S(2)}, u32[]{:S(2)}) collective-permute-start(s32[8,288]{1,0:T(8,128)S(1)} %shard_map.95), channel_id=1, source_target_pairs={{0,8},{8,0},{16,24},{24,16},{32,40},{40,32},{48,56},{56,48},{64,72... | collective-permute-start | bytes 27656 | tf_op jit(solution)/shard_map/ppermute | solution.py:357
  27.0 8.4 %collective-permute-start.4 = (bf16[2,512,256]{2,1,0:T(8,128)(2,1)S(1)}, bf16[2,512,256]{2,1,0:T(8,128)(2,1)S(1)}, u32[]{:S(2)}, u32[]{:S(2)}) collective-permute-start(bf16[2,512,256]{2,1,0:T(8,128)(2,1)S(1)} %shard_map.97), channel_id=1, source_target_pairs={{0,16},{8,72},{16,32},{24,88},{32,48},{40,104},{48,0},{56,120},{64... | collective-permute-start | bytes 1572872 | tf_op jit(solution)/shard_map/ppermute | solution.py:383
  27.5 7.9 %collective-permute-start.5 = (bf16[2,512,256]{2,1,0:T(8,128)(2,1)S(1)}, bf16[2,512,256]{2,1,0:T(8,128)(2,1)S(1)}, u32[]{:S(2)}, u32[]{:S(2)}) collective-permute-start(bf16[2,512,256]{2,1,0:T(8,128)(2,1)S(1)} %shard_map.97), channel_id=1, source_target_pairs={{0,48},{16,0},{32,16},{48,32},{64,112},{80,64},{96,80},{112,96},{1... | collective-permute-start | bytes 1572872 | tf_op jit(solution)/shard_map/ppermute | solution.py:383
  28.2 11.9 %collective-permute-start.6 = (bf16[2,512,256]{2,1,0:T(8,128)(2,1)S(1)}, bf16[2,512,256]{2,1,0:T(8,128)(2,1)S(1)}, u32[]{:S(2)}, u32[]{:S(2)}) collective-permute-start(bf16[2,512,256]{2,1,0:T(8,128)(2,1)S(1)} %shard_map.97), channel_id=1, source_target_pairs={{0,32},{16,48},{32,0},{48,16},{64,96},{80,112},{96,64},{112,80},{1... | collective-permute-start | bytes 1572872 | tf_op jit(solution)/shard_map/ppermute | solution.py:383
  28.9 16.6 %collective-permute-start.7 = (bf16[2,512,256]{2,1,0:T(8,128)(2,1)S(1)}, bf16[2,512,256]{2,1,0:T(8,128)(2,1)S(1)}, u32[]{:S(2)}, u32[]{:S(2)}) collective-permute-start(bf16[2,512,256]{2,1,0:T(8,128)(2,1)S(1)} %shard_map.97), channel_id=1, source_target_pairs={{0,64},{8,24},{16,80},{24,40},{32,96},{40,56},{48,112},{56,8},{64,... | collective-permute-start | bytes 1572872 | tf_op jit(solution)/shard_map/ppermute | solution.py:383
  36.3 21.3 %collective-permute-start.9 = (bf16[2,512,256]{2,1,0:T(8,128)(2,1)}, bf16[2,512,256]{2,1,0:T(8,128)(2,1)S(1)}, u32[]{:S(2)}, u32[]{:S(2)}) collective-permute-start(bf16[2,512,256]{2,1,0:T(8,128)(2,1)} %broadcast_select_fusion.1), channel_id=1, source_target_pairs={{0,64},{8,56},{16,80},{24,8},{32,96},{40,24},{48,112},{56,40},{64,... | collective-permute-start | bytes 1572872 | tf_op jit(solution)/shard_map/ppermute | solution.py:383
  40.9 14.8 %collective-permute-start.8 = (bf16[2,512,256]{2,1,0:T(8,128)(2,1)S(1)}, bf16[2,512,256]{2,1,0:T(8,128)(2,1)}, u32[]{:S(2)}, u32[]{:S(2)}) collective-permute-start(bf16[2,512,256]{2,1,0:T(8,128)(2,1)S(1)} %collective-permute-done.4), channel_id=1, source_target_pairs={{0,64},{8,24},{16,80},{24,40},{32,96},{40,56},{48,112},{56,8},{64,... | collective-permute-start | bytes 1572872 | tf_op jit(solution)/shard_map/ppermute | solution.py:383
  40.9 21.5 %collective-permute-start.10 = (bf16[2,512,256]{2,1,0:T(8,128)(2,1)}, bf16[2,512,256]{2,1,0:T(8,128)(2,1)}, u32[]{:S(2)}, u32[]{:S(2)}) collective-permute-start(bf16[2,512,256]{2,1,0:T(8,128)(2,1)} %broadcast_select_fusion), channel_id=1, source_target_pairs={{0,64},{8,40},{16,80},{24,56},{32,96},{40,8},{48,112},{56,24},{64,... | collective-permute-start | bytes 1572872 | tf_op jit(solution)/shard_map/ppermute | solution.py:383
  42.2 26.5 %collective-permute-start.11 = (bf16[2,512,256]{2,1,0:T(8,128)(2,1)S(1)}, bf16[2,512,256]{2,1,0:T(8,128)(2,1)}, u32[]{:S(2)}, u32[]{:S(2)}) collective-permute-start(bf16[2,512,256]{2,1,0:T(8,128)(2,1)S(1)} %collective-permute-done.4), channel_id=1, source_target_pairs={{8,56},{24,8},{40,24},{56,40},{72,120},{88,72},{104,88},{120,104},... | collective-permute-start | bytes 1572872 | tf_op jit(solution)/shard_map/ppermute | solution.py:383
  45.5 23.2 %collective-permute-start.12 = (bf16[2,512,256]{2,1,0:T(8,128)(2,1)S(1)}, bf16[2,512,256]{2,1,0:T(8,128)(2,1)}, u32[]{:S(2)}, u32[]{:S(2)}) collective-permute-start(bf16[2,512,256]{2,1,0:T(8,128)(2,1)S(1)} %collective-permute-done.4), channel_id=1, source_target_pairs={{8,40},{24,56},{40,8},{56,24},{72,104},{88,120},{104,72},{120,88},... | collective-permute-start | bytes 1572872 | tf_op jit(solution)/shard_map/ppermute | solution.py:383
  73.7 23.4 %collective-permute-start.13 = (bf16[4,512,256]{2,1,0:T(8,128)(2,1)S(1)}, bf16[4,512,256]{2,1,0:T(8,128)(2,1)S(1)}, u32[]{:S(2)}, u32[]{:S(2)}) collective-permute-start(bf16[4,512,256]{2,1,0:T(8,128)(2,1)S(1)} %get-tuple-element.37), channel_id=1, source_target_pairs={{0,4},{1,5},{2,6},{3,7},{4,0},{5,1},{6,2},{7,3},{8,12},{9,13},{10,... | collective-permute-start | bytes 3145736 | tf_op jit(solution)/shard_map/ppermute | solution.py:415
  83.7 46.4 %copy-start = (bf16[512,512]{1,0:T(8,128)(2,1)S(1)}, bf16[512,512]{1,0:T(8,128)(2,1)}, u32[]{:S(2)}) copy-start(bf16[512,512]{1,0:T(8,128)(2,1)} %weight_ref.1) | copy-start | bytes 1572868
  83.7 14.2 %collective-permute-start.14 = (bf16[2,512,256]{2,1,0:T(8,128)(2,1)S(1)}, bf16[2,512,256]{2,1,0:T(8,128)(2,1)S(1)}, u32[]{:S(2)}, u32[]{:S(2)}) collective-permute-start(bf16[2,512,256]{2,1,0:T(8,128)(2,1)S(1)} %get-tuple-element.42), channel_id=1, source_target_pairs={{0,1},{1,2},{2,3},{3,0},{4,5},{5,6},{6,7},{7,4},{8,9},{9,10},{10,1... | collective-permute-start | bytes 1572872 | tf_op jit(solution)/shard_map/ppermute | solution.py:414
  83.8 19.9 %collective-permute-start.15 = (bf16[2,512,256]{2,1,0:T(8,128)(2,1)S(1)}, bf16[2,512,256]{2,1,0:T(8,128)(2,1)S(1)}, u32[]{:S(2)}, u32[]{:S(2)}) collective-permute-start(bf16[2,512,256]{2,1,0:T(8,128)(2,1)S(1)} %get-tuple-element.43), channel_id=1, source_target_pairs={{0,2},{1,3},{2,0},{3,1},{4,6},{5,7},{6,4},{7,5},{8,10},{9,11},{10,... | collective-permute-start | bytes 1572872 | tf_op jit(solution)/shard_map/ppermute | solution.py:414
  84.1 24.9 %collective-permute-start.16 = (bf16[2,512,256]{2,1,0:T(8,128)(2,1)S(1)}, bf16[2,512,256]{2,1,0:T(8,128)(2,1)S(1)}, u32[]{:S(2)}, u32[]{:S(2)}) collective-permute-start(bf16[2,512,256]{2,1,0:T(8,128)(2,1)S(1)} %get-tuple-element.44), channel_id=1, source_target_pairs={{0,3},{1,0},{2,1},{3,2},{4,7},{5,4},{6,5},{7,6},{8,11},{9,8},{10,9... | collective-permute-start | bytes 1572872 | tf_op jit(solution)/shard_map/ppermute | solution.py:414
  109.8 7.2 %collective-permute-start.17 = (bf16[512,256]{1,0:T(8,128)(2,1)S(1)}, bf16[512,256]{1,0:T(8,128)(2,1)S(1)}, u32[]{:S(2)}, u32[]{:S(2)}) collective-permute-start(bf16[512,256]{1,0:T(8,128)(2,1)S(1)} %get-tuple-element.46), channel_id=1, source_target_pairs={{0,4},{1,5},{2,6},{3,7},{4,0},{5,1},{6,2},{7,3},{8,12},{9,13},{10,... | collective-permute-start | bytes 786440 | tf_op jit(solution)/shard_map/ppermute | solution.py:423
  110.2 8.5 %collective-permute-start.18 = (bf16[512,256]{1,0:T(8,128)(2,1)S(1)}, bf16[512,256]{1,0:T(8,128)(2,1)S(1)}, u32[]{:S(2)}, u32[]{:S(2)}) collective-permute-start(bf16[512,256]{1,0:T(8,128)(2,1)S(1)} %get-tuple-element.38), channel_id=1, source_target_pairs={{0,1},{1,2},{2,3},{3,0},{4,5},{5,6},{6,7},{7,4},{8,9},{9,10},{10,1... | collective-permute-start | bytes 786440 | tf_op jit(solution)/shard_map/ppermute | solution.py:424
  112.2 13.8 %collective-permute-start.19 = (bf16[512,256]{1,0:T(8,128)(2,1)S(1)}, bf16[512,256]{1,0:T(8,128)(2,1)S(1)}, u32[]{:S(2)}, u32[]{:S(2)}) collective-permute-start(bf16[512,256]{1,0:T(8,128)(2,1)S(1)} %get-tuple-element.39), channel_id=1, source_target_pairs={{0,2},{1,3},{2,0},{3,1},{4,6},{5,7},{6,4},{7,5},{8,10},{9,11},{10,... | collective-permute-start | bytes 786440 | tf_op jit(solution)/shard_map/ppermute | solution.py:424
  114.8 11.2 %collective-permute-start.20 = (bf16[512,256]{1,0:T(8,128)(2,1)S(1)}, bf16[512,256]{1,0:T(8,128)(2,1)S(1)}, u32[]{:S(2)}, u32[]{:S(2)}) collective-permute-start(bf16[512,256]{1,0:T(8,128)(2,1)S(1)} %get-tuple-element.40), channel_id=1, source_target_pairs={{0,3},{1,0},{2,1},{3,2},{4,7},{5,4},{6,5},{7,6},{8,11},{9,8},{10,9... | collective-permute-start | bytes 786440 | tf_op jit(solution)/shard_map/ppermute | solution.py:424
  126.8 3.3 %collective-permute-start.21 = (f32[512,256]{1,0:T(8,128)S(1)}, f32[512,256]{1,0:T(8,128)S(1)}, u32[]{:S(2)}, u32[]{:S(2)}) collective-permute-start(f32[512,256]{1,0:T(8,128)S(1)} %get-tuple-element.49.other_ref), channel_id=1, source_target_pairs={{0,8},{8,0},{16,24},{24,16},{32,40},{40,32},{48,56},{56,48},{64,72... | collective-permute-start | bytes 1572872 | tf_op jit(solution)/shard_map/ppermute | solution.py:428
  132.4 1.9 %collective-permute-start.22 = (bf16[512,512]{1,0:T(8,128)(2,1)S(1)}, bf16[512,512]{1,0:T(8,128)(2,1)S(1)}, u32[]{:S(2)}, u32[]{:S(2)}) collective-permute-start(bf16[512,512]{1,0:T(8,128)(2,1)S(1)} %get-tuple-element.51.slope_ref), channel_id=1, source_target_pairs={{0,8},{8,0},{16,24},{24,16},{32,40},{40,32},{48,56},{56,48},{64,72... | collective-permute-start | bytes 1572872 | tf_op jit(solution)/shard_map/ppermute | solution.py:435
  169.0 4.9 %collective-permute-start.23 = (bf16[256,512]{1,0:T(8,128)(2,1)S(1)}, bf16[256,512]{1,0:T(8,128)(2,1)S(1)}, u32[]{:S(2)}, u32[]{:S(2)}) collective-permute-start(bf16[256,512]{1,0:T(8,128)(2,1)S(1)} %bitcast.51), channel_id=1, source_target_pairs={{0,8},{8,0},{16,24},{24,16},{32,40},{40,32},{48,56},{56,48},{64,72... | collective-permute-start | bytes 786440 | tf_op jit(solution)/shard_map/ppermute | solution.py:446

commit v6 on v5

--- a/solution.py
+++ b/solution.py
@@ -13,13 +13,13 @@
 PER_PEER = 4
 HALF = 256
 CHIPS = 8
-BLOCKS = CHIPS + 2
+BLOCKS = CHIPS + 1
 SLOT_CAP = 192
 ROW_TILES = 32
 GROUP_BITS = 2
 GROUP = 1 << GROUP_BITS
 PLAN = SLOT_CAP + ROW_TILES * (GROUP - 1)
-UNROLL_BITS = 2
+UNROLL_BITS = 3
 UNROLL = 1 << UNROLL_BITS
 BF16 = jnp.bfloat16
 F32 = jnp.float32
@@ -335,14 +335,13 @@
     places = [
         near[0],
         jnp.where(first, near[1], far[0]),
-        jnp.where(first, near[3], CHIPS),
-        jnp.where(first, near[2], CHIPS + 1),
+        near[3],
+        near[2],
         jnp.where(first, far[0], near[1]),
         far[1],
-        jnp.where(first, far[3], near[3]),
-        jnp.where(first, far[2], near[2]),
+        jnp.where(first, far[3], CHIPS),
+        far[2],
         jnp.where(first, CHIPS, far[3]),
-        jnp.where(first, CHIPS + 1, far[2]),
     ]
     meta = jnp.stack([core, x, yh, z] + places).astype(jnp.int32)
 
@@ -356,13 +355,13 @@
     )
     other_plan = lax.ppermute(plan, "row", swap)
     plans = [jnp.where(core == c, plan, other_plan) for c in range(2)]
-    other_tiles = lax.ppermute(after(tiles, other_features, other_part), "row", swap)
     grouped = call(
         group_kernel,
         [smem, vmem, pinned, vmem, vmem],
         held(N_COL, 2, SLOTS // N_COL, HALF),
         [pltpu.VMEM((SLOTS, F), BF16), pltpu.SemaphoreType.DMA],
     )(meta, part, features, other_part, other_features)
+    other_tiles = lax.ppermute(after(tiles, grouped), "row", swap)
     arrived = lax.all_to_all(grouped, "col", split_axis=0, concat_axis=0, tiled=True)
     own = call(interleave_kernel, [vmem], array(2, SLOTS, HALF))(arrived)
     own = after(own, other_tiles, other_plan)
@@ -383,18 +382,16 @@
         return lax.ppermute(block, "row", row_moves(move))
 
     r1 = hop(own, (0, 1), (1, 0))
-    r2 = hop(own, (0, 3), None)
-    r3 = hop(own, (0, 2), None)
+    r2 = hop(own, (0, 3), (0, 3))
+    r3 = hop(own, (0, 2), (0, 2))
     r4 = hop(own, (1, 0), (0, 1))
     s1 = hop(r1, (1, 0), (0, 1))
-    second = jnp.where(first, after(r2, r1), own)
-    s2 = hop(second, (1, 0), (0, 3))
-    s3 = hop(jnp.where(first, after(r3, second), own), (1, 0), (0, 2))
+    s2 = hop(r2, (1, 0), None)
+    s3 = hop(r3, (1, 0), (1, 0))
     s4 = hop(r1, None, (0, 3))
-    s5 = hop(r1, None, (0, 2))
     blocks = [
         b.reshape(2, N_ROW, N_COL * PER_PEER, HALF)
-        for b in (own, r1, r2, r3, r4, s1, s2, s3, s4, s5)
+        for b in (own, r1, r2, r3, r4, s1, s2, s3, s4)
     ]
 
     total = pltpu.VMEM((ROW_TILES, TILE, HALF), F32)
@@ -417,11 +414,11 @@
     keep1, *send1 = call(y_summed_kernel, [smem] + [vmem] * 2, [wide] + [narrow] * 3)(
         meta, keep1, got1
     )
+    got1 = [lax.ppermute(send1[k - 1], "col", x_moves(k)) for k in (1, 2, 3)]
     keep0, send0 = call(x_summed_kernel, [smem] + [vmem] * 4, [wide, narrow])(
-        meta, after(row0[0], *send1), *got0
+        meta, after(row0[0], got1[0]), *got0
     )
     got0 = lax.ppermute(send0, "col", y_moves())
-    got1 = [lax.ppermute(send1[k - 1], "col", x_moves(k)) for k in (1, 2, 3)]
     mine, others = call(sums_kernel, [smem] + [vmem] * 6, [wide] * 2)(
         meta, keep0, got0, keep1, *got1
     )

time: 177 us -> 175 us (0.989)
  starting transfers between devices: 42.5 us -> 50.9 us
  waiting for transfers between devices: 65.1 us -> 58 us
  Pallas kernels: 25.9 us -> 23.1 us
    ppermute x3, waiting for transfers between devices: 11.1 us -> 0.01 us  [shards(): got0 = [lax.ppermute(row0[k], 'col', x_moves(k)) for k in (1, 2, 3)]]
    ppermute x1, starting transfers between devices: 0.42 us -> 8.22 us  [shards(): got0 = lax.ppermute(send0, 'col', y_moves())]
    ppermute x1, starting transfers between devices: 1.74 us -> 7.65 us  [shards(): theirs = lax.ppermute(others, 'row', swap)]
    ppermute x1, starting transfers between devices: 3.58 us -> 0.09 us  [shards(): got1 = lax.ppermute(send1, 'col', y_moves())]
    ppermute x9 -> x8, waiting for transfers between devices: 18.5 us -> 21.7 us  [hop(): return lax.ppermute(block, 'row', row_moves(move))]
    ppermute x3, starting transfers between devices: 4.6 us -> 1.55 us  [shards(): got1 = [lax.ppermute(send1[k - 1], 'col', x_moves(k)) for k in (1, 2, 3)]]
    pallas_call x11, Pallas kernels: 25.9 us -> 23.1 us  [run(): return made(*held)]
    ppermute x3, starting transfers between devices: 2.74 us -> 4.84 us  [shards(): got0 = [lax.ppermute(row0[k], 'col', x_moves(k)) for k in (1, 2, 3)]]
  transfers between devices with their start and end apart: 25 -> 24, of which waited for: 16 -> 11; matrix products, arithmetic and copies ran while one was open for 2% -> 1% of each run, Pallas kernels for 9% -> 6%
where the time goes in v6:
time: 175 us; the launch traced here: 173 us
  waiting for transfers between devices  58 us (33%)
  starting transfers between devices  50.9 us (29%)
  blocking collectives  35 us (20%)
  Pallas kernels  23.1 us (13%)
  local copies, waits for them, and re-layouts  3.27 us (2%)
    all_to_all x3, blocking collectives, exchange(): lax.all_to_all(parts, axis, split_axis=0, concat_axis=0, axis_index_group...  35 us
    pallas_call x11, Pallas kernels, run(): return made(*held)  23.1 us
    ppermute x8, waiting for transfers between devices, hop(): return lax.ppermute(block, 'row', row_moves(move))  21.7 us
    ppermute x8, starting transfers between devices, hop(): return lax.ppermute(block, 'row', row_moves(move))  15.2 us
    ppermute x1, waiting for transfers between devices, shards(): got1 = lax.ppermute(send1, 'col', y_moves())  10 us
    all_to_all x1, waiting for transfers between devices, shards(): lax.all_to_all(grouped, 'col', split_axis=0, concat_axis=0, tiled=True)  8.84 us
    ppermute x3, waiting for transfers between devices, shards(): got1 = [lax.ppermute(send1[k - 1], 'col', x_moves(k)) for k in (1, 2, 3)]  8.68 us
    ppermute x1, starting transfers between devices, shards(): got0 = lax.ppermute(send0, 'col', y_moves())  8.22 us
  transfers between devices with their start and end apart: 24, of which 11 were waited for; matrix products, arithmetic and copies ran while one was open for 1% of the time, Pallas kernels for 6%

profile of v6, /device:TPU:1, one launch (start us, length us, event | category | flops | bytes accessed | tf_op | source)
XLA Modules:
  0.0 173.1 jit_solution(14972222364550219915)
XLA Ops:
  0.6 1.5 collective-permute-start.2
  2.1 0.1 collective-permute-start.1
  2.2 0.1 stack.55.meta_ref
  2.3 1.6 collective-permute-done.1.other_part_ref
  3.9 0.7 copy-done.1
  4.6 3.0 %shard_map.96 = bf16[8,2,64,256]{3,2,1,0:T(8,128)(2,1)} custom-call(s32[13]{0:T(128)S(1)} %stack.55.meta_ref, s32[1,512]{1,0:T(1,128)S(1)} %bitcast.44, bf16[512,512]{1,0:T(8,128)(2,1)} %features_hbm.1, s32[1,512]{1,0:T(1,128)S(1)} %collective-permute-done.1.other_part_ref, bf16[512,512]{1,0:T(8,128)(2,1)S(1)} %collective-permute-done.2.other_ref), custom_call_target="tpu_custom_call" | custom-call | tf_op jit(solution)/shard_map/pallas_call | solution.py:302
  7.6 0.5 collective-permute-start.3
  8.0 6.7 %all-to-all-start = ((bf16[8,2,64,256]{3,2,1,0:T(8,128)(2,1)}), bf16[8,2,64,256]{3,2,1,0:T(8,128)(2,1)S(1)}, u32[]{:S(2)}, u32[]{:S(2)}) async-start(bf16[8,2,64,256]{3,2,1,0:T(8,128)(2,1)} %shard_map.96), calls=%async_computation | async-start | bytes 1048576 | tf_op jit(solution)/shard_map/all_to_all | solution.py:365
  15.4 0.0 copy-start.2
  15.4 0.7 copy-done.2
  16.1 0.7 copy-done.3
  16.8 0.5 shard_map.95
  17.3 0.5 collective-permute-start
  17.7 8.8 %all-to-all-done.arrived_ref = bf16[8,2,64,256]{3,2,1,0:T(8,128)(2,1)S(1)} async-done(((bf16[8,2,64,256]{3,2,1,0:T(8,128)(2,1)}), bf16[8,2,64,256]{3,2,1,0:T(8,128)(2,1)S(1)}, u32[]{:S(2)}, u32[]{:S(2)}) %all-to-all-start) | async-done | bytes 524320 | tf_op jit(solution)/shard_map/all_to_all | solution.py:365
  26.6 0.4 shard_map.97
  27.0 0.0 collective-permute-done.3.other_hbm
  27.0 0.5 collective-permute-start.4
  27.5 3.8 %collective-permute-start.5 = (bf16[2,512,256]{2,1,0:T(8,128)(2,1)S(1)}, bf16[2,512,256]{2,1,0:T(8,128)(2,1)S(1)}, u32[]{:S(2)}, u32[]{:S(2)}) collective-permute-start(bf16[2,512,256]{2,1,0:T(8,128)(2,1)S(1)} %shard_map.97), channel_id=1, source_target_pairs={{0,48},{8,56},{16,0},{24,8},{32,16},{40,24},{48,32},{56,40},{64,11... | collective-permute-start | bytes 1572872 | tf_op jit(solution)/shard_map/ppermute | solution.py:382
  31.2 0.0 collective-permute-start.6
  31.2 0.7 collective-permute-start.7
  31.9 3.5 %collective-permute-done.4 = bf16[2,512,256]{2,1,0:T(8,128)(2,1)S(1)} collective-permute-done((bf16[2,512,256]{2,1,0:T(8,128)(2,1)S(1)}, bf16[2,512,256]{2,1,0:T(8,128)(2,1)S(1)}, u32[]{:S(2)}, u32[]{:S(2)}) %collective-permute-start.4) | collective-permute-done | bytes 524320 | tf_op jit(solution)/shard_map/ppermute | solution.py:382
  35.4 1.6 collective-permute-start.8
  37.1 16.1 %collective-permute-done.5 = bf16[2,512,256]{2,1,0:T(8,128)(2,1)S(1)} collective-permute-done((bf16[2,512,256]{2,1,0:T(8,128)(2,1)S(1)}, bf16[2,512,256]{2,1,0:T(8,128)(2,1)S(1)}, u32[]{:S(2)}, u32[]{:S(2)}) %collective-permute-start.5) | collective-permute-done | bytes 524320 | tf_op jit(solution)/shard_map/ppermute | solution.py:382
  53.2 1.5 collective-permute-start.9
  54.6 0.0 collective-permute-done.6
  54.6 1.9 %collective-permute-start.10 = (bf16[2,512,256]{2,1,0:T(8,128)(2,1)S(1)}, bf16[2,512,256]{2,1,0:T(8,128)(2,1)}, u32[]{:S(2)}, u32[]{:S(2)}) collective-permute-start(bf16[2,512,256]{2,1,0:T(8,128)(2,1)S(1)} %collective-permute-done.6), channel_id=1, source_target_pairs={{0,64},{8,72},{16,80},{24,88},{32,96},{40,104},{48,112},{56,120},{... | collective-permute-start | bytes 1572872 | tf_op jit(solution)/shard_map/ppermute | solution.py:382
  56.5 5.3 %collective-permute-start.11 = (bf16[2,512,256]{2,1,0:T(8,128)(2,1)S(1)}, bf16[2,512,256]{2,1,0:T(8,128)(2,1)}, u32[]{:S(2)}, u32[]{:S(2)}) collective-permute-start(bf16[2,512,256]{2,1,0:T(8,128)(2,1)S(1)} %collective-permute-done.4), channel_id=1, source_target_pairs={{8,56},{24,8},{40,24},{56,40},{72,120},{88,72},{104,88},{120,104},... | collective-permute-start | bytes 1572872 | tf_op jit(solution)/shard_map/ppermute | solution.py:382
  61.8 5.2 %shard_map.98 = (bf16[193,128,128]{2,1,0:T(8,128)(2,1)S(1)}, bf16[193,128,128]{2,1,0:T(8,128)(2,1)S(1)}) custom-call(s32[13]{0:T(128)S(1)} %stack.55.meta_ref, bf16[192,128,128]{2,1,0:T(8,128)(2,1)} %bitcast.48, bf16[192,128,128]{2,1,0:T(8,128)(2,1)} %collective-permute-done.3.other_hbm), custom_call_target="tpu_custom_call" | custom-call | tf_op jit(solution)/shard_map/pallas_call | solution.py:302
  67.0 0.0 collective-permute-done.7
  67.0 0.0 collective-permute-done.9
  67.1 2.1 %collective-permute-done.10 = bf16[2,512,256]{2,1,0:T(8,128)(2,1)} collective-permute-done((bf16[2,512,256]{2,1,0:T(8,128)(2,1)S(1)}, bf16[2,512,256]{2,1,0:T(8,128)(2,1)}, u32[]{:S(2)}, u32[]{:S(2)}) %collective-permute-start.10) | collective-permute-done | bytes 524320 | tf_op jit(solution)/shard_map/ppermute | solution.py:382
  69.2 0.0 collective-permute-done.11
  69.2 5.3 %shard_map.99 = (bf16[4,512,256]{2,1,0:T(8,128)(2,1)S(1)}, bf16[4,512,256]{2,1,0:T(8,128)(2,1)S(1)}, bf16[9,2,16,32,256]{4,3,2,1,0:T(8,128)(2,1)S(1)}) custom-call(s32[13]{0:T(128)S(1)} %stack.55.meta_ref, s32[8,288]{1,0:T(8,128)S(1)} %get-tuple-element.50.plan_ref, bf16[193,128,128]{2,1,0:T(8,128)(2,1)S(1)} %get-tuple-element.29.tiles, ...), custom_call_target="tpu_custom_call" | custom-call | tf_op jit(solution)/shard_map/pallas_call | solution.py:302
  74.5 0.1 collective-permute-start.12
  74.6 3.3 %shard_map.100 = (bf16[2,512,256]{2,1,0:T(8,128)(2,1)S(1)}, bf16[2,512,256]{2,1,0:T(8,128)(2,1)S(1)}, bf16[2,512,256]{2,1,0:T(8,128)(2,1)S(1)}, bf16[2,512,256]{2,1,0:T(8,128)(2,1)S(1)}) custom-call(s32[13]{0:T(128)S(1)} %stack.55.meta_ref, s32[8,288]{1,0:T(8,128)S(1)} %get-tuple-element.51.plan_ref, bf16[193,128,128]{2,1,0:T(8,128)(2,1)S(1)} %get-tuple-element.28.tiles, ...), custom_call_target="tpu_custom_call" | custom-call | tf_op jit(solution)/shard_map/pallas_call | solution.py:302
  77.9 0.0 copy-start
  77.9 2.4 %collective-permute-start.14 = (bf16[2,512,256]{2,1,0:T(8,128)(2,1)S(1)}, bf16[2,512,256]{2,1,0:T(8,128)(2,1)S(1)}, u32[]{:S(2)}, u32[]{:S(2)}) collective-permute-start(bf16[2,512,256]{2,1,0:T(8,128)(2,1)S(1)} %get-tuple-element.36), channel_id=1, source_target_pairs={{0,1},{1,2},{2,3},{3,0},{4,5},{5,6},{6,7},{7,4},{8,9},{9,10},{10,1... | collective-permute-start | bytes 1572872 | tf_op jit(solution)/shard_map/ppermute | solution.py:411
  80.2 1.9 %collective-permute-start.15 = (bf16[2,512,256]{2,1,0:T(8,128)(2,1)S(1)}, bf16[2,512,256]{2,1,0:T(8,128)(2,1)S(1)}, u32[]{:S(2)}, u32[]{:S(2)}) collective-permute-start(bf16[2,512,256]{2,1,0:T(8,128)(2,1)S(1)} %get-tuple-element.37), channel_id=1, source_target_pairs={{0,2},{1,3},{2,0},{3,1},{4,6},{5,7},{6,4},{7,5},{8,10},{9,11},{10,... | collective-permute-start | bytes 1572872 | tf_op jit(solution)/shard_map/ppermute | solution.py:411
  82.1 0.6 collective-permute-start.16
  82.7 10.0 %collective-permute-done.12.got_ref = bf16[4,512,256]{2,1,0:T(8,128)(2,1)S(1)} collective-permute-done((bf16[4,512,256]{2,1,0:T(8,128)(2,1)S(1)}, bf16[4,512,256]{2,1,0:T(8,128)(2,1)S(1)}, u32[]{:S(2)}, u32[]{:S(2)}) %collective-permute-start.12) | collective-permute-done | bytes 1048608 | tf_op jit(solution)/shard_map/ppermute | solution.py:412
  92.7 0.8 shard_map.101
  93.5 0.1 collective-permute-start.13
  93.6 1.5 collective-permute-start.18
  95.1 8.7 %collective-permute-done.13.a_ref = bf16[512,256]{1,0:T(8,128)(2,1)S(1)} collective-permute-done((bf16[512,256]{1,0:T(8,128)(2,1)S(1)}, bf16[512,256]{1,0:T(8,128)(2,1)S(1)}, u32[]{:S(2)}, u32[]{:S(2)}) %collective-permute-start.13) | collective-permute-done | bytes 262176 | tf_op jit(solution)/shard_map/ppermute | solution.py:417
  103.8 0.0 collective-permute-start.19
  103.8 0.8 shard_map.102
  104.6 8.2 %collective-permute-start.17 = (bf16[512,256]{1,0:T(8,128)(2,1)S(1)}, bf16[512,256]{1,0:T(8,128)(2,1)S(1)}, u32[]{:S(2)}, u32[]{:S(2)}) collective-permute-start(bf16[512,256]{1,0:T(8,128)(2,1)S(1)} %get-tuple-element.40), channel_id=1, source_target_pairs={{0,4},{1,5},{2,6},{3,7},{4,0},{5,1},{6,2},{7,3},{8,12},{9,13},{10,... | collective-permute-start | bytes 786440 | tf_op jit(solution)/shard_map/ppermute | solution.py:421
  112.8 4.1 %collective-permute-done.17.got0 = bf16[512,256]{1,0:T(8,128)(2,1)S(1)} collective-permute-done((bf16[512,256]{1,0:T(8,128)(2,1)S(1)}, bf16[512,256]{1,0:T(8,128)(2,1)S(1)}, u32[]{:S(2)}, u32[]{:S(2)}) %collective-permute-start.17) | collective-permute-done | bytes 262176 | tf_op jit(solution)/shard_map/ppermute | solution.py:421
  116.9 0.7 shard_map.103
  117.6 7.7 %collective-permute-start.20 = (f32[512,256]{1,0:T(8,128)S(1)}, f32[512,256]{1,0:T(8,128)S(1)}, u32[]{:S(2)}, u32[]{:S(2)}) collective-permute-start(f32[512,256]{1,0:T(8,128)S(1)} %get-tuple-element.45.other_ref), channel_id=1, source_target_pairs={{0,8},{8,0},{16,24},{24,16},{32,40},{40,32},{48,56},{56,48},{64,72... | collective-permute-start | bytes 1572872 | tf_op jit(solution)/shard_map/ppermute | solution.py:425
  125.3 1.1 constant_dynamic-slice_fusion.cotangent_ref
  126.4 0.5 collective-permute-done.20.got_ref
  126.8 2.3 %shard_map.104 = (bf16[512,512]{1,0:T(8,128)(2,1)}, bf16[512,512]{1,0:T(8,128)(2,1)S(1)}) custom-call(s32[13]{0:T(128)S(1)} %stack.55.meta_ref, f32[512,256]{1,0:T(8,128)S(1)} %get-tuple-element.44.mine_ref, f32[512,256]{1,0:T(8,128)S(1)} %collective-permute-done.20.got_ref, bf16[512,512]{1,0:T(8,128)(2,1)S(1)} %copy-done, ...), custom_call_target="tpu_custom_call" | custom-call | tf_op jit(solution)/shard_map/pallas_call | solution.py:302
  129.1 0.4 collective-permute-start.21
  129.5 1.5 collective-permute-done.21.other_slope_ref
  131.0 0.7 shard_map.105
  131.8 12.5 %all_to_all.20 = bf16[8,32,512]{2,1,0:T(8,128)(2,1)S(1)} all-to-all(bf16[8,32,512]{2,1,0:T(8,128)(2,1)S(1)} %bitcast.37), channel_id=1, replica_groups={{0,16,32,48,64,80,96,112},{8,24,40,56,72,88,104,120},{1,17,33,49,65,81,..., dimensions={0} | all-to-all | bytes 524288 | tf_op jit(solution)/shard_map/all_to_all | solution.py:274
  144.4 0.1 broadcast_in_dim.6
  144.5 12.8 %all_to_all.21 = f32[8,32,512]{2,1,0:T(8,128)S(1)} all-to-all(f32[8,32,512]{2,1,0:T(8,128)S(1)} %broadcast_in_dim.6), channel_id=1, replica_groups=mesh['row'=16,'col'=8] {'col'}, dimensions={0} | all-to-all | bytes 1048576 | tf_op jit(solution)/shard_map/all_to_all | solution.py:274
  157.4 9.7 %all_to_all.22 = bf16[8,32,512]{2,1,0:T(8,128)(2,1)S(1)} all-to-all(bf16[8,32,512]{2,1,0:T(8,128)(2,1)S(1)} %broadcast_in_dim.7), channel_id=1, replica_groups={{0,16,32,48,64,80,96,112},{8,24,40,56,72,88,104,120},{1,17,33,49,65,81,..., dimensions={0} | all-to-all | bytes 524288 | tf_op jit(solution)/shard_map/all_to_all | solution.py:274
  167.0 3.7 %collective-permute-start.22 = (bf16[256,512]{1,0:T(8,128)(2,1)S(1)}, bf16[256,512]{1,0:T(8,128)(2,1)S(1)}, u32[]{:S(2)}, u32[]{:S(2)}) collective-permute-start(bf16[256,512]{1,0:T(8,128)(2,1)S(1)} %bitcast.49), channel_id=1, source_target_pairs={{0,8},{8,0},{16,24},{24,16},{32,40},{40,32},{48,56},{56,48},{64,72... | collective-permute-start | bytes 786440 | tf_op jit(solution)/shard_map/ppermute | solution.py:443
  170.7 1.2 collective-permute-done.22
  171.9 0.1 broadcast_select_fusion.1
  172.0 1.1 maximum_convert_fusion
  (16 shorter events, 0.2 us)
Async XLA Ops:
  0.6 3.3 %collective-permute-start.2 = (bf16[512,512]{1,0:T(8,128)(2,1)}, bf16[512,512]{1,0:T(8,128)(2,1)S(1)}, u32[]{:S(2)}, u32[]{:S(2)}) collective-permute-start(bf16[512,512]{1,0:T(8,128)(2,1)} %features_hbm.1), channel_id=1, source_target_pairs={{0,8},{8,0},{16,24},{24,16},{32,40},{40,32},{48,56},{56,48},{64,72... | collective-permute-start | bytes 1572872 | tf_op jit(solution)/shard_map/ppermute | solution.py:352
  2.1 1.8 %collective-permute-start.1 = (s32[1,512]{1,0:T(1,128)}, s32[1,512]{1,0:T(1,128)S(1)}, u32[]{:S(2)}, u32[]{:S(2)}) collective-permute-start(s32[1,512]{1,0:T(1,128)} %bitcast.43), channel_id=1, source_target_pairs={{0,8},{8,0},{16,24},{24,16},{32,40},{40,32},{48,56},{56,48},{64,72... | collective-permute-start | bytes 6152 | tf_op jit(solution)/shard_map/ppermute | solution.py:351
  3.9 0.7 copy-start.1
  7.6 19.4 %collective-permute-start.3 = (bf16[192,128,128]{2,1,0:T(8,128)(2,1)}, bf16[192,128,128]{2,1,0:T(8,128)(2,1)}, u32[]{:S(2)}, u32[]{:S(2)}) collective-permute-start(bf16[192,128,128]{2,1,0:T(8,128)(2,1)} %bitcast.47), channel_id=1, source_target_pairs={{0,8},{8,0},{16,24},{24,16},{32,40},{40,32},{48,56},{56,48},{64,72... | collective-permute-start | bytes 18874376 | tf_op jit(solution)/shard_map/ppermute | solution.py:364
  8.0 18.5 %all-to-all-start = ((bf16[8,2,64,256]{3,2,1,0:T(8,128)(2,1)}), bf16[8,2,64,256]{3,2,1,0:T(8,128)(2,1)S(1)}, u32[]{:S(2)}, u32[]{:S(2)}) async-start(bf16[8,2,64,256]{3,2,1,0:T(8,128)(2,1)} %shard_map.96), calls=%async_computation | async-start | bytes 1048576 | tf_op jit(solution)/shard_map/all_to_all | solution.py:365
  15.4 0.7 copy-start.2
  16.1 0.7 copy-start.3
  17.3 9.8 %collective-permute-start = (s32[8,288]{1,0:T(8,128)S(1)}, s32[8,288]{1,0:T(8,128)S(1)}, u32[]{:S(2)}, u32[]{:S(2)}) collective-permute-start(s32[8,288]{1,0:T(8,128)S(1)} %shard_map.95), channel_id=1, source_target_pairs={{0,8},{8,0},{16,24},{24,16},{32,40},{40,32},{48,56},{56,48},{64,72... | collective-permute-start | bytes 27656 | tf_op jit(solution)/shard_map/ppermute | solution.py:356
  27.0 8.4 %collective-permute-start.4 = (bf16[2,512,256]{2,1,0:T(8,128)(2,1)S(1)}, bf16[2,512,256]{2,1,0:T(8,128)(2,1)S(1)}, u32[]{:S(2)}, u32[]{:S(2)}) collective-permute-start(bf16[2,512,256]{2,1,0:T(8,128)(2,1)S(1)} %shard_map.97), channel_id=1, source_target_pairs={{0,16},{8,72},{16,32},{24,88},{32,48},{40,104},{48,0},{56,120},{64... | collective-permute-start | bytes 1572872 | tf_op jit(solution)/shard_map/ppermute | solution.py:382
  27.5 25.7 %collective-permute-start.5 = (bf16[2,512,256]{2,1,0:T(8,128)(2,1)S(1)}, bf16[2,512,256]{2,1,0:T(8,128)(2,1)S(1)}, u32[]{:S(2)}, u32[]{:S(2)}) collective-permute-start(bf16[2,512,256]{2,1,0:T(8,128)(2,1)S(1)} %shard_map.97), channel_id=1, source_target_pairs={{0,48},{8,56},{16,0},{24,8},{32,16},{40,24},{48,32},{56,40},{64,11... | collective-permute-start | bytes 1572872 | tf_op jit(solution)/shard_map/ppermute | solution.py:382
  31.2 23.4 %collective-permute-start.6 = (bf16[2,512,256]{2,1,0:T(8,128)(2,1)S(1)}, bf16[2,512,256]{2,1,0:T(8,128)(2,1)S(1)}, u32[]{:S(2)}, u32[]{:S(2)}) collective-permute-start(bf16[2,512,256]{2,1,0:T(8,128)(2,1)S(1)} %shard_map.97), channel_id=1, source_target_pairs={{0,32},{8,40},{16,48},{24,56},{32,0},{40,8},{48,16},{56,24},{64,96... | collective-permute-start | bytes 1572872 | tf_op jit(solution)/shard_map/ppermute | solution.py:382
  31.2 35.8 %collective-permute-start.7 = (bf16[2,512,256]{2,1,0:T(8,128)(2,1)S(1)}, bf16[2,512,256]{2,1,0:T(8,128)(2,1)S(1)}, u32[]{:S(2)}, u32[]{:S(2)}) collective-permute-start(bf16[2,512,256]{2,1,0:T(8,128)(2,1)S(1)} %shard_map.97), channel_id=1, source_target_pairs={{0,64},{8,24},{16,80},{24,40},{32,96},{40,56},{48,112},{56,8},{64,... | collective-permute-start | bytes 1572872 | tf_op jit(solution)/shard_map/ppermute | solution.py:382
  35.4 31.6 %collective-permute-start.8 = (bf16[2,512,256]{2,1,0:T(8,128)(2,1)S(1)}, bf16[2,512,256]{2,1,0:T(8,128)(2,1)S(1)}, u32[]{:S(2)}, u32[]{:S(2)}) collective-permute-start(bf16[2,512,256]{2,1,0:T(8,128)(2,1)S(1)} %collective-permute-done.4), channel_id=1, source_target_pairs={{0,64},{8,24},{16,80},{24,40},{32,96},{40,56},{48,112},{56,8},{64,... | collective-permute-start | bytes 1572872 | tf_op jit(solution)/shard_map/ppermute | solution.py:382
  53.2 13.9 %collective-permute-start.9 = (bf16[2,512,256]{2,1,0:T(8,128)(2,1)S(1)}, bf16[2,512,256]{2,1,0:T(8,128)(2,1)}, u32[]{:S(2)}, u32[]{:S(2)}) collective-permute-start(bf16[2,512,256]{2,1,0:T(8,128)(2,1)S(1)} %collective-permute-done.5), channel_id=1, source_target_pairs={{0,64},{16,80},{32,96},{48,112},{64,0},{80,16},{96,32},{112,48},{1... | collective-permute-start | bytes 1572872 | tf_op jit(solution)/shard_map/ppermute | solution.py:382
  54.6 14.5 %collective-permute-start.10 = (bf16[2,512,256]{2,1,0:T(8,128)(2,1)S(1)}, bf16[2,512,256]{2,1,0:T(8,128)(2,1)}, u32[]{:S(2)}, u32[]{:S(2)}) collective-permute-start(bf16[2,512,256]{2,1,0:T(8,128)(2,1)S(1)} %collective-permute-done.6), channel_id=1, source_target_pairs={{0,64},{8,72},{16,80},{24,88},{32,96},{40,104},{48,112},{56,120},{... | collective-permute-start | bytes 1572872 | tf_op jit(solution)/shard_map/ppermute | solution.py:382
  56.5 12.7 %collective-permute-start.11 = (bf16[2,512,256]{2,1,0:T(8,128)(2,1)S(1)}, bf16[2,512,256]{2,1,0:T(8,128)(2,1)}, u32[]{:S(2)}, u32[]{:S(2)}) collective-permute-start(bf16[2,512,256]{2,1,0:T(8,128)(2,1)S(1)} %collective-permute-done.4), channel_id=1, source_target_pairs={{8,56},{24,8},{40,24},{56,40},{72,120},{88,72},{104,88},{120,104},... | collective-permute-start | bytes 1572872 | tf_op jit(solution)/shard_map/ppermute | solution.py:382
  74.5 18.2 %collective-permute-start.12 = (bf16[4,512,256]{2,1,0:T(8,128)(2,1)S(1)}, bf16[4,512,256]{2,1,0:T(8,128)(2,1)S(1)}, u32[]{:S(2)}, u32[]{:S(2)}) collective-permute-start(bf16[4,512,256]{2,1,0:T(8,128)(2,1)S(1)} %get-tuple-element.33), channel_id=1, source_target_pairs={{0,4},{1,5},{2,6},{3,7},{4,0},{5,1},{6,2},{7,3},{8,12},{9,13},{10,... | collective-permute-start | bytes 3145736 | tf_op jit(solution)/shard_map/ppermute | solution.py:412
  77.9 49.0 %copy-start = (bf16[512,512]{1,0:T(8,128)(2,1)S(1)}, bf16[512,512]{1,0:T(8,128)(2,1)}, u32[]{:S(2)}) copy-start(bf16[512,512]{1,0:T(8,128)(2,1)} %weight_ref.1) | copy-start | bytes 1572868
  77.9 25.9 %collective-permute-start.14 = (bf16[2,512,256]{2,1,0:T(8,128)(2,1)S(1)}, bf16[2,512,256]{2,1,0:T(8,128)(2,1)S(1)}, u32[]{:S(2)}, u32[]{:S(2)}) collective-permute-start(bf16[2,512,256]{2,1,0:T(8,128)(2,1)S(1)} %get-tuple-element.36), channel_id=1, source_target_pairs={{0,1},{1,2},{2,3},{3,0},{4,5},{5,6},{6,7},{7,4},{8,9},{9,10},{10,1... | collective-permute-start | bytes 1572872 | tf_op jit(solution)/shard_map/ppermute | solution.py:411
  80.2 23.6 %collective-permute-start.15 = (bf16[2,512,256]{2,1,0:T(8,128)(2,1)S(1)}, bf16[2,512,256]{2,1,0:T(8,128)(2,1)S(1)}, u32[]{:S(2)}, u32[]{:S(2)}) collective-permute-start(bf16[2,512,256]{2,1,0:T(8,128)(2,1)S(1)} %get-tuple-element.37), channel_id=1, source_target_pairs={{0,2},{1,3},{2,0},{3,1},{4,6},{5,7},{6,4},{7,5},{8,10},{9,11},{10,... | collective-permute-start | bytes 1572872 | tf_op jit(solution)/shard_map/ppermute | solution.py:411
  82.1 21.7 %collective-permute-start.16 = (bf16[2,512,256]{2,1,0:T(8,128)(2,1)S(1)}, bf16[2,512,256]{2,1,0:T(8,128)(2,1)S(1)}, u32[]{:S(2)}, u32[]{:S(2)}) collective-permute-start(bf16[2,512,256]{2,1,0:T(8,128)(2,1)S(1)} %get-tuple-element.38), channel_id=1, source_target_pairs={{0,3},{1,0},{2,1},{3,2},{4,7},{5,4},{6,5},{7,6},{8,11},{9,8},{10,9... | collective-permute-start | bytes 1572872 | tf_op jit(solution)/shard_map/ppermute | solution.py:411
  93.5 10.2 %collective-permute-start.13 = (bf16[512,256]{1,0:T(8,128)(2,1)S(1)}, bf16[512,256]{1,0:T(8,128)(2,1)S(1)}, u32[]{:S(2)}, u32[]{:S(2)}) collective-permute-start(bf16[512,256]{1,0:T(8,128)(2,1)S(1)} %get-tuple-element.34), channel_id=1, source_target_pairs={{0,1},{1,2},{2,3},{3,0},{4,5},{5,6},{6,7},{7,4},{8,9},{9,10},{10,1... | collective-permute-start | bytes 786440 | tf_op jit(solution)/shard_map/ppermute | solution.py:417
  93.6 19.2 %collective-permute-start.18 = (bf16[512,256]{1,0:T(8,128)(2,1)S(1)}, bf16[512,256]{1,0:T(8,128)(2,1)S(1)}, u32[]{:S(2)}, u32[]{:S(2)}) collective-permute-start(bf16[512,256]{1,0:T(8,128)(2,1)S(1)} %get-tuple-element.42), channel_id=1, source_target_pairs={{0,2},{1,3},{2,0},{3,1},{4,6},{5,7},{6,4},{7,5},{8,10},{9,11},{10,... | collective-permute-start | bytes 786440 | tf_op jit(solution)/shard_map/ppermute | solution.py:417
  103.8 9.1 %collective-permute-start.19 = (bf16[512,256]{1,0:T(8,128)(2,1)S(1)}, bf16[512,256]{1,0:T(8,128)(2,1)S(1)}, u32[]{:S(2)}, u32[]{:S(2)}) collective-permute-start(bf16[512,256]{1,0:T(8,128)(2,1)S(1)} %get-tuple-element.43), channel_id=1, source_target_pairs={{0,3},{1,0},{2,1},{3,2},{4,7},{5,4},{6,5},{7,6},{8,11},{9,8},{10,9... | collective-permute-start | bytes 786440 | tf_op jit(solution)/shard_map/ppermute | solution.py:417
  104.6 12.3 %collective-permute-start.17 = (bf16[512,256]{1,0:T(8,128)(2,1)S(1)}, bf16[512,256]{1,0:T(8,128)(2,1)S(1)}, u32[]{:S(2)}, u32[]{:S(2)}) collective-permute-start(bf16[512,256]{1,0:T(8,128)(2,1)S(1)} %get-tuple-element.40), channel_id=1, source_target_pairs={{0,4},{1,5},{2,6},{3,7},{4,0},{5,1},{6,2},{7,3},{8,12},{9,13},{10,... | collective-permute-start | bytes 786440 | tf_op jit(solution)/shard_map/ppermute | solution.py:421
  117.6 9.2 %collective-permute-start.20 = (f32[512,256]{1,0:T(8,128)S(1)}, f32[512,256]{1,0:T(8,128)S(1)}, u32[]{:S(2)}, u32[]{:S(2)}) collective-permute-start(f32[512,256]{1,0:T(8,128)S(1)} %get-tuple-element.45.other_ref), channel_id=1, source_target_pairs={{0,8},{8,0},{16,24},{24,16},{32,40},{40,32},{48,56},{56,48},{64,72... | collective-permute-start | bytes 1572872 | tf_op jit(solution)/shard_map/ppermute | solution.py:425
  129.1 1.9 %collective-permute-start.21 = (bf16[512,512]{1,0:T(8,128)(2,1)S(1)}, bf16[512,512]{1,0:T(8,128)(2,1)S(1)}, u32[]{:S(2)}, u32[]{:S(2)}) collective-permute-start(bf16[512,512]{1,0:T(8,128)(2,1)S(1)} %get-tuple-element.47.slope_ref), channel_id=1, source_target_pairs={{0,8},{8,0},{16,24},{24,16},{32,40},{40,32},{48,56},{56,48},{64,72... | collective-permute-start | bytes 1572872 | tf_op jit(solution)/shard_map/ppermute | solution.py:432
  167.0 4.9 %collective-permute-start.22 = (bf16[256,512]{1,0:T(8,128)(2,1)S(1)}, bf16[256,512]{1,0:T(8,128)(2,1)S(1)}, u32[]{:S(2)}, u32[]{:S(2)}) collective-permute-start(bf16[256,512]{1,0:T(8,128)(2,1)S(1)} %bitcast.49), channel_id=1, source_target_pairs={{0,8},{8,0},{16,24},{24,16},{32,40},{40,32},{48,56},{56,48},{64,72... | collective-permute-start | bytes 786440 | tf_op jit(solution)/shard_map/ppermute | solution.py:443

commit v7 on v6

--- a/solution.py
+++ b/solution.py
@@ -13,7 +13,8 @@
 PER_PEER = 4
 HALF = 256
 CHIPS = 8
-BLOCKS = CHIPS + 1
+SHARED = 4
+BLOCKS = 2 * CHIPS - SHARED
 SLOT_CAP = 192
 ROW_TILES = 32
 GROUP_BITS = 2
@@ -166,14 +167,22 @@
     blocks, (keep_ref, send_ref, source) = refs[:BLOCKS], refs[BLOCKS : BLOCKS + 3]
     total, sems = refs[BLOCKS + 3 :]
     yh = meta_ref[2]
-    copies = [
-        pltpu.make_async_copy(blocks[k], source.at[meta_ref[4 + k]], sems.at[k])
-        for k in range(BLOCKS)
-    ]
-    for copy in copies:
-        copy.start()
-    for copy in copies:
-        copy.wait()
+    core = meta_ref[0]
+
+    def fetch(block, k):
+        return pltpu.make_async_copy(block, source.at[meta_ref[4 + k]], sems.at[k])
+
+    for k in range(SHARED):
+        fetch(blocks[k], k).start()
+    for c in range(2):
+
+        @pl.when(core == c)
+        def _():
+            for k in range(SHARED, CHIPS):
+                fetch(blocks[k + c * (CHIPS - SHARED)], k).start()
+
+    for k in range(CHIPS):
+        fetch(blocks[k], k).wait()
     add_tiles(plan_ref, tiles, source, total)
     for out, to in ((send_ref, 1 - yh), (keep_ref, yh)):
         for x in range(4):
@@ -335,13 +344,12 @@
     places = [
         near[0],
         jnp.where(first, near[1], far[0]),
-        near[3],
-        near[2],
         jnp.where(first, far[0], near[1]),
         far[1],
-        jnp.where(first, far[3], CHIPS),
+        jnp.where(first, near[3], far[3]),
+        jnp.where(first, near[2], near[3]),
+        jnp.where(first, far[3], near[2]),
         far[2],
-        jnp.where(first, CHIPS, far[3]),
     ]
     meta = jnp.stack([core, x, yh, z] + places).astype(jnp.int32)
 
@@ -382,25 +390,29 @@
         return lax.ppermute(block, "row", row_moves(move))
 
     r1 = hop(own, (0, 1), (1, 0))
-    r2 = hop(own, (0, 3), (0, 3))
-    r3 = hop(own, (0, 2), (0, 2))
+    r2 = hop(own, (0, 3), None)
+    r3 = hop(own, (0, 2), None)
     r4 = hop(own, (1, 0), (0, 1))
     s1 = hop(r1, (1, 0), (0, 1))
     s2 = hop(r2, (1, 0), None)
-    s3 = hop(r3, (1, 0), (1, 0))
-    s4 = hop(r1, None, (0, 3))
+    s3 = hop(r3, (1, 0), None)
+    later = after(own, r1)
+    t1 = hop(r1, None, (0, 3))
+    t2 = hop(later, None, (0, 3))
+    t3 = hop(later, None, (0, 2))
+    t4 = hop(r1, None, (0, 2))
     blocks = [
         b.reshape(2, N_ROW, N_COL * PER_PEER, HALF)
-        for b in (own, r1, r2, r3, r4, s1, s2, s3, s4)
+        for b in (own, r1, r4, s1, r2, r3, s2, s3, t1, t2, t3, t4)
     ]
 
     total = pltpu.VMEM((ROW_TILES, TILE, HALF), F32)
-    source = held(BLOCKS, 2, N_ROW, N_COL * PER_PEER, HALF)
+    source = held(CHIPS, 2, N_ROW, N_COL * PER_PEER, HALF)
     keep1, send1, source = call(
         tiles_y_kernel,
         [smem, smem, vmem] + [hbm] * BLOCKS,
         [held(4, SLOTS, HALF), held(4, SLOTS, HALF), source],
-        [total, pltpu.SemaphoreType.DMA((BLOCKS,))],
+        [total, pltpu.SemaphoreType.DMA((CHIPS,))],
     )(meta, plans[1], tiles1, *blocks)
     row0 = call(
         tiles_x_kernel,
@@ -408,13 +420,13 @@
         [held(2, SLOTS, HALF)] * 4,
         [total],
     )(meta, plans[0], tiles0, source)
-    got0 = [lax.ppermute(row0[k], "col", x_moves(k)) for k in (1, 2, 3)]
+    got0 = [lax.ppermute(row0[k], "col", x_moves(k)) for k in (1, 3, 2)]
     got1 = lax.ppermute(send1, "col", y_moves())
     wide, narrow = held(SLOTS, HALF, dtype=F32), held(SLOTS, HALF)
     keep1, *send1 = call(y_summed_kernel, [smem] + [vmem] * 2, [wide] + [narrow] * 3)(
         meta, keep1, got1
     )
-    got1 = [lax.ppermute(send1[k - 1], "col", x_moves(k)) for k in (1, 2, 3)]
+    got1 = [lax.ppermute(send1[k - 1], "col", x_moves(k)) for k in (1, 3, 2)]
     keep0, send0 = call(x_summed_kernel, [smem] + [vmem] * 4, [wide, narrow])(
         meta, after(row0[0], got1[0]), *got0
     )

time: 175 us -> 171 us (0.977); the launches traced: 173 us -> 171 us
  starting transfers between devices: 50.9 us -> 44.8 us
  waiting for transfers between devices: 58 us -> 62 us
  blocking collectives: 35 us -> 32.3 us
  Pallas kernels: 23.1 us -> 25.2 us
    ppermute x6, waiting for transfers between devices: 8.69 us -> 18.1 us  [the longest x3 18.1 us: shards(): got1 = [lax.ppermute(send1[k - 1], 'col', x_moves(k)) for k in (1, 3, 2)]]
    ppermute x1, starting transfers between devices: 8.22 us -> 0.15 us  [shards(): got0 = lax.ppermute(send0, 'col', y_moves())]
    ppermute x8 -> x11, starting transfers between devices: 15.2 us -> 22.1 us  [hop(): return lax.ppermute(block, 'row', row_moves(move))]
    ppermute x1, starting transfers between devices: 7.65 us -> 1.63 us  [shards(): theirs = lax.ppermute(others, 'row', swap)]
    ppermute x8 -> x11, waiting for transfers between devices: 21.7 us -> 16 us  [hop(): return lax.ppermute(block, 'row', row_moves(move))]
    ppermute x1, waiting for transfers between devices: 10 us -> 13.8 us  [shards(): got1 = lax.ppermute(send1, 'col', y_moves())]
    ppermute x1, waiting for transfers between devices: 4.05 us -> 0.55 us  [shards(): got0 = lax.ppermute(send0, 'col', y_moves())]
    all_to_all x3, blocking collectives: 35 us -> 32.3 us  [exchange(): lax.all_to_all(parts, axis, split_axis=0, concat_axis=0, axis_index_group...]
  transfers between devices with their start and end apart: 24 -> 27, of which waited for: 11 -> 14; matrix products, arithmetic and copies ran while one was open for 1% -> 1% of each run, Pallas kernels for 6% -> 8%
where the time goes in v7:
time: 171 us
  waiting for transfers between devices  62 us (36%)
  starting transfers between devices  44.8 us (26%)
  blocking collectives  32.3 us (19%)
  Pallas kernels  25.2 us (15%)
  local copies, waits for them, and re-layouts  4.07 us (2%)
    all_to_all x3, blocking collectives, exchange(): lax.all_to_all(parts, axis, split_axis=0, concat_axis=0, axis_index_group...  32.3 us
    pallas_call x11, Pallas kernels, run(): return made(*held)  25.2 us
    ppermute x11, starting transfers between devices, hop(): return lax.ppermute(block, 'row', row_moves(move))  22.1 us
    ppermute x3, waiting for transfers between devices, shards(): got1 = [lax.ppermute(send1[k - 1], 'col', x_moves(k)) for k in (1, 3, 2)]  18.1 us
    ppermute x11, waiting for transfers between devices, hop(): return lax.ppermute(block, 'row', row_moves(move))  16 us
    ppermute x1, waiting for transfers between devices, shards(): got1 = lax.ppermute(send1, 'col', y_moves())  13.8 us
    all_to_all x1, waiting for transfers between devices, shards(): lax.all_to_all(grouped, 'col', split_axis=0, concat_axis=0, tiled=True)  8.84 us
    all_to_all x1, starting transfers between devices, shards(): lax.all_to_all(grouped, 'col', split_axis=0, concat_axis=0, tiled=True)  6.73 us
  transfers between devices with their start and end apart: 27, of which 14 were waited for; matrix products, arithmetic and copies ran while one was open for 1% of the time, Pallas kernels for 8%

profile of v7, /device:TPU:1, one launch (start us, length us, event | category | flops | bytes accessed | tf_op | source)
XLA Modules:
  0.0 171.3 jit_solution(6475208767209092092)
XLA Ops:
  0.6 1.5 collective-permute-start.2
  2.1 0.1 collective-permute-start.1
  2.2 0.1 stack.51.meta_ref
  2.3 1.6 collective-permute-done.1.other_part_ref
  3.9 0.7 copy-done.3
  4.6 3.0 %shard_map.96 = bf16[8,2,64,256]{3,2,1,0:T(8,128)(2,1)} custom-call(s32[12]{0:T(128)S(1)} %stack.51.meta_ref, s32[1,512]{1,0:T(1,128)S(1)} %bitcast.47, bf16[512,512]{1,0:T(8,128)(2,1)} %features_hbm.1, s32[1,512]{1,0:T(1,128)S(1)} %collective-permute-done.1.other_part_ref, bf16[512,512]{1,0:T(8,128)(2,1)S(1)} %collective-permute-done.2.other_ref), custom_call_target="tpu_custom_call" | custom-call | tf_op jit(solution)/shard_map/pallas_call | solution.py:311
  7.6 0.5 collective-permute-start.3
  8.0 6.7 %all-to-all-start = ((bf16[8,2,64,256]{3,2,1,0:T(8,128)(2,1)}), bf16[8,2,64,256]{3,2,1,0:T(8,128)(2,1)S(1)}, u32[]{:S(2)}, u32[]{:S(2)}) async-start(bf16[8,2,64,256]{3,2,1,0:T(8,128)(2,1)} %shard_map.96), calls=%async_computation | async-start | bytes 1048576 | tf_op jit(solution)/shard_map/all_to_all | solution.py:373
  15.4 0.0 copy-start.4
  15.4 0.7 copy-done.4
  16.1 0.7 copy-done.5
  16.8 0.5 shard_map.95
  17.3 0.5 collective-permute-start
  17.7 8.8 %all-to-all-done.arrived_ref = bf16[8,2,64,256]{3,2,1,0:T(8,128)(2,1)S(1)} async-done(((bf16[8,2,64,256]{3,2,1,0:T(8,128)(2,1)}), bf16[8,2,64,256]{3,2,1,0:T(8,128)(2,1)S(1)}, u32[]{:S(2)}, u32[]{:S(2)}) %all-to-all-start) | async-done | bytes 524320 | tf_op jit(solution)/shard_map/all_to_all | solution.py:373
  26.6 0.4 shard_map.97
  27.0 0.5 collective-permute-start.4
  27.5 0.7 collective-permute-start.7
  28.2 1.7 collective-permute-start.5
  29.9 0.7 collective-permute-start.8
  30.6 4.8 %collective-permute-done.4 = bf16[2,512,256]{2,1,0:T(8,128)(2,1)S(1)} collective-permute-done((bf16[2,512,256]{2,1,0:T(8,128)(2,1)S(1)}, bf16[2,512,256]{2,1,0:T(8,128)(2,1)S(1)}, u32[]{:S(2)}, u32[]{:S(2)}) %collective-permute-start.4) | collective-permute-done | bytes 524320 | tf_op jit(solution)/shard_map/ppermute | solution.py:390
  35.4 2.0 %collective-permute-start.6 = (bf16[2,512,256]{2,1,0:T(8,128)(2,1)S(1)}, bf16[2,512,256]{2,1,0:T(8,128)(2,1)S(1)}, u32[]{:S(2)}, u32[]{:S(2)}) collective-permute-start(bf16[2,512,256]{2,1,0:T(8,128)(2,1)S(1)} %collective-permute-done.4), channel_id=1, source_target_pairs={{0,64},{8,24},{16,80},{24,40},{32,96},{40,56},{48,112},{56,8},{64,... | collective-permute-start | bytes 1572872 | tf_op jit(solution)/shard_map/ppermute | solution.py:390
  37.4 0.7 collective-permute-start.9
  38.1 4.0 %collective-permute-start.12 = (bf16[2,512,256]{2,1,0:T(8,128)(2,1)S(1)}, bf16[2,512,256]{2,1,0:T(8,128)(2,1)}, u32[]{:S(2)}, u32[]{:S(2)}) collective-permute-start(bf16[2,512,256]{2,1,0:T(8,128)(2,1)S(1)} %shard_map.97), channel_id=1, source_target_pairs={{8,56},{24,8},{40,24},{56,40},{72,120},{88,72},{104,88},{120,104},... | collective-permute-start | bytes 1572872 | tf_op jit(solution)/shard_map/ppermute | solution.py:390
  42.1 2.0 %collective-permute-done.5 = bf16[2,512,256]{2,1,0:T(8,128)(2,1)S(1)} collective-permute-done((bf16[2,512,256]{2,1,0:T(8,128)(2,1)S(1)}, bf16[2,512,256]{2,1,0:T(8,128)(2,1)S(1)}, u32[]{:S(2)}, u32[]{:S(2)}) %collective-permute-start.5) | collective-permute-done | bytes 524320 | tf_op jit(solution)/shard_map/ppermute | solution.py:390
  44.1 3.7 %collective-permute-start.11 = (bf16[2,512,256]{2,1,0:T(8,128)(2,1)S(1)}, bf16[2,512,256]{2,1,0:T(8,128)(2,1)}, u32[]{:S(2)}, u32[]{:S(2)}) collective-permute-start(bf16[2,512,256]{2,1,0:T(8,128)(2,1)S(1)} %collective-permute-done.4), channel_id=1, source_target_pairs={{8,56},{24,8},{40,24},{56,40},{72,120},{88,72},{104,88},{120,104},... | collective-permute-start | bytes 1572872 | tf_op jit(solution)/shard_map/ppermute | solution.py:390
  47.8 1.5 collective-permute-start.10
  49.2 4.8 %collective-permute-done.6 = bf16[2,512,256]{2,1,0:T(8,128)(2,1)S(1)} collective-permute-done((bf16[2,512,256]{2,1,0:T(8,128)(2,1)S(1)}, bf16[2,512,256]{2,1,0:T(8,128)(2,1)S(1)}, u32[]{:S(2)}, u32[]{:S(2)}) %collective-permute-start.6) | collective-permute-done | bytes 524320 | tf_op jit(solution)/shard_map/ppermute | solution.py:390
  54.1 4.9 %collective-permute-start.13 = (bf16[2,512,256]{2,1,0:T(8,128)(2,1)S(1)}, bf16[2,512,256]{2,1,0:T(8,128)(2,1)}, u32[]{:S(2)}, u32[]{:S(2)}) collective-permute-start(bf16[2,512,256]{2,1,0:T(8,128)(2,1)S(1)} %shard_map.97), channel_id=1, source_target_pairs={{8,40},{24,56},{40,8},{56,24},{72,104},{88,120},{104,72},{120,88},... | collective-permute-start | bytes 1572872 | tf_op jit(solution)/shard_map/ppermute | solution.py:390
  59.0 0.8 copy-done.1
  59.7 1.9 %collective-permute-start.14 = (bf16[2,512,256]{2,1,0:T(8,128)(2,1)S(1)}, bf16[2,512,256]{2,1,0:T(8,128)(2,1)}, u32[]{:S(2)}, u32[]{:S(2)}) collective-permute-start(bf16[2,512,256]{2,1,0:T(8,128)(2,1)S(1)} %collective-permute-done.4), channel_id=1, source_target_pairs={{8,40},{24,56},{40,8},{56,24},{72,104},{88,120},{104,72},{120,88},... | collective-permute-start | bytes 1572872 | tf_op jit(solution)/shard_map/ppermute | solution.py:390
  61.7 5.2 %shard_map.98 = (bf16[193,128,128]{2,1,0:T(8,128)(2,1)S(1)}, bf16[193,128,128]{2,1,0:T(8,128)(2,1)S(1)}) custom-call(s32[12]{0:T(128)S(1)} %stack.51.meta_ref, bf16[192,128,128]{2,1,0:T(8,128)(2,1)} %bitcast.51, bf16[192,128,128]{2,1,0:T(8,128)(2,1)} %collective-permute-done.3.other_hbm), custom_call_target="tpu_custom_call" | custom-call | tf_op jit(solution)/shard_map/pallas_call | solution.py:311
  66.9 4.4 %collective-permute-done.14 = bf16[2,512,256]{2,1,0:T(8,128)(2,1)} collective-permute-done((bf16[2,512,256]{2,1,0:T(8,128)(2,1)S(1)}, bf16[2,512,256]{2,1,0:T(8,128)(2,1)}, u32[]{:S(2)}, u32[]{:S(2)}) %collective-permute-start.14) | collective-permute-done | bytes 524320 | tf_op jit(solution)/shard_map/ppermute | solution.py:390
  71.3 5.4 %shard_map.99 = (bf16[4,512,256]{2,1,0:T(8,128)(2,1)S(1)}, bf16[4,512,256]{2,1,0:T(8,128)(2,1)S(1)}, bf16[8,2,16,32,256]{4,3,2,1,0:T(8,128)(2,1)S(1)}) custom-call(s32[12]{0:T(128)S(1)} %stack.51.meta_ref, s32[8,288]{1,0:T(8,128)S(1)} %get-tuple-element.52.plan_ref, bf16[193,128,128]{2,1,0:T(8,128)(2,1)S(1)} %get-tuple-element.30.tiles, ...), custom_call_target="tpu_custom_call" | custom-call | tf_op jit(solution)/shard_map/pallas_call | solution.py:311
  76.7 2.2 %collective-permute-start.15 = (bf16[4,512,256]{2,1,0:T(8,128)(2,1)S(1)}, bf16[4,512,256]{2,1,0:T(8,128)(2,1)S(1)}, u32[]{:S(2)}, u32[]{:S(2)}) collective-permute-start(bf16[4,512,256]{2,1,0:T(8,128)(2,1)S(1)} %get-tuple-element.35), channel_id=1, source_target_pairs={{0,4},{1,5},{2,6},{3,7},{4,0},{5,1},{6,2},{7,3},{8,12},{9,13},{10,... | collective-permute-start | bytes 3145736 | tf_op jit(solution)/shard_map/ppermute | solution.py:424
  78.9 5.3 %shard_map.100 = (bf16[2,512,256]{2,1,0:T(8,128)(2,1)S(1)}, bf16[2,512,256]{2,1,0:T(8,128)(2,1)S(1)}, bf16[2,512,256]{2,1,0:T(8,128)(2,1)S(1)}, bf16[2,512,256]{2,1,0:T(8,128)(2,1)S(1)}) custom-call(s32[12]{0:T(128)S(1)} %stack.51.meta_ref, s32[8,288]{1,0:T(8,128)S(1)} %get-tuple-element.53.plan_ref, bf16[193,128,128]{2,1,0:T(8,128)(2,1)S(1)} %get-tuple-element.29.tiles, ...), custom_call_target="tpu_custom_call" | custom-call | tf_op jit(solution)/shard_map/pallas_call | solution.py:311
  84.2 0.1 collective-permute-start.17
  84.3 2.7 %collective-permute-start.18 = (bf16[2,512,256]{2,1,0:T(8,128)(2,1)S(1)}, bf16[2,512,256]{2,1,0:T(8,128)(2,1)S(1)}, u32[]{:S(2)}, u32[]{:S(2)}) collective-permute-start(bf16[2,512,256]{2,1,0:T(8,128)(2,1)S(1)} %get-tuple-element.39), channel_id=1, source_target_pairs={{0,3},{1,0},{2,1},{3,2},{4,7},{5,4},{6,5},{7,6},{8,11},{9,8},{10,9... | collective-permute-start | bytes 1572872 | tf_op jit(solution)/shard_map/ppermute | solution.py:423
  87.0 13.8 %collective-permute-done.15.got_ref = bf16[4,512,256]{2,1,0:T(8,128)(2,1)S(1)} collective-permute-done((bf16[4,512,256]{2,1,0:T(8,128)(2,1)S(1)}, bf16[4,512,256]{2,1,0:T(8,128)(2,1)S(1)}, u32[]{:S(2)}, u32[]{:S(2)}) %collective-permute-start.15) | collective-permute-done | bytes 1048608 | tf_op jit(solution)/shard_map/ppermute | solution.py:424
  100.8 0.8 shard_map.101
  101.6 0.1 collective-permute-start.16
  101.7 2.7 %collective-permute-start.21 = (bf16[512,256]{1,0:T(8,128)(2,1)S(1)}, bf16[512,256]{1,0:T(8,128)(2,1)S(1)}, u32[]{:S(2)}, u32[]{:S(2)}) collective-permute-start(bf16[512,256]{1,0:T(8,128)(2,1)S(1)} %get-tuple-element.44), channel_id=1, source_target_pairs={{0,3},{1,0},{2,1},{3,2},{4,7},{5,4},{6,5},{7,6},{8,11},{9,8},{10,9... | collective-permute-start | bytes 786440 | tf_op jit(solution)/shard_map/ppermute | solution.py:429
  104.4 10.0 %collective-permute-done.16.a_ref = bf16[512,256]{1,0:T(8,128)(2,1)S(1)} collective-permute-done((bf16[512,256]{1,0:T(8,128)(2,1)S(1)}, bf16[512,256]{1,0:T(8,128)(2,1)S(1)}, u32[]{:S(2)}, u32[]{:S(2)}) %collective-permute-start.16) | collective-permute-done | bytes 262176 | tf_op jit(solution)/shard_map/ppermute | solution.py:429
  114.4 0.2 collective-permute-start.22
  114.6 0.8 shard_map.102
  115.4 0.2 collective-permute-start.20
  115.6 4.2 %collective-permute-done.21.b_ref = bf16[512,256]{1,0:T(8,128)(2,1)S(1)} collective-permute-done((bf16[512,256]{1,0:T(8,128)(2,1)S(1)}, bf16[512,256]{1,0:T(8,128)(2,1)S(1)}, u32[]{:S(2)}, u32[]{:S(2)}) %collective-permute-start.21) | collective-permute-done | bytes 262176 | tf_op jit(solution)/shard_map/ppermute | solution.py:429
  119.8 3.8 %collective-permute-done.22.c_ref = bf16[512,256]{1,0:T(8,128)(2,1)S(1)} collective-permute-done((bf16[512,256]{1,0:T(8,128)(2,1)S(1)}, bf16[512,256]{1,0:T(8,128)(2,1)S(1)}, u32[]{:S(2)}, u32[]{:S(2)}) %collective-permute-start.22) | collective-permute-done | bytes 262176 | tf_op jit(solution)/shard_map/ppermute | solution.py:429
  123.6 0.6 collective-permute-done.20.got0
  124.2 0.7 shard_map.103
  124.9 1.6 collective-permute-start.23
  126.6 1.1 constant_dynamic-slice_fusion.cotangent_ref
  127.7 0.5 collective-permute-done.23.got_ref
  128.1 2.3 %shard_map.104 = (bf16[512,512]{1,0:T(8,128)(2,1)}, bf16[512,512]{1,0:T(8,128)(2,1)S(1)}) custom-call(s32[12]{0:T(128)S(1)} %stack.51.meta_ref, f32[512,256]{1,0:T(8,128)S(1)} %get-tuple-element.46.mine_ref, f32[512,256]{1,0:T(8,128)S(1)} %collective-permute-done.23.got_ref, bf16[512,512]{1,0:T(8,128)(2,1)S(1)} %copy-done, ...), custom_call_target="tpu_custom_call" | custom-call | tf_op jit(solution)/shard_map/pallas_call | solution.py:311
  130.4 0.4 collective-permute-start.24
  130.8 1.5 collective-permute-done.24.other_slope_ref
  132.3 0.7 shard_map.105
  133.1 8.5 %all_to_all.20 = bf16[8,32,512]{2,1,0:T(8,128)(2,1)S(1)} all-to-all(bf16[8,32,512]{2,1,0:T(8,128)(2,1)S(1)} %bitcast.39), channel_id=1, replica_groups={{0,16,32,48,64,80,96,112},{8,24,40,56,72,88,104,120},{1,17,33,49,65,81,..., dimensions={0} | all-to-all | bytes 524288 | tf_op jit(solution)/shard_map/all_to_all | solution.py:283
  141.7 0.1 broadcast_in_dim.6
  141.8 12.9 %all_to_all.21 = f32[8,32,512]{2,1,0:T(8,128)S(1)} all-to-all(f32[8,32,512]{2,1,0:T(8,128)S(1)} %broadcast_in_dim.6), channel_id=1, replica_groups=mesh['row'=16,'col'=8] {'col'}, dimensions={0} | all-to-all | bytes 1048576 | tf_op jit(solution)/shard_map/all_to_all | solution.py:283
  154.7 10.9 %all_to_all.22 = bf16[8,32,512]{2,1,0:T(8,128)(2,1)S(1)} all-to-all(bf16[8,32,512]{2,1,0:T(8,128)(2,1)S(1)} %broadcast_in_dim.7), channel_id=1, replica_groups={{0,16,32,48,64,80,96,112},{8,24,40,56,72,88,104,120},{1,17,33,49,65,81,..., dimensions={0} | all-to-all | bytes 524288 | tf_op jit(solution)/shard_map/all_to_all | solution.py:283
  165.6 3.3 %collective-permute-start.25 = (bf16[256,512]{1,0:T(8,128)(2,1)S(1)}, bf16[256,512]{1,0:T(8,128)(2,1)S(1)}, u32[]{:S(2)}, u32[]{:S(2)}) collective-permute-start(bf16[256,512]{1,0:T(8,128)(2,1)S(1)} %bitcast.52), channel_id=1, source_target_pairs={{0,8},{8,0},{16,24},{24,16},{32,40},{40,32},{48,56},{56,48},{64,72... | collective-permute-start | bytes 786440 | tf_op jit(solution)/shard_map/ppermute | solution.py:455
  168.9 1.2 collective-permute-done.25
  170.1 0.1 broadcast_select_fusion.1
  170.2 1.1 maximum_convert_fusion
  (26 shorter events, 0.2 us)
Async XLA Ops:
  0.6 3.3 %collective-permute-start.2 = (bf16[512,512]{1,0:T(8,128)(2,1)}, bf16[512,512]{1,0:T(8,128)(2,1)S(1)}, u32[]{:S(2)}, u32[]{:S(2)}) collective-permute-start(bf16[512,512]{1,0:T(8,128)(2,1)} %features_hbm.1), channel_id=1, source_target_pairs={{0,8},{8,0},{16,24},{24,16},{32,40},{40,32},{48,56},{56,48},{64,72... | collective-permute-start | bytes 1572872 | tf_op jit(solution)/shard_map/ppermute | solution.py:360
  2.1 1.8 %collective-permute-start.1 = (s32[1,512]{1,0:T(1,128)}, s32[1,512]{1,0:T(1,128)S(1)}, u32[]{:S(2)}, u32[]{:S(2)}) collective-permute-start(s32[1,512]{1,0:T(1,128)} %bitcast.46), channel_id=1, source_target_pairs={{0,8},{8,0},{16,24},{24,16},{32,40},{40,32},{48,56},{56,48},{64,72... | collective-permute-start | bytes 6152 | tf_op jit(solution)/shard_map/ppermute | solution.py:359
  3.9 0.7 copy-start.3
  7.6 19.4 %collective-permute-start.3 = (bf16[192,128,128]{2,1,0:T(8,128)(2,1)}, bf16[192,128,128]{2,1,0:T(8,128)(2,1)}, u32[]{:S(2)}, u32[]{:S(2)}) collective-permute-start(bf16[192,128,128]{2,1,0:T(8,128)(2,1)} %bitcast.50), channel_id=1, source_target_pairs={{0,8},{8,0},{16,24},{24,16},{32,40},{40,32},{48,56},{56,48},{64,72... | collective-permute-start | bytes 18874376 | tf_op jit(solution)/shard_map/ppermute | solution.py:372
  8.0 18.5 %all-to-all-start = ((bf16[8,2,64,256]{3,2,1,0:T(8,128)(2,1)}), bf16[8,2,64,256]{3,2,1,0:T(8,128)(2,1)S(1)}, u32[]{:S(2)}, u32[]{:S(2)}) async-start(bf16[8,2,64,256]{3,2,1,0:T(8,128)(2,1)} %shard_map.96), calls=%async_computation | async-start | bytes 1048576 | tf_op jit(solution)/shard_map/all_to_all | solution.py:373
  15.4 0.7 copy-start.4
  16.1 0.7 copy-start.5
  17.3 9.8 %collective-permute-start = (s32[8,288]{1,0:T(8,128)S(1)}, s32[8,288]{1,0:T(8,128)S(1)}, u32[]{:S(2)}, u32[]{:S(2)}) collective-permute-start(s32[8,288]{1,0:T(8,128)S(1)} %shard_map.95), channel_id=1, source_target_pairs={{0,8},{8,0},{16,24},{24,16},{32,40},{40,32},{48,56},{56,48},{64,72... | collective-permute-start | bytes 27656 | tf_op jit(solution)/shard_map/ppermute | solution.py:364
  27.0 8.4 %collective-permute-start.4 = (bf16[2,512,256]{2,1,0:T(8,128)(2,1)S(1)}, bf16[2,512,256]{2,1,0:T(8,128)(2,1)S(1)}, u32[]{:S(2)}, u32[]{:S(2)}) collective-permute-start(bf16[2,512,256]{2,1,0:T(8,128)(2,1)S(1)} %shard_map.97), channel_id=1, source_target_pairs={{0,16},{8,72},{16,32},{24,88},{32,48},{40,104},{48,0},{56,120},{64... | collective-permute-start | bytes 1572872 | tf_op jit(solution)/shard_map/ppermute | solution.py:390
  27.5 9.9 %collective-permute-start.7 = (bf16[2,512,256]{2,1,0:T(8,128)(2,1)S(1)}, bf16[2,512,256]{2,1,0:T(8,128)(2,1)S(1)}, u32[]{:S(2)}, u32[]{:S(2)}) collective-permute-start(bf16[2,512,256]{2,1,0:T(8,128)(2,1)S(1)} %shard_map.97), channel_id=1, source_target_pairs={{0,48},{16,0},{32,16},{48,32},{64,112},{80,64},{96,80},{112,96},{1... | collective-permute-start | bytes 1572872 | tf_op jit(solution)/shard_map/ppermute | solution.py:390
  28.2 15.9 %collective-permute-start.5 = (bf16[2,512,256]{2,1,0:T(8,128)(2,1)S(1)}, bf16[2,512,256]{2,1,0:T(8,128)(2,1)S(1)}, u32[]{:S(2)}, u32[]{:S(2)}) collective-permute-start(bf16[2,512,256]{2,1,0:T(8,128)(2,1)S(1)} %shard_map.97), channel_id=1, source_target_pairs={{0,64},{8,24},{16,80},{24,40},{32,96},{40,56},{48,112},{56,8},{64,... | collective-permute-start | bytes 1572872 | tf_op jit(solution)/shard_map/ppermute | solution.py:390
  29.9 17.9 %collective-permute-start.8 = (bf16[2,512,256]{2,1,0:T(8,128)(2,1)S(1)}, bf16[2,512,256]{2,1,0:T(8,128)(2,1)S(1)}, u32[]{:S(2)}, u32[]{:S(2)}) collective-permute-start(bf16[2,512,256]{2,1,0:T(8,128)(2,1)S(1)} %shard_map.97), channel_id=1, source_target_pairs={{0,32},{16,48},{32,0},{48,16},{64,96},{80,112},{96,64},{112,80},{1... | collective-permute-start | bytes 1572872 | tf_op jit(solution)/shard_map/ppermute | solution.py:390
  35.4 18.6 %collective-permute-start.6 = (bf16[2,512,256]{2,1,0:T(8,128)(2,1)S(1)}, bf16[2,512,256]{2,1,0:T(8,128)(2,1)S(1)}, u32[]{:S(2)}, u32[]{:S(2)}) collective-permute-start(bf16[2,512,256]{2,1,0:T(8,128)(2,1)S(1)} %collective-permute-done.4), channel_id=1, source_target_pairs={{0,64},{8,24},{16,80},{24,40},{32,96},{40,56},{48,112},{56,8},{64,... | collective-permute-start | bytes 1572872 | tf_op jit(solution)/shard_map/ppermute | solution.py:390
  37.4 21.6 %collective-permute-start.9 = (bf16[2,512,256]{2,1,0:T(8,128)(2,1)S(1)}, bf16[2,512,256]{2,1,0:T(8,128)(2,1)S(1)}, u32[]{:S(2)}, u32[]{:S(2)}) collective-permute-start(bf16[2,512,256]{2,1,0:T(8,128)(2,1)S(1)} %collective-permute-done.7), channel_id=1, source_target_pairs={{0,64},{16,80},{32,96},{48,112},{64,0},{80,16},{96,32},{112,48},{1... | collective-permute-start | bytes 1572872 | tf_op jit(solution)/shard_map/ppermute | solution.py:390
  38.1 28.8 %collective-permute-start.12 = (bf16[2,512,256]{2,1,0:T(8,128)(2,1)S(1)}, bf16[2,512,256]{2,1,0:T(8,128)(2,1)}, u32[]{:S(2)}, u32[]{:S(2)}) collective-permute-start(bf16[2,512,256]{2,1,0:T(8,128)(2,1)S(1)} %shard_map.97), channel_id=1, source_target_pairs={{8,56},{24,8},{40,24},{56,40},{72,120},{88,72},{104,88},{120,104},... | collective-permute-start | bytes 1572872 | tf_op jit(solution)/shard_map/ppermute | solution.py:390
  44.1 22.8 %collective-permute-start.11 = (bf16[2,512,256]{2,1,0:T(8,128)(2,1)S(1)}, bf16[2,512,256]{2,1,0:T(8,128)(2,1)}, u32[]{:S(2)}, u32[]{:S(2)}) collective-permute-start(bf16[2,512,256]{2,1,0:T(8,128)(2,1)S(1)} %collective-permute-done.4), channel_id=1, source_target_pairs={{8,56},{24,8},{40,24},{56,40},{72,120},{88,72},{104,88},{120,104},... | collective-permute-start | bytes 1572872 | tf_op jit(solution)/shard_map/ppermute | solution.py:390
  47.8 19.1 %collective-permute-start.10 = (bf16[2,512,256]{2,1,0:T(8,128)(2,1)S(1)}, bf16[2,512,256]{2,1,0:T(8,128)(2,1)}, u32[]{:S(2)}, u32[]{:S(2)}) collective-permute-start(bf16[2,512,256]{2,1,0:T(8,128)(2,1)S(1)} %collective-permute-done.8), channel_id=1, source_target_pairs={{0,64},{16,80},{32,96},{48,112},{64,0},{80,16},{96,32},{112,48},{1... | collective-permute-start | bytes 1572872 | tf_op jit(solution)/shard_map/ppermute | solution.py:390
  54.1 12.8 %collective-permute-start.13 = (bf16[2,512,256]{2,1,0:T(8,128)(2,1)S(1)}, bf16[2,512,256]{2,1,0:T(8,128)(2,1)}, u32[]{:S(2)}, u32[]{:S(2)}) collective-permute-start(bf16[2,512,256]{2,1,0:T(8,128)(2,1)S(1)} %shard_map.97), channel_id=1, source_target_pairs={{8,40},{24,56},{40,8},{56,24},{72,104},{88,120},{104,72},{120,88},... | collective-permute-start | bytes 1572872 | tf_op jit(solution)/shard_map/ppermute | solution.py:390
  58.9 0.8 copy-start.1
  59.7 11.5 %collective-permute-start.14 = (bf16[2,512,256]{2,1,0:T(8,128)(2,1)S(1)}, bf16[2,512,256]{2,1,0:T(8,128)(2,1)}, u32[]{:S(2)}, u32[]{:S(2)}) collective-permute-start(bf16[2,512,256]{2,1,0:T(8,128)(2,1)S(1)} %collective-permute-done.4), channel_id=1, source_target_pairs={{8,40},{24,56},{40,8},{56,24},{72,104},{88,120},{104,72},{120,88},... | collective-permute-start | bytes 1572872 | tf_op jit(solution)/shard_map/ppermute | solution.py:390
  61.7 9.6 %copy-start.2 = (bf16[2,512,256]{2,1,0:T(8,128)(2,1)S(1)}, bf16[2,512,256]{2,1,0:T(8,128)(2,1)}, u32[]{:S(2)}) copy-start(bf16[2,512,256]{2,1,0:T(8,128)(2,1)} %copy-done.1) | copy-start | bytes 1572868
  76.7 24.1 %collective-permute-start.15 = (bf16[4,512,256]{2,1,0:T(8,128)(2,1)S(1)}, bf16[4,512,256]{2,1,0:T(8,128)(2,1)S(1)}, u32[]{:S(2)}, u32[]{:S(2)}) collective-permute-start(bf16[4,512,256]{2,1,0:T(8,128)(2,1)S(1)} %get-tuple-element.35), channel_id=1, source_target_pairs={{0,4},{1,5},{2,6},{3,7},{4,0},{5,1},{6,2},{7,3},{8,12},{9,13},{10,... | collective-permute-start | bytes 3145736 | tf_op jit(solution)/shard_map/ppermute | solution.py:424
  84.2 43.9 %copy-start = (bf16[512,512]{1,0:T(8,128)(2,1)S(1)}, bf16[512,512]{1,0:T(8,128)(2,1)}, u32[]{:S(2)}) copy-start(bf16[512,512]{1,0:T(8,128)(2,1)} %weight_ref.1) | copy-start | bytes 1572868
  84.2 30.4 %collective-permute-start.17 = (bf16[2,512,256]{2,1,0:T(8,128)(2,1)S(1)}, bf16[2,512,256]{2,1,0:T(8,128)(2,1)S(1)}, u32[]{:S(2)}, u32[]{:S(2)}) collective-permute-start(bf16[2,512,256]{2,1,0:T(8,128)(2,1)S(1)} %get-tuple-element.38), channel_id=1, source_target_pairs={{0,1},{1,2},{2,3},{3,0},{4,5},{5,6},{6,7},{7,4},{8,9},{9,10},{10,1... | collective-permute-start | bytes 1572872 | tf_op jit(solution)/shard_map/ppermute | solution.py:423
  84.3 30.3 %collective-permute-start.18 = (bf16[2,512,256]{2,1,0:T(8,128)(2,1)S(1)}, bf16[2,512,256]{2,1,0:T(8,128)(2,1)S(1)}, u32[]{:S(2)}, u32[]{:S(2)}) collective-permute-start(bf16[2,512,256]{2,1,0:T(8,128)(2,1)S(1)} %get-tuple-element.39), channel_id=1, source_target_pairs={{0,3},{1,0},{2,1},{3,2},{4,7},{5,4},{6,5},{7,6},{8,11},{9,8},{10,9... | collective-permute-start | bytes 1572872 | tf_op jit(solution)/shard_map/ppermute | solution.py:423
  87.0 27.6 %collective-permute-start.19 = (bf16[2,512,256]{2,1,0:T(8,128)(2,1)S(1)}, bf16[2,512,256]{2,1,0:T(8,128)(2,1)S(1)}, u32[]{:S(2)}, u32[]{:S(2)}) collective-permute-start(bf16[2,512,256]{2,1,0:T(8,128)(2,1)S(1)} %get-tuple-element.40), channel_id=1, source_target_pairs={{0,2},{1,3},{2,0},{3,1},{4,6},{5,7},{6,4},{7,5},{8,10},{9,11},{10,... | collective-permute-start | bytes 1572872 | tf_op jit(solution)/shard_map/ppermute | solution.py:423
  101.6 12.8 %collective-permute-start.16 = (bf16[512,256]{1,0:T(8,128)(2,1)S(1)}, bf16[512,256]{1,0:T(8,128)(2,1)S(1)}, u32[]{:S(2)}, u32[]{:S(2)}) collective-permute-start(bf16[512,256]{1,0:T(8,128)(2,1)S(1)} %get-tuple-element.36), channel_id=1, source_target_pairs={{0,1},{1,2},{2,3},{3,0},{4,5},{5,6},{6,7},{7,4},{8,9},{9,10},{10,1... | collective-permute-start | bytes 786440 | tf_op jit(solution)/shard_map/ppermute | solution.py:429
  101.7 18.1 %collective-permute-start.21 = (bf16[512,256]{1,0:T(8,128)(2,1)S(1)}, bf16[512,256]{1,0:T(8,128)(2,1)S(1)}, u32[]{:S(2)}, u32[]{:S(2)}) collective-permute-start(bf16[512,256]{1,0:T(8,128)(2,1)S(1)} %get-tuple-element.44), channel_id=1, source_target_pairs={{0,3},{1,0},{2,1},{3,2},{4,7},{5,4},{6,5},{7,6},{8,11},{9,8},{10,9... | collective-permute-start | bytes 786440 | tf_op jit(solution)/shard_map/ppermute | solution.py:429
  114.4 9.3 %collective-permute-start.22 = (bf16[512,256]{1,0:T(8,128)(2,1)S(1)}, bf16[512,256]{1,0:T(8,128)(2,1)S(1)}, u32[]{:S(2)}, u32[]{:S(2)}) collective-permute-start(bf16[512,256]{1,0:T(8,128)(2,1)S(1)} %get-tuple-element.45), channel_id=1, source_target_pairs={{0,2},{1,3},{2,0},{3,1},{4,6},{5,7},{6,4},{7,5},{8,10},{9,11},{10,... | collective-permute-start | bytes 786440 | tf_op jit(solution)/shard_map/ppermute | solution.py:429
  115.4 8.8 %collective-permute-start.20 = (bf16[512,256]{1,0:T(8,128)(2,1)S(1)}, bf16[512,256]{1,0:T(8,128)(2,1)S(1)}, u32[]{:S(2)}, u32[]{:S(2)}) collective-permute-start(bf16[512,256]{1,0:T(8,128)(2,1)S(1)} %get-tuple-element.42), channel_id=1, source_target_pairs={{0,4},{1,5},{2,6},{3,7},{4,0},{5,1},{6,2},{7,3},{8,12},{9,13},{10,... | collective-permute-start | bytes 786440 | tf_op jit(solution)/shard_map/ppermute | solution.py:433
  124.9 3.2 %collective-permute-start.23 = (f32[512,256]{1,0:T(8,128)S(1)}, f32[512,256]{1,0:T(8,128)S(1)}, u32[]{:S(2)}, u32[]{:S(2)}) collective-permute-start(f32[512,256]{1,0:T(8,128)S(1)} %get-tuple-element.47.other_ref), channel_id=1, source_target_pairs={{0,8},{8,0},{16,24},{24,16},{32,40},{40,32},{48,56},{56,48},{64,72... | collective-permute-start | bytes 1572872 | tf_op jit(solution)/shard_map/ppermute | solution.py:437
  130.4 1.9 %collective-permute-start.24 = (bf16[512,512]{1,0:T(8,128)(2,1)S(1)}, bf16[512,512]{1,0:T(8,128)(2,1)S(1)}, u32[]{:S(2)}, u32[]{:S(2)}) collective-permute-start(bf16[512,512]{1,0:T(8,128)(2,1)S(1)} %get-tuple-element.49.slope_ref), channel_id=1, source_target_pairs={{0,8},{8,0},{16,24},{24,16},{32,40},{40,32},{48,56},{56,48},{64,72... | collective-permute-start | bytes 1572872 | tf_op jit(solution)/shard_map/ppermute | solution.py:444
  165.6 4.5 %collective-permute-start.25 = (bf16[256,512]{1,0:T(8,128)(2,1)S(1)}, bf16[256,512]{1,0:T(8,128)(2,1)S(1)}, u32[]{:S(2)}, u32[]{:S(2)}) collective-permute-start(bf16[256,512]{1,0:T(8,128)(2,1)S(1)} %bitcast.52), channel_id=1, source_target_pairs={{0,8},{8,0},{16,24},{24,16},{32,40},{40,32},{48,56},{56,48},{64,72... | collective-permute-start | bytes 786440 | tf_op jit(solution)/shard_map/ppermute | solution.py:455

commit v8 on v7

--- a/solution.py
+++ b/solution.py
@@ -35,12 +35,10 @@
     return jnp.where(position == wanted, 1.0, 0.0).astype(BF16)
 
 
-def group_kernel(
-    meta_ref, part_ref, features_hbm, other_part_ref, other_ref, out_ref, features_ref, sem
-):
+def group_kernel(part_ref, features_hbm, out_ref, features_ref, sem):
     copy = pltpu.make_async_copy(features_hbm, features_ref, sem)
     copy.start()
-    core = meta_ref[0]
+    part = part_ref[...]
     devices = N_ROW * N_COL
     before = jnp.where(
         lax.broadcasted_iota(jnp.int32, (SLOTS, SLOTS), 0)
@@ -48,22 +46,18 @@
         1.0,
         0.0,
     ).astype(BF16)
-
-    def grouped(part, rows):
-        member = jnp.where(
-            part == lax.broadcasted_iota(jnp.int32, (devices, SLOTS), 0), 1.0, 0.0
-        )
-        earlier = jnp.dot(member.astype(BF16), before, preferred_element_type=F32)
-        rank = jnp.sum(member * earlier, axis=0, keepdims=True).astype(jnp.int32)
-        place = ((part & (N_COL - 1)) * N_ROW + (part >> 3)) * PER_PEER + rank
-        pick = selection(place, SLOTS, SLOTS)
-        wanted = jnp.where(core == 0, rows[:, :HALF], rows[:, HALF:])
+    member = jnp.where(
+        part == lax.broadcasted_iota(jnp.int32, (devices, SLOTS), 0), 1.0, 0.0
+    )
+    earlier = jnp.dot(member.astype(BF16), before, preferred_element_type=F32)
+    rank = jnp.sum(member * earlier, axis=0, keepdims=True).astype(jnp.int32)
+    place = ((part & (N_COL - 1)) * N_ROW + (part >> 3)) * PER_PEER + rank
+    pick = selection(place, SLOTS, SLOTS)
+    copy.wait()
+    for c in range(2):
+        wanted = features_ref[:, c * HALF : (c + 1) * HALF]
         picked = jnp.dot(pick, wanted, preferred_element_type=F32).astype(BF16)
-        return picked.reshape(N_COL, 1, SLOTS // N_COL, HALF)
-
-    out_ref[:, pl.ds(1 - core, 1)] = grouped(other_part_ref[...], other_ref[...])
-    copy.wait()
-    out_ref[:, pl.ds(core, 1)] = grouped(part_ref[...], features_ref[...])
+        out_ref[c * N_COL : (c + 1) * N_COL] = picked.reshape(N_COL, SLOTS // N_COL, HALF)
 
 
 def interleave_kernel(arrived_ref, out_ref):
@@ -72,7 +66,7 @@
     place = (inner >> 2) * (N_COL * PER_PEER) + giver * PER_PEER + (inner & 3)
     pick = selection(place, SLOTS, SLOTS)
     for c in range(2):
-        rows = arrived_ref[:, c].reshape(SLOTS, HALF)
+        rows = arrived_ref[c * N_COL : (c + 1) * N_COL].reshape(SLOTS, HALF)
         out_ref[c] = jnp.dot(pick, rows, preferred_element_type=F32).astype(BF16)
 
 
@@ -115,20 +109,19 @@
     plan_ref[...] = found.astype(jnp.int32)
 
 
-def stage_kernel(meta_ref, own_hbm, other_hbm, first_ref, second_ref, sems):
-    core = meta_ref[0]
-    refs = (first_ref, second_ref)
-    for out in refs:
-        out[SLOT_CAP] = jnp.zeros((TILE, TILE), BF16)
-    for c in range(2):
-
-        @pl.when(core == c)
+def start_tiles(part, core, own_hbm, other_hbm, out, sem):
+    out[SLOT_CAP] = jnp.zeros((TILE, TILE), BF16)
+    for mine, hbm in ((True, own_hbm), (False, other_hbm)):
+
+        @pl.when((core == part) == mine)
         def _():
-            for hbm, out, k in ((own_hbm, refs[c], 0), (other_hbm, refs[1 - c], 1)):
-                pltpu.make_async_copy(hbm, out.at[pl.ds(0, SLOT_CAP)], sems.at[k]).start()
-
-    for hbm, k in ((own_hbm, 0), (other_hbm, 1)):
-        pltpu.make_async_copy(hbm, refs[k].at[pl.ds(0, SLOT_CAP)], sems.at[k]).wait()
+            pltpu.make_async_copy(hbm, out.at[pl.ds(0, SLOT_CAP)], sem).start()
+
+    return pltpu.make_async_copy(own_hbm, out.at[pl.ds(0, SLOT_CAP)], sem)
+
+
+def stage_kernel(meta_ref, own_hbm, other_hbm, out_ref, sem):
+    start_tiles(1, meta_ref[0], own_hbm, other_hbm, out_ref, sem).wait()
 
 
 def add_tiles(plan_ref, tiles, source, total):
@@ -163,11 +156,10 @@
     return rows.reshape(SLOTS, HALF)
 
 
-def tiles_y_kernel(meta_ref, plan_ref, tiles, *refs):
-    blocks, (keep_ref, send_ref, source) = refs[:BLOCKS], refs[BLOCKS : BLOCKS + 3]
-    total, sems = refs[BLOCKS + 3 :]
-    yh = meta_ref[2]
-    core = meta_ref[0]
+def tiles_y_kernel(meta_ref, plan_ref, tiles, own_hbm, other_hbm, *refs):
+    blocks, (keep_ref, send_ref, source, next_tiles) = refs[:BLOCKS], refs[BLOCKS:-3]
+    total, sems, tiles_sem = refs[-3:]
+    core, yh = meta_ref[0], meta_ref[2]
 
     def fetch(block, k):
         return pltpu.make_async_copy(block, source.at[meta_ref[4 + k]], sems.at[k])
@@ -183,10 +175,12 @@
 
     for k in range(CHIPS):
         fetch(blocks[k], k).wait()
+    coming = start_tiles(0, core, own_hbm, other_hbm, next_tiles, tiles_sem)
     add_tiles(plan_ref, tiles, source, total)
     for out, to in ((send_ref, 1 - yh), (keep_ref, yh)):
         for x in range(4):
             out[x] = narrow_block(total, to, x)
+    coming.wait()
 
 
 def tiles_x_kernel(meta_ref, plan_ref, tiles, source, *refs):
@@ -356,8 +350,6 @@
     swap = row_moves(lambda yl, z, c: (yl, z, 1 - c))
     tiles = tile_values.reshape(-1, TILE, TILE)
     part = partition_of.reshape(1, SLOTS)
-    other_part = lax.ppermute(part, "row", swap)
-    other_features = lax.ppermute(features, "row", swap)
     plan = call(plan_kernel, [smem, vmem, vmem], array(8, PLAN, dtype=jnp.int32))(
         tile_count.reshape(1), tile_rows.reshape(1, -1), tile_cols.reshape(1, -1)
     )
@@ -365,21 +357,20 @@
     plans = [jnp.where(core == c, plan, other_plan) for c in range(2)]
     grouped = call(
         group_kernel,
-        [smem, vmem, pinned, vmem, vmem],
-        held(N_COL, 2, SLOTS // N_COL, HALF),
+        [vmem, pinned],
+        held(2 * N_COL, SLOTS // N_COL, HALF),
         [pltpu.VMEM((SLOTS, F), BF16), pltpu.SemaphoreType.DMA],
-    )(meta, part, features, other_part, other_features)
+    )(part, features)
     other_tiles = lax.ppermute(after(tiles, grouped), "row", swap)
-    arrived = lax.all_to_all(grouped, "col", split_axis=0, concat_axis=0, tiled=True)
+    near_chips = [[k * 2 * N_COL + m for m in range(2 * N_COL)] for k in range(CHIPS)]
+    arrived = exchange(grouped, ("row", "col"), near_chips)
     own = call(interleave_kernel, [vmem], array(2, SLOTS, HALF))(arrived)
     own = after(own, other_tiles, other_plan)
 
-    tiles0, tiles1 = call(
-        stage_kernel,
-        [smem, pinned, pinned],
-        [held(SLOT_CAP + 1, TILE, TILE)] * 2,
-        [pltpu.SemaphoreType.DMA((2,))],
-    )(meta, tiles, after(other_tiles, own))
+    staged = held(SLOT_CAP + 1, TILE, TILE)
+    tiles1 = call(stage_kernel, [smem, pinned, pinned], staged, [pltpu.SemaphoreType.DMA])(
+        meta, tiles, after(other_tiles, own)
+    )
 
     def hop(block, *moves):
         def move(yl, z, c):
@@ -408,12 +399,12 @@
 
     total = pltpu.VMEM((ROW_TILES, TILE, HALF), F32)
     source = held(CHIPS, 2, N_ROW, N_COL * PER_PEER, HALF)
-    keep1, send1, source = call(
+    keep1, send1, source, tiles0 = call(
         tiles_y_kernel,
-        [smem, smem, vmem] + [hbm] * BLOCKS,
-        [held(4, SLOTS, HALF), held(4, SLOTS, HALF), source],
-        [total, pltpu.SemaphoreType.DMA((CHIPS,))],
-    )(meta, plans[1], tiles1, *blocks)
+        [smem, smem, vmem, pinned, pinned] + [hbm] * BLOCKS,
+        [held(4, SLOTS, HALF), held(4, SLOTS, HALF), source, staged],
+        [total, pltpu.SemaphoreType.DMA((CHIPS,)), pltpu.SemaphoreType.DMA],
+    )(meta, plans[1], tiles1, tiles, other_tiles, *blocks)
     row0 = call(
         tiles_x_kernel,
         [smem, smem, vmem, vmem],

time: 171 us -> 168 us (0.982)
  waiting for transfers between devices: 62 us -> 58.1 us
  Pallas kernels: 25.2 us -> 22.3 us
  starting transfers between devices: 44.8 us -> 47.6 us
    ppermute x3, waiting for transfers between devices: 18.1 us -> 14.4 us  [shards(): got1 = [lax.ppermute(send1[k - 1], 'col', x_moves(k)) for k in (1, 3, 2)]]
    pallas_call x11, Pallas kernels: 25.2 us -> 22.3 us  [run(): return made(*held)]
    ppermute x1, starting transfers between devices: 0.15 us -> 2.77 us  [shards(): got0 = lax.ppermute(send0, 'col', y_moves())]
  transfers between devices with their start and end apart: 27 -> 25, of which waited for: 14 -> 14; matrix products, arithmetic and copies ran while one was open for 1% -> 1% of each run, Pallas kernels for 8% -> 7%
where the time goes in v8:
time: 168 us
  waiting for transfers between devices  58.1 us (35%)
  starting transfers between devices  47.6 us (28%)
  blocking collectives  32.7 us (19%)
  Pallas kernels  22.3 us (13%)
  local copies, waits for them, and re-layouts  4.06 us (2%)
  between operations  1.72 us (1%)
    all_to_all x3, blocking collectives, exchange(): lax.all_to_all(parts, axis, split_axis=0, concat_axis=0, axis_index_group...  32.7 us
    ppermute x11, starting transfers between devices, hop(): return lax.ppermute(block, 'row', row_moves(move))  23.3 us
    pallas_call x11, Pallas kernels, run(): return made(*held)  22.3 us
    ppermute x11, waiting for transfers between devices, hop(): return lax.ppermute(block, 'row', row_moves(move))  16.2 us
    ppermute x3, waiting for transfers between devices, shards(): got1 = [lax.ppermute(send1[k - 1], 'col', x_moves(k)) for k in (1, 3, 2)]  14.4 us
    ppermute x1, waiting for transfers between devices, shards(): got1 = lax.ppermute(send1, 'col', y_moves())  13.4 us
    all_to_all x1, waiting for transfers between devices, exchange(): lax.all_to_all(parts, axis, split_axis=0, concat_axis=0, axis_index_group...  9.51 us
    all_to_all x1, starting transfers between devices, exchange(): lax.all_to_all(parts, axis, split_axis=0, concat_axis=0, axis_index_group...  7.14 us
  transfers between devices with their start and end apart: 25, of which 14 were waited for; matrix products, arithmetic and copies ran while one was open for 1% of the time, Pallas kernels for 7%

profile of v8, /device:TPU:1, one launch (start us, length us, event | category | flops | bytes accessed | tf_op | source)
XLA Modules:
  0.0 167.8 jit_solution(10606608108395417862)
XLA Ops:
  0.6 0.7 copy-done.3
  1.3 2.3 %shard_map.96 = bf16[16,64,256]{2,1,0:T(8,128)(2,1)} custom-call(s32[1,512]{1,0:T(1,128)S(1)} %bitcast.46, bf16[512,512]{1,0:T(8,128)(2,1)} %features_hbm.1), custom_call_target="tpu_custom_call" | custom-call | tf_op jit(solution)/shard_map/pallas_call | solution.py:305
  3.6 1.5 collective-permute-start.1
  5.1 7.1 %all-to-all-start = ((bf16[16,64,256]{2,1,0:T(8,128)(2,1)}), bf16[16,64,256]{2,1,0:T(8,128)(2,1)S(1)}, u32[]{:S(2)}, u32[]{:S(2)}) async-start(bf16[16,64,256]{2,1,0:T(8,128)(2,1)} %shard_map.96), calls=%async_computation | async-start | bytes 1048576 | tf_op jit(solution)/shard_map/all_to_all | solution.py:277
  12.9 0.0 copy-start.4
  12.9 0.7 copy-done.4
  13.6 0.7 copy-done.5
  14.3 0.5 shard_map.95
  14.7 0.1 collective-permute-start
  14.8 9.5 %all-to-all-done.arrived_ref = bf16[16,64,256]{2,1,0:T(8,128)(2,1)S(1)} async-done(((bf16[16,64,256]{2,1,0:T(8,128)(2,1)}), bf16[16,64,256]{2,1,0:T(8,128)(2,1)S(1)}, u32[]{:S(2)}, u32[]{:S(2)}) %all-to-all-start) | async-done | bytes 524320 | tf_op jit(solution)/shard_map/all_to_all | solution.py:277
  24.4 0.4 shard_map.97
  24.8 0.5 collective-permute-start.2
  25.3 0.7 collective-permute-start.5
  26.0 1.7 %collective-permute-start.3 = (bf16[2,512,256]{2,1,0:T(8,128)(2,1)S(1)}, bf16[2,512,256]{2,1,0:T(8,128)(2,1)S(1)}, u32[]{:S(2)}, u32[]{:S(2)}) collective-permute-start(bf16[2,512,256]{2,1,0:T(8,128)(2,1)S(1)} %shard_map.97), channel_id=1, source_target_pairs={{0,64},{8,24},{16,80},{24,40},{32,96},{40,56},{48,112},{56,8},{64,... | collective-permute-start | bytes 1572872 | tf_op jit(solution)/shard_map/ppermute | solution.py:381
  27.7 0.7 collective-permute-start.6
  28.4 4.8 %collective-permute-done.2 = bf16[2,512,256]{2,1,0:T(8,128)(2,1)S(1)} collective-permute-done((bf16[2,512,256]{2,1,0:T(8,128)(2,1)S(1)}, bf16[2,512,256]{2,1,0:T(8,128)(2,1)S(1)}, u32[]{:S(2)}, u32[]{:S(2)}) %collective-permute-start.2) | collective-permute-done | bytes 524320 | tf_op jit(solution)/shard_map/ppermute | solution.py:381
  33.2 2.5 %collective-permute-start.4 = (bf16[2,512,256]{2,1,0:T(8,128)(2,1)S(1)}, bf16[2,512,256]{2,1,0:T(8,128)(2,1)S(1)}, u32[]{:S(2)}, u32[]{:S(2)}) collective-permute-start(bf16[2,512,256]{2,1,0:T(8,128)(2,1)S(1)} %collective-permute-done.2), channel_id=1, source_target_pairs={{0,64},{8,24},{16,80},{24,40},{32,96},{40,56},{48,112},{56,8},{64,... | collective-permute-start | bytes 1572872 | tf_op jit(solution)/shard_map/ppermute | solution.py:381
  35.7 0.7 collective-permute-start.7
  36.4 4.0 %collective-permute-start.10 = (bf16[2,512,256]{2,1,0:T(8,128)(2,1)S(1)}, bf16[2,512,256]{2,1,0:T(8,128)(2,1)}, u32[]{:S(2)}, u32[]{:S(2)}) collective-permute-start(bf16[2,512,256]{2,1,0:T(8,128)(2,1)S(1)} %shard_map.97), channel_id=1, source_target_pairs={{8,56},{24,8},{40,24},{56,40},{72,120},{88,72},{104,88},{120,104},... | collective-permute-start | bytes 1572872 | tf_op jit(solution)/shard_map/ppermute | solution.py:381
  40.5 0.8 collective-permute-done.3
  41.2 4.3 %collective-permute-start.9 = (bf16[2,512,256]{2,1,0:T(8,128)(2,1)S(1)}, bf16[2,512,256]{2,1,0:T(8,128)(2,1)}, u32[]{:S(2)}, u32[]{:S(2)}) collective-permute-start(bf16[2,512,256]{2,1,0:T(8,128)(2,1)S(1)} %collective-permute-done.2), channel_id=1, source_target_pairs={{8,56},{24,8},{40,24},{56,40},{72,120},{88,72},{104,88},{120,104},... | collective-permute-start | bytes 1572872 | tf_op jit(solution)/shard_map/ppermute | solution.py:381
  45.6 1.5 collective-permute-start.8
  47.0 4.7 %collective-permute-done.4 = bf16[2,512,256]{2,1,0:T(8,128)(2,1)S(1)} collective-permute-done((bf16[2,512,256]{2,1,0:T(8,128)(2,1)S(1)}, bf16[2,512,256]{2,1,0:T(8,128)(2,1)S(1)}, u32[]{:S(2)}, u32[]{:S(2)}) %collective-permute-start.4) | collective-permute-done | bytes 524320 | tf_op jit(solution)/shard_map/ppermute | solution.py:381
  51.7 4.5 %collective-permute-start.11 = (bf16[2,512,256]{2,1,0:T(8,128)(2,1)S(1)}, bf16[2,512,256]{2,1,0:T(8,128)(2,1)}, u32[]{:S(2)}, u32[]{:S(2)}) collective-permute-start(bf16[2,512,256]{2,1,0:T(8,128)(2,1)S(1)} %shard_map.97), channel_id=1, source_target_pairs={{8,40},{24,56},{40,8},{56,24},{72,104},{88,120},{104,72},{120,88},... | collective-permute-start | bytes 1572872 | tf_op jit(solution)/shard_map/ppermute | solution.py:381
  56.3 0.8 copy-done.1
  57.1 2.2 %collective-permute-start.12 = (bf16[2,512,256]{2,1,0:T(8,128)(2,1)S(1)}, bf16[2,512,256]{2,1,0:T(8,128)(2,1)}, u32[]{:S(2)}, u32[]{:S(2)}) collective-permute-start(bf16[2,512,256]{2,1,0:T(8,128)(2,1)S(1)} %collective-permute-done.2), channel_id=1, source_target_pairs={{8,40},{24,56},{40,8},{56,24},{72,104},{88,120},{104,72},{120,88},... | collective-permute-start | bytes 1572872 | tf_op jit(solution)/shard_map/ppermute | solution.py:381
  59.4 0.1 stack.51.meta_ref
  59.5 0.0 copy-start.2
  59.6 3.3 %shard_map.98.tiles = bf16[193,128,128]{2,1,0:T(8,128)(2,1)S(1)} custom-call(s32[12]{0:T(128)S(1)} %stack.51.meta_ref, bf16[192,128,128]{2,1,0:T(8,128)(2,1)} %bitcast.50, bf16[192,128,128]{2,1,0:T(8,128)(2,1)} %collective-permute-done.1.other_hbm), custom_call_target="tpu_custom_call" | custom-call | tf_op jit(solution)/shard_map/pallas_call | solution.py:305
  62.9 0.3 collective-permute-done.11
  63.2 5.6 %collective-permute-done.12 = bf16[2,512,256]{2,1,0:T(8,128)(2,1)} collective-permute-done((bf16[2,512,256]{2,1,0:T(8,128)(2,1)S(1)}, bf16[2,512,256]{2,1,0:T(8,128)(2,1)}, u32[]{:S(2)}, u32[]{:S(2)}) %collective-permute-start.12) | collective-permute-done | bytes 524320 | tf_op jit(solution)/shard_map/ppermute | solution.py:381
  68.8 5.3 %shard_map.99 = (bf16[4,512,256]{2,1,0:T(8,128)(2,1)S(1)}, bf16[4,512,256]{2,1,0:T(8,128)(2,1)S(1)}, bf16[8,2,16,32,256]{4,3,2,1,0:T(8,128)(2,1)S(1)}, bf16[193,128,128]{2,1,0:T(8,128)(2,1)S(1)}) custom-call(s32[12]{0:T(128)S(1)} %stack.51.meta_ref, s32[8,288]{1,0:T(8,128)S(1)} %get-tuple-element.50.plan_ref, bf16[193,128,128]{2,1,0:T(8,128)(2,1)S(1)} %shard_map.98.tiles, ...), custom_call_target="tpu_custom_call" | custom-call | tf_op jit(solution)/shard_map/pallas_call | solution.py:305
  74.1 2.2 %collective-permute-start.13 = (bf16[4,512,256]{2,1,0:T(8,128)(2,1)S(1)}, bf16[4,512,256]{2,1,0:T(8,128)(2,1)S(1)}, u32[]{:S(2)}, u32[]{:S(2)}) collective-permute-start(bf16[4,512,256]{2,1,0:T(8,128)(2,1)S(1)} %get-tuple-element.33), channel_id=1, source_target_pairs={{0,4},{1,5},{2,6},{3,7},{4,0},{5,1},{6,2},{7,3},{8,12},{9,13},{10,... | collective-permute-start | bytes 3145736 | tf_op jit(solution)/shard_map/ppermute | solution.py:415
  76.3 5.1 %shard_map.100 = (bf16[2,512,256]{2,1,0:T(8,128)(2,1)S(1)}, bf16[2,512,256]{2,1,0:T(8,128)(2,1)S(1)}, bf16[2,512,256]{2,1,0:T(8,128)(2,1)S(1)}, bf16[2,512,256]{2,1,0:T(8,128)(2,1)S(1)}) custom-call(s32[12]{0:T(128)S(1)} %stack.51.meta_ref, s32[8,288]{1,0:T(8,128)S(1)} %get-tuple-element.51.plan_ref, bf16[193,128,128]{2,1,0:T(8,128)(2,1)S(1)} %get-tuple-element.29.tiles, ...), custom_call_target="tpu_custom_call" | custom-call | tf_op jit(solution)/shard_map/pallas_call | solution.py:305
  81.5 0.1 collective-permute-start.15
  81.5 2.7 %collective-permute-start.16 = (bf16[2,512,256]{2,1,0:T(8,128)(2,1)S(1)}, bf16[2,512,256]{2,1,0:T(8,128)(2,1)S(1)}, u32[]{:S(2)}, u32[]{:S(2)}) collective-permute-start(bf16[2,512,256]{2,1,0:T(8,128)(2,1)S(1)} %get-tuple-element.37), channel_id=1, source_target_pairs={{0,3},{1,0},{2,1},{3,2},{4,7},{5,4},{6,5},{7,6},{8,11},{9,8},{10,9... | collective-permute-start | bytes 1572872 | tf_op jit(solution)/shard_map/ppermute | solution.py:414
  84.2 13.4 %collective-permute-done.13.got_ref = bf16[4,512,256]{2,1,0:T(8,128)(2,1)S(1)} collective-permute-done((bf16[4,512,256]{2,1,0:T(8,128)(2,1)S(1)}, bf16[4,512,256]{2,1,0:T(8,128)(2,1)S(1)}, u32[]{:S(2)}, u32[]{:S(2)}) %collective-permute-start.13) | collective-permute-done | bytes 1048608 | tf_op jit(solution)/shard_map/ppermute | solution.py:415
  97.6 0.8 shard_map.101
  98.4 1.7 collective-permute-start.14
  100.1 1.1 collective-permute-start.19
  101.1 9.6 %collective-permute-done.14.a_ref = bf16[512,256]{1,0:T(8,128)(2,1)S(1)} collective-permute-done((bf16[512,256]{1,0:T(8,128)(2,1)S(1)}, bf16[512,256]{1,0:T(8,128)(2,1)S(1)}, u32[]{:S(2)}, u32[]{:S(2)}) %collective-permute-start.14) | collective-permute-done | bytes 262176 | tf_op jit(solution)/shard_map/ppermute | solution.py:420
  110.7 0.0 collective-permute-start.20
  110.8 0.8 shard_map.102
  111.6 2.8 %collective-permute-start.18 = (bf16[512,256]{1,0:T(8,128)(2,1)S(1)}, bf16[512,256]{1,0:T(8,128)(2,1)S(1)}, u32[]{:S(2)}, u32[]{:S(2)}) collective-permute-start(bf16[512,256]{1,0:T(8,128)(2,1)S(1)} %get-tuple-element.40), channel_id=1, source_target_pairs={{0,4},{1,5},{2,6},{3,7},{4,0},{5,1},{6,2},{7,3},{8,12},{9,13},{10,... | collective-permute-start | bytes 786440 | tf_op jit(solution)/shard_map/ppermute | solution.py:424
  114.3 1.9 %collective-permute-done.19.b_ref = bf16[512,256]{1,0:T(8,128)(2,1)S(1)} collective-permute-done((bf16[512,256]{1,0:T(8,128)(2,1)S(1)}, bf16[512,256]{1,0:T(8,128)(2,1)S(1)}, u32[]{:S(2)}, u32[]{:S(2)}) %collective-permute-start.19) | collective-permute-done | bytes 262176 | tf_op jit(solution)/shard_map/ppermute | solution.py:420
  116.2 2.9 %collective-permute-done.20.c_ref = bf16[512,256]{1,0:T(8,128)(2,1)S(1)} collective-permute-done((bf16[512,256]{1,0:T(8,128)(2,1)S(1)}, bf16[512,256]{1,0:T(8,128)(2,1)S(1)}, u32[]{:S(2)}, u32[]{:S(2)}) %collective-permute-start.20) | collective-permute-done | bytes 262176 | tf_op jit(solution)/shard_map/ppermute | solution.py:420
  119.1 1.5 collective-permute-done.18.got0
  120.6 0.8 shard_map.103
  121.4 1.4 collective-permute-start.21
  122.7 1.1 constant_dynamic-slice_fusion.cotangent_ref
  123.8 0.5 collective-permute-done.21.got_ref
  124.3 2.3 %shard_map.104 = (bf16[512,512]{1,0:T(8,128)(2,1)}, bf16[512,512]{1,0:T(8,128)(2,1)S(1)}) custom-call(s32[12]{0:T(128)S(1)} %stack.51.meta_ref, f32[512,256]{1,0:T(8,128)S(1)} %get-tuple-element.44.mine_ref, f32[512,256]{1,0:T(8,128)S(1)} %collective-permute-done.21.got_ref, bf16[512,512]{1,0:T(8,128)(2,1)S(1)} %copy-done, ...), custom_call_target="tpu_custom_call" | custom-call | tf_op jit(solution)/shard_map/pallas_call | solution.py:305
  126.6 0.4 collective-permute-start.22
  126.9 1.5 collective-permute-done.22.other_slope_ref
  128.5 0.7 shard_map.105
  129.2 8.5 %all_to_all.20 = bf16[8,32,512]{2,1,0:T(8,128)(2,1)S(1)} all-to-all(bf16[8,32,512]{2,1,0:T(8,128)(2,1)S(1)} %bitcast.39), channel_id=1, replica_groups={{0,16,32,48,64,80,96,112},{8,24,40,56,72,88,104,120},{1,17,33,49,65,81,..., dimensions={0} | all-to-all | bytes 524288 | tf_op jit(solution)/shard_map/all_to_all | solution.py:277
  137.8 0.1 convert_element_type.11
  137.9 0.1 broadcast_in_dim.6
  137.9 13.5 %all_to_all.21 = f32[8,32,512]{2,1,0:T(8,128)S(1)} all-to-all(f32[8,32,512]{2,1,0:T(8,128)S(1)} %broadcast_in_dim.6), channel_id=1, replica_groups=mesh['row'=16,'col'=8] {'col'}, dimensions={0} | all-to-all | bytes 1048576 | tf_op jit(solution)/shard_map/all_to_all | solution.py:277
  151.4 10.7 %all_to_all.22 = bf16[8,32,512]{2,1,0:T(8,128)(2,1)S(1)} all-to-all(bf16[8,32,512]{2,1,0:T(8,128)(2,1)S(1)} %broadcast_in_dim.7), channel_id=1, replica_groups={{0,16,32,48,64,80,96,112},{8,24,40,56,72,88,104,120},{1,17,33,49,65,81,..., dimensions={0} | all-to-all | bytes 524288 | tf_op jit(solution)/shard_map/all_to_all | solution.py:277
  162.1 3.3 %collective-permute-start.23 = (bf16[256,512]{1,0:T(8,128)(2,1)S(1)}, bf16[256,512]{1,0:T(8,128)(2,1)S(1)}, u32[]{:S(2)}, u32[]{:S(2)}) collective-permute-start(bf16[256,512]{1,0:T(8,128)(2,1)S(1)} %bitcast.52), channel_id=1, source_target_pairs={{0,8},{8,0},{16,24},{24,16},{32,40},{40,32},{48,56},{56,48},{64,72... | collective-permute-start | bytes 786440 | tf_op jit(solution)/shard_map/ppermute | solution.py:446
  165.5 1.2 collective-permute-done.23
  166.6 0.1 broadcast_select_fusion.1
  166.7 1.1 maximum_convert_fusion
  (22 shorter events, 0.2 us)
Async XLA Ops:
  0.6 0.7 copy-start.3
  3.6 21.2 %collective-permute-start.1 = (bf16[192,128,128]{2,1,0:T(8,128)(2,1)}, bf16[192,128,128]{2,1,0:T(8,128)(2,1)}, u32[]{:S(2)}, u32[]{:S(2)}) collective-permute-start(bf16[192,128,128]{2,1,0:T(8,128)(2,1)} %bitcast.49), channel_id=1, source_target_pairs={{0,8},{8,0},{16,24},{24,16},{32,40},{40,32},{48,56},{56,48},{64,72... | collective-permute-start | bytes 18874376 | tf_op jit(solution)/shard_map/ppermute | solution.py:364
  5.1 19.2 %all-to-all-start = ((bf16[16,64,256]{2,1,0:T(8,128)(2,1)}), bf16[16,64,256]{2,1,0:T(8,128)(2,1)S(1)}, u32[]{:S(2)}, u32[]{:S(2)}) async-start(bf16[16,64,256]{2,1,0:T(8,128)(2,1)} %shard_map.96), calls=%async_computation | async-start | bytes 1048576 | tf_op jit(solution)/shard_map/all_to_all | solution.py:277
  12.9 0.7 copy-start.4
  13.6 0.7 copy-start.5
  14.7 10.1 %collective-permute-start = (s32[8,288]{1,0:T(8,128)S(1)}, s32[8,288]{1,0:T(8,128)S(1)}, u32[]{:S(2)}, u32[]{:S(2)}) collective-permute-start(s32[8,288]{1,0:T(8,128)S(1)} %shard_map.95), channel_id=1, source_target_pairs={{0,8},{8,0},{16,24},{24,16},{32,40},{40,32},{48,56},{56,48},{64,72... | collective-permute-start | bytes 27656 | tf_op jit(solution)/shard_map/ppermute | solution.py:356
  24.8 8.4 %collective-permute-start.2 = (bf16[2,512,256]{2,1,0:T(8,128)(2,1)S(1)}, bf16[2,512,256]{2,1,0:T(8,128)(2,1)S(1)}, u32[]{:S(2)}, u32[]{:S(2)}) collective-permute-start(bf16[2,512,256]{2,1,0:T(8,128)(2,1)S(1)} %shard_map.97), channel_id=1, source_target_pairs={{0,16},{8,72},{16,32},{24,88},{32,48},{40,104},{48,0},{56,120},{64... | collective-permute-start | bytes 1572872 | tf_op jit(solution)/shard_map/ppermute | solution.py:381
  25.3 10.4 %collective-permute-start.5 = (bf16[2,512,256]{2,1,0:T(8,128)(2,1)S(1)}, bf16[2,512,256]{2,1,0:T(8,128)(2,1)S(1)}, u32[]{:S(2)}, u32[]{:S(2)}) collective-permute-start(bf16[2,512,256]{2,1,0:T(8,128)(2,1)S(1)} %shard_map.97), channel_id=1, source_target_pairs={{0,48},{16,0},{32,16},{48,32},{64,112},{80,64},{96,80},{112,96},{1... | collective-permute-start | bytes 1572872 | tf_op jit(solution)/shard_map/ppermute | solution.py:381
  26.0 15.3 %collective-permute-start.3 = (bf16[2,512,256]{2,1,0:T(8,128)(2,1)S(1)}, bf16[2,512,256]{2,1,0:T(8,128)(2,1)S(1)}, u32[]{:S(2)}, u32[]{:S(2)}) collective-permute-start(bf16[2,512,256]{2,1,0:T(8,128)(2,1)S(1)} %shard_map.97), channel_id=1, source_target_pairs={{0,64},{8,24},{16,80},{24,40},{32,96},{40,56},{48,112},{56,8},{64,... | collective-permute-start | bytes 1572872 | tf_op jit(solution)/shard_map/ppermute | solution.py:381
  27.7 17.9 %collective-permute-start.6 = (bf16[2,512,256]{2,1,0:T(8,128)(2,1)S(1)}, bf16[2,512,256]{2,1,0:T(8,128)(2,1)S(1)}, u32[]{:S(2)}, u32[]{:S(2)}) collective-permute-start(bf16[2,512,256]{2,1,0:T(8,128)(2,1)S(1)} %shard_map.97), channel_id=1, source_target_pairs={{0,32},{16,48},{32,0},{48,16},{64,96},{80,112},{96,64},{112,80},{1... | collective-permute-start | bytes 1572872 | tf_op jit(solution)/shard_map/ppermute | solution.py:381
  33.2 18.5 %collective-permute-start.4 = (bf16[2,512,256]{2,1,0:T(8,128)(2,1)S(1)}, bf16[2,512,256]{2,1,0:T(8,128)(2,1)S(1)}, u32[]{:S(2)}, u32[]{:S(2)}) collective-permute-start(bf16[2,512,256]{2,1,0:T(8,128)(2,1)S(1)} %collective-permute-done.2), channel_id=1, source_target_pairs={{0,64},{8,24},{16,80},{24,40},{32,96},{40,56},{48,112},{56,8},{64,... | collective-permute-start | bytes 1572872 | tf_op jit(solution)/shard_map/ppermute | solution.py:381
  35.7 20.5 %collective-permute-start.7 = (bf16[2,512,256]{2,1,0:T(8,128)(2,1)S(1)}, bf16[2,512,256]{2,1,0:T(8,128)(2,1)S(1)}, u32[]{:S(2)}, u32[]{:S(2)}) collective-permute-start(bf16[2,512,256]{2,1,0:T(8,128)(2,1)S(1)} %collective-permute-done.5), channel_id=1, source_target_pairs={{0,64},{16,80},{32,96},{48,112},{64,0},{80,16},{96,32},{112,48},{1... | collective-permute-start | bytes 1572872 | tf_op jit(solution)/shard_map/ppermute | solution.py:381
  36.4 26.5 %collective-permute-start.10 = (bf16[2,512,256]{2,1,0:T(8,128)(2,1)S(1)}, bf16[2,512,256]{2,1,0:T(8,128)(2,1)}, u32[]{:S(2)}, u32[]{:S(2)}) collective-permute-start(bf16[2,512,256]{2,1,0:T(8,128)(2,1)S(1)} %shard_map.97), channel_id=1, source_target_pairs={{8,56},{24,8},{40,24},{56,40},{72,120},{88,72},{104,88},{120,104},... | collective-permute-start | bytes 1572872 | tf_op jit(solution)/shard_map/ppermute | solution.py:381
  41.2 21.7 %collective-permute-start.9 = (bf16[2,512,256]{2,1,0:T(8,128)(2,1)S(1)}, bf16[2,512,256]{2,1,0:T(8,128)(2,1)}, u32[]{:S(2)}, u32[]{:S(2)}) collective-permute-start(bf16[2,512,256]{2,1,0:T(8,128)(2,1)S(1)} %collective-permute-done.2), channel_id=1, source_target_pairs={{8,56},{24,8},{40,24},{56,40},{72,120},{88,72},{104,88},{120,104},... | collective-permute-start | bytes 1572872 | tf_op jit(solution)/shard_map/ppermute | solution.py:381
  45.6 17.3 %collective-permute-start.8 = (bf16[2,512,256]{2,1,0:T(8,128)(2,1)S(1)}, bf16[2,512,256]{2,1,0:T(8,128)(2,1)}, u32[]{:S(2)}, u32[]{:S(2)}) collective-permute-start(bf16[2,512,256]{2,1,0:T(8,128)(2,1)S(1)} %collective-permute-done.6), channel_id=1, source_target_pairs={{0,64},{16,80},{32,96},{48,112},{64,0},{80,16},{96,32},{112,48},{1... | collective-permute-start | bytes 1572872 | tf_op jit(solution)/shard_map/ppermute | solution.py:381
  51.7 11.5 %collective-permute-start.11 = (bf16[2,512,256]{2,1,0:T(8,128)(2,1)S(1)}, bf16[2,512,256]{2,1,0:T(8,128)(2,1)}, u32[]{:S(2)}, u32[]{:S(2)}) collective-permute-start(bf16[2,512,256]{2,1,0:T(8,128)(2,1)S(1)} %shard_map.97), channel_id=1, source_target_pairs={{8,40},{24,56},{40,8},{56,24},{72,104},{88,120},{104,72},{120,88},... | collective-permute-start | bytes 1572872 | tf_op jit(solution)/shard_map/ppermute | solution.py:381
  56.3 0.8 copy-start.1
  57.1 11.8 %collective-permute-start.12 = (bf16[2,512,256]{2,1,0:T(8,128)(2,1)S(1)}, bf16[2,512,256]{2,1,0:T(8,128)(2,1)}, u32[]{:S(2)}, u32[]{:S(2)}) collective-permute-start(bf16[2,512,256]{2,1,0:T(8,128)(2,1)S(1)} %collective-permute-done.2), channel_id=1, source_target_pairs={{8,40},{24,56},{40,8},{56,24},{72,104},{88,120},{104,72},{120,88},... | collective-permute-start | bytes 1572872 | tf_op jit(solution)/shard_map/ppermute | solution.py:381
  59.5 9.3 %copy-start.2 = (bf16[2,512,256]{2,1,0:T(8,128)(2,1)S(1)}, bf16[2,512,256]{2,1,0:T(8,128)(2,1)}, u32[]{:S(2)}) copy-start(bf16[2,512,256]{2,1,0:T(8,128)(2,1)} %copy-done.1) | copy-start | bytes 1572868
  74.1 23.4 %collective-permute-start.13 = (bf16[4,512,256]{2,1,0:T(8,128)(2,1)S(1)}, bf16[4,512,256]{2,1,0:T(8,128)(2,1)S(1)}, u32[]{:S(2)}, u32[]{:S(2)}) collective-permute-start(bf16[4,512,256]{2,1,0:T(8,128)(2,1)S(1)} %get-tuple-element.33), channel_id=1, source_target_pairs={{0,4},{1,5},{2,6},{3,7},{4,0},{5,1},{6,2},{7,3},{8,12},{9,13},{10,... | collective-permute-start | bytes 3145736 | tf_op jit(solution)/shard_map/ppermute | solution.py:415
  81.4 42.8 %copy-start = (bf16[512,512]{1,0:T(8,128)(2,1)S(1)}, bf16[512,512]{1,0:T(8,128)(2,1)}, u32[]{:S(2)}) copy-start(bf16[512,512]{1,0:T(8,128)(2,1)} %weight_ref.1) | copy-start | bytes 1572868
  81.5 29.3 %collective-permute-start.15 = (bf16[2,512,256]{2,1,0:T(8,128)(2,1)S(1)}, bf16[2,512,256]{2,1,0:T(8,128)(2,1)S(1)}, u32[]{:S(2)}, u32[]{:S(2)}) collective-permute-start(bf16[2,512,256]{2,1,0:T(8,128)(2,1)S(1)} %get-tuple-element.36), channel_id=1, source_target_pairs={{0,1},{1,2},{2,3},{3,0},{4,5},{5,6},{6,7},{7,4},{8,9},{9,10},{10,1... | collective-permute-start | bytes 1572872 | tf_op jit(solution)/shard_map/ppermute | solution.py:414
  81.5 29.2 %collective-permute-start.16 = (bf16[2,512,256]{2,1,0:T(8,128)(2,1)S(1)}, bf16[2,512,256]{2,1,0:T(8,128)(2,1)S(1)}, u32[]{:S(2)}, u32[]{:S(2)}) collective-permute-start(bf16[2,512,256]{2,1,0:T(8,128)(2,1)S(1)} %get-tuple-element.37), channel_id=1, source_target_pairs={{0,3},{1,0},{2,1},{3,2},{4,7},{5,4},{6,5},{7,6},{8,11},{9,8},{10,9... | collective-permute-start | bytes 1572872 | tf_op jit(solution)/shard_map/ppermute | solution.py:414
  84.2 26.6 %collective-permute-start.17 = (bf16[2,512,256]{2,1,0:T(8,128)(2,1)S(1)}, bf16[2,512,256]{2,1,0:T(8,128)(2,1)S(1)}, u32[]{:S(2)}, u32[]{:S(2)}) collective-permute-start(bf16[2,512,256]{2,1,0:T(8,128)(2,1)S(1)} %get-tuple-element.38), channel_id=1, source_target_pairs={{0,2},{1,3},{2,0},{3,1},{4,6},{5,7},{6,4},{7,5},{8,10},{9,11},{10,... | collective-permute-start | bytes 1572872 | tf_op jit(solution)/shard_map/ppermute | solution.py:414
  98.4 12.3 %collective-permute-start.14 = (bf16[512,256]{1,0:T(8,128)(2,1)S(1)}, bf16[512,256]{1,0:T(8,128)(2,1)S(1)}, u32[]{:S(2)}, u32[]{:S(2)}) collective-permute-start(bf16[512,256]{1,0:T(8,128)(2,1)S(1)} %get-tuple-element.34), channel_id=1, source_target_pairs={{0,1},{1,2},{2,3},{3,0},{4,5},{5,6},{6,7},{7,4},{8,9},{9,10},{10,1... | collective-permute-start | bytes 786440 | tf_op jit(solution)/shard_map/ppermute | solution.py:420
  100.1 16.1 %collective-permute-start.19 = (bf16[512,256]{1,0:T(8,128)(2,1)S(1)}, bf16[512,256]{1,0:T(8,128)(2,1)S(1)}, u32[]{:S(2)}, u32[]{:S(2)}) collective-permute-start(bf16[512,256]{1,0:T(8,128)(2,1)S(1)} %get-tuple-element.42), channel_id=1, source_target_pairs={{0,3},{1,0},{2,1},{3,2},{4,7},{5,4},{6,5},{7,6},{8,11},{9,8},{10,9... | collective-permute-start | bytes 786440 | tf_op jit(solution)/shard_map/ppermute | solution.py:420
  110.7 8.4 %collective-permute-start.20 = (bf16[512,256]{1,0:T(8,128)(2,1)S(1)}, bf16[512,256]{1,0:T(8,128)(2,1)S(1)}, u32[]{:S(2)}, u32[]{:S(2)}) collective-permute-start(bf16[512,256]{1,0:T(8,128)(2,1)S(1)} %get-tuple-element.43), channel_id=1, source_target_pairs={{0,2},{1,3},{2,0},{3,1},{4,6},{5,7},{6,4},{7,5},{8,10},{9,11},{10,... | collective-permute-start | bytes 786440 | tf_op jit(solution)/shard_map/ppermute | solution.py:420
  111.6 9.0 %collective-permute-start.18 = (bf16[512,256]{1,0:T(8,128)(2,1)S(1)}, bf16[512,256]{1,0:T(8,128)(2,1)S(1)}, u32[]{:S(2)}, u32[]{:S(2)}) collective-permute-start(bf16[512,256]{1,0:T(8,128)(2,1)S(1)} %get-tuple-element.40), channel_id=1, source_target_pairs={{0,4},{1,5},{2,6},{3,7},{4,0},{5,1},{6,2},{7,3},{8,12},{9,13},{10,... | collective-permute-start | bytes 786440 | tf_op jit(solution)/shard_map/ppermute | solution.py:424
  121.4 2.9 %collective-permute-start.21 = (f32[512,256]{1,0:T(8,128)S(1)}, f32[512,256]{1,0:T(8,128)S(1)}, u32[]{:S(2)}, u32[]{:S(2)}) collective-permute-start(f32[512,256]{1,0:T(8,128)S(1)} %get-tuple-element.45.other_ref), channel_id=1, source_target_pairs={{0,8},{8,0},{16,24},{24,16},{32,40},{40,32},{48,56},{56,48},{64,72... | collective-permute-start | bytes 1572872 | tf_op jit(solution)/shard_map/ppermute | solution.py:428
  126.6 1.9 %collective-permute-start.22 = (bf16[512,512]{1,0:T(8,128)(2,1)S(1)}, bf16[512,512]{1,0:T(8,128)(2,1)S(1)}, u32[]{:S(2)}, u32[]{:S(2)}) collective-permute-start(bf16[512,512]{1,0:T(8,128)(2,1)S(1)} %get-tuple-element.47.slope_ref), channel_id=1, source_target_pairs={{0,8},{8,0},{16,24},{24,16},{32,40},{40,32},{48,56},{56,48},{64,72... | collective-permute-start | bytes 1572872 | tf_op jit(solution)/shard_map/ppermute | solution.py:435
  162.1 4.5 %collective-permute-start.23 = (bf16[256,512]{1,0:T(8,128)(2,1)S(1)}, bf16[256,512]{1,0:T(8,128)(2,1)S(1)}, u32[]{:S(2)}, u32[]{:S(2)}) collective-permute-start(bf16[256,512]{1,0:T(8,128)(2,1)S(1)} %bitcast.52), channel_id=1, source_target_pairs={{0,8},{8,0},{16,24},{24,16},{32,40},{40,32},{48,56},{56,48},{64,72... | collective-permute-start | bytes 786440 | tf_op jit(solution)/shard_map/ppermute | solution.py:446

commit v9 on v8

--- a/solution.py
+++ b/solution.py
@@ -13,8 +13,7 @@
 PER_PEER = 4
 HALF = 256
 CHIPS = 8
-SHARED = 4
-BLOCKS = 2 * CHIPS - SHARED
+BLOCKS = 7
 SLOT_CAP = 192
 ROW_TILES = 32
 GROUP_BITS = 2
@@ -68,6 +67,24 @@
     for c in range(2):
         rows = arrived_ref[c * N_COL : (c + 1) * N_COL].reshape(SLOTS, HALF)
         out_ref[c] = jnp.dot(pick, rows, preferred_element_type=F32).astype(BF16)
+
+
+def pair_kernel(a_ref, b_ref, out_ref):
+    out_ref[0] = a_ref[...]
+    out_ref[1] = b_ref[...]
+
+
+def rest_kernel(meta_ref, pair_ref, a_ref, b_ref, out_ref):
+    core = meta_ref[0]
+
+    @pl.when(core == 0)
+    def _():
+        out_ref[0] = a_ref[...]
+        out_ref[1] = b_ref[...]
+
+    @pl.when(core != 0)
+    def _():
+        out_ref[...] = pair_ref[...]
 
 
 def plan_kernel(count_ref, rows_ref, cols_ref, plan_ref):
@@ -161,20 +178,25 @@
     total, sems, tiles_sem = refs[-3:]
     core, yh = meta_ref[0], meta_ref[2]
 
+    own, r1, r2, r3, s1, s3, s2 = blocks
+    shared = [(own, 0), (r1, 0), (s1, 0), (s1, 1), (s3, 0), (s3, 1)]
+
     def fetch(block, k):
-        return pltpu.make_async_copy(block, source.at[meta_ref[4 + k]], sems.at[k])
-
-    for k in range(SHARED):
-        fetch(blocks[k], k).start()
-    for c in range(2):
+        return pltpu.make_async_copy(
+            block[0].at[block[1]], source.at[meta_ref[4 + k]], sems.at[k]
+        )
+
+    for k, block in enumerate(shared):
+        fetch(block, k).start()
+    for c, rest in enumerate((((r2, 0), (r3, 0)), ((s2, 0), (s2, 1)))):
 
         @pl.when(core == c)
         def _():
-            for k in range(SHARED, CHIPS):
-                fetch(blocks[k + c * (CHIPS - SHARED)], k).start()
+            for k, block in enumerate(rest):
+                fetch(block, len(shared) + k).start()
 
     for k in range(CHIPS):
-        fetch(blocks[k], k).wait()
+        fetch(shared[0], k).wait()
     coming = start_tiles(0, core, own_hbm, other_hbm, next_tiles, tiles_sem)
     add_tiles(plan_ref, tiles, source, total)
     for out, to in ((send_ref, 1 - yh), (keep_ref, yh)):
@@ -340,10 +362,10 @@
         jnp.where(first, near[1], far[0]),
         jnp.where(first, far[0], near[1]),
         far[1],
-        jnp.where(first, near[3], far[3]),
-        jnp.where(first, near[2], near[3]),
-        jnp.where(first, far[3], near[2]),
-        far[2],
+        jnp.where(first, far[3], near[3]),
+        jnp.where(first, far[2], far[3]),
+        jnp.where(first, near[3], near[2]),
+        jnp.where(first, near[2], far[2]),
     ]
     meta = jnp.stack([core, x, yh, z] + places).astype(jnp.int32)
 
@@ -383,19 +405,15 @@
     r1 = hop(own, (0, 1), (1, 0))
     r2 = hop(own, (0, 3), None)
     r3 = hop(own, (0, 2), None)
-    r4 = hop(own, (1, 0), (0, 1))
-    s1 = hop(r1, (1, 0), (0, 1))
-    s2 = hop(r2, (1, 0), None)
-    s3 = hop(r3, (1, 0), None)
-    later = after(own, r1)
-    t1 = hop(r1, None, (0, 3))
-    t2 = hop(later, None, (0, 3))
-    t3 = hop(later, None, (0, 2))
-    t4 = hop(r1, None, (0, 2))
-    blocks = [
-        b.reshape(2, N_ROW, N_COL * PER_PEER, HALF)
-        for b in (own, r1, r4, s1, r2, r3, s2, s3, t1, t2, t3, t4)
-    ]
+    both = held(2, 2, SLOTS, HALF)
+    pair = call(pair_kernel, [vmem] * 2, both)(own, r1)
+    s1 = hop(pair, (1, 0), (0, 1))
+    s2 = hop(pair, None, (0, 2))
+    rest = call(rest_kernel, [smem] + [vmem] * 3, both)(meta, pair, r2, r3)
+    s3 = hop(rest, (1, 0), (0, 3))
+    shape = (N_ROW, N_COL * PER_PEER, HALF)
+    blocks = [b.reshape(1, 2, *shape) for b in (own, r1, r2, r3)]
+    blocks += [b.reshape(2, 2, *shape) for b in (s1, s3, s2)]
 
     total = pltpu.VMEM((ROW_TILES, TILE, HALF), F32)
     source = held(CHIPS, 2, N_ROW, N_COL * PER_PEER, HALF)

time: 168 us -> 169 us (level)
  starting transfers between devices: 47.6 us -> 29.9 us
  waiting for transfers between devices: 58.1 us -> 73.5 us
  Pallas kernels: 22.3 us -> 25.6 us
    ppermute x11 -> x6, starting transfers between devices: 23.3 us -> 8.87 us  [hop(): return lax.ppermute(block, 'row', row_moves(move))]
    ppermute x11 -> x6, waiting for transfers between devices: 16.2 us -> 26.6 us  [hop(): return lax.ppermute(block, 'row', row_moves(move))]
    ppermute x1, waiting for transfers between devices: 13.4 us -> 16.7 us  [shards(): got1 = lax.ppermute(send1, 'col', y_moves())]
    pallas_call x11 -> x13, Pallas kernels: 22.3 us -> 25.6 us  [run(): return made(*held)]
    ppermute x1, starting transfers between devices: 2.77 us -> 0.09 us  [shards(): got0 = lax.ppermute(send0, 'col', y_moves())]
    ppermute x3, waiting for transfers between devices: 14.4 us -> 16.8 us  [shards(): got1 = [lax.ppermute(send1[k - 1], 'col', x_moves(k)) for k in (1, 3, 2)]]
  transfers between devices with their start and end apart: 25 -> 20, of which waited for: 14 -> 11; matrix products, arithmetic and copies ran while one was open for 1% -> 1% of each run, Pallas kernels for 7% -> 7%
where the time goes in v9:
time: 169 us
  waiting for transfers between devices  73.5 us (43%)
  blocking collectives  33.6 us (20%)
  starting transfers between devices  29.9 us (18%)
  Pallas kernels  25.6 us (15%)
  local copies, waits for them, and re-layouts  3.27 us (2%)
    all_to_all x3, blocking collectives, exchange(): lax.all_to_all(parts, axis, split_axis=0, concat_axis=0, axis_index_group...  33.6 us
    ppermute x6, waiting for transfers between devices, hop(): return lax.ppermute(block, 'row', row_moves(move))  26.6 us
    pallas_call x13, Pallas kernels, run(): return made(*held)  25.6 us
    ppermute x3, waiting for transfers between devices, shards(): got1 = [lax.ppermute(send1[k - 1], 'col', x_moves(k)) for k in (1, 3, 2)]  16.8 us
    ppermute x1, waiting for transfers between devices, shards(): got1 = lax.ppermute(send1, 'col', y_moves())  16.7 us
    all_to_all x1, waiting for transfers between devices, exchange(): lax.all_to_all(parts, axis, split_axis=0, concat_axis=0, axis_index_group...  9.51 us
    ppermute x6, starting transfers between devices, hop(): return lax.ppermute(block, 'row', row_moves(move))  8.87 us
    all_to_all x1, starting transfers between devices, exchange(): lax.all_to_all(parts, axis, split_axis=0, concat_axis=0, axis_index_group...  7.14 us
  transfers between devices with their start and end apart: 20, of which 11 were waited for; matrix products, arithmetic and copies ran while one was open for 1% of the time, Pallas kernels for 7%

profile of v9, /device:TPU:1, one launch (start us, length us, event | category | flops | bytes accessed | tf_op | source)
XLA Modules:
  0.0 168.8 jit_solution(398731033951957538)
XLA Ops:
  0.6 0.7 copy-done.1
  1.3 2.3 %shard_map.96 = bf16[16,64,256]{2,1,0:T(8,128)(2,1)} custom-call(s32[1,512]{1,0:T(1,128)S(1)} %bitcast.38, bf16[512,512]{1,0:T(8,128)(2,1)} %features_hbm.1), custom_call_target="tpu_custom_call" | custom-call | tf_op jit(solution)/shard_map/pallas_call | solution.py:327
  3.6 1.5 collective-permute-start.1
  5.1 7.1 %all-to-all-start = ((bf16[16,64,256]{2,1,0:T(8,128)(2,1)}), bf16[16,64,256]{2,1,0:T(8,128)(2,1)S(1)}, u32[]{:S(2)}, u32[]{:S(2)}) async-start(bf16[16,64,256]{2,1,0:T(8,128)(2,1)} %shard_map.96), calls=%async_computation | async-start | bytes 1048576 | tf_op jit(solution)/shard_map/all_to_all | solution.py:299
  12.9 0.0 copy-start.2
  12.9 0.7 copy-done.2
  13.6 0.7 copy-done.3
  14.3 0.5 shard_map.95
  14.7 0.1 collective-permute-start
  14.8 9.5 %all-to-all-done.arrived_ref = bf16[16,64,256]{2,1,0:T(8,128)(2,1)S(1)} async-done(((bf16[16,64,256]{2,1,0:T(8,128)(2,1)}), bf16[16,64,256]{2,1,0:T(8,128)(2,1)S(1)}, u32[]{:S(2)}, u32[]{:S(2)}) %all-to-all-start) | async-done | bytes 524320 | tf_op jit(solution)/shard_map/all_to_all | solution.py:299
  24.4 0.4 shard_map.97.a_ref
  24.8 0.0 collective-permute-done
  24.8 0.0 collective-permute-done.1.other_hbm
  24.8 0.5 collective-permute-start.2
  25.3 0.7 collective-permute-start.3
  26.0 0.7 collective-permute-start.4
  26.8 0.1 stack.51.meta_ref
  26.9 6.3 %collective-permute-done.2.b_ref = bf16[2,512,256]{2,1,0:T(8,128)(2,1)S(1)} collective-permute-done((bf16[2,512,256]{2,1,0:T(8,128)(2,1)S(1)}, bf16[2,512,256]{2,1,0:T(8,128)(2,1)S(1)}, u32[]{:S(2)}, u32[]{:S(2)}) %collective-permute-start.2) | collective-permute-done | bytes 524320 | tf_op jit(solution)/shard_map/ppermute | solution.py:403
  33.2 0.1 shard_map.99.pair_ref
  33.3 1.7 %collective-permute-start.5 = (bf16[2,2,512,256]{3,2,1,0:T(8,128)(2,1)S(1)}, bf16[2,2,512,256]{3,2,1,0:T(8,128)(2,1)}, u32[]{:S(2)}, u32[]{:S(2)}) collective-permute-start(bf16[2,2,512,256]{3,2,1,0:T(8,128)(2,1)S(1)} %shard_map.99.pair_ref), channel_id=1, source_target_pairs={{0,64},{8,24},{16,80},{24,40},{32,96},{40,56},{48,112},{56,8},{64,... | collective-permute-start | bytes 3145736 | tf_op jit(solution)/shard_map/ppermute | solution.py:403
  35.0 0.0 collective-permute-done.3.a_ref
  35.0 1.6 shard_map.100
  36.6 2.1 %collective-permute-start.6 = (bf16[2,2,512,256]{3,2,1,0:T(8,128)(2,1)}, bf16[2,2,512,256]{3,2,1,0:T(8,128)(2,1)}, u32[]{:S(2)}, u32[]{:S(2)}) collective-permute-start(bf16[2,2,512,256]{3,2,1,0:T(8,128)(2,1)} %shard_map.100), channel_id=1, source_target_pairs={{0,64},{8,56},{16,80},{24,8},{32,96},{40,24},{48,112},{56,40},{64,... | collective-permute-start | bytes 3145736 | tf_op jit(solution)/shard_map/ppermute | solution.py:403
  38.7 3.2 %collective-permute-start.7 = (bf16[2,2,512,256]{3,2,1,0:T(8,128)(2,1)S(1)}, bf16[2,2,512,256]{3,2,1,0:T(8,128)(2,1)}, u32[]{:S(2)}, u32[]{:S(2)}) collective-permute-start(bf16[2,2,512,256]{3,2,1,0:T(8,128)(2,1)S(1)} %shard_map.99.pair_ref), channel_id=1, source_target_pairs={{8,40},{24,56},{40,8},{56,24},{72,104},{88,120},{104,72},{120,88},... | collective-permute-start | bytes 3145736 | tf_op jit(solution)/shard_map/ppermute | solution.py:403
  41.9 3.3 %shard_map.98.tiles = bf16[193,128,128]{2,1,0:T(8,128)(2,1)S(1)} custom-call(s32[12]{0:T(128)S(1)} %stack.51.meta_ref, bf16[192,128,128]{2,1,0:T(8,128)(2,1)} %bitcast.42, bf16[192,128,128]{2,1,0:T(8,128)(2,1)} %collective-permute-done.1.other_hbm), custom_call_target="tpu_custom_call" | custom-call | tf_op jit(solution)/shard_map/pallas_call | solution.py:327
  45.3 9.0 %collective-permute-done.5 = bf16[2,2,512,256]{3,2,1,0:T(8,128)(2,1)} collective-permute-done((bf16[2,2,512,256]{3,2,1,0:T(8,128)(2,1)S(1)}, bf16[2,2,512,256]{3,2,1,0:T(8,128)(2,1)}, u32[]{:S(2)}, u32[]{:S(2)}) %collective-permute-start.5) | collective-permute-done | bytes 1048608 | tf_op jit(solution)/shard_map/ppermute | solution.py:403
  54.3 11.3 %collective-permute-done.6 = bf16[2,2,512,256]{3,2,1,0:T(8,128)(2,1)} collective-permute-done((bf16[2,2,512,256]{3,2,1,0:T(8,128)(2,1)}, bf16[2,2,512,256]{3,2,1,0:T(8,128)(2,1)}, u32[]{:S(2)}, u32[]{:S(2)}) %collective-permute-start.6) | collective-permute-done | bytes 1048608 | tf_op jit(solution)/shard_map/ppermute | solution.py:403
  65.6 0.0 collective-permute-done.7
  65.6 7.0 %shard_map.101 = (bf16[4,512,256]{2,1,0:T(8,128)(2,1)S(1)}, bf16[4,512,256]{2,1,0:T(8,128)(2,1)S(1)}, bf16[8,2,16,32,256]{4,3,2,1,0:T(8,128)(2,1)S(1)}, bf16[193,128,128]{2,1,0:T(8,128)(2,1)S(1)}) custom-call(s32[12]{0:T(128)S(1)} %stack.51.meta_ref, s32[8,288]{1,0:T(8,128)S(1)} %get-tuple-element.48.plan_ref, bf16[193,128,128]{2,1,0:T(8,128)(2,1)S(1)} %shard_map.98.tiles, ...), custom_call_target="tpu_custom_call" | custom-call | tf_op jit(solution)/shard_map/pallas_call | solution.py:327
  72.6 0.8 collective-permute-start.8
  73.4 5.0 %shard_map.102 = (bf16[2,512,256]{2,1,0:T(8,128)(2,1)S(1)}, bf16[2,512,256]{2,1,0:T(8,128)(2,1)S(1)}, bf16[2,512,256]{2,1,0:T(8,128)(2,1)S(1)}, bf16[2,512,256]{2,1,0:T(8,128)(2,1)S(1)}) custom-call(s32[12]{0:T(128)S(1)} %stack.51.meta_ref, s32[8,288]{1,0:T(8,128)S(1)} %get-tuple-element.49.plan_ref, bf16[193,128,128]{2,1,0:T(8,128)(2,1)S(1)} %get-tuple-element.27.tiles, ...), custom_call_target="tpu_custom_call" | custom-call | tf_op jit(solution)/shard_map/pallas_call | solution.py:327
  78.4 0.0 copy-start
  78.4 0.1 collective-permute-start.10
  78.5 2.7 %collective-permute-start.11 = (bf16[2,512,256]{2,1,0:T(8,128)(2,1)S(1)}, bf16[2,512,256]{2,1,0:T(8,128)(2,1)S(1)}, u32[]{:S(2)}, u32[]{:S(2)}) collective-permute-start(bf16[2,512,256]{2,1,0:T(8,128)(2,1)S(1)} %get-tuple-element.35), channel_id=1, source_target_pairs={{0,3},{1,0},{2,1},{3,2},{4,7},{5,4},{6,5},{7,6},{8,11},{9,8},{10,9... | collective-permute-start | bytes 1572872 | tf_op jit(solution)/shard_map/ppermute | solution.py:432
  81.2 0.0 collective-permute-start.12
  81.2 16.7 %collective-permute-done.8.got_ref = bf16[4,512,256]{2,1,0:T(8,128)(2,1)S(1)} collective-permute-done((bf16[4,512,256]{2,1,0:T(8,128)(2,1)S(1)}, bf16[4,512,256]{2,1,0:T(8,128)(2,1)S(1)}, u32[]{:S(2)}, u32[]{:S(2)}) %collective-permute-start.8) | collective-permute-done | bytes 1048608 | tf_op jit(solution)/shard_map/ppermute | solution.py:433
  97.9 0.8 shard_map.103
  98.7 0.1 collective-permute-start.9
  98.8 2.7 %collective-permute-start.14 = (bf16[512,256]{1,0:T(8,128)(2,1)S(1)}, bf16[512,256]{1,0:T(8,128)(2,1)S(1)}, u32[]{:S(2)}, u32[]{:S(2)}) collective-permute-start(bf16[512,256]{1,0:T(8,128)(2,1)S(1)} %get-tuple-element.40), channel_id=1, source_target_pairs={{0,3},{1,0},{2,1},{3,2},{4,7},{5,4},{6,5},{7,6},{8,11},{9,8},{10,9... | collective-permute-start | bytes 786440 | tf_op jit(solution)/shard_map/ppermute | solution.py:438
  101.4 8.9 %collective-permute-done.9.a_ref = bf16[512,256]{1,0:T(8,128)(2,1)S(1)} collective-permute-done((bf16[512,256]{1,0:T(8,128)(2,1)S(1)}, bf16[512,256]{1,0:T(8,128)(2,1)S(1)}, u32[]{:S(2)}, u32[]{:S(2)}) %collective-permute-start.9) | collective-permute-done | bytes 262176 | tf_op jit(solution)/shard_map/ppermute | solution.py:438
  110.3 0.1 collective-permute-start.15
  110.4 0.0 collective-permute-done.10.a_ref
  110.4 0.0 collective-permute-done.11.b_ref
  110.4 0.8 shard_map.104
  111.2 0.1 collective-permute-start.13
  111.3 7.9 %collective-permute-done.15.c_ref = bf16[512,256]{1,0:T(8,128)(2,1)S(1)} collective-permute-done((bf16[512,256]{1,0:T(8,128)(2,1)S(1)}, bf16[512,256]{1,0:T(8,128)(2,1)S(1)}, u32[]{:S(2)}, u32[]{:S(2)}) %collective-permute-start.15) | collective-permute-done | bytes 262176 | tf_op jit(solution)/shard_map/ppermute | solution.py:438
  119.3 0.7 collective-permute-done.13.got0
  120.0 0.8 shard_map.105
  120.8 1.6 collective-permute-start.16
  122.4 1.1 constant_dynamic-slice_fusion.cotangent_ref
  123.5 0.5 collective-permute-done.16.got_ref
  124.0 2.3 %shard_map.106 = (bf16[512,512]{1,0:T(8,128)(2,1)}, bf16[512,512]{1,0:T(8,128)(2,1)S(1)}) custom-call(s32[12]{0:T(128)S(1)} %stack.51.meta_ref, f32[512,256]{1,0:T(8,128)S(1)} %get-tuple-element.42.mine_ref, f32[512,256]{1,0:T(8,128)S(1)} %collective-permute-done.16.got_ref, bf16[512,512]{1,0:T(8,128)(2,1)S(1)} %copy-done, ...), custom_call_target="tpu_custom_call" | custom-call | tf_op jit(solution)/shard_map/pallas_call | solution.py:327
  126.3 0.4 collective-permute-start.17
  126.6 1.5 collective-permute-done.17.other_slope_ref
  128.2 0.7 shard_map.107
  128.9 8.8 %all_to_all.20 = bf16[8,32,512]{2,1,0:T(8,128)(2,1)S(1)} all-to-all(bf16[8,32,512]{2,1,0:T(8,128)(2,1)S(1)} %bitcast.37), channel_id=1, replica_groups={{0,16,32,48,64,80,96,112},{8,24,40,56,72,88,104,120},{1,17,33,49,65,81,..., dimensions={0} | all-to-all | bytes 524288 | tf_op jit(solution)/shard_map/all_to_all | solution.py:299
  137.7 0.1 convert_element_type.11
  137.8 0.1 broadcast_in_dim.6
  137.9 15.2 %all_to_all.21 = f32[8,32,512]{2,1,0:T(8,128)S(1)} all-to-all(f32[8,32,512]{2,1,0:T(8,128)S(1)} %broadcast_in_dim.6), channel_id=1, replica_groups=mesh['row'=16,'col'=8] {'col'}, dimensions={0} | all-to-all | bytes 1048576 | tf_op jit(solution)/shard_map/all_to_all | solution.py:299
  153.1 9.7 %all_to_all.22 = bf16[8,32,512]{2,1,0:T(8,128)(2,1)S(1)} all-to-all(bf16[8,32,512]{2,1,0:T(8,128)(2,1)S(1)} %broadcast_in_dim.7), channel_id=1, replica_groups={{0,16,32,48,64,80,96,112},{8,24,40,56,72,88,104,120},{1,17,33,49,65,81,..., dimensions={0} | all-to-all | bytes 524288 | tf_op jit(solution)/shard_map/all_to_all | solution.py:299
  162.8 3.7 %collective-permute-start.18 = (bf16[256,512]{1,0:T(8,128)(2,1)S(1)}, bf16[256,512]{1,0:T(8,128)(2,1)S(1)}, u32[]{:S(2)}, u32[]{:S(2)}) collective-permute-start(bf16[256,512]{1,0:T(8,128)(2,1)S(1)} %bitcast.44), channel_id=1, source_target_pairs={{0,8},{8,0},{16,24},{24,16},{32,40},{40,32},{48,56},{56,48},{64,72... | collective-permute-start | bytes 786440 | tf_op jit(solution)/shard_map/ppermute | solution.py:464
  166.5 1.2 collective-permute-done.18
  167.7 0.1 broadcast_select_fusion.1
  167.7 1.1 maximum_convert_fusion
  (10 shorter events, 0.1 us)
Async XLA Ops:
  0.6 0.7 copy-start.1
  3.6 21.2 %collective-permute-start.1 = (bf16[192,128,128]{2,1,0:T(8,128)(2,1)}, bf16[192,128,128]{2,1,0:T(8,128)(2,1)}, u32[]{:S(2)}, u32[]{:S(2)}) collective-permute-start(bf16[192,128,128]{2,1,0:T(8,128)(2,1)} %bitcast.41), channel_id=1, source_target_pairs={{0,8},{8,0},{16,24},{24,16},{32,40},{40,32},{48,56},{56,48},{64,72... | collective-permute-start | bytes 18874376 | tf_op jit(solution)/shard_map/ppermute | solution.py:386
  5.1 19.2 %all-to-all-start = ((bf16[16,64,256]{2,1,0:T(8,128)(2,1)}), bf16[16,64,256]{2,1,0:T(8,128)(2,1)S(1)}, u32[]{:S(2)}, u32[]{:S(2)}) async-start(bf16[16,64,256]{2,1,0:T(8,128)(2,1)} %shard_map.96), calls=%async_computation | async-start | bytes 1048576 | tf_op jit(solution)/shard_map/all_to_all | solution.py:299
  12.9 0.7 copy-start.2
  13.6 0.7 copy-start.3
  14.7 10.1 %collective-permute-start = (s32[8,288]{1,0:T(8,128)S(1)}, s32[8,288]{1,0:T(8,128)S(1)}, u32[]{:S(2)}, u32[]{:S(2)}) collective-permute-start(s32[8,288]{1,0:T(8,128)S(1)} %shard_map.95), channel_id=1, source_target_pairs={{0,8},{8,0},{16,24},{24,16},{32,40},{40,32},{48,56},{56,48},{64,72... | collective-permute-start | bytes 27656 | tf_op jit(solution)/shard_map/ppermute | solution.py:378
  24.8 8.4 %collective-permute-start.2 = (bf16[2,512,256]{2,1,0:T(8,128)(2,1)S(1)}, bf16[2,512,256]{2,1,0:T(8,128)(2,1)S(1)}, u32[]{:S(2)}, u32[]{:S(2)}) collective-permute-start(bf16[2,512,256]{2,1,0:T(8,128)(2,1)S(1)} %shard_map.97.a_ref), channel_id=1, source_target_pairs={{0,16},{8,72},{16,32},{24,88},{32,48},{40,104},{48,0},{56,120},{64... | collective-permute-start | bytes 1572872 | tf_op jit(solution)/shard_map/ppermute | solution.py:403
  25.3 9.7 %collective-permute-start.3 = (bf16[2,512,256]{2,1,0:T(8,128)(2,1)S(1)}, bf16[2,512,256]{2,1,0:T(8,128)(2,1)S(1)}, u32[]{:S(2)}, u32[]{:S(2)}) collective-permute-start(bf16[2,512,256]{2,1,0:T(8,128)(2,1)S(1)} %shard_map.97.a_ref), channel_id=1, source_target_pairs={{0,48},{16,0},{32,16},{48,32},{64,112},{80,64},{96,80},{112,96},{1... | collective-permute-start | bytes 1572872 | tf_op jit(solution)/shard_map/ppermute | solution.py:403
  26.0 9.0 %collective-permute-start.4 = (bf16[2,512,256]{2,1,0:T(8,128)(2,1)S(1)}, bf16[2,512,256]{2,1,0:T(8,128)(2,1)S(1)}, u32[]{:S(2)}, u32[]{:S(2)}) collective-permute-start(bf16[2,512,256]{2,1,0:T(8,128)(2,1)S(1)} %shard_map.97.a_ref), channel_id=1, source_target_pairs={{0,32},{16,48},{32,0},{48,16},{64,96},{80,112},{96,64},{112,80},{1... | collective-permute-start | bytes 1572872 | tf_op jit(solution)/shard_map/ppermute | solution.py:403
  33.3 21.0 %collective-permute-start.5 = (bf16[2,2,512,256]{3,2,1,0:T(8,128)(2,1)S(1)}, bf16[2,2,512,256]{3,2,1,0:T(8,128)(2,1)}, u32[]{:S(2)}, u32[]{:S(2)}) collective-permute-start(bf16[2,2,512,256]{3,2,1,0:T(8,128)(2,1)S(1)} %shard_map.99.pair_ref), channel_id=1, source_target_pairs={{0,64},{8,24},{16,80},{24,40},{32,96},{40,56},{48,112},{56,8},{64,... | collective-permute-start | bytes 3145736 | tf_op jit(solution)/shard_map/ppermute | solution.py:403
  36.6 29.0 %collective-permute-start.6 = (bf16[2,2,512,256]{3,2,1,0:T(8,128)(2,1)}, bf16[2,2,512,256]{3,2,1,0:T(8,128)(2,1)}, u32[]{:S(2)}, u32[]{:S(2)}) collective-permute-start(bf16[2,2,512,256]{3,2,1,0:T(8,128)(2,1)} %shard_map.100), channel_id=1, source_target_pairs={{0,64},{8,56},{16,80},{24,8},{32,96},{40,24},{48,112},{56,40},{64,... | collective-permute-start | bytes 3145736 | tf_op jit(solution)/shard_map/ppermute | solution.py:403
  38.7 26.8 %collective-permute-start.7 = (bf16[2,2,512,256]{3,2,1,0:T(8,128)(2,1)S(1)}, bf16[2,2,512,256]{3,2,1,0:T(8,128)(2,1)}, u32[]{:S(2)}, u32[]{:S(2)}) collective-permute-start(bf16[2,2,512,256]{3,2,1,0:T(8,128)(2,1)S(1)} %shard_map.99.pair_ref), channel_id=1, source_target_pairs={{8,40},{24,56},{40,8},{56,24},{72,104},{88,120},{104,72},{120,88},... | collective-permute-start | bytes 3145736 | tf_op jit(solution)/shard_map/ppermute | solution.py:403
  72.6 25.3 %collective-permute-start.8 = (bf16[4,512,256]{2,1,0:T(8,128)(2,1)S(1)}, bf16[4,512,256]{2,1,0:T(8,128)(2,1)S(1)}, u32[]{:S(2)}, u32[]{:S(2)}) collective-permute-start(bf16[4,512,256]{2,1,0:T(8,128)(2,1)S(1)} %get-tuple-element.31), channel_id=1, source_target_pairs={{0,4},{1,5},{2,6},{3,7},{4,0},{5,1},{6,2},{7,3},{8,12},{9,13},{10,... | collective-permute-start | bytes 3145736 | tf_op jit(solution)/shard_map/ppermute | solution.py:433
  78.4 45.5 %copy-start = (bf16[512,512]{1,0:T(8,128)(2,1)S(1)}, bf16[512,512]{1,0:T(8,128)(2,1)}, u32[]{:S(2)}) copy-start(bf16[512,512]{1,0:T(8,128)(2,1)} %weight_ref.1) | copy-start | bytes 1572868
  78.4 32.0 %collective-permute-start.10 = (bf16[2,512,256]{2,1,0:T(8,128)(2,1)S(1)}, bf16[2,512,256]{2,1,0:T(8,128)(2,1)S(1)}, u32[]{:S(2)}, u32[]{:S(2)}) collective-permute-start(bf16[2,512,256]{2,1,0:T(8,128)(2,1)S(1)} %get-tuple-element.34), channel_id=1, source_target_pairs={{0,1},{1,2},{2,3},{3,0},{4,5},{5,6},{6,7},{7,4},{8,9},{9,10},{10,1... | collective-permute-start | bytes 1572872 | tf_op jit(solution)/shard_map/ppermute | solution.py:432
  78.5 31.9 %collective-permute-start.11 = (bf16[2,512,256]{2,1,0:T(8,128)(2,1)S(1)}, bf16[2,512,256]{2,1,0:T(8,128)(2,1)S(1)}, u32[]{:S(2)}, u32[]{:S(2)}) collective-permute-start(bf16[2,512,256]{2,1,0:T(8,128)(2,1)S(1)} %get-tuple-element.35), channel_id=1, source_target_pairs={{0,3},{1,0},{2,1},{3,2},{4,7},{5,4},{6,5},{7,6},{8,11},{9,8},{10,9... | collective-permute-start | bytes 1572872 | tf_op jit(solution)/shard_map/ppermute | solution.py:432
  81.2 29.2 %collective-permute-start.12 = (bf16[2,512,256]{2,1,0:T(8,128)(2,1)S(1)}, bf16[2,512,256]{2,1,0:T(8,128)(2,1)S(1)}, u32[]{:S(2)}, u32[]{:S(2)}) collective-permute-start(bf16[2,512,256]{2,1,0:T(8,128)(2,1)S(1)} %get-tuple-element.36), channel_id=1, source_target_pairs={{0,2},{1,3},{2,0},{3,1},{4,6},{5,7},{6,4},{7,5},{8,10},{9,11},{10,... | collective-permute-start | bytes 1572872 | tf_op jit(solution)/shard_map/ppermute | solution.py:432
  98.7 11.6 %collective-permute-start.9 = (bf16[512,256]{1,0:T(8,128)(2,1)S(1)}, bf16[512,256]{1,0:T(8,128)(2,1)S(1)}, u32[]{:S(2)}, u32[]{:S(2)}) collective-permute-start(bf16[512,256]{1,0:T(8,128)(2,1)S(1)} %get-tuple-element.32), channel_id=1, source_target_pairs={{0,1},{1,2},{2,3},{3,0},{4,5},{5,6},{6,7},{7,4},{8,9},{9,10},{10,1... | collective-permute-start | bytes 786440 | tf_op jit(solution)/shard_map/ppermute | solution.py:438
  98.8 12.6 %collective-permute-start.14 = (bf16[512,256]{1,0:T(8,128)(2,1)S(1)}, bf16[512,256]{1,0:T(8,128)(2,1)S(1)}, u32[]{:S(2)}, u32[]{:S(2)}) collective-permute-start(bf16[512,256]{1,0:T(8,128)(2,1)S(1)} %get-tuple-element.40), channel_id=1, source_target_pairs={{0,3},{1,0},{2,1},{3,2},{4,7},{5,4},{6,5},{7,6},{8,11},{9,8},{10,9... | collective-permute-start | bytes 786440 | tf_op jit(solution)/shard_map/ppermute | solution.py:438
  110.3 9.0 %collective-permute-start.15 = (bf16[512,256]{1,0:T(8,128)(2,1)S(1)}, bf16[512,256]{1,0:T(8,128)(2,1)S(1)}, u32[]{:S(2)}, u32[]{:S(2)}) collective-permute-start(bf16[512,256]{1,0:T(8,128)(2,1)S(1)} %get-tuple-element.41), channel_id=1, source_target_pairs={{0,2},{1,3},{2,0},{3,1},{4,6},{5,7},{6,4},{7,5},{8,10},{9,11},{10,... | collective-permute-start | bytes 786440 | tf_op jit(solution)/shard_map/ppermute | solution.py:438
  111.2 8.8 %collective-permute-start.13 = (bf16[512,256]{1,0:T(8,128)(2,1)S(1)}, bf16[512,256]{1,0:T(8,128)(2,1)S(1)}, u32[]{:S(2)}, u32[]{:S(2)}) collective-permute-start(bf16[512,256]{1,0:T(8,128)(2,1)S(1)} %get-tuple-element.38), channel_id=1, source_target_pairs={{0,4},{1,5},{2,6},{3,7},{4,0},{5,1},{6,2},{7,3},{8,12},{9,13},{10,... | collective-permute-start | bytes 786440 | tf_op jit(solution)/shard_map/ppermute | solution.py:442
  120.8 3.2 %collective-permute-start.16 = (f32[512,256]{1,0:T(8,128)S(1)}, f32[512,256]{1,0:T(8,128)S(1)}, u32[]{:S(2)}, u32[]{:S(2)}) collective-permute-start(f32[512,256]{1,0:T(8,128)S(1)} %get-tuple-element.43.other_ref), channel_id=1, source_target_pairs={{0,8},{8,0},{16,24},{24,16},{32,40},{40,32},{48,56},{56,48},{64,72... | collective-permute-start | bytes 1572872 | tf_op jit(solution)/shard_map/ppermute | solution.py:446
  126.3 1.9 %collective-permute-start.17 = (bf16[512,512]{1,0:T(8,128)(2,1)S(1)}, bf16[512,512]{1,0:T(8,128)(2,1)S(1)}, u32[]{:S(2)}, u32[]{:S(2)}) collective-permute-start(bf16[512,512]{1,0:T(8,128)(2,1)S(1)} %get-tuple-element.45.slope_ref), channel_id=1, source_target_pairs={{0,8},{8,0},{16,24},{24,16},{32,40},{40,32},{48,56},{56,48},{64,72... | collective-permute-start | bytes 1572872 | tf_op jit(solution)/shard_map/ppermute | solution.py:453
  162.8 4.9 %collective-permute-start.18 = (bf16[256,512]{1,0:T(8,128)(2,1)S(1)}, bf16[256,512]{1,0:T(8,128)(2,1)S(1)}, u32[]{:S(2)}, u32[]{:S(2)}) collective-permute-start(bf16[256,512]{1,0:T(8,128)(2,1)S(1)} %bitcast.44), channel_id=1, source_target_pairs={{0,8},{8,0},{16,24},{24,16},{32,40},{40,32},{48,56},{56,48},{64,72... | collective-permute-start | bytes 786440 | tf_op jit(solution)/shard_map/ppermute | solution.py:464

commit v10 on v9

--- a/solution.py
+++ b/solution.py
@@ -13,6 +13,7 @@
 PER_PEER = 4
 HALF = 256
 CHIPS = 8
+STEPS = (0, 1, 3, 2)
 BLOCKS = 7
 SLOT_CAP = 192
 ROW_TILES = 32
@@ -173,11 +174,10 @@
     return rows.reshape(SLOTS, HALF)
 
 
-def tiles_y_kernel(meta_ref, plan_ref, tiles, own_hbm, other_hbm, *refs):
-    blocks, (keep_ref, send_ref, source, next_tiles) = refs[:BLOCKS], refs[BLOCKS:-3]
-    total, sems, tiles_sem = refs[-3:]
-    core, yh = meta_ref[0], meta_ref[2]
-
+def tiles_kernel(meta_ref, plan0_ref, plan1_ref, tiles1, own_hbm, other_hbm, *refs):
+    blocks, outs = refs[:BLOCKS], refs[BLOCKS : BLOCKS + 4]
+    source, tiles0, total, sems, tiles_sem = refs[BLOCKS + 4 :]
+    core, x, yh = meta_ref[0], meta_ref[1], meta_ref[2]
     own, r1, r2, r3, s1, s3, s2 = blocks
     shared = [(own, 0), (r1, 0), (s1, 0), (s1, 1), (s3, 0), (s3, 1)]
 
@@ -197,52 +197,59 @@
 
     for k in range(CHIPS):
         fetch(shared[0], k).wait()
-    coming = start_tiles(0, core, own_hbm, other_hbm, next_tiles, tiles_sem)
-    add_tiles(plan_ref, tiles, source, total)
-    for out, to in ((send_ref, 1 - yh), (keep_ref, yh)):
-        for x in range(4):
-            out[x] = narrow_block(total, to, x)
-    coming.wait()
-
-
-def tiles_x_kernel(meta_ref, plan_ref, tiles, source, *refs):
-    outs, total = refs[:4], refs[4]
-    x = meta_ref[1]
-    add_tiles(plan_ref, tiles, source, total)
-    for k, out in enumerate(outs):
-        for yh in range(2):
-            out[yh] = narrow_block(total, yh, (x + k) & 3)
-
-
-def x_summed_kernel(meta_ref, own_ref, a_ref, b_ref, c_ref, keep_ref, send_ref):
-    yh = meta_ref[2]
-
-    def summed(k):
-        pair = own_ref[k].astype(F32) + a_ref[k].astype(F32)
-        return pair + (b_ref[k].astype(F32) + c_ref[k].astype(F32))
-
-    keep_ref[...] = summed(yh)
-    send_ref[...] = summed(1 - yh).astype(BF16)
-
-
-def y_summed_kernel(meta_ref, own_ref, got_ref, keep_ref, a_ref, b_ref, c_ref):
-    x = meta_ref[1]
-
-    def summed(k):
-        return own_ref[k].astype(F32) + got_ref[k].astype(F32)
-
-    keep_ref[...] = summed(x)
-    for k, out in ((1, a_ref), (2, b_ref), (3, c_ref)):
-        out[...] = summed((x + k) & 3).astype(BF16)
-
-
-def sums_kernel(meta_ref, keep0, got0, keep1, a_ref, b_ref, c_ref, mine_ref, send_ref):
+    coming = start_tiles(0, core, own_hbm, other_hbm, tiles0, tiles_sem)
+    for part, plan_ref, tiles in ((1, plan1_ref, tiles1), (0, plan0_ref, tiles0)):
+        if part == 0:
+            coming.wait()
+        add_tiles(plan_ref, tiles, source, total)
+
+        @pl.when(core == 0)
+        def _():
+            for k, out in enumerate(outs):
+                for to in range(2):
+                    out[part * 2 + to] = narrow_block(total, to, (x + STEPS[k]) & 3)
+
+        @pl.when(core != 0)
+        def _():
+            for to in range(4):
+                outs[0][part * 4 + to] = narrow_block(total, yh, to)
+                outs[1 + part][to] = narrow_block(total, 1 - yh, to)
+
+
+def first_sums_kernel(meta_ref, kept_ref, a_ref, b_ref, c_ref, keep_ref, *sends):
+    core, x, yh = meta_ref[0], meta_ref[1], meta_ref[2]
+
+    @pl.when(core == 0)
+    def _():
+        for part in range(2):
+            for to, out in ((yh, keep_ref), (1 - yh, sends[0])):
+                k = part * 2 + to
+                pair = kept_ref[k].astype(F32) + a_ref[k].astype(F32)
+                pair = pair + (b_ref[k].astype(F32) + c_ref[k].astype(F32))
+                out[part] = pair.astype(out.dtype)
+
+    @pl.when(core != 0)
+    def _():
+        for part, got in enumerate((a_ref, b_ref)):
+            for step, out in zip(STEPS, (keep_ref, *sends)):
+                k = (x + step) & 3
+                pair = kept_ref[part * 4 + k].astype(F32) + got[k].astype(F32)
+                out[part] = pair.astype(out.dtype)
+
+
+def sums_kernel(meta_ref, keep_ref, a_ref, b_ref, c_ref, mine_ref, send_ref):
     core = meta_ref[0]
-    first = keep0[...] + got0[...].astype(F32)
-    second = keep1[...] + a_ref[...].astype(F32)
-    second = second + (b_ref[...].astype(F32) + c_ref[...].astype(F32))
-    mine_ref[...] = jnp.where(core == 0, first, second)
-    send_ref[...] = jnp.where(core == 0, second, first)
+
+    @pl.when(core == 0)
+    def _():
+        for part, out in ((0, mine_ref), (1, send_ref)):
+            out[...] = keep_ref[part] + a_ref[part].astype(F32)
+
+    @pl.when(core != 0)
+    def _():
+        for part, out in ((1, mine_ref), (0, send_ref)):
+            pair = keep_ref[part] + a_ref[part].astype(F32)
+            out[...] = pair + (b_ref[part].astype(F32) + c_ref[part].astype(F32))
 
 
 def two_parts(value):
@@ -287,12 +294,15 @@
     return pairs
 
 
-def x_moves(k):
-    return [(yh * 4 + x, yh * 4 + (x + k) % 4) for yh in range(2) for x in range(4)]
-
-
-def y_moves():
-    return [(yh * 4 + x, (1 - yh) * 4 + x) for yh in range(2) for x in range(4)]
+def col_moves(move0, move1):
+    pairs = []
+    for row in range(N_ROW):
+        move = (move0, move1)[row % 2]
+        if move is not None:
+            for col in range(N_COL):
+                yh, x = move(col // 4, col % 4)
+                pairs.append((row * N_COL + col, row * N_COL + yh * 4 + x))
+    return pairs
 
 
 def exchange(parts, axis, groups=None):
@@ -402,9 +412,9 @@
 
         return lax.ppermute(block, "row", row_moves(move))
 
+    r3 = hop(own, (0, 2), None)
     r1 = hop(own, (0, 1), (1, 0))
     r2 = hop(own, (0, 3), None)
-    r3 = hop(own, (0, 2), None)
     both = held(2, 2, SLOTS, HALF)
     pair = call(pair_kernel, [vmem] * 2, both)(own, r1)
     s1 = hop(pair, (1, 0), (0, 1))
@@ -415,34 +425,43 @@
     blocks = [b.reshape(1, 2, *shape) for b in (own, r1, r2, r3)]
     blocks += [b.reshape(2, 2, *shape) for b in (s1, s3, s2)]
 
-    total = pltpu.VMEM((ROW_TILES, TILE, HALF), F32)
-    source = held(CHIPS, 2, N_ROW, N_COL * PER_PEER, HALF)
-    keep1, send1, source, tiles0 = call(
-        tiles_y_kernel,
-        [smem, smem, vmem, pinned, pinned] + [hbm] * BLOCKS,
-        [held(4, SLOTS, HALF), held(4, SLOTS, HALF), source, staged],
-        [total, pltpu.SemaphoreType.DMA((CHIPS,)), pltpu.SemaphoreType.DMA],
-    )(meta, plans[1], tiles1, tiles, other_tiles, *blocks)
-    row0 = call(
-        tiles_x_kernel,
-        [smem, smem, vmem, vmem],
-        [held(2, SLOTS, HALF)] * 4,
-        [total],
-    )(meta, plans[0], tiles0, source)
-    got0 = [lax.ppermute(row0[k], "col", x_moves(k)) for k in (1, 3, 2)]
-    got1 = lax.ppermute(send1, "col", y_moves())
-    wide, narrow = held(SLOTS, HALF, dtype=F32), held(SLOTS, HALF)
-    keep1, *send1 = call(y_summed_kernel, [smem] + [vmem] * 2, [wide] + [narrow] * 3)(
-        meta, keep1, got1
-    )
-    got1 = [lax.ppermute(send1[k - 1], "col", x_moves(k)) for k in (1, 3, 2)]
-    keep0, send0 = call(x_summed_kernel, [smem] + [vmem] * 4, [wide, narrow])(
-        meta, after(row0[0], got1[0]), *got0
-    )
-    got0 = lax.ppermute(send0, "col", y_moves())
-    mine, others = call(sums_kernel, [smem] + [vmem] * 6, [wide] * 2)(
-        meta, keep0, got0, keep1, *got1
-    )
+    four = held(4, SLOTS, HALF)
+    kept, *sends = call(
+        tiles_kernel,
+        [smem, smem, smem, vmem, pinned, pinned] + [hbm] * BLOCKS,
+        [held(8, SLOTS, HALF), four, four, four],
+        [
+            pltpu.VMEM((CHIPS, 2, N_ROW, N_COL * PER_PEER, HALF), BF16),
+            pltpu.VMEM((SLOT_CAP + 1, TILE, TILE), BF16),
+            pltpu.VMEM((ROW_TILES, TILE, HALF), F32),
+            pltpu.SemaphoreType.DMA((CHIPS,)),
+            pltpu.SemaphoreType.DMA,
+        ],
+        limit=24,
+    )(meta, *plans, tiles1, tiles, other_tiles, *blocks)
+
+    along_x = [lambda yh, x, k=k: (yh, (x + k) % 4) for k in STEPS]
+    along_y = lambda yh, x: (1 - yh, x)
+    got = [
+        lax.ppermute(block, ("row", "col"), col_moves(*moves))
+        for block, moves in zip(
+            sends, ((along_x[1], along_y), (along_x[2], along_y), (along_x[3], None))
+        )
+    ]
+    two = held(2, SLOTS, HALF)
+    keep, *sends = call(
+        first_sums_kernel,
+        [smem] + [vmem] * 4,
+        [held(2, SLOTS, HALF, dtype=F32), two, two, two],
+    )(meta, kept, *got)
+    got = [
+        lax.ppermute(block, ("row", "col"), col_moves(*moves))
+        for block, moves in zip(
+            sends, ((along_y, along_x[1]), (None, along_x[2]), (None, along_x[3]))
+        )
+    ]
+    wide = held(SLOTS, HALF, dtype=F32)
+    mine, others = call(sums_kernel, [smem] + [vmem] * 4, [wide] * 2)(meta, keep, *got)
     theirs = lax.ppermute(others, "row", swap)
     cotangent = lax.dynamic_slice_in_dim(out_cotangent, col * SLOTS, SLOTS, 0)
     activations, slope = call(

time: 169 us -> 186 us (1.10)
  starting transfers between devices: 29.9 us -> 41.4 us
  blocking collectives: 33.6 us -> 43.7 us
  Pallas kernels: 25.6 us -> 20.7 us
    all_to_all x3, blocking collectives: 33.6 us -> 43.7 us  [exchange(): lax.all_to_all(parts, axis, split_axis=0, concat_axis=0, axis_index_group...]
    ppermute x8 -> x6, starting transfers between devices: 6.53 us -> 13 us  [shards(): lax.ppermute(block, ('row', 'col'), col_moves(*moves))]
    ppermute x1, starting transfers between devices: 1.63 us -> 6.73 us  [shards(): theirs = lax.ppermute(others, 'row', swap)]
    pallas_call x13 -> x11, Pallas kernels: 25.6 us -> 20.7 us  [run(): return made(*held)]
    ppermute x8 -> x6, waiting for transfers between devices: 34.2 us -> 33.2 us  [shards(): lax.ppermute(block, ('row', 'col'), col_moves(*moves))]
  transfers between devices with their start and end apart: 20 -> 18, of which waited for: 11 -> 12; matrix products, arithmetic and copies ran while one was open for 1% -> 1% of each run, Pallas kernels for 7% -> 2%
where the time goes in v10:
time: 186 us; the launch traced here: 185 us
  waiting for transfers between devices  73.1 us (39%)
  blocking collectives  43.7 us (23%)
  starting transfers between devices  41.4 us (22%)
  Pallas kernels  20.7 us (11%)
  local copies, waits for them, and re-layouts  3.27 us (2%)
    all_to_all x3, blocking collectives, exchange(): lax.all_to_all(parts, axis, split_axis=0, concat_axis=0, axis_index_group...  43.7 us
    ppermute x6, waiting for transfers between devices, shards(): lax.ppermute(block, ('row', 'col'), col_moves(*moves))  33.2 us
    ppermute x6, waiting for transfers between devices, hop(): return lax.ppermute(block, 'row', row_moves(move))  27.3 us
    pallas_call x11, Pallas kernels, run(): return made(*held)  20.7 us
    ppermute x6, starting transfers between devices, shards(): lax.ppermute(block, ('row', 'col'), col_moves(*moves))  13 us
    all_to_all x1, waiting for transfers between devices, exchange(): lax.all_to_all(parts, axis, split_axis=0, concat_axis=0, axis_index_group...  9.51 us
    ppermute x6, starting transfers between devices, hop(): return lax.ppermute(block, 'row', row_moves(move))  8.8 us
    all_to_all x1, starting transfers between devices, exchange(): lax.all_to_all(parts, axis, split_axis=0, concat_axis=0, axis_index_group...  7.14 us
  transfers between devices with their start and end apart: 18, of which 12 were waited for; matrix products, arithmetic and copies ran while one was open for 1% of the time, Pallas kernels for 2%

profile of v10, /device:TPU:1, one launch (start us, length us, event | category | flops | bytes accessed | tf_op | source)
XLA Modules:
  0.0 185.1 jit_solution(1519849430498528400)
XLA Ops:
  0.6 0.0 copy-start.1
  0.6 0.7 copy-done.1
  1.3 2.3 %shard_map.96 = bf16[16,64,256]{2,1,0:T(8,128)(2,1)} custom-call(s32[1,512]{1,0:T(1,128)S(1)} %bitcast.38, bf16[512,512]{1,0:T(8,128)(2,1)} %features_hbm.1), custom_call_target="tpu_custom_call" | custom-call | tf_op jit(solution)/shard_map/pallas_call | solution.py:337
  3.6 1.5 collective-permute-start.1
  5.1 7.1 %all-to-all-start = ((bf16[16,64,256]{2,1,0:T(8,128)(2,1)}), bf16[16,64,256]{2,1,0:T(8,128)(2,1)S(1)}, u32[]{:S(2)}, u32[]{:S(2)}) async-start(bf16[16,64,256]{2,1,0:T(8,128)(2,1)} %shard_map.96), calls=%async_computation | async-start | bytes 1048576 | tf_op jit(solution)/shard_map/all_to_all | solution.py:309
  12.9 0.0 copy-start.2
  12.9 0.7 copy-done.2
  13.6 0.0 copy-start.3
  13.6 0.7 copy-done.3
  14.3 0.5 shard_map.95
  14.7 0.1 collective-permute-start
  14.8 9.5 %all-to-all-done.arrived_ref = bf16[16,64,256]{2,1,0:T(8,128)(2,1)S(1)} async-done(((bf16[16,64,256]{2,1,0:T(8,128)(2,1)}), bf16[16,64,256]{2,1,0:T(8,128)(2,1)S(1)}, u32[]{:S(2)}, u32[]{:S(2)}) %all-to-all-start) | async-done | bytes 524320 | tf_op jit(solution)/shard_map/all_to_all | solution.py:309
  24.4 0.4 shard_map.97.a_ref
  24.8 0.0 collective-permute-done
  24.8 0.0 collective-permute-done.1.other_hbm
  24.8 0.5 collective-permute-start.2
  25.3 0.7 collective-permute-start.3
  26.0 0.7 collective-permute-start.4
  26.8 0.1 stack.51.meta_ref
  26.9 6.3 %collective-permute-done.2.b_ref = bf16[2,512,256]{2,1,0:T(8,128)(2,1)S(1)} collective-permute-done((bf16[2,512,256]{2,1,0:T(8,128)(2,1)S(1)}, bf16[2,512,256]{2,1,0:T(8,128)(2,1)S(1)}, u32[]{:S(2)}, u32[]{:S(2)}) %collective-permute-start.2) | collective-permute-done | bytes 524320 | tf_op jit(solution)/shard_map/ppermute | solution.py:413
  33.2 0.1 shard_map.99.pair_ref
  33.3 0.0 collective-permute-done.3.a_ref
  33.3 0.0 collective-permute-done.4.b_ref
  33.3 1.6 shard_map.100
  34.9 3.8 %collective-permute-start.6 = (bf16[2,2,512,256]{3,2,1,0:T(8,128)(2,1)}, bf16[2,2,512,256]{3,2,1,0:T(8,128)(2,1)}, u32[]{:S(2)}, u32[]{:S(2)}) collective-permute-start(bf16[2,2,512,256]{3,2,1,0:T(8,128)(2,1)} %shard_map.100), channel_id=1, source_target_pairs={{0,64},{8,56},{16,80},{24,8},{32,96},{40,24},{48,112},{56,40},{64,... | collective-permute-start | bytes 3145736 | tf_op jit(solution)/shard_map/ppermute | solution.py:413
  38.7 0.0 collective-permute-start.5
  38.7 3.2 %collective-permute-start.7 = (bf16[2,2,512,256]{3,2,1,0:T(8,128)(2,1)S(1)}, bf16[2,2,512,256]{3,2,1,0:T(8,128)(2,1)}, u32[]{:S(2)}, u32[]{:S(2)}) collective-permute-start(bf16[2,2,512,256]{3,2,1,0:T(8,128)(2,1)S(1)} %shard_map.99.pair_ref), channel_id=1, source_target_pairs={{8,40},{24,56},{40,8},{56,24},{72,104},{88,120},{104,72},{120,88},... | collective-permute-start | bytes 3145736 | tf_op jit(solution)/shard_map/ppermute | solution.py:413
  41.9 3.3 %shard_map.98.tiles1 = bf16[193,128,128]{2,1,0:T(8,128)(2,1)S(1)} custom-call(s32[12]{0:T(128)S(1)} %stack.51.meta_ref, bf16[192,128,128]{2,1,0:T(8,128)(2,1)} %bitcast.42, bf16[192,128,128]{2,1,0:T(8,128)(2,1)} %collective-permute-done.1.other_hbm), custom_call_target="tpu_custom_call" | custom-call | tf_op jit(solution)/shard_map/pallas_call | solution.py:337
  45.2 20.8 %collective-permute-done.6 = bf16[2,2,512,256]{3,2,1,0:T(8,128)(2,1)} collective-permute-done((bf16[2,2,512,256]{3,2,1,0:T(8,128)(2,1)}, bf16[2,2,512,256]{3,2,1,0:T(8,128)(2,1)}, u32[]{:S(2)}, u32[]{:S(2)}) %collective-permute-start.6) | collective-permute-done | bytes 1048608 | tf_op jit(solution)/shard_map/ppermute | solution.py:413
  66.1 0.1 collective-permute-done.5
  66.2 0.0 collective-permute-done.7
  66.2 7.7 %shard_map.101 = (bf16[8,512,256]{2,1,0:T(8,128)(2,1)S(1)}, bf16[4,512,256]{2,1,0:T(8,128)(2,1)S(1)}, bf16[4,512,256]{2,1,0:T(8,128)(2,1)S(1)}, bf16[4,512,256]{2,1,0:T(8,128)(2,1)S(1)}) custom-call(s32[12]{0:T(128)S(1)} %stack.51.meta_ref, s32[8,288]{1,0:T(8,128)S(1)} %get-tuple-element.35.plan0_ref, s32[8,288]{1,0:T(8,128)S(1)} %get-tuple-element.34.plan1_ref, ...), custom_call_target="tpu_custom_call" | custom-call | tf_op jit(solution)/shard_map/pallas_call | solution.py:337
  73.9 0.0 copy-start
  73.9 0.9 collective-permute-start.10
  74.8 3.3 %collective-permute-start.8 = (bf16[4,512,256]{2,1,0:T(8,128)(2,1)S(1)}, bf16[4,512,256]{2,1,0:T(8,128)(2,1)S(1)}, u32[]{:S(2)}, u32[]{:S(2)}) collective-permute-start(bf16[4,512,256]{2,1,0:T(8,128)(2,1)S(1)} %get-tuple-element.21), channel_id=1, source_target_pairs={{0,1},{1,2},{2,3},{3,0},{4,5},{5,6},{6,7},{7,4},{8,12},{9,13},{10,... | collective-permute-start | bytes 3145736 | tf_op jit(solution)/shard_map/ppermute | solution.py:446
  78.1 0.1 collective-permute-start.9
  78.2 0.0 collective-permute-done.10.c_ref
  78.2 12.4 %collective-permute-done.8.a_ref = bf16[4,512,256]{2,1,0:T(8,128)(2,1)S(1)} collective-permute-done((bf16[4,512,256]{2,1,0:T(8,128)(2,1)S(1)}, bf16[4,512,256]{2,1,0:T(8,128)(2,1)S(1)}, u32[]{:S(2)}, u32[]{:S(2)}) %collective-permute-start.8) | collective-permute-done | bytes 1048608 | tf_op jit(solution)/shard_map/ppermute | solution.py:446
  90.6 10.9 %collective-permute-done.9.b_ref = bf16[4,512,256]{2,1,0:T(8,128)(2,1)S(1)} collective-permute-done((bf16[4,512,256]{2,1,0:T(8,128)(2,1)S(1)}, bf16[4,512,256]{2,1,0:T(8,128)(2,1)S(1)}, u32[]{:S(2)}, u32[]{:S(2)}) %collective-permute-start.9) | collective-permute-done | bytes 1048608 | tf_op jit(solution)/shard_map/ppermute | solution.py:446
  101.6 1.0 shard_map.102
  102.6 3.1 %collective-permute-start.11 = (bf16[2,512,256]{2,1,0:T(8,128)(2,1)S(1)}, bf16[2,512,256]{2,1,0:T(8,128)(2,1)S(1)}, u32[]{:S(2)}, u32[]{:S(2)}) collective-permute-start(bf16[2,512,256]{2,1,0:T(8,128)(2,1)S(1)} %get-tuple-element.25), channel_id=1, source_target_pairs={{0,4},{1,5},{2,6},{3,7},{4,0},{5,1},{6,2},{7,3},{8,9},{9,10},{10,1... | collective-permute-start | bytes 1572872 | tf_op jit(solution)/shard_map/ppermute | solution.py:458
  105.7 1.9 %collective-permute-start.12 = (bf16[2,512,256]{2,1,0:T(8,128)(2,1)S(1)}, bf16[2,512,256]{2,1,0:T(8,128)(2,1)S(1)}, u32[]{:S(2)}, u32[]{:S(2)}) collective-permute-start(bf16[2,512,256]{2,1,0:T(8,128)(2,1)S(1)} %get-tuple-element.26), channel_id=1, source_target_pairs={{8,11},{9,8},{10,9},{11,10},{12,15},{13,12},{14,13},{15,14},{24,27... | collective-permute-start | bytes 1572872 | tf_op jit(solution)/shard_map/ppermute | solution.py:458
  107.6 3.7 %collective-permute-start.13 = (bf16[2,512,256]{2,1,0:T(8,128)(2,1)S(1)}, bf16[2,512,256]{2,1,0:T(8,128)(2,1)S(1)}, u32[]{:S(2)}, u32[]{:S(2)}) collective-permute-start(bf16[2,512,256]{2,1,0:T(8,128)(2,1)S(1)} %get-tuple-element.27), channel_id=1, source_target_pairs={{8,10},{9,11},{10,8},{11,9},{12,14},{13,15},{14,12},{15,13},{24,26... | collective-permute-start | bytes 1572872 | tf_op jit(solution)/shard_map/ppermute | solution.py:458
  111.3 4.2 %collective-permute-done.11.a_ref = bf16[2,512,256]{2,1,0:T(8,128)(2,1)S(1)} collective-permute-done((bf16[2,512,256]{2,1,0:T(8,128)(2,1)S(1)}, bf16[2,512,256]{2,1,0:T(8,128)(2,1)S(1)}, u32[]{:S(2)}, u32[]{:S(2)}) %collective-permute-start.11) | collective-permute-done | bytes 524320 | tf_op jit(solution)/shard_map/ppermute | solution.py:458
  115.5 1.6 collective-permute-done.12.b_ref
  117.1 4.0 %collective-permute-done.13.c_ref = bf16[2,512,256]{2,1,0:T(8,128)(2,1)S(1)} collective-permute-done((bf16[2,512,256]{2,1,0:T(8,128)(2,1)S(1)}, bf16[2,512,256]{2,1,0:T(8,128)(2,1)S(1)}, u32[]{:S(2)}, u32[]{:S(2)}) %collective-permute-start.13) | collective-permute-done | bytes 524320 | tf_op jit(solution)/shard_map/ppermute | solution.py:458
  121.2 0.8 shard_map.103
  121.9 6.7 %collective-permute-start.14 = (f32[512,256]{1,0:T(8,128)S(1)}, f32[512,256]{1,0:T(8,128)S(1)}, u32[]{:S(2)}, u32[]{:S(2)}) collective-permute-start(f32[512,256]{1,0:T(8,128)S(1)} %get-tuple-element.29.other_ref), channel_id=1, source_target_pairs={{0,8},{8,0},{16,24},{24,16},{32,40},{40,32},{48,56},{56,48},{64,72... | collective-permute-start | bytes 1572872 | tf_op jit(solution)/shard_map/ppermute | solution.py:465
  128.6 1.1 constant_dynamic-slice_fusion.cotangent_ref
  129.7 0.5 collective-permute-done.14.got_ref
  130.2 0.0 copy-done
  130.2 2.3 %shard_map.104 = (bf16[512,512]{1,0:T(8,128)(2,1)}, bf16[512,512]{1,0:T(8,128)(2,1)S(1)}) custom-call(s32[12]{0:T(128)S(1)} %stack.51.meta_ref, f32[512,256]{1,0:T(8,128)S(1)} %get-tuple-element.28.mine_ref, f32[512,256]{1,0:T(8,128)S(1)} %collective-permute-done.14.got_ref, bf16[512,512]{1,0:T(8,128)(2,1)S(1)} %copy-done, ...), custom_call_target="tpu_custom_call" | custom-call | tf_op jit(solution)/shard_map/pallas_call | solution.py:337
  132.5 0.4 collective-permute-start.15
  132.9 1.5 collective-permute-done.15.other_slope_ref
  134.4 0.7 shard_map.105
  135.2 19.8 %all_to_all.20 = bf16[8,32,512]{2,1,0:T(8,128)(2,1)S(1)} all-to-all(bf16[8,32,512]{2,1,0:T(8,128)(2,1)S(1)} %bitcast.37), channel_id=1, replica_groups={{0,16,32,48,64,80,96,112},{8,24,40,56,72,88,104,120},{1,17,33,49,65,81,..., dimensions={0} | all-to-all | bytes 524288 | tf_op jit(solution)/shard_map/all_to_all | solution.py:309
  155.0 0.1 convert_element_type.11
  155.1 0.1 broadcast_in_dim.6
  155.1 14.2 %all_to_all.21 = f32[8,32,512]{2,1,0:T(8,128)S(1)} all-to-all(f32[8,32,512]{2,1,0:T(8,128)S(1)} %broadcast_in_dim.6), channel_id=1, replica_groups=mesh['row'=16,'col'=8] {'col'}, dimensions={0} | all-to-all | bytes 1048576 | tf_op jit(solution)/shard_map/all_to_all | solution.py:309
  169.4 9.7 %all_to_all.22 = bf16[8,32,512]{2,1,0:T(8,128)(2,1)S(1)} all-to-all(bf16[8,32,512]{2,1,0:T(8,128)(2,1)S(1)} %broadcast_in_dim.7), channel_id=1, replica_groups={{0,16,32,48,64,80,96,112},{8,24,40,56,72,88,104,120},{1,17,33,49,65,81,..., dimensions={0} | all-to-all | bytes 524288 | tf_op jit(solution)/shard_map/all_to_all | solution.py:309
  179.1 3.7 %collective-permute-start.16 = (bf16[256,512]{1,0:T(8,128)(2,1)S(1)}, bf16[256,512]{1,0:T(8,128)(2,1)S(1)}, u32[]{:S(2)}, u32[]{:S(2)}) collective-permute-start(bf16[256,512]{1,0:T(8,128)(2,1)S(1)} %bitcast.44), channel_id=1, source_target_pairs={{0,8},{8,0},{16,24},{24,16},{32,40},{40,32},{48,56},{56,48},{64,72... | collective-permute-start | bytes 786440 | tf_op jit(solution)/shard_map/ppermute | solution.py:483
  182.8 1.2 collective-permute-done.16
  184.0 0.1 broadcast_select_fusion.1
  184.0 1.1 maximum_convert_fusion
  (4 shorter events, 0.1 us)
Async XLA Ops:
  0.6 0.7 copy-start.1
  3.6 21.2 %collective-permute-start.1 = (bf16[192,128,128]{2,1,0:T(8,128)(2,1)}, bf16[192,128,128]{2,1,0:T(8,128)(2,1)}, u32[]{:S(2)}, u32[]{:S(2)}) collective-permute-start(bf16[192,128,128]{2,1,0:T(8,128)(2,1)} %bitcast.41), channel_id=1, source_target_pairs={{0,8},{8,0},{16,24},{24,16},{32,40},{40,32},{48,56},{56,48},{64,72... | collective-permute-start | bytes 18874376 | tf_op jit(solution)/shard_map/ppermute | solution.py:396
  5.1 19.2 %all-to-all-start = ((bf16[16,64,256]{2,1,0:T(8,128)(2,1)}), bf16[16,64,256]{2,1,0:T(8,128)(2,1)S(1)}, u32[]{:S(2)}, u32[]{:S(2)}) async-start(bf16[16,64,256]{2,1,0:T(8,128)(2,1)} %shard_map.96), calls=%async_computation | async-start | bytes 1048576 | tf_op jit(solution)/shard_map/all_to_all | solution.py:309
  12.9 0.7 copy-start.2
  13.6 0.7 copy-start.3
  14.7 10.1 %collective-permute-start = (s32[8,288]{1,0:T(8,128)S(1)}, s32[8,288]{1,0:T(8,128)S(1)}, u32[]{:S(2)}, u32[]{:S(2)}) collective-permute-start(s32[8,288]{1,0:T(8,128)S(1)} %shard_map.95), channel_id=1, source_target_pairs={{0,8},{8,0},{16,24},{24,16},{32,40},{40,32},{48,56},{56,48},{64,72... | collective-permute-start | bytes 27656 | tf_op jit(solution)/shard_map/ppermute | solution.py:388
  24.8 8.4 %collective-permute-start.2 = (bf16[2,512,256]{2,1,0:T(8,128)(2,1)S(1)}, bf16[2,512,256]{2,1,0:T(8,128)(2,1)S(1)}, u32[]{:S(2)}, u32[]{:S(2)}) collective-permute-start(bf16[2,512,256]{2,1,0:T(8,128)(2,1)S(1)} %shard_map.97.a_ref), channel_id=1, source_target_pairs={{0,16},{8,72},{16,32},{24,88},{32,48},{40,104},{48,0},{56,120},{64... | collective-permute-start | bytes 1572872 | tf_op jit(solution)/shard_map/ppermute | solution.py:413
  25.3 8.0 %collective-permute-start.3 = (bf16[2,512,256]{2,1,0:T(8,128)(2,1)S(1)}, bf16[2,512,256]{2,1,0:T(8,128)(2,1)S(1)}, u32[]{:S(2)}, u32[]{:S(2)}) collective-permute-start(bf16[2,512,256]{2,1,0:T(8,128)(2,1)S(1)} %shard_map.97.a_ref), channel_id=1, source_target_pairs={{0,48},{16,0},{32,16},{48,32},{64,112},{80,64},{96,80},{112,96},{1... | collective-permute-start | bytes 1572872 | tf_op jit(solution)/shard_map/ppermute | solution.py:413
  26.0 7.3 %collective-permute-start.4 = (bf16[2,512,256]{2,1,0:T(8,128)(2,1)S(1)}, bf16[2,512,256]{2,1,0:T(8,128)(2,1)S(1)}, u32[]{:S(2)}, u32[]{:S(2)}) collective-permute-start(bf16[2,512,256]{2,1,0:T(8,128)(2,1)S(1)} %shard_map.97.a_ref), channel_id=1, source_target_pairs={{0,32},{16,48},{32,0},{48,16},{64,96},{80,112},{96,64},{112,80},{1... | collective-permute-start | bytes 1572872 | tf_op jit(solution)/shard_map/ppermute | solution.py:413
  34.9 31.2 %collective-permute-start.6 = (bf16[2,2,512,256]{3,2,1,0:T(8,128)(2,1)}, bf16[2,2,512,256]{3,2,1,0:T(8,128)(2,1)}, u32[]{:S(2)}, u32[]{:S(2)}) collective-permute-start(bf16[2,2,512,256]{3,2,1,0:T(8,128)(2,1)} %shard_map.100), channel_id=1, source_target_pairs={{0,64},{8,56},{16,80},{24,8},{32,96},{40,24},{48,112},{56,40},{64,... | collective-permute-start | bytes 3145736 | tf_op jit(solution)/shard_map/ppermute | solution.py:413
  38.7 27.5 %collective-permute-start.5 = (bf16[2,2,512,256]{3,2,1,0:T(8,128)(2,1)S(1)}, bf16[2,2,512,256]{3,2,1,0:T(8,128)(2,1)}, u32[]{:S(2)}, u32[]{:S(2)}) collective-permute-start(bf16[2,2,512,256]{3,2,1,0:T(8,128)(2,1)S(1)} %shard_map.99.pair_ref), channel_id=1, source_target_pairs={{0,64},{8,24},{16,80},{24,40},{32,96},{40,56},{48,112},{56,8},{64,... | collective-permute-start | bytes 3145736 | tf_op jit(solution)/shard_map/ppermute | solution.py:413
  38.7 27.5 %collective-permute-start.7 = (bf16[2,2,512,256]{3,2,1,0:T(8,128)(2,1)S(1)}, bf16[2,2,512,256]{3,2,1,0:T(8,128)(2,1)}, u32[]{:S(2)}, u32[]{:S(2)}) collective-permute-start(bf16[2,2,512,256]{3,2,1,0:T(8,128)(2,1)S(1)} %shard_map.99.pair_ref), channel_id=1, source_target_pairs={{8,40},{24,56},{40,8},{56,24},{72,104},{88,120},{104,72},{120,88},... | collective-permute-start | bytes 3145736 | tf_op jit(solution)/shard_map/ppermute | solution.py:413
  73.9 56.3 %copy-start = (bf16[512,512]{1,0:T(8,128)(2,1)S(1)}, bf16[512,512]{1,0:T(8,128)(2,1)}, u32[]{:S(2)}) copy-start(bf16[512,512]{1,0:T(8,128)(2,1)} %weight_ref.1) | copy-start | bytes 1572868
  73.9 4.3 %collective-permute-start.10 = (bf16[4,512,256]{2,1,0:T(8,128)(2,1)S(1)}, bf16[4,512,256]{2,1,0:T(8,128)(2,1)S(1)}, u32[]{:S(2)}, u32[]{:S(2)}) collective-permute-start(bf16[4,512,256]{2,1,0:T(8,128)(2,1)S(1)} %get-tuple-element.23), channel_id=1, source_target_pairs={{0,2},{1,3},{2,0},{3,1},{4,6},{5,7},{6,4},{7,5},{16,18},{17,19},{1... | collective-permute-start | bytes 3145736 | tf_op jit(solution)/shard_map/ppermute | solution.py:446
  74.8 15.8 %collective-permute-start.8 = (bf16[4,512,256]{2,1,0:T(8,128)(2,1)S(1)}, bf16[4,512,256]{2,1,0:T(8,128)(2,1)S(1)}, u32[]{:S(2)}, u32[]{:S(2)}) collective-permute-start(bf16[4,512,256]{2,1,0:T(8,128)(2,1)S(1)} %get-tuple-element.21), channel_id=1, source_target_pairs={{0,1},{1,2},{2,3},{3,0},{4,5},{5,6},{6,7},{7,4},{8,12},{9,13},{10,... | collective-permute-start | bytes 3145736 | tf_op jit(solution)/shard_map/ppermute | solution.py:446
  78.1 23.4 %collective-permute-start.9 = (bf16[4,512,256]{2,1,0:T(8,128)(2,1)S(1)}, bf16[4,512,256]{2,1,0:T(8,128)(2,1)S(1)}, u32[]{:S(2)}, u32[]{:S(2)}) collective-permute-start(bf16[4,512,256]{2,1,0:T(8,128)(2,1)S(1)} %get-tuple-element.22), channel_id=1, source_target_pairs={{0,3},{1,0},{2,1},{3,2},{4,7},{5,4},{6,5},{7,6},{8,12},{9,13},{10,... | collective-permute-start | bytes 3145736 | tf_op jit(solution)/shard_map/ppermute | solution.py:446
  102.6 12.9 %collective-permute-start.11 = (bf16[2,512,256]{2,1,0:T(8,128)(2,1)S(1)}, bf16[2,512,256]{2,1,0:T(8,128)(2,1)S(1)}, u32[]{:S(2)}, u32[]{:S(2)}) collective-permute-start(bf16[2,512,256]{2,1,0:T(8,128)(2,1)S(1)} %get-tuple-element.25), channel_id=1, source_target_pairs={{0,4},{1,5},{2,6},{3,7},{4,0},{5,1},{6,2},{7,3},{8,9},{9,10},{10,1... | collective-permute-start | bytes 1572872 | tf_op jit(solution)/shard_map/ppermute | solution.py:458
  105.7 11.5 %collective-permute-start.12 = (bf16[2,512,256]{2,1,0:T(8,128)(2,1)S(1)}, bf16[2,512,256]{2,1,0:T(8,128)(2,1)S(1)}, u32[]{:S(2)}, u32[]{:S(2)}) collective-permute-start(bf16[2,512,256]{2,1,0:T(8,128)(2,1)S(1)} %get-tuple-element.26), channel_id=1, source_target_pairs={{8,11},{9,8},{10,9},{11,10},{12,15},{13,12},{14,13},{15,14},{24,27... | collective-permute-start | bytes 1572872 | tf_op jit(solution)/shard_map/ppermute | solution.py:458
  107.6 13.6 %collective-permute-start.13 = (bf16[2,512,256]{2,1,0:T(8,128)(2,1)S(1)}, bf16[2,512,256]{2,1,0:T(8,128)(2,1)S(1)}, u32[]{:S(2)}, u32[]{:S(2)}) collective-permute-start(bf16[2,512,256]{2,1,0:T(8,128)(2,1)S(1)} %get-tuple-element.27), channel_id=1, source_target_pairs={{8,10},{9,11},{10,8},{11,9},{12,14},{13,15},{14,12},{15,13},{24,26... | collective-permute-start | bytes 1572872 | tf_op jit(solution)/shard_map/ppermute | solution.py:458
  121.9 8.3 %collective-permute-start.14 = (f32[512,256]{1,0:T(8,128)S(1)}, f32[512,256]{1,0:T(8,128)S(1)}, u32[]{:S(2)}, u32[]{:S(2)}) collective-permute-start(f32[512,256]{1,0:T(8,128)S(1)} %get-tuple-element.29.other_ref), channel_id=1, source_target_pairs={{0,8},{8,0},{16,24},{24,16},{32,40},{40,32},{48,56},{56,48},{64,72... | collective-permute-start | bytes 1572872 | tf_op jit(solution)/shard_map/ppermute | solution.py:465
  132.5 1.9 %collective-permute-start.15 = (bf16[512,512]{1,0:T(8,128)(2,1)S(1)}, bf16[512,512]{1,0:T(8,128)(2,1)S(1)}, u32[]{:S(2)}, u32[]{:S(2)}) collective-permute-start(bf16[512,512]{1,0:T(8,128)(2,1)S(1)} %get-tuple-element.31.slope_ref), channel_id=1, source_target_pairs={{0,8},{8,0},{16,24},{24,16},{32,40},{40,32},{48,56},{56,48},{64,72... | collective-permute-start | bytes 1572872 | tf_op jit(solution)/shard_map/ppermute | solution.py:472
  179.1 4.9 %collective-permute-start.16 = (bf16[256,512]{1,0:T(8,128)(2,1)S(1)}, bf16[256,512]{1,0:T(8,128)(2,1)S(1)}, u32[]{:S(2)}, u32[]{:S(2)}) collective-permute-start(bf16[256,512]{1,0:T(8,128)(2,1)S(1)} %bitcast.44), channel_id=1, source_target_pairs={{0,8},{8,0},{16,24},{24,16},{32,40},{40,32},{48,56},{56,48},{64,72... | collective-permute-start | bytes 786440 | tf_op jit(solution)/shard_map/ppermute | solution.py:483

commit v11 on v9

--- a/solution.py
+++ b/solution.py
@@ -404,11 +404,11 @@
 
     r1 = hop(own, (0, 1), (1, 0))
     r2 = hop(own, (0, 3), None)
-    r3 = hop(own, (0, 2), None)
+    r3 = hop(r2, (0, 3), None)
     both = held(2, 2, SLOTS, HALF)
     pair = call(pair_kernel, [vmem] * 2, both)(own, r1)
     s1 = hop(pair, (1, 0), (0, 1))
-    s2 = hop(pair, None, (0, 2))
+    s2 = hop(s1, None, (0, 1))
     rest = call(rest_kernel, [smem] + [vmem] * 3, both)(meta, pair, r2, r3)
     s3 = hop(rest, (1, 0), (0, 3))
     shape = (N_ROW, N_COL * PER_PEER, HALF)
@@ -419,7 +419,7 @@
     source = held(CHIPS, 2, N_ROW, N_COL * PER_PEER, HALF)
     keep1, send1, source, tiles0 = call(
         tiles_y_kernel,
-        [smem, smem, vmem, pinned, pinned] + [hbm] * BLOCKS,
+        [smem, smem, vmem, pinned, pinned] + [pinned] * BLOCKS,
         [held(4, SLOTS, HALF), held(4, SLOTS, HALF), source, staged],
         [total, pltpu.SemaphoreType.DMA((CHIPS,)), pltpu.SemaphoreType.DMA],
     )(meta, plans[1], tiles1, tiles, other_tiles, *blocks)

time: 169 us -> 170 us (level)
  starting transfers between devices: 29.9 us -> 40.3 us
  waiting for transfers between devices: 73.5 us -> 64.1 us
  blocking collectives: 33.6 us -> 36.9 us
  Pallas kernels: 25.6 us -> 22.9 us
    ppermute x3, waiting for transfers between devices: 16.8 us -> 7.83 us  [shards(): got1 = [lax.ppermute(send1[k - 1], 'col', x_moves(k)) for k in (1, 3, 2)]]
    ppermute x1, starting transfers between devices: 1.63 us -> 6.87 us  [shards(): theirs = lax.ppermute(others, 'row', swap)]
    ppermute x3, starting transfers between devices: 2.87 us -> 6.94 us  [shards(): got1 = [lax.ppermute(send1[k - 1], 'col', x_moves(k)) for k in (1, 3, 2)]]
    ppermute x1, waiting for transfers between devices: 16.7 us -> 13.1 us  [shards(): got1 = lax.ppermute(send1, 'col', y_moves())]
    all_to_all x3, blocking collectives: 33.6 us -> 36.9 us  [exchange(): lax.all_to_all(parts, axis, split_axis=0, concat_axis=0, axis_index_group...]
    pallas_call x13, Pallas kernels: 25.6 us -> 22.9 us  [run(): return made(*held)]
    ppermute x1, starting transfers between devices: 0.09 us -> 2.42 us  [shards(): got0 = lax.ppermute(send0, 'col', y_moves())]
    ppermute x6, waiting for transfers between devices: 26.6 us -> 28.7 us  [hop(): return lax.ppermute(block, 'row', row_moves(move))]
  transfers between devices with their start and end apart: 20 -> 20, of which waited for: 11 -> 12; matrix products, arithmetic and copies ran while one was open for 1% -> 1% of each run, Pallas kernels for 7% -> 6%
where the time goes in v11:
time: 170 us; the launch traced here: 171 us
  waiting for transfers between devices  64.1 us (38%)
  starting transfers between devices  40.3 us (24%)
  blocking collectives  36.9 us (22%)
  Pallas kernels  22.9 us (13%)
  local copies, waits for them, and re-layouts  3.29 us (2%)
  between operations  1.7 us (1%)
    all_to_all x3, blocking collectives, exchange(): lax.all_to_all(parts, axis, split_axis=0, concat_axis=0, axis_index_group...  36.9 us
    ppermute x6, waiting for transfers between devices, hop(): return lax.ppermute(block, 'row', row_moves(move))  28.7 us
    pallas_call x13, Pallas kernels, run(): return made(*held)  22.9 us
    ppermute x1, waiting for transfers between devices, shards(): got1 = lax.ppermute(send1, 'col', y_moves())  13.1 us
    all_to_all x1, waiting for transfers between devices, exchange(): lax.all_to_all(parts, axis, split_axis=0, concat_axis=0, axis_index_group...  9.51 us
    ppermute x3, waiting for transfers between devices, shards(): got1 = [lax.ppermute(send1[k - 1], 'col', x_moves(k)) for k in (1, 3, 2)]  7.83 us
    ppermute x6, starting transfers between devices, hop(): return lax.ppermute(block, 'row', row_moves(move))  7.61 us
    all_to_all x1, starting transfers between devices, exchange(): lax.all_to_all(parts, axis, split_axis=0, concat_axis=0, axis_index_group...  7.14 us
  transfers between devices with their start and end apart: 20, of which 12 were waited for; matrix products, arithmetic and copies ran while one was open for 1% of the time, Pallas kernels for 6%

profile of v11, /device:TPU:1, one launch (start us, length us, event | category | flops | bytes accessed | tf_op | source)
XLA Modules:
  0.0 170.5 jit_solution(711560191727393567)
XLA Ops:
  0.6 0.7 copy-done.5
  1.3 2.3 %shard_map.96 = bf16[16,64,256]{2,1,0:T(8,128)(2,1)} custom-call(s32[1,512]{1,0:T(1,128)S(1)} %bitcast.38, bf16[512,512]{1,0:T(8,128)(2,1)} %features_hbm.1), custom_call_target="tpu_custom_call" | custom-call | tf_op jit(solution)/shard_map/pallas_call | solution.py:327
  3.6 1.5 collective-permute-start.1
  5.1 7.1 %all-to-all-start = ((bf16[16,64,256]{2,1,0:T(8,128)(2,1)}), bf16[16,64,256]{2,1,0:T(8,128)(2,1)S(1)}, u32[]{:S(2)}, u32[]{:S(2)}) async-start(bf16[16,64,256]{2,1,0:T(8,128)(2,1)} %shard_map.96), calls=%async_computation | async-start | bytes 1048576 | tf_op jit(solution)/shard_map/all_to_all | solution.py:299
  12.9 0.0 copy-start.6
  12.9 0.7 copy-done.6
  13.6 0.7 copy-done.7
  14.3 0.5 shard_map.95
  14.7 0.1 collective-permute-start
  14.8 9.5 %all-to-all-done.arrived_ref = bf16[16,64,256]{2,1,0:T(8,128)(2,1)S(1)} async-done(((bf16[16,64,256]{2,1,0:T(8,128)(2,1)}), bf16[16,64,256]{2,1,0:T(8,128)(2,1)S(1)}, u32[]{:S(2)}, u32[]{:S(2)}) %all-to-all-start) | async-done | bytes 524320 | tf_op jit(solution)/shard_map/all_to_all | solution.py:299
  24.4 0.4 shard_map.97.a_ref
  24.8 0.0 copy-start
  24.8 0.0 collective-permute-done
  24.8 0.0 collective-permute-done.1.other_hbm
  24.8 0.5 collective-permute-start.2
  25.3 0.7 collective-permute-start.3
  26.0 7.2 %collective-permute-done.2.b_ref = bf16[2,512,256]{2,1,0:T(8,128)(2,1)S(1)} collective-permute-done((bf16[2,512,256]{2,1,0:T(8,128)(2,1)S(1)}, bf16[2,512,256]{2,1,0:T(8,128)(2,1)S(1)}, u32[]{:S(2)}, u32[]{:S(2)}) %collective-permute-start.2) | collective-permute-done | bytes 524320 | tf_op jit(solution)/shard_map/ppermute | solution.py:403
  33.2 0.1 shard_map.99.pair_ref
  33.3 1.7 collective-permute-start.5
  35.0 0.7 collective-permute-start.4
  35.8 0.1 stack.51.meta_ref
  35.9 0.0 collective-permute-done.4.b_ref
  36.0 1.6 shard_map.100
  37.5 2.2 %collective-permute-start.6 = (bf16[2,2,512,256]{3,2,1,0:T(8,128)(2,1)}, bf16[2,2,512,256]{3,2,1,0:T(8,128)(2,1)}, u32[]{:S(2)}, u32[]{:S(2)}) collective-permute-start(bf16[2,2,512,256]{3,2,1,0:T(8,128)(2,1)} %shard_map.100), channel_id=1, source_target_pairs={{0,64},{8,56},{16,80},{24,8},{32,96},{40,24},{48,112},{56,40},{64,... | collective-permute-start | bytes 3145736 | tf_op jit(solution)/shard_map/ppermute | solution.py:403
  39.7 9.7 %collective-permute-done.5 = bf16[2,2,512,256]{3,2,1,0:T(8,128)(2,1)} collective-permute-done((bf16[2,2,512,256]{3,2,1,0:T(8,128)(2,1)S(1)}, bf16[2,2,512,256]{3,2,1,0:T(8,128)(2,1)}, u32[]{:S(2)}, u32[]{:S(2)}) %collective-permute-start.5) | collective-permute-done | bytes 1048608 | tf_op jit(solution)/shard_map/ppermute | solution.py:403
  49.4 1.9 %collective-permute-start.7 = (bf16[2,2,512,256]{3,2,1,0:T(8,128)(2,1)}, bf16[2,2,512,256]{3,2,1,0:T(8,128)(2,1)}, u32[]{:S(2)}, u32[]{:S(2)}) collective-permute-start(bf16[2,2,512,256]{3,2,1,0:T(8,128)(2,1)} %collective-permute-done.5), channel_id=1, source_target_pairs={{8,24},{24,40},{40,56},{56,8},{72,88},{88,104},{104,120},{120,72},... | collective-permute-start | bytes 3145736 | tf_op jit(solution)/shard_map/ppermute | solution.py:403
  51.4 3.3 %shard_map.98.tiles = bf16[193,128,128]{2,1,0:T(8,128)(2,1)S(1)} custom-call(s32[12]{0:T(128)S(1)} %stack.51.meta_ref, bf16[192,128,128]{2,1,0:T(8,128)(2,1)} %bitcast.42, bf16[192,128,128]{2,1,0:T(8,128)(2,1)} %collective-permute-done.1.other_hbm), custom_call_target="tpu_custom_call" | custom-call | tf_op jit(solution)/shard_map/pallas_call | solution.py:327
  54.7 2.6 %collective-permute-done.6 = bf16[2,2,512,256]{3,2,1,0:T(8,128)(2,1)} collective-permute-done((bf16[2,2,512,256]{3,2,1,0:T(8,128)(2,1)}, bf16[2,2,512,256]{3,2,1,0:T(8,128)(2,1)}, u32[]{:S(2)}, u32[]{:S(2)}) %collective-permute-start.6) | collective-permute-done | bytes 1048608 | tf_op jit(solution)/shard_map/ppermute | solution.py:403
  57.4 9.1 %collective-permute-done.7 = bf16[2,2,512,256]{3,2,1,0:T(8,128)(2,1)} collective-permute-done((bf16[2,2,512,256]{3,2,1,0:T(8,128)(2,1)}, bf16[2,2,512,256]{3,2,1,0:T(8,128)(2,1)}, u32[]{:S(2)}, u32[]{:S(2)}) %collective-permute-start.7) | collective-permute-done | bytes 1048608 | tf_op jit(solution)/shard_map/ppermute | solution.py:403
  66.5 5.8 %shard_map.101 = (bf16[4,512,256]{2,1,0:T(8,128)(2,1)S(1)}, bf16[4,512,256]{2,1,0:T(8,128)(2,1)S(1)}, bf16[8,2,16,32,256]{4,3,2,1,0:T(8,128)(2,1)S(1)}, bf16[193,128,128]{2,1,0:T(8,128)(2,1)S(1)}) custom-call(s32[12]{0:T(128)S(1)} %stack.51.meta_ref, s32[8,288]{1,0:T(8,128)S(1)} %get-tuple-element.48.plan_ref, bf16[193,128,128]{2,1,0:T(8,128)(2,1)S(1)} %shard_map.98.tiles, ...), custom_call_target="tpu_custom_call" | custom-call | tf_op jit(solution)/shard_map/pallas_call | solution.py:327
  72.3 0.1 collective-permute-start.8
  72.3 3.6 %shard_map.102 = (bf16[2,512,256]{2,1,0:T(8,128)(2,1)S(1)}, bf16[2,512,256]{2,1,0:T(8,128)(2,1)S(1)}, bf16[2,512,256]{2,1,0:T(8,128)(2,1)S(1)}, bf16[2,512,256]{2,1,0:T(8,128)(2,1)S(1)}) custom-call(s32[12]{0:T(128)S(1)} %stack.51.meta_ref, s32[8,288]{1,0:T(8,128)S(1)} %get-tuple-element.49.plan_ref, bf16[193,128,128]{2,1,0:T(8,128)(2,1)S(1)} %get-tuple-element.27.tiles, ...), custom_call_target="tpu_custom_call" | custom-call | tf_op jit(solution)/shard_map/pallas_call | solution.py:327
  75.9 0.0 copy-start.4
  76.0 0.1 collective-permute-start.10
  76.0 2.7 %collective-permute-start.11 = (bf16[2,512,256]{2,1,0:T(8,128)(2,1)S(1)}, bf16[2,512,256]{2,1,0:T(8,128)(2,1)S(1)}, u32[]{:S(2)}, u32[]{:S(2)}) collective-permute-start(bf16[2,512,256]{2,1,0:T(8,128)(2,1)S(1)} %get-tuple-element.35), channel_id=1, source_target_pairs={{0,3},{1,0},{2,1},{3,2},{4,7},{5,4},{6,5},{7,6},{8,11},{9,8},{10,9... | collective-permute-start | bytes 1572872 | tf_op jit(solution)/shard_map/ppermute | solution.py:432
  78.7 0.8 collective-permute-start.12
  79.5 13.1 %collective-permute-done.8.got_ref = bf16[4,512,256]{2,1,0:T(8,128)(2,1)S(1)} collective-permute-done((bf16[4,512,256]{2,1,0:T(8,128)(2,1)S(1)}, bf16[4,512,256]{2,1,0:T(8,128)(2,1)S(1)}, u32[]{:S(2)}, u32[]{:S(2)}) %collective-permute-start.8) | collective-permute-done | bytes 1048608 | tf_op jit(solution)/shard_map/ppermute | solution.py:433
  92.5 0.8 shard_map.103
  93.3 0.4 collective-permute-start.9
  93.7 2.4 %collective-permute-start.14 = (bf16[512,256]{1,0:T(8,128)(2,1)S(1)}, bf16[512,256]{1,0:T(8,128)(2,1)S(1)}, u32[]{:S(2)}, u32[]{:S(2)}) collective-permute-start(bf16[512,256]{1,0:T(8,128)(2,1)S(1)} %get-tuple-element.40), channel_id=1, source_target_pairs={{0,3},{1,0},{2,1},{3,2},{4,7},{5,4},{6,5},{7,6},{8,11},{9,8},{10,9... | collective-permute-start | bytes 786440 | tf_op jit(solution)/shard_map/ppermute | solution.py:438
  96.1 5.3 %collective-permute-done.9.a_ref = bf16[512,256]{1,0:T(8,128)(2,1)S(1)} collective-permute-done((bf16[512,256]{1,0:T(8,128)(2,1)S(1)}, bf16[512,256]{1,0:T(8,128)(2,1)S(1)}, u32[]{:S(2)}, u32[]{:S(2)}) %collective-permute-start.9) | collective-permute-done | bytes 262176 | tf_op jit(solution)/shard_map/ppermute | solution.py:438
  101.4 4.2 %collective-permute-start.15 = (bf16[512,256]{1,0:T(8,128)(2,1)S(1)}, bf16[512,256]{1,0:T(8,128)(2,1)S(1)}, u32[]{:S(2)}, u32[]{:S(2)}) collective-permute-start(bf16[512,256]{1,0:T(8,128)(2,1)S(1)} %get-tuple-element.41), channel_id=1, source_target_pairs={{0,2},{1,3},{2,0},{3,1},{4,6},{5,7},{6,4},{7,5},{8,10},{9,11},{10,... | collective-permute-start | bytes 786440 | tf_op jit(solution)/shard_map/ppermute | solution.py:438
  105.6 0.8 shard_map.104
  106.4 2.4 %collective-permute-start.13 = (bf16[512,256]{1,0:T(8,128)(2,1)S(1)}, bf16[512,256]{1,0:T(8,128)(2,1)S(1)}, u32[]{:S(2)}, u32[]{:S(2)}) collective-permute-start(bf16[512,256]{1,0:T(8,128)(2,1)S(1)} %get-tuple-element.38), channel_id=1, source_target_pairs={{0,4},{1,5},{2,6},{3,7},{4,0},{5,1},{6,2},{7,3},{8,12},{9,13},{10,... | collective-permute-start | bytes 786440 | tf_op jit(solution)/shard_map/ppermute | solution.py:442
  108.8 0.0 collective-permute-done.14.b_ref
  108.8 2.5 %collective-permute-done.15.c_ref = bf16[512,256]{1,0:T(8,128)(2,1)S(1)} collective-permute-done((bf16[512,256]{1,0:T(8,128)(2,1)S(1)}, bf16[512,256]{1,0:T(8,128)(2,1)S(1)}, u32[]{:S(2)}, u32[]{:S(2)}) %collective-permute-start.15) | collective-permute-done | bytes 262176 | tf_op jit(solution)/shard_map/ppermute | solution.py:438
  111.3 1.8 %collective-permute-done.13.got0 = bf16[512,256]{1,0:T(8,128)(2,1)S(1)} collective-permute-done((bf16[512,256]{1,0:T(8,128)(2,1)S(1)}, bf16[512,256]{1,0:T(8,128)(2,1)S(1)}, u32[]{:S(2)}, u32[]{:S(2)}) %collective-permute-start.13) | collective-permute-done | bytes 262176 | tf_op jit(solution)/shard_map/ppermute | solution.py:442
  113.2 0.8 shard_map.105
  114.0 6.9 %collective-permute-start.16 = (f32[512,256]{1,0:T(8,128)S(1)}, f32[512,256]{1,0:T(8,128)S(1)}, u32[]{:S(2)}, u32[]{:S(2)}) collective-permute-start(f32[512,256]{1,0:T(8,128)S(1)} %get-tuple-element.43.other_ref), channel_id=1, source_target_pairs={{0,8},{8,0},{16,24},{24,16},{32,40},{40,32},{48,56},{56,48},{64,72... | collective-permute-start | bytes 1572872 | tf_op jit(solution)/shard_map/ppermute | solution.py:446
  120.8 1.1 constant_dynamic-slice_fusion.cotangent_ref
  121.9 0.5 collective-permute-done.16.got_ref
  122.4 2.3 %shard_map.106 = (bf16[512,512]{1,0:T(8,128)(2,1)}, bf16[512,512]{1,0:T(8,128)(2,1)S(1)}) custom-call(s32[12]{0:T(128)S(1)} %stack.51.meta_ref, f32[512,256]{1,0:T(8,128)S(1)} %get-tuple-element.42.mine_ref, f32[512,256]{1,0:T(8,128)S(1)} %collective-permute-done.16.got_ref, bf16[512,512]{1,0:T(8,128)(2,1)S(1)} %copy-done.4, ...), custom_call_target="tpu_custom_call" | custom-call | tf_op jit(solution)/shard_map/pallas_call | solution.py:327
  124.7 0.4 collective-permute-start.17
  125.0 1.5 collective-permute-done.17.other_slope_ref
  126.6 0.7 shard_map.107
  127.3 10.8 %all_to_all.20 = bf16[8,32,512]{2,1,0:T(8,128)(2,1)S(1)} all-to-all(bf16[8,32,512]{2,1,0:T(8,128)(2,1)S(1)} %bitcast.37), channel_id=1, replica_groups={{0,16,32,48,64,80,96,112},{8,24,40,56,72,88,104,120},{1,17,33,49,65,81,..., dimensions={0} | all-to-all | bytes 524288 | tf_op jit(solution)/shard_map/all_to_all | solution.py:299
  138.1 0.1 convert_element_type.11
  138.2 0.1 broadcast_in_dim.6
  138.2 16.5 %all_to_all.21 = f32[8,32,512]{2,1,0:T(8,128)S(1)} all-to-all(f32[8,32,512]{2,1,0:T(8,128)S(1)} %broadcast_in_dim.6), channel_id=1, replica_groups=mesh['row'=16,'col'=8] {'col'}, dimensions={0} | all-to-all | bytes 1048576 | tf_op jit(solution)/shard_map/all_to_all | solution.py:299
  154.8 9.7 %all_to_all.22 = bf16[8,32,512]{2,1,0:T(8,128)(2,1)S(1)} all-to-all(bf16[8,32,512]{2,1,0:T(8,128)(2,1)S(1)} %broadcast_in_dim.7), channel_id=1, replica_groups={{0,16,32,48,64,80,96,112},{8,24,40,56,72,88,104,120},{1,17,33,49,65,81,..., dimensions={0} | all-to-all | bytes 524288 | tf_op jit(solution)/shard_map/all_to_all | solution.py:299
  164.5 3.7 %collective-permute-start.18 = (bf16[256,512]{1,0:T(8,128)(2,1)S(1)}, bf16[256,512]{1,0:T(8,128)(2,1)S(1)}, u32[]{:S(2)}, u32[]{:S(2)}) collective-permute-start(bf16[256,512]{1,0:T(8,128)(2,1)S(1)} %bitcast.44), channel_id=1, source_target_pairs={{0,8},{8,0},{16,24},{24,16},{32,40},{40,32},{48,56},{56,48},{64,72... | collective-permute-start | bytes 786440 | tf_op jit(solution)/shard_map/ppermute | solution.py:464
  168.2 1.2 collective-permute-done.18
  169.4 0.1 broadcast_select_fusion.1
  169.4 1.1 maximum_convert_fusion
  (18 shorter events, 0.1 us)
Async XLA Ops:
  0.6 0.7 copy-start.5
  3.6 21.2 %collective-permute-start.1 = (bf16[192,128,128]{2,1,0:T(8,128)(2,1)}, bf16[192,128,128]{2,1,0:T(8,128)(2,1)}, u32[]{:S(2)}, u32[]{:S(2)}) collective-permute-start(bf16[192,128,128]{2,1,0:T(8,128)(2,1)} %bitcast.41), channel_id=1, source_target_pairs={{0,8},{8,0},{16,24},{24,16},{32,40},{40,32},{48,56},{56,48},{64,72... | collective-permute-start | bytes 18874376 | tf_op jit(solution)/shard_map/ppermute | solution.py:386
  5.1 19.2 %all-to-all-start = ((bf16[16,64,256]{2,1,0:T(8,128)(2,1)}), bf16[16,64,256]{2,1,0:T(8,128)(2,1)S(1)}, u32[]{:S(2)}, u32[]{:S(2)}) async-start(bf16[16,64,256]{2,1,0:T(8,128)(2,1)} %shard_map.96), calls=%async_computation | async-start | bytes 1048576 | tf_op jit(solution)/shard_map/all_to_all | solution.py:299
  12.9 0.7 copy-start.6
  13.6 0.7 copy-start.7
  14.7 10.1 %collective-permute-start = (s32[8,288]{1,0:T(8,128)S(1)}, s32[8,288]{1,0:T(8,128)S(1)}, u32[]{:S(2)}, u32[]{:S(2)}) collective-permute-start(s32[8,288]{1,0:T(8,128)S(1)} %shard_map.95), channel_id=1, source_target_pairs={{0,8},{8,0},{16,24},{24,16},{32,40},{40,32},{48,56},{56,48},{64,72... | collective-permute-start | bytes 27656 | tf_op jit(solution)/shard_map/ppermute | solution.py:378
  24.8 29.9 %copy-start = (bf16[2,512,256]{2,1,0:T(8,128)(2,1)}, bf16[2,512,256]{2,1,0:T(8,128)(2,1)S(1)}, u32[]{:S(2)}) copy-start(bf16[2,512,256]{2,1,0:T(8,128)(2,1)S(1)} %shard_map.97.a_ref) | copy-start | bytes 1572868
  24.8 8.4 %collective-permute-start.2 = (bf16[2,512,256]{2,1,0:T(8,128)(2,1)S(1)}, bf16[2,512,256]{2,1,0:T(8,128)(2,1)S(1)}, u32[]{:S(2)}, u32[]{:S(2)}) collective-permute-start(bf16[2,512,256]{2,1,0:T(8,128)(2,1)S(1)} %shard_map.97.a_ref), channel_id=1, source_target_pairs={{0,16},{8,72},{16,32},{24,88},{32,48},{40,104},{48,0},{56,120},{64... | collective-permute-start | bytes 1572872 | tf_op jit(solution)/shard_map/ppermute | solution.py:403
  25.3 9.7 %collective-permute-start.3 = (bf16[2,512,256]{2,1,0:T(8,128)(2,1)S(1)}, bf16[2,512,256]{2,1,0:T(8,128)(2,1)S(1)}, u32[]{:S(2)}, u32[]{:S(2)}) collective-permute-start(bf16[2,512,256]{2,1,0:T(8,128)(2,1)S(1)} %shard_map.97.a_ref), channel_id=1, source_target_pairs={{0,48},{16,0},{32,16},{48,32},{64,112},{80,64},{96,80},{112,96},{1... | collective-permute-start | bytes 1572872 | tf_op jit(solution)/shard_map/ppermute | solution.py:403
  33.2 21.5 %copy-start.1 = (bf16[2,512,256]{2,1,0:T(8,128)(2,1)}, bf16[2,512,256]{2,1,0:T(8,128)(2,1)S(1)}, u32[]{:S(2)}) copy-start(bf16[2,512,256]{2,1,0:T(8,128)(2,1)S(1)} %collective-permute-done.2.b_ref) | copy-start | bytes 1572868
  33.3 16.1 %collective-permute-start.5 = (bf16[2,2,512,256]{3,2,1,0:T(8,128)(2,1)S(1)}, bf16[2,2,512,256]{3,2,1,0:T(8,128)(2,1)}, u32[]{:S(2)}, u32[]{:S(2)}) collective-permute-start(bf16[2,2,512,256]{3,2,1,0:T(8,128)(2,1)S(1)} %shard_map.99.pair_ref), channel_id=1, source_target_pairs={{0,64},{8,24},{16,80},{24,40},{32,96},{40,56},{48,112},{56,8},{64,... | collective-permute-start | bytes 3145736 | tf_op jit(solution)/shard_map/ppermute | solution.py:403
  35.0 19.7 %copy-start.2 = (bf16[2,512,256]{2,1,0:T(8,128)(2,1)}, bf16[2,512,256]{2,1,0:T(8,128)(2,1)S(1)}, u32[]{:S(2)}) copy-start(bf16[2,512,256]{2,1,0:T(8,128)(2,1)S(1)} %collective-permute-done.3.a_ref) | copy-start | bytes 1572868
  35.0 0.9 collective-permute-start.4
  36.0 18.8 %copy-start.3 = (bf16[2,512,256]{2,1,0:T(8,128)(2,1)}, bf16[2,512,256]{2,1,0:T(8,128)(2,1)S(1)}, u32[]{:S(2)}) copy-start(bf16[2,512,256]{2,1,0:T(8,128)(2,1)S(1)} %collective-permute-done.4.b_ref) | copy-start | bytes 1572868
  37.5 19.8 %collective-permute-start.6 = (bf16[2,2,512,256]{3,2,1,0:T(8,128)(2,1)}, bf16[2,2,512,256]{3,2,1,0:T(8,128)(2,1)}, u32[]{:S(2)}, u32[]{:S(2)}) collective-permute-start(bf16[2,2,512,256]{3,2,1,0:T(8,128)(2,1)} %shard_map.100), channel_id=1, source_target_pairs={{0,64},{8,56},{16,80},{24,8},{32,96},{40,24},{48,112},{56,40},{64,... | collective-permute-start | bytes 3145736 | tf_op jit(solution)/shard_map/ppermute | solution.py:403
  49.4 17.1 %collective-permute-start.7 = (bf16[2,2,512,256]{3,2,1,0:T(8,128)(2,1)}, bf16[2,2,512,256]{3,2,1,0:T(8,128)(2,1)}, u32[]{:S(2)}, u32[]{:S(2)}) collective-permute-start(bf16[2,2,512,256]{3,2,1,0:T(8,128)(2,1)} %collective-permute-done.5), channel_id=1, source_target_pairs={{8,24},{24,40},{40,56},{56,8},{72,88},{88,104},{104,120},{120,72},... | collective-permute-start | bytes 3145736 | tf_op jit(solution)/shard_map/ppermute | solution.py:403
  72.3 20.3 %collective-permute-start.8 = (bf16[4,512,256]{2,1,0:T(8,128)(2,1)S(1)}, bf16[4,512,256]{2,1,0:T(8,128)(2,1)S(1)}, u32[]{:S(2)}, u32[]{:S(2)}) collective-permute-start(bf16[4,512,256]{2,1,0:T(8,128)(2,1)S(1)} %get-tuple-element.31), channel_id=1, source_target_pairs={{0,4},{1,5},{2,6},{3,7},{4,0},{5,1},{6,2},{7,3},{8,12},{9,13},{10,... | collective-permute-start | bytes 3145736 | tf_op jit(solution)/shard_map/ppermute | solution.py:433
  75.9 46.4 %copy-start.4 = (bf16[512,512]{1,0:T(8,128)(2,1)S(1)}, bf16[512,512]{1,0:T(8,128)(2,1)}, u32[]{:S(2)}) copy-start(bf16[512,512]{1,0:T(8,128)(2,1)} %weight_ref.1) | copy-start | bytes 1572868
  76.0 29.6 %collective-permute-start.10 = (bf16[2,512,256]{2,1,0:T(8,128)(2,1)S(1)}, bf16[2,512,256]{2,1,0:T(8,128)(2,1)S(1)}, u32[]{:S(2)}, u32[]{:S(2)}) collective-permute-start(bf16[2,512,256]{2,1,0:T(8,128)(2,1)S(1)} %get-tuple-element.34), channel_id=1, source_target_pairs={{0,1},{1,2},{2,3},{3,0},{4,5},{5,6},{6,7},{7,4},{8,9},{9,10},{10,1... | collective-permute-start | bytes 1572872 | tf_op jit(solution)/shard_map/ppermute | solution.py:432
  76.0 29.5 %collective-permute-start.11 = (bf16[2,512,256]{2,1,0:T(8,128)(2,1)S(1)}, bf16[2,512,256]{2,1,0:T(8,128)(2,1)S(1)}, u32[]{:S(2)}, u32[]{:S(2)}) collective-permute-start(bf16[2,512,256]{2,1,0:T(8,128)(2,1)S(1)} %get-tuple-element.35), channel_id=1, source_target_pairs={{0,3},{1,0},{2,1},{3,2},{4,7},{5,4},{6,5},{7,6},{8,11},{9,8},{10,9... | collective-permute-start | bytes 1572872 | tf_op jit(solution)/shard_map/ppermute | solution.py:432
  78.7 26.9 %collective-permute-start.12 = (bf16[2,512,256]{2,1,0:T(8,128)(2,1)S(1)}, bf16[2,512,256]{2,1,0:T(8,128)(2,1)S(1)}, u32[]{:S(2)}, u32[]{:S(2)}) collective-permute-start(bf16[2,512,256]{2,1,0:T(8,128)(2,1)S(1)} %get-tuple-element.36), channel_id=1, source_target_pairs={{0,2},{1,3},{2,0},{3,1},{4,6},{5,7},{6,4},{7,5},{8,10},{9,11},{10,... | collective-permute-start | bytes 1572872 | tf_op jit(solution)/shard_map/ppermute | solution.py:432
  93.3 8.0 %collective-permute-start.9 = (bf16[512,256]{1,0:T(8,128)(2,1)S(1)}, bf16[512,256]{1,0:T(8,128)(2,1)S(1)}, u32[]{:S(2)}, u32[]{:S(2)}) collective-permute-start(bf16[512,256]{1,0:T(8,128)(2,1)S(1)} %get-tuple-element.32), channel_id=1, source_target_pairs={{0,1},{1,2},{2,3},{3,0},{4,5},{5,6},{6,7},{7,4},{8,9},{9,10},{10,1... | collective-permute-start | bytes 786440 | tf_op jit(solution)/shard_map/ppermute | solution.py:438
  93.7 15.1 %collective-permute-start.14 = (bf16[512,256]{1,0:T(8,128)(2,1)S(1)}, bf16[512,256]{1,0:T(8,128)(2,1)S(1)}, u32[]{:S(2)}, u32[]{:S(2)}) collective-permute-start(bf16[512,256]{1,0:T(8,128)(2,1)S(1)} %get-tuple-element.40), channel_id=1, source_target_pairs={{0,3},{1,0},{2,1},{3,2},{4,7},{5,4},{6,5},{7,6},{8,11},{9,8},{10,9... | collective-permute-start | bytes 786440 | tf_op jit(solution)/shard_map/ppermute | solution.py:438
  101.4 10.0 %collective-permute-start.15 = (bf16[512,256]{1,0:T(8,128)(2,1)S(1)}, bf16[512,256]{1,0:T(8,128)(2,1)S(1)}, u32[]{:S(2)}, u32[]{:S(2)}) collective-permute-start(bf16[512,256]{1,0:T(8,128)(2,1)S(1)} %get-tuple-element.41), channel_id=1, source_target_pairs={{0,2},{1,3},{2,0},{3,1},{4,6},{5,7},{6,4},{7,5},{8,10},{9,11},{10,... | collective-permute-start | bytes 786440 | tf_op jit(solution)/shard_map/ppermute | solution.py:438
  106.4 6.8 %collective-permute-start.13 = (bf16[512,256]{1,0:T(8,128)(2,1)S(1)}, bf16[512,256]{1,0:T(8,128)(2,1)S(1)}, u32[]{:S(2)}, u32[]{:S(2)}) collective-permute-start(bf16[512,256]{1,0:T(8,128)(2,1)S(1)} %get-tuple-element.38), channel_id=1, source_target_pairs={{0,4},{1,5},{2,6},{3,7},{4,0},{5,1},{6,2},{7,3},{8,12},{9,13},{10,... | collective-permute-start | bytes 786440 | tf_op jit(solution)/shard_map/ppermute | solution.py:442
  114.0 8.4 %collective-permute-start.16 = (f32[512,256]{1,0:T(8,128)S(1)}, f32[512,256]{1,0:T(8,128)S(1)}, u32[]{:S(2)}, u32[]{:S(2)}) collective-permute-start(f32[512,256]{1,0:T(8,128)S(1)} %get-tuple-element.43.other_ref), channel_id=1, source_target_pairs={{0,8},{8,0},{16,24},{24,16},{32,40},{40,32},{48,56},{56,48},{64,72... | collective-permute-start | bytes 1572872 | tf_op jit(solution)/shard_map/ppermute | solution.py:446
  124.7 1.9 %collective-permute-start.17 = (bf16[512,512]{1,0:T(8,128)(2,1)S(1)}, bf16[512,512]{1,0:T(8,128)(2,1)S(1)}, u32[]{:S(2)}, u32[]{:S(2)}) collective-permute-start(bf16[512,512]{1,0:T(8,128)(2,1)S(1)} %get-tuple-element.45.slope_ref), channel_id=1, source_target_pairs={{0,8},{8,0},{16,24},{24,16},{32,40},{40,32},{48,56},{56,48},{64,72... | collective-permute-start | bytes 1572872 | tf_op jit(solution)/shard_map/ppermute | solution.py:453
  164.5 4.9 %collective-permute-start.18 = (bf16[256,512]{1,0:T(8,128)(2,1)S(1)}, bf16[256,512]{1,0:T(8,128)(2,1)S(1)}, u32[]{:S(2)}, u32[]{:S(2)}) collective-permute-start(bf16[256,512]{1,0:T(8,128)(2,1)S(1)} %bitcast.44), channel_id=1, source_target_pairs={{0,8},{8,0},{16,24},{24,16},{32,40},{40,32},{48,56},{56,48},{64,72... | collective-permute-start | bytes 786440 | tf_op jit(solution)/shard_map/ppermute | solution.py:464

commit v12 on v11

--- a/solution.py
+++ b/solution.py
@@ -74,7 +74,7 @@
     out_ref[1] = b_ref[...]
 
 
-def rest_kernel(meta_ref, pair_ref, a_ref, b_ref, out_ref):
+def rest_kernel(meta_ref, pair_ref, a_ref, b_ref, passed_hbm, out_ref):
     core = meta_ref[0]
 
     @pl.when(core == 0)
@@ -409,7 +409,7 @@
     pair = call(pair_kernel, [vmem] * 2, both)(own, r1)
     s1 = hop(pair, (1, 0), (0, 1))
     s2 = hop(s1, None, (0, 1))
-    rest = call(rest_kernel, [smem] + [vmem] * 3, both)(meta, pair, r2, r3)
+    rest = call(rest_kernel, [smem] + [vmem] * 3 + [pinned], both)(meta, pair, r2, r3, s1)
     s3 = hop(rest, (1, 0), (0, 3))
     shape = (N_ROW, N_COL * PER_PEER, HALF)
     blocks = [b.reshape(1, 2, *shape) for b in (own, r1, r2, r3)]

time: 170 us -> 172 us (1.012); the launches traced: 171 us -> 170 us
  waiting for transfers between devices: 64.1 us -> 78.4 us
  starting transfers between devices: 40.3 us -> 30.3 us
  blocking collectives: 36.9 us -> 31.1 us
    ppermute x3, waiting for transfers between devices: 7.83 us -> 13.6 us  [shards(): got1 = [lax.ppermute(send1[k - 1], 'col', x_moves(k)) for k in (1, 3, 2)]]
    all_to_all x3, blocking collectives: 36.9 us -> 31.1 us  [exchange(): lax.all_to_all(parts, axis, split_axis=0, concat_axis=0, axis_index_group...]
    ppermute x1, starting transfers between devices: 6.87 us -> 1.65 us  [shards(): theirs = lax.ppermute(others, 'row', swap)]
    ppermute x1, waiting for transfers between devices: 13.1 us -> 16.9 us  [shards(): got1 = lax.ppermute(send1, 'col', y_moves())]
    ppermute x6, waiting for transfers between devices: 28.7 us -> 32.4 us  [hop(): return lax.ppermute(block, 'row', row_moves(move))]
    ppermute x1, starting transfers between devices: 2.42 us -> 0.09 us  [shards(): got0 = lax.ppermute(send0, 'col', y_moves())]
    ppermute x3, starting transfers between devices: 6.94 us -> 4.93 us  [shards(): got1 = [lax.ppermute(send1[k - 1], 'col', x_moves(k)) for k in (1, 3, 2)]]
where the time goes in v12:
time: 172 us; the launch traced here: 170 us
  waiting for transfers between devices  78.4 us (46%)
  blocking collectives  31.1 us (18%)
  starting transfers between devices  30.3 us (18%)
  Pallas kernels  24.3 us (14%)
  local copies, waits for them, and re-layouts  3.29 us (2%)
  between operations  1.72 us (1%)
    ppermute x6, waiting for transfers between devices, hop(): return lax.ppermute(block, 'row', row_moves(move))  32.4 us
    all_to_all x3, blocking collectives, exchange(): lax.all_to_all(parts, axis, split_axis=0, concat_axis=0, axis_index_group...  31.1 us
    pallas_call x13, Pallas kernels, run(): return made(*held)  24.3 us
    ppermute x1, waiting for transfers between devices, shards(): got1 = lax.ppermute(send1, 'col', y_moves())  16.9 us
    ppermute x3, waiting for transfers between devices, shards(): got1 = [lax.ppermute(send1[k - 1], 'col', x_moves(k)) for k in (1, 3, 2)]  13.6 us
    all_to_all x1, waiting for transfers between devices, exchange(): lax.all_to_all(parts, axis, split_axis=0, concat_axis=0, axis_index_group...  9.51 us
    ppermute x6, starting transfers between devices, hop(): return lax.ppermute(block, 'row', row_moves(move))  7.2 us
    all_to_all x1, starting transfers between devices, exchange(): lax.all_to_all(parts, axis, split_axis=0, concat_axis=0, axis_index_group...  7.14 us
  transfers between devices with their start and end apart: 20, of which 12 were waited for; matrix products, arithmetic and copies ran while one was open for 1% of the time, Pallas kernels for 6%

profile of v12, /device:TPU:1, one launch (start us, length us, event | category | flops | bytes accessed | tf_op | source)
XLA Modules:
  0.0 170.4 jit_solution(13375530419381822130)
XLA Ops:
  0.6 0.7 copy-done.5
  1.3 2.3 %shard_map.96 = bf16[16,64,256]{2,1,0:T(8,128)(2,1)} custom-call(s32[1,512]{1,0:T(1,128)S(1)} %bitcast.38, bf16[512,512]{1,0:T(8,128)(2,1)} %features_hbm.1), custom_call_target="tpu_custom_call" | custom-call | tf_op jit(solution)/shard_map/pallas_call | solution.py:327
  3.6 1.5 collective-permute-start.1
  5.1 7.1 %all-to-all-start = ((bf16[16,64,256]{2,1,0:T(8,128)(2,1)}), bf16[16,64,256]{2,1,0:T(8,128)(2,1)S(1)}, u32[]{:S(2)}, u32[]{:S(2)}) async-start(bf16[16,64,256]{2,1,0:T(8,128)(2,1)} %shard_map.96), calls=%async_computation | async-start | bytes 1048576 | tf_op jit(solution)/shard_map/all_to_all | solution.py:299
  12.9 0.0 copy-start.6
  12.9 0.7 copy-done.6
  13.6 0.7 copy-done.7
  14.3 0.5 shard_map.95
  14.7 0.1 collective-permute-start
  14.8 9.5 %all-to-all-done.arrived_ref = bf16[16,64,256]{2,1,0:T(8,128)(2,1)S(1)} async-done(((bf16[16,64,256]{2,1,0:T(8,128)(2,1)}), bf16[16,64,256]{2,1,0:T(8,128)(2,1)S(1)}, u32[]{:S(2)}, u32[]{:S(2)}) %all-to-all-start) | async-done | bytes 524320 | tf_op jit(solution)/shard_map/all_to_all | solution.py:299
  24.4 0.4 shard_map.97.a_ref
  24.8 0.0 copy-start
  24.8 0.0 collective-permute-done
  24.8 0.5 collective-permute-start.2
  25.3 0.7 collective-permute-start.3
  26.0 7.2 %collective-permute-done.2.b_ref = bf16[2,512,256]{2,1,0:T(8,128)(2,1)S(1)} collective-permute-done((bf16[2,512,256]{2,1,0:T(8,128)(2,1)S(1)}, bf16[2,512,256]{2,1,0:T(8,128)(2,1)S(1)}, u32[]{:S(2)}, u32[]{:S(2)}) %collective-permute-start.2) | collective-permute-done | bytes 524320 | tf_op jit(solution)/shard_map/ppermute | solution.py:403
  33.2 0.1 shard_map.99.pair_ref
  33.3 1.7 collective-permute-start.5
  35.0 0.7 collective-permute-start.4
  35.8 0.1 stack.51.meta_ref
  35.9 0.0 collective-permute-done.4.b_ref
  36.0 13.5 %collective-permute-done.5.passed_hbm = bf16[2,2,512,256]{3,2,1,0:T(8,128)(2,1)} collective-permute-done((bf16[2,2,512,256]{3,2,1,0:T(8,128)(2,1)S(1)}, bf16[2,2,512,256]{3,2,1,0:T(8,128)(2,1)}, u32[]{:S(2)}, u32[]{:S(2)}) %collective-permute-start.5) | collective-permute-done | bytes 1048608 | tf_op jit(solution)/shard_map/ppermute | solution.py:403
  49.4 1.6 shard_map.100
  51.0 1.8 %collective-permute-start.6 = (bf16[2,2,512,256]{3,2,1,0:T(8,128)(2,1)}, bf16[2,2,512,256]{3,2,1,0:T(8,128)(2,1)}, u32[]{:S(2)}, u32[]{:S(2)}) collective-permute-start(bf16[2,2,512,256]{3,2,1,0:T(8,128)(2,1)} %shard_map.100), channel_id=1, source_target_pairs={{0,64},{8,56},{16,80},{24,8},{32,96},{40,24},{48,112},{56,40},{64,... | collective-permute-start | bytes 3145736 | tf_op jit(solution)/shard_map/ppermute | solution.py:403
  52.8 1.9 %collective-permute-start.7 = (bf16[2,2,512,256]{3,2,1,0:T(8,128)(2,1)}, bf16[2,2,512,256]{3,2,1,0:T(8,128)(2,1)}, u32[]{:S(2)}, u32[]{:S(2)}) collective-permute-start(bf16[2,2,512,256]{3,2,1,0:T(8,128)(2,1)} %collective-permute-done.5.passed_hbm), channel_id=1, source_target_pairs={{8,24},{24,40},{40,56},{56,8},{72,88},{88,104},{104,120},{120,72},... | collective-permute-start | bytes 3145736 | tf_op jit(solution)/shard_map/ppermute | solution.py:403
  54.7 3.3 %shard_map.98.tiles = bf16[193,128,128]{2,1,0:T(8,128)(2,1)S(1)} custom-call(s32[12]{0:T(128)S(1)} %stack.51.meta_ref, bf16[192,128,128]{2,1,0:T(8,128)(2,1)} %bitcast.42, bf16[192,128,128]{2,1,0:T(8,128)(2,1)} %collective-permute-done.1.other_hbm), custom_call_target="tpu_custom_call" | custom-call | tf_op jit(solution)/shard_map/pallas_call | solution.py:327
  58.1 7.2 %collective-permute-done.6 = bf16[2,2,512,256]{3,2,1,0:T(8,128)(2,1)} collective-permute-done((bf16[2,2,512,256]{3,2,1,0:T(8,128)(2,1)}, bf16[2,2,512,256]{3,2,1,0:T(8,128)(2,1)}, u32[]{:S(2)}, u32[]{:S(2)}) %collective-permute-start.6) | collective-permute-done | bytes 1048608 | tf_op jit(solution)/shard_map/ppermute | solution.py:403
  65.3 4.6 %collective-permute-done.7 = bf16[2,2,512,256]{3,2,1,0:T(8,128)(2,1)} collective-permute-done((bf16[2,2,512,256]{3,2,1,0:T(8,128)(2,1)}, bf16[2,2,512,256]{3,2,1,0:T(8,128)(2,1)}, u32[]{:S(2)}, u32[]{:S(2)}) %collective-permute-start.7) | collective-permute-done | bytes 1048608 | tf_op jit(solution)/shard_map/ppermute | solution.py:403
  69.8 5.8 %shard_map.101 = (bf16[4,512,256]{2,1,0:T(8,128)(2,1)S(1)}, bf16[4,512,256]{2,1,0:T(8,128)(2,1)S(1)}, bf16[8,2,16,32,256]{4,3,2,1,0:T(8,128)(2,1)S(1)}, bf16[193,128,128]{2,1,0:T(8,128)(2,1)S(1)}) custom-call(s32[12]{0:T(128)S(1)} %stack.51.meta_ref, s32[8,288]{1,0:T(8,128)S(1)} %get-tuple-element.48.plan_ref, bf16[193,128,128]{2,1,0:T(8,128)(2,1)S(1)} %shard_map.98.tiles, ...), custom_call_target="tpu_custom_call" | custom-call | tf_op jit(solution)/shard_map/pallas_call | solution.py:327
  75.6 0.1 collective-permute-start.8
  75.7 5.0 %shard_map.102 = (bf16[2,512,256]{2,1,0:T(8,128)(2,1)S(1)}, bf16[2,512,256]{2,1,0:T(8,128)(2,1)S(1)}, bf16[2,512,256]{2,1,0:T(8,128)(2,1)S(1)}, bf16[2,512,256]{2,1,0:T(8,128)(2,1)S(1)}) custom-call(s32[12]{0:T(128)S(1)} %stack.51.meta_ref, s32[8,288]{1,0:T(8,128)S(1)} %get-tuple-element.49.plan_ref, bf16[193,128,128]{2,1,0:T(8,128)(2,1)S(1)} %get-tuple-element.27.tiles, ...), custom_call_target="tpu_custom_call" | custom-call | tf_op jit(solution)/shard_map/pallas_call | solution.py:327
  80.7 0.0 copy-start.4
  80.7 1.6 collective-permute-start.10
  82.3 1.1 collective-permute-start.11
  83.5 0.7 collective-permute-start.12
  84.2 16.9 %collective-permute-done.8.got_ref = bf16[4,512,256]{2,1,0:T(8,128)(2,1)S(1)} collective-permute-done((bf16[4,512,256]{2,1,0:T(8,128)(2,1)S(1)}, bf16[4,512,256]{2,1,0:T(8,128)(2,1)S(1)}, u32[]{:S(2)}, u32[]{:S(2)}) %collective-permute-start.8) | collective-permute-done | bytes 1048608 | tf_op jit(solution)/shard_map/ppermute | solution.py:433
  101.1 0.8 shard_map.103
  101.8 0.1 collective-permute-start.9
  101.9 2.7 %collective-permute-start.14 = (bf16[512,256]{1,0:T(8,128)(2,1)S(1)}, bf16[512,256]{1,0:T(8,128)(2,1)S(1)}, u32[]{:S(2)}, u32[]{:S(2)}) collective-permute-start(bf16[512,256]{1,0:T(8,128)(2,1)S(1)} %get-tuple-element.40), channel_id=1, source_target_pairs={{0,3},{1,0},{2,1},{3,2},{4,7},{5,4},{6,5},{7,6},{8,11},{9,8},{10,9... | collective-permute-start | bytes 786440 | tf_op jit(solution)/shard_map/ppermute | solution.py:438
  104.6 7.8 %collective-permute-done.9.a_ref = bf16[512,256]{1,0:T(8,128)(2,1)S(1)} collective-permute-done((bf16[512,256]{1,0:T(8,128)(2,1)S(1)}, bf16[512,256]{1,0:T(8,128)(2,1)S(1)}, u32[]{:S(2)}, u32[]{:S(2)}) %collective-permute-start.9) | collective-permute-done | bytes 262176 | tf_op jit(solution)/shard_map/ppermute | solution.py:438
  112.3 2.2 %collective-permute-start.15 = (bf16[512,256]{1,0:T(8,128)(2,1)S(1)}, bf16[512,256]{1,0:T(8,128)(2,1)S(1)}, u32[]{:S(2)}, u32[]{:S(2)}) collective-permute-start(bf16[512,256]{1,0:T(8,128)(2,1)S(1)} %get-tuple-element.41), channel_id=1, source_target_pairs={{0,2},{1,3},{2,0},{3,1},{4,6},{5,7},{6,4},{7,5},{8,10},{9,11},{10,... | collective-permute-start | bytes 786440 | tf_op jit(solution)/shard_map/ppermute | solution.py:438
  114.5 0.0 collective-permute-done.10.a_ref
  114.5 0.0 collective-permute-done.11.b_ref
  114.5 0.8 shard_map.104
  115.3 0.1 collective-permute-start.13
  115.4 5.9 %collective-permute-done.15.c_ref = bf16[512,256]{1,0:T(8,128)(2,1)S(1)} collective-permute-done((bf16[512,256]{1,0:T(8,128)(2,1)S(1)}, bf16[512,256]{1,0:T(8,128)(2,1)S(1)}, u32[]{:S(2)}, u32[]{:S(2)}) %collective-permute-start.15) | collective-permute-done | bytes 262176 | tf_op jit(solution)/shard_map/ppermute | solution.py:438
  121.3 2.7 %collective-permute-done.13.got0 = bf16[512,256]{1,0:T(8,128)(2,1)S(1)} collective-permute-done((bf16[512,256]{1,0:T(8,128)(2,1)S(1)}, bf16[512,256]{1,0:T(8,128)(2,1)S(1)}, u32[]{:S(2)}, u32[]{:S(2)}) %collective-permute-start.13) | collective-permute-done | bytes 262176 | tf_op jit(solution)/shard_map/ppermute | solution.py:442
  124.1 0.8 shard_map.105
  124.9 1.7 collective-permute-start.16
  126.5 1.1 constant_dynamic-slice_fusion.cotangent_ref
  127.6 0.5 collective-permute-done.16.got_ref
  128.0 2.3 %shard_map.106 = (bf16[512,512]{1,0:T(8,128)(2,1)}, bf16[512,512]{1,0:T(8,128)(2,1)S(1)}) custom-call(s32[12]{0:T(128)S(1)} %stack.51.meta_ref, f32[512,256]{1,0:T(8,128)S(1)} %get-tuple-element.42.mine_ref, f32[512,256]{1,0:T(8,128)S(1)} %collective-permute-done.16.got_ref, bf16[512,512]{1,0:T(8,128)(2,1)S(1)} %copy-done.4, ...), custom_call_target="tpu_custom_call" | custom-call | tf_op jit(solution)/shard_map/pallas_call | solution.py:327
  130.4 0.4 collective-permute-start.17
  130.7 1.5 collective-permute-done.17.other_slope_ref
  132.3 0.7 shard_map.107
  133.0 8.5 %all_to_all.20 = bf16[8,32,512]{2,1,0:T(8,128)(2,1)S(1)} all-to-all(bf16[8,32,512]{2,1,0:T(8,128)(2,1)S(1)} %bitcast.37), channel_id=1, replica_groups={{0,16,32,48,64,80,96,112},{8,24,40,56,72,88,104,120},{1,17,33,49,65,81,..., dimensions={0} | all-to-all | bytes 524288 | tf_op jit(solution)/shard_map/all_to_all | solution.py:299
  141.5 0.1 convert_element_type.11
  141.6 0.1 broadcast_in_dim.6
  141.7 12.9 %all_to_all.21 = f32[8,32,512]{2,1,0:T(8,128)S(1)} all-to-all(f32[8,32,512]{2,1,0:T(8,128)S(1)} %broadcast_in_dim.6), channel_id=1, replica_groups=mesh['row'=16,'col'=8] {'col'}, dimensions={0} | all-to-all | bytes 1048576 | tf_op jit(solution)/shard_map/all_to_all | solution.py:299
  154.7 9.7 %all_to_all.22 = bf16[8,32,512]{2,1,0:T(8,128)(2,1)S(1)} all-to-all(bf16[8,32,512]{2,1,0:T(8,128)(2,1)S(1)} %broadcast_in_dim.7), channel_id=1, replica_groups={{0,16,32,48,64,80,96,112},{8,24,40,56,72,88,104,120},{1,17,33,49,65,81,..., dimensions={0} | all-to-all | bytes 524288 | tf_op jit(solution)/shard_map/all_to_all | solution.py:299
  164.4 3.7 %collective-permute-start.18 = (bf16[256,512]{1,0:T(8,128)(2,1)S(1)}, bf16[256,512]{1,0:T(8,128)(2,1)S(1)}, u32[]{:S(2)}, u32[]{:S(2)}) collective-permute-start(bf16[256,512]{1,0:T(8,128)(2,1)S(1)} %bitcast.44), channel_id=1, source_target_pairs={{0,8},{8,0},{16,24},{24,16},{32,40},{40,32},{48,56},{56,48},{64,72... | collective-permute-start | bytes 786440 | tf_op jit(solution)/shard_map/ppermute | solution.py:464
  168.1 1.2 collective-permute-done.18
  169.3 0.1 broadcast_select_fusion.1
  169.3 1.1 maximum_convert_fusion
  (18 shorter events, 0.1 us)
Async XLA Ops:
  0.6 0.7 copy-start.5
  3.6 21.2 %collective-permute-start.1 = (bf16[192,128,128]{2,1,0:T(8,128)(2,1)}, bf16[192,128,128]{2,1,0:T(8,128)(2,1)}, u32[]{:S(2)}, u32[]{:S(2)}) collective-permute-start(bf16[192,128,128]{2,1,0:T(8,128)(2,1)} %bitcast.41), channel_id=1, source_target_pairs={{0,8},{8,0},{16,24},{24,16},{32,40},{40,32},{48,56},{56,48},{64,72... | collective-permute-start | bytes 18874376 | tf_op jit(solution)/shard_map/ppermute | solution.py:386
  5.1 19.2 %all-to-all-start = ((bf16[16,64,256]{2,1,0:T(8,128)(2,1)}), bf16[16,64,256]{2,1,0:T(8,128)(2,1)S(1)}, u32[]{:S(2)}, u32[]{:S(2)}) async-start(bf16[16,64,256]{2,1,0:T(8,128)(2,1)} %shard_map.96), calls=%async_computation | async-start | bytes 1048576 | tf_op jit(solution)/shard_map/all_to_all | solution.py:299
  12.9 0.7 copy-start.6
  13.6 0.7 copy-start.7
  14.7 10.1 %collective-permute-start = (s32[8,288]{1,0:T(8,128)S(1)}, s32[8,288]{1,0:T(8,128)S(1)}, u32[]{:S(2)}, u32[]{:S(2)}) collective-permute-start(s32[8,288]{1,0:T(8,128)S(1)} %shard_map.95), channel_id=1, source_target_pairs={{0,8},{8,0},{16,24},{24,16},{32,40},{40,32},{48,56},{56,48},{64,72... | collective-permute-start | bytes 27656 | tf_op jit(solution)/shard_map/ppermute | solution.py:378
  24.8 33.3 %copy-start = (bf16[2,512,256]{2,1,0:T(8,128)(2,1)}, bf16[2,512,256]{2,1,0:T(8,128)(2,1)S(1)}, u32[]{:S(2)}) copy-start(bf16[2,512,256]{2,1,0:T(8,128)(2,1)S(1)} %shard_map.97.a_ref) | copy-start | bytes 1572868
  24.8 8.4 %collective-permute-start.2 = (bf16[2,512,256]{2,1,0:T(8,128)(2,1)S(1)}, bf16[2,512,256]{2,1,0:T(8,128)(2,1)S(1)}, u32[]{:S(2)}, u32[]{:S(2)}) collective-permute-start(bf16[2,512,256]{2,1,0:T(8,128)(2,1)S(1)} %shard_map.97.a_ref), channel_id=1, source_target_pairs={{0,16},{8,72},{16,32},{24,88},{32,48},{40,104},{48,0},{56,120},{64... | collective-permute-start | bytes 1572872 | tf_op jit(solution)/shard_map/ppermute | solution.py:403
  25.3 9.7 %collective-permute-start.3 = (bf16[2,512,256]{2,1,0:T(8,128)(2,1)S(1)}, bf16[2,512,256]{2,1,0:T(8,128)(2,1)S(1)}, u32[]{:S(2)}, u32[]{:S(2)}) collective-permute-start(bf16[2,512,256]{2,1,0:T(8,128)(2,1)S(1)} %shard_map.97.a_ref), channel_id=1, source_target_pairs={{0,48},{16,0},{32,16},{48,32},{64,112},{80,64},{96,80},{112,96},{1... | collective-permute-start | bytes 1572872 | tf_op jit(solution)/shard_map/ppermute | solution.py:403
  33.2 24.8 %copy-start.3 = (bf16[2,512,256]{2,1,0:T(8,128)(2,1)}, bf16[2,512,256]{2,1,0:T(8,128)(2,1)S(1)}, u32[]{:S(2)}) copy-start(bf16[2,512,256]{2,1,0:T(8,128)(2,1)S(1)} %collective-permute-done.2.b_ref) | copy-start | bytes 1572868
  33.3 16.1 %collective-permute-start.5 = (bf16[2,2,512,256]{3,2,1,0:T(8,128)(2,1)S(1)}, bf16[2,2,512,256]{3,2,1,0:T(8,128)(2,1)}, u32[]{:S(2)}, u32[]{:S(2)}) collective-permute-start(bf16[2,2,512,256]{3,2,1,0:T(8,128)(2,1)S(1)} %shard_map.99.pair_ref), channel_id=1, source_target_pairs={{0,64},{8,24},{16,80},{24,40},{32,96},{40,56},{48,112},{56,8},{64,... | collective-permute-start | bytes 3145736 | tf_op jit(solution)/shard_map/ppermute | solution.py:403
  35.0 23.1 %copy-start.1 = (bf16[2,512,256]{2,1,0:T(8,128)(2,1)}, bf16[2,512,256]{2,1,0:T(8,128)(2,1)S(1)}, u32[]{:S(2)}) copy-start(bf16[2,512,256]{2,1,0:T(8,128)(2,1)S(1)} %collective-permute-done.3.a_ref) | copy-start | bytes 1572868
  35.0 0.9 collective-permute-start.4
  36.0 22.1 %copy-start.2 = (bf16[2,512,256]{2,1,0:T(8,128)(2,1)}, bf16[2,512,256]{2,1,0:T(8,128)(2,1)S(1)}, u32[]{:S(2)}) copy-start(bf16[2,512,256]{2,1,0:T(8,128)(2,1)S(1)} %collective-permute-done.4.b_ref) | copy-start | bytes 1572868
  51.0 14.3 %collective-permute-start.6 = (bf16[2,2,512,256]{3,2,1,0:T(8,128)(2,1)}, bf16[2,2,512,256]{3,2,1,0:T(8,128)(2,1)}, u32[]{:S(2)}, u32[]{:S(2)}) collective-permute-start(bf16[2,2,512,256]{3,2,1,0:T(8,128)(2,1)} %shard_map.100), channel_id=1, source_target_pairs={{0,64},{8,56},{16,80},{24,8},{32,96},{40,24},{48,112},{56,40},{64,... | collective-permute-start | bytes 3145736 | tf_op jit(solution)/shard_map/ppermute | solution.py:403
  52.8 17.1 %collective-permute-start.7 = (bf16[2,2,512,256]{3,2,1,0:T(8,128)(2,1)}, bf16[2,2,512,256]{3,2,1,0:T(8,128)(2,1)}, u32[]{:S(2)}, u32[]{:S(2)}) collective-permute-start(bf16[2,2,512,256]{3,2,1,0:T(8,128)(2,1)} %collective-permute-done.5.passed_hbm), channel_id=1, source_target_pairs={{8,24},{24,40},{40,56},{56,8},{72,88},{88,104},{104,120},{120,72},... | collective-permute-start | bytes 3145736 | tf_op jit(solution)/shard_map/ppermute | solution.py:403
  75.6 25.5 %collective-permute-start.8 = (bf16[4,512,256]{2,1,0:T(8,128)(2,1)S(1)}, bf16[4,512,256]{2,1,0:T(8,128)(2,1)S(1)}, u32[]{:S(2)}, u32[]{:S(2)}) collective-permute-start(bf16[4,512,256]{2,1,0:T(8,128)(2,1)S(1)} %get-tuple-element.31), channel_id=1, source_target_pairs={{0,4},{1,5},{2,6},{3,7},{4,0},{5,1},{6,2},{7,3},{8,12},{9,13},{10,... | collective-permute-start | bytes 3145736 | tf_op jit(solution)/shard_map/ppermute | solution.py:433
  80.7 47.3 %copy-start.4 = (bf16[512,512]{1,0:T(8,128)(2,1)S(1)}, bf16[512,512]{1,0:T(8,128)(2,1)}, u32[]{:S(2)}) copy-start(bf16[512,512]{1,0:T(8,128)(2,1)} %weight_ref.1) | copy-start | bytes 1572868
  80.7 33.8 %collective-permute-start.10 = (bf16[2,512,256]{2,1,0:T(8,128)(2,1)S(1)}, bf16[2,512,256]{2,1,0:T(8,128)(2,1)S(1)}, u32[]{:S(2)}, u32[]{:S(2)}) collective-permute-start(bf16[2,512,256]{2,1,0:T(8,128)(2,1)S(1)} %get-tuple-element.34), channel_id=1, source_target_pairs={{0,1},{1,2},{2,3},{3,0},{4,5},{5,6},{6,7},{7,4},{8,9},{9,10},{10,1... | collective-permute-start | bytes 1572872 | tf_op jit(solution)/shard_map/ppermute | solution.py:432
  82.3 32.2 %collective-permute-start.11 = (bf16[2,512,256]{2,1,0:T(8,128)(2,1)S(1)}, bf16[2,512,256]{2,1,0:T(8,128)(2,1)S(1)}, u32[]{:S(2)}, u32[]{:S(2)}) collective-permute-start(bf16[2,512,256]{2,1,0:T(8,128)(2,1)S(1)} %get-tuple-element.35), channel_id=1, source_target_pairs={{0,3},{1,0},{2,1},{3,2},{4,7},{5,4},{6,5},{7,6},{8,11},{9,8},{10,9... | collective-permute-start | bytes 1572872 | tf_op jit(solution)/shard_map/ppermute | solution.py:432
  83.5 31.1 %collective-permute-start.12 = (bf16[2,512,256]{2,1,0:T(8,128)(2,1)S(1)}, bf16[2,512,256]{2,1,0:T(8,128)(2,1)S(1)}, u32[]{:S(2)}, u32[]{:S(2)}) collective-permute-start(bf16[2,512,256]{2,1,0:T(8,128)(2,1)S(1)} %get-tuple-element.36), channel_id=1, source_target_pairs={{0,2},{1,3},{2,0},{3,1},{4,6},{5,7},{6,4},{7,5},{8,10},{9,11},{10,... | collective-permute-start | bytes 1572872 | tf_op jit(solution)/shard_map/ppermute | solution.py:432
  101.8 10.5 %collective-permute-start.9 = (bf16[512,256]{1,0:T(8,128)(2,1)S(1)}, bf16[512,256]{1,0:T(8,128)(2,1)S(1)}, u32[]{:S(2)}, u32[]{:S(2)}) collective-permute-start(bf16[512,256]{1,0:T(8,128)(2,1)S(1)} %get-tuple-element.32), channel_id=1, source_target_pairs={{0,1},{1,2},{2,3},{3,0},{4,5},{5,6},{6,7},{7,4},{8,9},{9,10},{10,1... | collective-permute-start | bytes 786440 | tf_op jit(solution)/shard_map/ppermute | solution.py:438
  101.9 13.5 %collective-permute-start.14 = (bf16[512,256]{1,0:T(8,128)(2,1)S(1)}, bf16[512,256]{1,0:T(8,128)(2,1)S(1)}, u32[]{:S(2)}, u32[]{:S(2)}) collective-permute-start(bf16[512,256]{1,0:T(8,128)(2,1)S(1)} %get-tuple-element.40), channel_id=1, source_target_pairs={{0,3},{1,0},{2,1},{3,2},{4,7},{5,4},{6,5},{7,6},{8,11},{9,8},{10,9... | collective-permute-start | bytes 786440 | tf_op jit(solution)/shard_map/ppermute | solution.py:438
  112.3 9.0 %collective-permute-start.15 = (bf16[512,256]{1,0:T(8,128)(2,1)S(1)}, bf16[512,256]{1,0:T(8,128)(2,1)S(1)}, u32[]{:S(2)}, u32[]{:S(2)}) collective-permute-start(bf16[512,256]{1,0:T(8,128)(2,1)S(1)} %get-tuple-element.41), channel_id=1, source_target_pairs={{0,2},{1,3},{2,0},{3,1},{4,6},{5,7},{6,4},{7,5},{8,10},{9,11},{10,... | collective-permute-start | bytes 786440 | tf_op jit(solution)/shard_map/ppermute | solution.py:438
  115.3 8.7 %collective-permute-start.13 = (bf16[512,256]{1,0:T(8,128)(2,1)S(1)}, bf16[512,256]{1,0:T(8,128)(2,1)S(1)}, u32[]{:S(2)}, u32[]{:S(2)}) collective-permute-start(bf16[512,256]{1,0:T(8,128)(2,1)S(1)} %get-tuple-element.38), channel_id=1, source_target_pairs={{0,4},{1,5},{2,6},{3,7},{4,0},{5,1},{6,2},{7,3},{8,12},{9,13},{10,... | collective-permute-start | bytes 786440 | tf_op jit(solution)/shard_map/ppermute | solution.py:442
  124.9 3.2 %collective-permute-start.16 = (f32[512,256]{1,0:T(8,128)S(1)}, f32[512,256]{1,0:T(8,128)S(1)}, u32[]{:S(2)}, u32[]{:S(2)}) collective-permute-start(f32[512,256]{1,0:T(8,128)S(1)} %get-tuple-element.43.other_ref), channel_id=1, source_target_pairs={{0,8},{8,0},{16,24},{24,16},{32,40},{40,32},{48,56},{56,48},{64,72... | collective-permute-start | bytes 1572872 | tf_op jit(solution)/shard_map/ppermute | solution.py:446
  130.4 1.9 %collective-permute-start.17 = (bf16[512,512]{1,0:T(8,128)(2,1)S(1)}, bf16[512,512]{1,0:T(8,128)(2,1)S(1)}, u32[]{:S(2)}, u32[]{:S(2)}) collective-permute-start(bf16[512,512]{1,0:T(8,128)(2,1)S(1)} %get-tuple-element.45.slope_ref), channel_id=1, source_target_pairs={{0,8},{8,0},{16,24},{24,16},{32,40},{40,32},{48,56},{56,48},{64,72... | collective-permute-start | bytes 1572872 | tf_op jit(solution)/shard_map/ppermute | solution.py:453
  164.4 4.9 %collective-permute-start.18 = (bf16[256,512]{1,0:T(8,128)(2,1)S(1)}, bf16[256,512]{1,0:T(8,128)(2,1)S(1)}, u32[]{:S(2)}, u32[]{:S(2)}) collective-permute-start(bf16[256,512]{1,0:T(8,128)(2,1)S(1)} %bitcast.44), channel_id=1, source_target_pairs={{0,8},{8,0},{16,24},{24,16},{32,40},{40,32},{48,56},{56,48},{64,72... | collective-permute-start | bytes 786440 | tf_op jit(solution)/shard_map/ppermute | solution.py:464

commit v13 on v8

--- a/solution.py
+++ b/solution.py
@@ -391,7 +391,7 @@
     t1 = hop(r1, None, (0, 3))
     t2 = hop(later, None, (0, 3))
     t3 = hop(later, None, (0, 2))
-    t4 = hop(r1, None, (0, 2))
+    t4 = hop(s1, None, (0, 1))
     blocks = [
         b.reshape(2, N_ROW, N_COL * PER_PEER, HALF)
         for b in (own, r1, r4, s1, r2, r3, s2, s3, t1, t2, t3, t4)

time: 168 us -> 167 us (level)
  starting transfers between devices: 47.6 us -> 45.6 us
  waiting for transfers between devices: 58.1 us -> 60.1 us
    ppermute x1, starting transfers between devices: 2.77 us -> 0.09 us  [shards(): got0 = lax.ppermute(send0, 'col', y_moves())]
    ppermute x3, waiting for transfers between devices: 14.4 us -> 16.7 us  [shards(): got1 = [lax.ppermute(send1[k - 1], 'col', x_moves(k)) for k in (1, 3, 2)]]
  transfers between devices with their start and end apart: 25 -> 25, of which waited for: 14 -> 13; matrix products, arithmetic and copies ran while one was open for 1% -> 1% of each run, Pallas kernels for 7% -> 7%
where the time goes in v13:
time: 167 us
  waiting for transfers between devices  60.1 us (36%)
  starting transfers between devices  45.6 us (27%)
  blocking collectives  31.6 us (19%)
  Pallas kernels  22.5 us (13%)
  local copies, waits for them, and re-layouts  4.06 us (2%)
  between operations  1.74 us (1%)
    all_to_all x3, blocking collectives, exchange(): lax.all_to_all(parts, axis, split_axis=0, concat_axis=0, axis_index_group...  31.6 us
    ppermute x11, starting transfers between devices, hop(): return lax.ppermute(block, 'row', row_moves(move))  23.7 us
    pallas_call x11, Pallas kernels, run(): return made(*held)  22.5 us
    ppermute x3, waiting for transfers between devices, shards(): got1 = [lax.ppermute(send1[k - 1], 'col', x_moves(k)) for k in (1, 3, 2)]  16.7 us
    ppermute x11, waiting for transfers between devices, hop(): return lax.ppermute(block, 'row', row_moves(move))  15.8 us
    ppermute x1, waiting for transfers between devices, shards(): got1 = lax.ppermute(send1, 'col', y_moves())  13.5 us
    all_to_all x1, waiting for transfers between devices, exchange(): lax.all_to_all(parts, axis, split_axis=0, concat_axis=0, axis_index_group...  9.51 us
    all_to_all x1, starting transfers between devices, exchange(): lax.all_to_all(parts, axis, split_axis=0, concat_axis=0, axis_index_group...  7.14 us
  transfers between devices with their start and end apart: 25, of which 13 were waited for; matrix products, arithmetic and copies ran while one was open for 1% of the time, Pallas kernels for 7%

profile of v13, /device:TPU:1, one launch (start us, length us, event | category | flops | bytes accessed | tf_op | source)
XLA Modules:
  0.0 166.8 jit_solution(10178049533672420039)
XLA Ops:
  0.6 0.7 copy-done.3
  1.3 2.3 %shard_map.96 = bf16[16,64,256]{2,1,0:T(8,128)(2,1)} custom-call(s32[1,512]{1,0:T(1,128)S(1)} %bitcast.46, bf16[512,512]{1,0:T(8,128)(2,1)} %features_hbm.1), custom_call_target="tpu_custom_call" | custom-call | tf_op jit(solution)/shard_map/pallas_call | solution.py:305
  3.6 1.5 collective-permute-start.1
  5.1 7.1 %all-to-all-start = ((bf16[16,64,256]{2,1,0:T(8,128)(2,1)}), bf16[16,64,256]{2,1,0:T(8,128)(2,1)S(1)}, u32[]{:S(2)}, u32[]{:S(2)}) async-start(bf16[16,64,256]{2,1,0:T(8,128)(2,1)} %shard_map.96), calls=%async_computation | async-start | bytes 1048576 | tf_op jit(solution)/shard_map/all_to_all | solution.py:277
  12.9 0.0 copy-start.4
  12.9 0.7 copy-done.4
  13.6 0.7 copy-done.5
  14.3 0.5 shard_map.95
  14.7 0.1 collective-permute-start
  14.8 9.5 %all-to-all-done.arrived_ref = bf16[16,64,256]{2,1,0:T(8,128)(2,1)S(1)} async-done(((bf16[16,64,256]{2,1,0:T(8,128)(2,1)}), bf16[16,64,256]{2,1,0:T(8,128)(2,1)S(1)}, u32[]{:S(2)}, u32[]{:S(2)}) %all-to-all-start) | async-done | bytes 524320 | tf_op jit(solution)/shard_map/all_to_all | solution.py:277
  24.4 0.4 shard_map.97
  24.8 0.5 collective-permute-start.2
  25.3 0.7 collective-permute-start.5
  26.0 1.7 %collective-permute-start.3 = (bf16[2,512,256]{2,1,0:T(8,128)(2,1)S(1)}, bf16[2,512,256]{2,1,0:T(8,128)(2,1)S(1)}, u32[]{:S(2)}, u32[]{:S(2)}) collective-permute-start(bf16[2,512,256]{2,1,0:T(8,128)(2,1)S(1)} %shard_map.97), channel_id=1, source_target_pairs={{0,64},{8,24},{16,80},{24,40},{32,96},{40,56},{48,112},{56,8},{64,... | collective-permute-start | bytes 1572872 | tf_op jit(solution)/shard_map/ppermute | solution.py:381
  27.7 0.7 collective-permute-start.6
  28.4 4.8 %collective-permute-done.2 = bf16[2,512,256]{2,1,0:T(8,128)(2,1)S(1)} collective-permute-done((bf16[2,512,256]{2,1,0:T(8,128)(2,1)S(1)}, bf16[2,512,256]{2,1,0:T(8,128)(2,1)S(1)}, u32[]{:S(2)}, u32[]{:S(2)}) %collective-permute-start.2) | collective-permute-done | bytes 524320 | tf_op jit(solution)/shard_map/ppermute | solution.py:381
  33.2 2.5 %collective-permute-start.4 = (bf16[2,512,256]{2,1,0:T(8,128)(2,1)S(1)}, bf16[2,512,256]{2,1,0:T(8,128)(2,1)S(1)}, u32[]{:S(2)}, u32[]{:S(2)}) collective-permute-start(bf16[2,512,256]{2,1,0:T(8,128)(2,1)S(1)} %collective-permute-done.2), channel_id=1, source_target_pairs={{0,64},{8,24},{16,80},{24,40},{32,96},{40,56},{48,112},{56,8},{64,... | collective-permute-start | bytes 1572872 | tf_op jit(solution)/shard_map/ppermute | solution.py:381
  35.7 0.7 collective-permute-start.7
  36.4 4.0 %collective-permute-start.10 = (bf16[2,512,256]{2,1,0:T(8,128)(2,1)S(1)}, bf16[2,512,256]{2,1,0:T(8,128)(2,1)}, u32[]{:S(2)}, u32[]{:S(2)}) collective-permute-start(bf16[2,512,256]{2,1,0:T(8,128)(2,1)S(1)} %shard_map.97), channel_id=1, source_target_pairs={{8,56},{24,8},{40,24},{56,40},{72,120},{88,72},{104,88},{120,104},... | collective-permute-start | bytes 1572872 | tf_op jit(solution)/shard_map/ppermute | solution.py:381
  40.5 0.8 collective-permute-done.3
  41.2 4.3 %collective-permute-start.9 = (bf16[2,512,256]{2,1,0:T(8,128)(2,1)S(1)}, bf16[2,512,256]{2,1,0:T(8,128)(2,1)}, u32[]{:S(2)}, u32[]{:S(2)}) collective-permute-start(bf16[2,512,256]{2,1,0:T(8,128)(2,1)S(1)} %collective-permute-done.2), channel_id=1, source_target_pairs={{8,56},{24,8},{40,24},{56,40},{72,120},{88,72},{104,88},{120,104},... | collective-permute-start | bytes 1572872 | tf_op jit(solution)/shard_map/ppermute | solution.py:381
  45.6 1.5 collective-permute-start.8
  47.0 4.7 %collective-permute-done.4 = bf16[2,512,256]{2,1,0:T(8,128)(2,1)S(1)} collective-permute-done((bf16[2,512,256]{2,1,0:T(8,128)(2,1)S(1)}, bf16[2,512,256]{2,1,0:T(8,128)(2,1)S(1)}, u32[]{:S(2)}, u32[]{:S(2)}) %collective-permute-start.4) | collective-permute-done | bytes 524320 | tf_op jit(solution)/shard_map/ppermute | solution.py:381
  51.7 4.5 %collective-permute-start.11 = (bf16[2,512,256]{2,1,0:T(8,128)(2,1)S(1)}, bf16[2,512,256]{2,1,0:T(8,128)(2,1)}, u32[]{:S(2)}, u32[]{:S(2)}) collective-permute-start(bf16[2,512,256]{2,1,0:T(8,128)(2,1)S(1)} %shard_map.97), channel_id=1, source_target_pairs={{8,40},{24,56},{40,8},{56,24},{72,104},{88,120},{104,72},{120,88},... | collective-permute-start | bytes 1572872 | tf_op jit(solution)/shard_map/ppermute | solution.py:381
  56.3 0.0 copy-start.1
  56.3 0.8 copy-done.1
  57.1 2.6 %collective-permute-start.12 = (bf16[2,512,256]{2,1,0:T(8,128)(2,1)S(1)}, bf16[2,512,256]{2,1,0:T(8,128)(2,1)}, u32[]{:S(2)}, u32[]{:S(2)}) collective-permute-start(bf16[2,512,256]{2,1,0:T(8,128)(2,1)S(1)} %collective-permute-done.4), channel_id=1, source_target_pairs={{8,24},{24,40},{40,56},{56,8},{72,88},{88,104},{104,120},{120,72},... | collective-permute-start | bytes 1572872 | tf_op jit(solution)/shard_map/ppermute | solution.py:381
  59.8 0.1 stack.51.meta_ref
  60.0 3.3 %shard_map.98.tiles = bf16[193,128,128]{2,1,0:T(8,128)(2,1)S(1)} custom-call(s32[12]{0:T(128)S(1)} %stack.51.meta_ref, bf16[192,128,128]{2,1,0:T(8,128)(2,1)} %bitcast.50, bf16[192,128,128]{2,1,0:T(8,128)(2,1)} %collective-permute-done.1.other_hbm), custom_call_target="tpu_custom_call" | custom-call | tf_op jit(solution)/shard_map/pallas_call | solution.py:305
  63.3 5.5 %collective-permute-done.12 = bf16[2,512,256]{2,1,0:T(8,128)(2,1)} collective-permute-done((bf16[2,512,256]{2,1,0:T(8,128)(2,1)S(1)}, bf16[2,512,256]{2,1,0:T(8,128)(2,1)}, u32[]{:S(2)}, u32[]{:S(2)}) %collective-permute-start.12) | collective-permute-done | bytes 524320 | tf_op jit(solution)/shard_map/ppermute | solution.py:381
  68.8 5.4 %shard_map.99 = (bf16[4,512,256]{2,1,0:T(8,128)(2,1)S(1)}, bf16[4,512,256]{2,1,0:T(8,128)(2,1)S(1)}, bf16[8,2,16,32,256]{4,3,2,1,0:T(8,128)(2,1)S(1)}, bf16[193,128,128]{2,1,0:T(8,128)(2,1)S(1)}) custom-call(s32[12]{0:T(128)S(1)} %stack.51.meta_ref, s32[8,288]{1,0:T(8,128)S(1)} %get-tuple-element.50.plan_ref, bf16[193,128,128]{2,1,0:T(8,128)(2,1)S(1)} %shard_map.98.tiles, ...), custom_call_target="tpu_custom_call" | custom-call | tf_op jit(solution)/shard_map/pallas_call | solution.py:305
  74.3 2.0 %collective-permute-start.13 = (bf16[4,512,256]{2,1,0:T(8,128)(2,1)S(1)}, bf16[4,512,256]{2,1,0:T(8,128)(2,1)S(1)}, u32[]{:S(2)}, u32[]{:S(2)}) collective-permute-start(bf16[4,512,256]{2,1,0:T(8,128)(2,1)S(1)} %get-tuple-element.33), channel_id=1, source_target_pairs={{0,4},{1,5},{2,6},{3,7},{4,0},{5,1},{6,2},{7,3},{8,12},{9,13},{10,... | collective-permute-start | bytes 3145736 | tf_op jit(solution)/shard_map/ppermute | solution.py:415
  76.3 5.1 %shard_map.100 = (bf16[2,512,256]{2,1,0:T(8,128)(2,1)S(1)}, bf16[2,512,256]{2,1,0:T(8,128)(2,1)S(1)}, bf16[2,512,256]{2,1,0:T(8,128)(2,1)S(1)}, bf16[2,512,256]{2,1,0:T(8,128)(2,1)S(1)}) custom-call(s32[12]{0:T(128)S(1)} %stack.51.meta_ref, s32[8,288]{1,0:T(8,128)S(1)} %get-tuple-element.51.plan_ref, bf16[193,128,128]{2,1,0:T(8,128)(2,1)S(1)} %get-tuple-element.29.tiles, ...), custom_call_target="tpu_custom_call" | custom-call | tf_op jit(solution)/shard_map/pallas_call | solution.py:305
  81.4 0.0 copy-start
  81.5 0.1 collective-permute-start.15
  81.5 2.7 %collective-permute-start.16 = (bf16[2,512,256]{2,1,0:T(8,128)(2,1)S(1)}, bf16[2,512,256]{2,1,0:T(8,128)(2,1)S(1)}, u32[]{:S(2)}, u32[]{:S(2)}) collective-permute-start(bf16[2,512,256]{2,1,0:T(8,128)(2,1)S(1)} %get-tuple-element.37), channel_id=1, source_target_pairs={{0,3},{1,0},{2,1},{3,2},{4,7},{5,4},{6,5},{7,6},{8,11},{9,8},{10,9... | collective-permute-start | bytes 1572872 | tf_op jit(solution)/shard_map/ppermute | solution.py:414
  84.2 13.5 %collective-permute-done.13.got_ref = bf16[4,512,256]{2,1,0:T(8,128)(2,1)S(1)} collective-permute-done((bf16[4,512,256]{2,1,0:T(8,128)(2,1)S(1)}, bf16[4,512,256]{2,1,0:T(8,128)(2,1)S(1)}, u32[]{:S(2)}, u32[]{:S(2)}) %collective-permute-start.13) | collective-permute-done | bytes 1048608 | tf_op jit(solution)/shard_map/ppermute | solution.py:415
  97.7 0.8 shard_map.101
  98.5 0.1 collective-permute-start.14
  98.6 2.7 %collective-permute-start.19 = (bf16[512,256]{1,0:T(8,128)(2,1)S(1)}, bf16[512,256]{1,0:T(8,128)(2,1)S(1)}, u32[]{:S(2)}, u32[]{:S(2)}) collective-permute-start(bf16[512,256]{1,0:T(8,128)(2,1)S(1)} %get-tuple-element.42), channel_id=1, source_target_pairs={{0,3},{1,0},{2,1},{3,2},{4,7},{5,4},{6,5},{7,6},{8,11},{9,8},{10,9... | collective-permute-start | bytes 786440 | tf_op jit(solution)/shard_map/ppermute | solution.py:420
  101.3 9.4 %collective-permute-done.14.a_ref = bf16[512,256]{1,0:T(8,128)(2,1)S(1)} collective-permute-done((bf16[512,256]{1,0:T(8,128)(2,1)S(1)}, bf16[512,256]{1,0:T(8,128)(2,1)S(1)}, u32[]{:S(2)}, u32[]{:S(2)}) %collective-permute-start.14) | collective-permute-done | bytes 262176 | tf_op jit(solution)/shard_map/ppermute | solution.py:420
  110.7 0.2 collective-permute-start.20
  111.0 0.8 shard_map.102
  111.8 0.1 collective-permute-start.18
  111.9 4.3 %collective-permute-done.19.b_ref = bf16[512,256]{1,0:T(8,128)(2,1)S(1)} collective-permute-done((bf16[512,256]{1,0:T(8,128)(2,1)S(1)}, bf16[512,256]{1,0:T(8,128)(2,1)S(1)}, u32[]{:S(2)}, u32[]{:S(2)}) %collective-permute-start.19) | collective-permute-done | bytes 262176 | tf_op jit(solution)/shard_map/ppermute | solution.py:420
  116.2 2.9 %collective-permute-done.20.c_ref = bf16[512,256]{1,0:T(8,128)(2,1)S(1)} collective-permute-done((bf16[512,256]{1,0:T(8,128)(2,1)S(1)}, bf16[512,256]{1,0:T(8,128)(2,1)S(1)}, u32[]{:S(2)}, u32[]{:S(2)}) %collective-permute-start.20) | collective-permute-done | bytes 262176 | tf_op jit(solution)/shard_map/ppermute | solution.py:420
  119.1 1.4 collective-permute-done.18.got0
  120.5 0.8 shard_map.103
  121.3 1.6 collective-permute-start.21
  122.9 1.1 constant_dynamic-slice_fusion.cotangent_ref
  124.0 0.5 collective-permute-done.21.got_ref
  124.5 2.3 %shard_map.104 = (bf16[512,512]{1,0:T(8,128)(2,1)}, bf16[512,512]{1,0:T(8,128)(2,1)S(1)}) custom-call(s32[12]{0:T(128)S(1)} %stack.51.meta_ref, f32[512,256]{1,0:T(8,128)S(1)} %get-tuple-element.44.mine_ref, f32[512,256]{1,0:T(8,128)S(1)} %collective-permute-done.21.got_ref, bf16[512,512]{1,0:T(8,128)(2,1)S(1)} %copy-done, ...), custom_call_target="tpu_custom_call" | custom-call | tf_op jit(solution)/shard_map/pallas_call | solution.py:305
  126.8 0.4 collective-permute-start.22
  127.1 1.5 collective-permute-done.22.other_slope_ref
  128.7 0.7 shard_map.105
  129.4 8.5 %all_to_all.20 = bf16[8,32,512]{2,1,0:T(8,128)(2,1)S(1)} all-to-all(bf16[8,32,512]{2,1,0:T(8,128)(2,1)S(1)} %bitcast.39), channel_id=1, replica_groups={{0,16,32,48,64,80,96,112},{8,24,40,56,72,88,104,120},{1,17,33,49,65,81,..., dimensions={0} | all-to-all | bytes 524288 | tf_op jit(solution)/shard_map/all_to_all | solution.py:277
  138.0 0.1 convert_element_type.11
  138.1 0.1 broadcast_in_dim.6
  138.1 13.2 %all_to_all.21 = f32[8,32,512]{2,1,0:T(8,128)S(1)} all-to-all(f32[8,32,512]{2,1,0:T(8,128)S(1)} %broadcast_in_dim.6), channel_id=1, replica_groups=mesh['row'=16,'col'=8] {'col'}, dimensions={0} | all-to-all | bytes 1048576 | tf_op jit(solution)/shard_map/all_to_all | solution.py:277
  151.3 9.9 %all_to_all.22 = bf16[8,32,512]{2,1,0:T(8,128)(2,1)S(1)} all-to-all(bf16[8,32,512]{2,1,0:T(8,128)(2,1)S(1)} %broadcast_in_dim.7), channel_id=1, replica_groups={{0,16,32,48,64,80,96,112},{8,24,40,56,72,88,104,120},{1,17,33,49,65,81,..., dimensions={0} | all-to-all | bytes 524288 | tf_op jit(solution)/shard_map/all_to_all | solution.py:277
  161.2 3.3 %collective-permute-start.23 = (bf16[256,512]{1,0:T(8,128)(2,1)S(1)}, bf16[256,512]{1,0:T(8,128)(2,1)S(1)}, u32[]{:S(2)}, u32[]{:S(2)}) collective-permute-start(bf16[256,512]{1,0:T(8,128)(2,1)S(1)} %bitcast.52), channel_id=1, source_target_pairs={{0,8},{8,0},{16,24},{24,16},{32,40},{40,32},{48,56},{56,48},{64,72... | collective-permute-start | bytes 786440 | tf_op jit(solution)/shard_map/ppermute | solution.py:446
  164.5 1.2 collective-permute-done.23
  165.7 0.1 broadcast_select_fusion.1
  165.7 1.1 maximum_convert_fusion
  (22 shorter events, 0.1 us)
Async XLA Ops:
  0.6 0.7 copy-start.3
  3.6 21.2 %collective-permute-start.1 = (bf16[192,128,128]{2,1,0:T(8,128)(2,1)}, bf16[192,128,128]{2,1,0:T(8,128)(2,1)}, u32[]{:S(2)}, u32[]{:S(2)}) collective-permute-start(bf16[192,128,128]{2,1,0:T(8,128)(2,1)} %bitcast.49), channel_id=1, source_target_pairs={{0,8},{8,0},{16,24},{24,16},{32,40},{40,32},{48,56},{56,48},{64,72... | collective-permute-start | bytes 18874376 | tf_op jit(solution)/shard_map/ppermute | solution.py:364
  5.1 19.2 %all-to-all-start = ((bf16[16,64,256]{2,1,0:T(8,128)(2,1)}), bf16[16,64,256]{2,1,0:T(8,128)(2,1)S(1)}, u32[]{:S(2)}, u32[]{:S(2)}) async-start(bf16[16,64,256]{2,1,0:T(8,128)(2,1)} %shard_map.96), calls=%async_computation | async-start | bytes 1048576 | tf_op jit(solution)/shard_map/all_to_all | solution.py:277
  12.9 0.7 copy-start.4
  13.6 0.7 copy-start.5
  14.7 10.1 %collective-permute-start = (s32[8,288]{1,0:T(8,128)S(1)}, s32[8,288]{1,0:T(8,128)S(1)}, u32[]{:S(2)}, u32[]{:S(2)}) collective-permute-start(s32[8,288]{1,0:T(8,128)S(1)} %shard_map.95), channel_id=1, source_target_pairs={{0,8},{8,0},{16,24},{24,16},{32,40},{40,32},{48,56},{56,48},{64,72... | collective-permute-start | bytes 27656 | tf_op jit(solution)/shard_map/ppermute | solution.py:356
  24.8 8.4 %collective-permute-start.2 = (bf16[2,512,256]{2,1,0:T(8,128)(2,1)S(1)}, bf16[2,512,256]{2,1,0:T(8,128)(2,1)S(1)}, u32[]{:S(2)}, u32[]{:S(2)}) collective-permute-start(bf16[2,512,256]{2,1,0:T(8,128)(2,1)S(1)} %shard_map.97), channel_id=1, source_target_pairs={{0,16},{8,72},{16,32},{24,88},{32,48},{40,104},{48,0},{56,120},{64... | collective-permute-start | bytes 1572872 | tf_op jit(solution)/shard_map/ppermute | solution.py:381
  25.3 10.4 %collective-permute-start.5 = (bf16[2,512,256]{2,1,0:T(8,128)(2,1)S(1)}, bf16[2,512,256]{2,1,0:T(8,128)(2,1)S(1)}, u32[]{:S(2)}, u32[]{:S(2)}) collective-permute-start(bf16[2,512,256]{2,1,0:T(8,128)(2,1)S(1)} %shard_map.97), channel_id=1, source_target_pairs={{0,48},{16,0},{32,16},{48,32},{64,112},{80,64},{96,80},{112,96},{1... | collective-permute-start | bytes 1572872 | tf_op jit(solution)/shard_map/ppermute | solution.py:381
  26.0 15.3 %collective-permute-start.3 = (bf16[2,512,256]{2,1,0:T(8,128)(2,1)S(1)}, bf16[2,512,256]{2,1,0:T(8,128)(2,1)S(1)}, u32[]{:S(2)}, u32[]{:S(2)}) collective-permute-start(bf16[2,512,256]{2,1,0:T(8,128)(2,1)S(1)} %shard_map.97), channel_id=1, source_target_pairs={{0,64},{8,24},{16,80},{24,40},{32,96},{40,56},{48,112},{56,8},{64,... | collective-permute-start | bytes 1572872 | tf_op jit(solution)/shard_map/ppermute | solution.py:381
  27.7 17.9 %collective-permute-start.6 = (bf16[2,512,256]{2,1,0:T(8,128)(2,1)S(1)}, bf16[2,512,256]{2,1,0:T(8,128)(2,1)S(1)}, u32[]{:S(2)}, u32[]{:S(2)}) collective-permute-start(bf16[2,512,256]{2,1,0:T(8,128)(2,1)S(1)} %shard_map.97), channel_id=1, source_target_pairs={{0,32},{16,48},{32,0},{48,16},{64,96},{80,112},{96,64},{112,80},{1... | collective-permute-start | bytes 1572872 | tf_op jit(solution)/shard_map/ppermute | solution.py:381
  33.2 18.5 %collective-permute-start.4 = (bf16[2,512,256]{2,1,0:T(8,128)(2,1)S(1)}, bf16[2,512,256]{2,1,0:T(8,128)(2,1)S(1)}, u32[]{:S(2)}, u32[]{:S(2)}) collective-permute-start(bf16[2,512,256]{2,1,0:T(8,128)(2,1)S(1)} %collective-permute-done.2), channel_id=1, source_target_pairs={{0,64},{8,24},{16,80},{24,40},{32,96},{40,56},{48,112},{56,8},{64,... | collective-permute-start | bytes 1572872 | tf_op jit(solution)/shard_map/ppermute | solution.py:381
  35.7 20.5 %collective-permute-start.7 = (bf16[2,512,256]{2,1,0:T(8,128)(2,1)S(1)}, bf16[2,512,256]{2,1,0:T(8,128)(2,1)S(1)}, u32[]{:S(2)}, u32[]{:S(2)}) collective-permute-start(bf16[2,512,256]{2,1,0:T(8,128)(2,1)S(1)} %collective-permute-done.5), channel_id=1, source_target_pairs={{0,64},{16,80},{32,96},{48,112},{64,0},{80,16},{96,32},{112,48},{1... | collective-permute-start | bytes 1572872 | tf_op jit(solution)/shard_map/ppermute | solution.py:381
  36.4 26.9 %collective-permute-start.10 = (bf16[2,512,256]{2,1,0:T(8,128)(2,1)S(1)}, bf16[2,512,256]{2,1,0:T(8,128)(2,1)}, u32[]{:S(2)}, u32[]{:S(2)}) collective-permute-start(bf16[2,512,256]{2,1,0:T(8,128)(2,1)S(1)} %shard_map.97), channel_id=1, source_target_pairs={{8,56},{24,8},{40,24},{56,40},{72,120},{88,72},{104,88},{120,104},... | collective-permute-start | bytes 1572872 | tf_op jit(solution)/shard_map/ppermute | solution.py:381
  41.2 22.1 %collective-permute-start.9 = (bf16[2,512,256]{2,1,0:T(8,128)(2,1)S(1)}, bf16[2,512,256]{2,1,0:T(8,128)(2,1)}, u32[]{:S(2)}, u32[]{:S(2)}) collective-permute-start(bf16[2,512,256]{2,1,0:T(8,128)(2,1)S(1)} %collective-permute-done.2), channel_id=1, source_target_pairs={{8,56},{24,8},{40,24},{56,40},{72,120},{88,72},{104,88},{120,104},... | collective-permute-start | bytes 1572872 | tf_op jit(solution)/shard_map/ppermute | solution.py:381
  45.6 17.7 %collective-permute-start.8 = (bf16[2,512,256]{2,1,0:T(8,128)(2,1)S(1)}, bf16[2,512,256]{2,1,0:T(8,128)(2,1)}, u32[]{:S(2)}, u32[]{:S(2)}) collective-permute-start(bf16[2,512,256]{2,1,0:T(8,128)(2,1)S(1)} %collective-permute-done.6), channel_id=1, source_target_pairs={{0,64},{16,80},{32,96},{48,112},{64,0},{80,16},{96,32},{112,48},{1... | collective-permute-start | bytes 1572872 | tf_op jit(solution)/shard_map/ppermute | solution.py:381
  51.7 11.6 %collective-permute-start.11 = (bf16[2,512,256]{2,1,0:T(8,128)(2,1)S(1)}, bf16[2,512,256]{2,1,0:T(8,128)(2,1)}, u32[]{:S(2)}, u32[]{:S(2)}) collective-permute-start(bf16[2,512,256]{2,1,0:T(8,128)(2,1)S(1)} %shard_map.97), channel_id=1, source_target_pairs={{8,40},{24,56},{40,8},{56,24},{72,104},{88,120},{104,72},{120,88},... | collective-permute-start | bytes 1572872 | tf_op jit(solution)/shard_map/ppermute | solution.py:381
  56.3 0.8 copy-start.1
  57.1 11.8 %collective-permute-start.12 = (bf16[2,512,256]{2,1,0:T(8,128)(2,1)S(1)}, bf16[2,512,256]{2,1,0:T(8,128)(2,1)}, u32[]{:S(2)}, u32[]{:S(2)}) collective-permute-start(bf16[2,512,256]{2,1,0:T(8,128)(2,1)S(1)} %collective-permute-done.4), channel_id=1, source_target_pairs={{8,24},{24,40},{40,56},{56,8},{72,88},{88,104},{104,120},{120,72},... | collective-permute-start | bytes 1572872 | tf_op jit(solution)/shard_map/ppermute | solution.py:381
  59.9 8.9 %copy-start.2 = (bf16[2,512,256]{2,1,0:T(8,128)(2,1)S(1)}, bf16[2,512,256]{2,1,0:T(8,128)(2,1)}, u32[]{:S(2)}) copy-start(bf16[2,512,256]{2,1,0:T(8,128)(2,1)} %copy-done.1) | copy-start | bytes 1572868
  74.3 23.4 %collective-permute-start.13 = (bf16[4,512,256]{2,1,0:T(8,128)(2,1)S(1)}, bf16[4,512,256]{2,1,0:T(8,128)(2,1)S(1)}, u32[]{:S(2)}, u32[]{:S(2)}) collective-permute-start(bf16[4,512,256]{2,1,0:T(8,128)(2,1)S(1)} %get-tuple-element.33), channel_id=1, source_target_pairs={{0,4},{1,5},{2,6},{3,7},{4,0},{5,1},{6,2},{7,3},{8,12},{9,13},{10,... | collective-permute-start | bytes 3145736 | tf_op jit(solution)/shard_map/ppermute | solution.py:415
  81.4 43.0 %copy-start = (bf16[512,512]{1,0:T(8,128)(2,1)S(1)}, bf16[512,512]{1,0:T(8,128)(2,1)}, u32[]{:S(2)}) copy-start(bf16[512,512]{1,0:T(8,128)(2,1)} %weight_ref.1) | copy-start | bytes 1572868
  81.5 29.5 %collective-permute-start.15 = (bf16[2,512,256]{2,1,0:T(8,128)(2,1)S(1)}, bf16[2,512,256]{2,1,0:T(8,128)(2,1)S(1)}, u32[]{:S(2)}, u32[]{:S(2)}) collective-permute-start(bf16[2,512,256]{2,1,0:T(8,128)(2,1)S(1)} %get-tuple-element.36), channel_id=1, source_target_pairs={{0,1},{1,2},{2,3},{3,0},{4,5},{5,6},{6,7},{7,4},{8,9},{9,10},{10,1... | collective-permute-start | bytes 1572872 | tf_op jit(solution)/shard_map/ppermute | solution.py:414
  81.5 29.4 %collective-permute-start.16 = (bf16[2,512,256]{2,1,0:T(8,128)(2,1)S(1)}, bf16[2,512,256]{2,1,0:T(8,128)(2,1)S(1)}, u32[]{:S(2)}, u32[]{:S(2)}) collective-permute-start(bf16[2,512,256]{2,1,0:T(8,128)(2,1)S(1)} %get-tuple-element.37), channel_id=1, source_target_pairs={{0,3},{1,0},{2,1},{3,2},{4,7},{5,4},{6,5},{7,6},{8,11},{9,8},{10,9... | collective-permute-start | bytes 1572872 | tf_op jit(solution)/shard_map/ppermute | solution.py:414
  84.2 26.8 %collective-permute-start.17 = (bf16[2,512,256]{2,1,0:T(8,128)(2,1)S(1)}, bf16[2,512,256]{2,1,0:T(8,128)(2,1)S(1)}, u32[]{:S(2)}, u32[]{:S(2)}) collective-permute-start(bf16[2,512,256]{2,1,0:T(8,128)(2,1)S(1)} %get-tuple-element.38), channel_id=1, source_target_pairs={{0,2},{1,3},{2,0},{3,1},{4,6},{5,7},{6,4},{7,5},{8,10},{9,11},{10,... | collective-permute-start | bytes 1572872 | tf_op jit(solution)/shard_map/ppermute | solution.py:414
  98.5 12.2 %collective-permute-start.14 = (bf16[512,256]{1,0:T(8,128)(2,1)S(1)}, bf16[512,256]{1,0:T(8,128)(2,1)S(1)}, u32[]{:S(2)}, u32[]{:S(2)}) collective-permute-start(bf16[512,256]{1,0:T(8,128)(2,1)S(1)} %get-tuple-element.34), channel_id=1, source_target_pairs={{0,1},{1,2},{2,3},{3,0},{4,5},{5,6},{6,7},{7,4},{8,9},{9,10},{10,1... | collective-permute-start | bytes 786440 | tf_op jit(solution)/shard_map/ppermute | solution.py:420
  98.6 17.6 %collective-permute-start.19 = (bf16[512,256]{1,0:T(8,128)(2,1)S(1)}, bf16[512,256]{1,0:T(8,128)(2,1)S(1)}, u32[]{:S(2)}, u32[]{:S(2)}) collective-permute-start(bf16[512,256]{1,0:T(8,128)(2,1)S(1)} %get-tuple-element.42), channel_id=1, source_target_pairs={{0,3},{1,0},{2,1},{3,2},{4,7},{5,4},{6,5},{7,6},{8,11},{9,8},{10,9... | collective-permute-start | bytes 786440 | tf_op jit(solution)/shard_map/ppermute | solution.py:420
  110.7 8.4 %collective-permute-start.20 = (bf16[512,256]{1,0:T(8,128)(2,1)S(1)}, bf16[512,256]{1,0:T(8,128)(2,1)S(1)}, u32[]{:S(2)}, u32[]{:S(2)}) collective-permute-start(bf16[512,256]{1,0:T(8,128)(2,1)S(1)} %get-tuple-element.43), channel_id=1, source_target_pairs={{0,2},{1,3},{2,0},{3,1},{4,6},{5,7},{6,4},{7,5},{8,10},{9,11},{10,... | collective-permute-start | bytes 786440 | tf_op jit(solution)/shard_map/ppermute | solution.py:420
  111.8 8.8 %collective-permute-start.18 = (bf16[512,256]{1,0:T(8,128)(2,1)S(1)}, bf16[512,256]{1,0:T(8,128)(2,1)S(1)}, u32[]{:S(2)}, u32[]{:S(2)}) collective-permute-start(bf16[512,256]{1,0:T(8,128)(2,1)S(1)} %get-tuple-element.40), channel_id=1, source_target_pairs={{0,4},{1,5},{2,6},{3,7},{4,0},{5,1},{6,2},{7,3},{8,12},{9,13},{10,... | collective-permute-start | bytes 786440 | tf_op jit(solution)/shard_map/ppermute | solution.py:424
  121.3 3.2 %collective-permute-start.21 = (f32[512,256]{1,0:T(8,128)S(1)}, f32[512,256]{1,0:T(8,128)S(1)}, u32[]{:S(2)}, u32[]{:S(2)}) collective-permute-start(f32[512,256]{1,0:T(8,128)S(1)} %get-tuple-element.45.other_ref), channel_id=1, source_target_pairs={{0,8},{8,0},{16,24},{24,16},{32,40},{40,32},{48,56},{56,48},{64,72... | collective-permute-start | bytes 1572872 | tf_op jit(solution)/shard_map/ppermute | solution.py:428
  126.8 1.9 %collective-permute-start.22 = (bf16[512,512]{1,0:T(8,128)(2,1)S(1)}, bf16[512,512]{1,0:T(8,128)(2,1)S(1)}, u32[]{:S(2)}, u32[]{:S(2)}) collective-permute-start(bf16[512,512]{1,0:T(8,128)(2,1)S(1)} %get-tuple-element.47.slope_ref), channel_id=1, source_target_pairs={{0,8},{8,0},{16,24},{24,16},{32,40},{40,32},{48,56},{56,48},{64,72... | collective-permute-start | bytes 1572872 | tf_op jit(solution)/shard_map/ppermute | solution.py:435
  161.2 4.4 %collective-permute-start.23 = (bf16[256,512]{1,0:T(8,128)(2,1)S(1)}, bf16[256,512]{1,0:T(8,128)(2,1)S(1)}, u32[]{:S(2)}, u32[]{:S(2)}) collective-permute-start(bf16[256,512]{1,0:T(8,128)(2,1)S(1)} %bitcast.52), channel_id=1, source_target_pairs={{0,8},{8,0},{16,24},{24,16},{32,40},{40,32},{48,56},{56,48},{64,72... | collective-permute-start | bytes 786440 | tf_op jit(solution)/shard_map/ppermute | solution.py:446

commit v14 on v8

--- a/solution.py
+++ b/solution.py
@@ -440,7 +440,7 @@
     same_core = [[chip * 2 + c for chip in range(CHIPS)] for c in range(2)]
     shape = (CHIPS, HALF // CHIPS, F)
     piece = added(exchange(half.reshape(shape), "row", same_core))
-    piece = added(exchange(jnp.broadcast_to(piece, shape), "col"))
+    piece = added(exchange(jnp.broadcast_to(piece.astype(BF16), shape), "col"))
     half = exchange(jnp.broadcast_to(piece.astype(BF16), shape), "row", same_core)
     half = half.reshape(HALF, F)
     other = lax.ppermute(half, "row", swap)

time: 168 us -> 165 us (0.982)
  blocking collectives: 32.7 us -> 30.1 us
  starting transfers between devices: 47.6 us -> 45.8 us
    ppermute x3, waiting for transfers between devices: 14.4 us -> 10.4 us  [shards(): got1 = [lax.ppermute(send1[k - 1], 'col', x_moves(k)) for k in (1, 3, 2)]]
    ppermute x1, waiting for transfers between devices: 13.4 us -> 17.1 us  [shards(): got1 = lax.ppermute(send1, 'col', y_moves())]
    all_to_all x3, blocking collectives: 32.7 us -> 30.1 us  [exchange(): lax.all_to_all(parts, axis, split_axis=0, concat_axis=0, axis_index_group...]
    ppermute x1, starting transfers between devices: 2.18 us -> 0.09 us  [shards(): got1 = lax.ppermute(send1, 'col', y_moves())]
    ppermute x3, starting transfers between devices: 2.76 us -> 4.74 us  [shards(): got1 = [lax.ppermute(send1[k - 1], 'col', x_moves(k)) for k in (1, 3, 2)]]
  transfers between devices with their start and end apart: 25 -> 25, of which waited for: 14 -> 14; matrix products, arithmetic and copies ran while one was open for 1% -> 1% of each run, Pallas kernels for 7% -> 5%
where the time goes in v14:
time: 165 us; the launch traced here: 164 us
  waiting for transfers between devices  59.2 us (36%)
  starting transfers between devices  45.8 us (28%)
  blocking collectives  30.1 us (18%)
  Pallas kernels  22 us (13%)
  local copies, waits for them, and re-layouts  4.03 us (2%)
  between operations  1.73 us (1%)
    all_to_all x3, blocking collectives, exchange(): lax.all_to_all(parts, axis, split_axis=0, concat_axis=0, axis_index_group...  30.1 us
    ppermute x11, starting transfers between devices, hop(): return lax.ppermute(block, 'row', row_moves(move))  23.3 us
    pallas_call x11, Pallas kernels, run(): return made(*held)  22 us
    ppermute x1, waiting for transfers between devices, shards(): got1 = lax.ppermute(send1, 'col', y_moves())  17.1 us
    ppermute x11, waiting for transfers between devices, hop(): return lax.ppermute(block, 'row', row_moves(move))  16.2 us
    ppermute x3, waiting for transfers between devices, shards(): got1 = [lax.ppermute(send1[k - 1], 'col', x_moves(k)) for k in (1, 3, 2)]  10.4 us
    all_to_all x1, waiting for transfers between devices, exchange(): lax.all_to_all(parts, axis, split_axis=0, concat_axis=0, axis_index_group...  9.51 us
    all_to_all x1, starting transfers between devices, exchange(): lax.all_to_all(parts, axis, split_axis=0, concat_axis=0, axis_index_group...  7.14 us
  transfers between devices with their start and end apart: 25, of which 14 were waited for; matrix products, arithmetic and copies ran while one was open for 1% of the time, Pallas kernels for 5%

profile of v14, /device:TPU:1, one launch (start us, length us, event | category | flops | bytes accessed | tf_op | source)
XLA Modules:
  0.0 164.2 jit_solution(16011429257195370112)
XLA Ops:
  0.6 0.7 copy-done.3
  1.3 2.3 %shard_map.96 = bf16[16,64,256]{2,1,0:T(8,128)(2,1)} custom-call(s32[1,512]{1,0:T(1,128)S(1)} %bitcast.46, bf16[512,512]{1,0:T(8,128)(2,1)} %features_hbm.1), custom_call_target="tpu_custom_call" | custom-call | tf_op jit(solution)/shard_map/pallas_call | solution.py:305
  3.6 1.5 collective-permute-start.1
  5.1 7.1 %all-to-all-start = ((bf16[16,64,256]{2,1,0:T(8,128)(2,1)}), bf16[16,64,256]{2,1,0:T(8,128)(2,1)S(1)}, u32[]{:S(2)}, u32[]{:S(2)}) async-start(bf16[16,64,256]{2,1,0:T(8,128)(2,1)} %shard_map.96), calls=%async_computation | async-start | bytes 1048576 | tf_op jit(solution)/shard_map/all_to_all | solution.py:277
  12.9 0.0 copy-start.4
  12.9 0.7 copy-done.4
  13.6 0.7 copy-done.5
  14.3 0.5 shard_map.95
  14.7 0.1 collective-permute-start
  14.8 9.5 %all-to-all-done.arrived_ref = bf16[16,64,256]{2,1,0:T(8,128)(2,1)S(1)} async-done(((bf16[16,64,256]{2,1,0:T(8,128)(2,1)}), bf16[16,64,256]{2,1,0:T(8,128)(2,1)S(1)}, u32[]{:S(2)}, u32[]{:S(2)}) %all-to-all-start) | async-done | bytes 524320 | tf_op jit(solution)/shard_map/all_to_all | solution.py:277
  24.4 0.4 shard_map.97
  24.8 0.5 collective-permute-start.2
  25.3 0.7 collective-permute-start.5
  26.0 1.7 %collective-permute-start.3 = (bf16[2,512,256]{2,1,0:T(8,128)(2,1)S(1)}, bf16[2,512,256]{2,1,0:T(8,128)(2,1)S(1)}, u32[]{:S(2)}, u32[]{:S(2)}) collective-permute-start(bf16[2,512,256]{2,1,0:T(8,128)(2,1)S(1)} %shard_map.97), channel_id=1, source_target_pairs={{0,64},{8,24},{16,80},{24,40},{32,96},{40,56},{48,112},{56,8},{64,... | collective-permute-start | bytes 1572872 | tf_op jit(solution)/shard_map/ppermute | solution.py:381
  27.7 0.7 collective-permute-start.6
  28.4 4.8 %collective-permute-done.2 = bf16[2,512,256]{2,1,0:T(8,128)(2,1)S(1)} collective-permute-done((bf16[2,512,256]{2,1,0:T(8,128)(2,1)S(1)}, bf16[2,512,256]{2,1,0:T(8,128)(2,1)S(1)}, u32[]{:S(2)}, u32[]{:S(2)}) %collective-permute-start.2) | collective-permute-done | bytes 524320 | tf_op jit(solution)/shard_map/ppermute | solution.py:381
  33.2 2.5 %collective-permute-start.4 = (bf16[2,512,256]{2,1,0:T(8,128)(2,1)S(1)}, bf16[2,512,256]{2,1,0:T(8,128)(2,1)S(1)}, u32[]{:S(2)}, u32[]{:S(2)}) collective-permute-start(bf16[2,512,256]{2,1,0:T(8,128)(2,1)S(1)} %collective-permute-done.2), channel_id=1, source_target_pairs={{0,64},{8,24},{16,80},{24,40},{32,96},{40,56},{48,112},{56,8},{64,... | collective-permute-start | bytes 1572872 | tf_op jit(solution)/shard_map/ppermute | solution.py:381
  35.7 0.7 collective-permute-start.7
  36.4 4.0 %collective-permute-start.10 = (bf16[2,512,256]{2,1,0:T(8,128)(2,1)S(1)}, bf16[2,512,256]{2,1,0:T(8,128)(2,1)}, u32[]{:S(2)}, u32[]{:S(2)}) collective-permute-start(bf16[2,512,256]{2,1,0:T(8,128)(2,1)S(1)} %shard_map.97), channel_id=1, source_target_pairs={{8,56},{24,8},{40,24},{56,40},{72,120},{88,72},{104,88},{120,104},... | collective-permute-start | bytes 1572872 | tf_op jit(solution)/shard_map/ppermute | solution.py:381
  40.5 0.8 collective-permute-done.3
  41.2 4.3 %collective-permute-start.9 = (bf16[2,512,256]{2,1,0:T(8,128)(2,1)S(1)}, bf16[2,512,256]{2,1,0:T(8,128)(2,1)}, u32[]{:S(2)}, u32[]{:S(2)}) collective-permute-start(bf16[2,512,256]{2,1,0:T(8,128)(2,1)S(1)} %collective-permute-done.2), channel_id=1, source_target_pairs={{8,56},{24,8},{40,24},{56,40},{72,120},{88,72},{104,88},{120,104},... | collective-permute-start | bytes 1572872 | tf_op jit(solution)/shard_map/ppermute | solution.py:381
  45.6 1.5 collective-permute-start.8
  47.0 4.7 %collective-permute-done.4 = bf16[2,512,256]{2,1,0:T(8,128)(2,1)S(1)} collective-permute-done((bf16[2,512,256]{2,1,0:T(8,128)(2,1)S(1)}, bf16[2,512,256]{2,1,0:T(8,128)(2,1)S(1)}, u32[]{:S(2)}, u32[]{:S(2)}) %collective-permute-start.4) | collective-permute-done | bytes 524320 | tf_op jit(solution)/shard_map/ppermute | solution.py:381
  51.7 4.5 %collective-permute-start.11 = (bf16[2,512,256]{2,1,0:T(8,128)(2,1)S(1)}, bf16[2,512,256]{2,1,0:T(8,128)(2,1)}, u32[]{:S(2)}, u32[]{:S(2)}) collective-permute-start(bf16[2,512,256]{2,1,0:T(8,128)(2,1)S(1)} %shard_map.97), channel_id=1, source_target_pairs={{8,40},{24,56},{40,8},{56,24},{72,104},{88,120},{104,72},{120,88},... | collective-permute-start | bytes 1572872 | tf_op jit(solution)/shard_map/ppermute | solution.py:381
  56.3 0.8 copy-done.1
  57.1 2.2 %collective-permute-start.12 = (bf16[2,512,256]{2,1,0:T(8,128)(2,1)S(1)}, bf16[2,512,256]{2,1,0:T(8,128)(2,1)}, u32[]{:S(2)}, u32[]{:S(2)}) collective-permute-start(bf16[2,512,256]{2,1,0:T(8,128)(2,1)S(1)} %collective-permute-done.2), channel_id=1, source_target_pairs={{8,40},{24,56},{40,8},{56,24},{72,104},{88,120},{104,72},{120,88},... | collective-permute-start | bytes 1572872 | tf_op jit(solution)/shard_map/ppermute | solution.py:381
  59.4 0.1 stack.51.meta_ref
  59.5 0.0 copy-start.2
  59.6 3.3 %shard_map.98.tiles = bf16[193,128,128]{2,1,0:T(8,128)(2,1)S(1)} custom-call(s32[12]{0:T(128)S(1)} %stack.51.meta_ref, bf16[192,128,128]{2,1,0:T(8,128)(2,1)} %bitcast.50, bf16[192,128,128]{2,1,0:T(8,128)(2,1)} %collective-permute-done.1.other_hbm), custom_call_target="tpu_custom_call" | custom-call | tf_op jit(solution)/shard_map/pallas_call | solution.py:305
  62.9 0.3 collective-permute-done.11
  63.2 5.6 %collective-permute-done.12 = bf16[2,512,256]{2,1,0:T(8,128)(2,1)} collective-permute-done((bf16[2,512,256]{2,1,0:T(8,128)(2,1)S(1)}, bf16[2,512,256]{2,1,0:T(8,128)(2,1)}, u32[]{:S(2)}, u32[]{:S(2)}) %collective-permute-start.12) | collective-permute-done | bytes 524320 | tf_op jit(solution)/shard_map/ppermute | solution.py:381
  68.8 6.9 %shard_map.99 = (bf16[4,512,256]{2,1,0:T(8,128)(2,1)S(1)}, bf16[4,512,256]{2,1,0:T(8,128)(2,1)S(1)}, bf16[8,2,16,32,256]{4,3,2,1,0:T(8,128)(2,1)S(1)}, bf16[193,128,128]{2,1,0:T(8,128)(2,1)S(1)}) custom-call(s32[12]{0:T(128)S(1)} %stack.51.meta_ref, s32[8,288]{1,0:T(8,128)S(1)} %get-tuple-element.50.plan_ref, bf16[193,128,128]{2,1,0:T(8,128)(2,1)S(1)} %shard_map.98.tiles, ...), custom_call_target="tpu_custom_call" | custom-call | tf_op jit(solution)/shard_map/pallas_call | solution.py:305
  75.7 0.1 collective-permute-start.13
  75.8 3.2 %shard_map.100 = (bf16[2,512,256]{2,1,0:T(8,128)(2,1)S(1)}, bf16[2,512,256]{2,1,0:T(8,128)(2,1)S(1)}, bf16[2,512,256]{2,1,0:T(8,128)(2,1)S(1)}, bf16[2,512,256]{2,1,0:T(8,128)(2,1)S(1)}) custom-call(s32[12]{0:T(128)S(1)} %stack.51.meta_ref, s32[8,288]{1,0:T(8,128)S(1)} %get-tuple-element.51.plan_ref, bf16[193,128,128]{2,1,0:T(8,128)(2,1)S(1)} %get-tuple-element.29.tiles, ...), custom_call_target="tpu_custom_call" | custom-call | tf_op jit(solution)/shard_map/pallas_call | solution.py:305
  79.0 0.8 collective-permute-start.15
  79.9 1.9 %collective-permute-start.16 = (bf16[2,512,256]{2,1,0:T(8,128)(2,1)S(1)}, bf16[2,512,256]{2,1,0:T(8,128)(2,1)S(1)}, u32[]{:S(2)}, u32[]{:S(2)}) collective-permute-start(bf16[2,512,256]{2,1,0:T(8,128)(2,1)S(1)} %get-tuple-element.37), channel_id=1, source_target_pairs={{0,3},{1,0},{2,1},{3,2},{4,7},{5,4},{6,5},{7,6},{8,11},{9,8},{10,9... | collective-permute-start | bytes 1572872 | tf_op jit(solution)/shard_map/ppermute | solution.py:414
  81.8 17.1 %collective-permute-done.13.got_ref = bf16[4,512,256]{2,1,0:T(8,128)(2,1)S(1)} collective-permute-done((bf16[4,512,256]{2,1,0:T(8,128)(2,1)S(1)}, bf16[4,512,256]{2,1,0:T(8,128)(2,1)S(1)}, u32[]{:S(2)}, u32[]{:S(2)}) %collective-permute-start.13) | collective-permute-done | bytes 1048608 | tf_op jit(solution)/shard_map/ppermute | solution.py:415
  98.9 0.8 shard_map.101
  99.7 0.1 collective-permute-start.14
  99.8 2.7 %collective-permute-start.19 = (bf16[512,256]{1,0:T(8,128)(2,1)S(1)}, bf16[512,256]{1,0:T(8,128)(2,1)S(1)}, u32[]{:S(2)}, u32[]{:S(2)}) collective-permute-start(bf16[512,256]{1,0:T(8,128)(2,1)S(1)} %get-tuple-element.42), channel_id=1, source_target_pairs={{0,3},{1,0},{2,1},{3,2},{4,7},{5,4},{6,5},{7,6},{8,11},{9,8},{10,9... | collective-permute-start | bytes 786440 | tf_op jit(solution)/shard_map/ppermute | solution.py:420
  102.5 5.0 %collective-permute-done.14.a_ref = bf16[512,256]{1,0:T(8,128)(2,1)S(1)} collective-permute-done((bf16[512,256]{1,0:T(8,128)(2,1)S(1)}, bf16[512,256]{1,0:T(8,128)(2,1)S(1)}, u32[]{:S(2)}, u32[]{:S(2)}) %collective-permute-start.14) | collective-permute-done | bytes 262176 | tf_op jit(solution)/shard_map/ppermute | solution.py:420
  107.5 2.0 %collective-permute-start.20 = (bf16[512,256]{1,0:T(8,128)(2,1)S(1)}, bf16[512,256]{1,0:T(8,128)(2,1)S(1)}, u32[]{:S(2)}, u32[]{:S(2)}) collective-permute-start(bf16[512,256]{1,0:T(8,128)(2,1)S(1)} %get-tuple-element.43), channel_id=1, source_target_pairs={{0,2},{1,3},{2,0},{3,1},{4,6},{5,7},{6,4},{7,5},{8,10},{9,11},{10,... | collective-permute-start | bytes 786440 | tf_op jit(solution)/shard_map/ppermute | solution.py:420
  109.5 0.8 shard_map.102
  110.3 1.2 collective-permute-start.18
  111.6 2.2 %collective-permute-done.19.b_ref = bf16[512,256]{1,0:T(8,128)(2,1)S(1)} collective-permute-done((bf16[512,256]{1,0:T(8,128)(2,1)S(1)}, bf16[512,256]{1,0:T(8,128)(2,1)S(1)}, u32[]{:S(2)}, u32[]{:S(2)}) %collective-permute-start.19) | collective-permute-done | bytes 262176 | tf_op jit(solution)/shard_map/ppermute | solution.py:420
  113.8 3.1 %collective-permute-done.20.c_ref = bf16[512,256]{1,0:T(8,128)(2,1)S(1)} collective-permute-done((bf16[512,256]{1,0:T(8,128)(2,1)S(1)}, bf16[512,256]{1,0:T(8,128)(2,1)S(1)}, u32[]{:S(2)}, u32[]{:S(2)}) %collective-permute-start.20) | collective-permute-done | bytes 262176 | tf_op jit(solution)/shard_map/ppermute | solution.py:420
  116.9 2.9 %collective-permute-done.18.got0 = bf16[512,256]{1,0:T(8,128)(2,1)S(1)} collective-permute-done((bf16[512,256]{1,0:T(8,128)(2,1)S(1)}, bf16[512,256]{1,0:T(8,128)(2,1)S(1)}, u32[]{:S(2)}, u32[]{:S(2)}) %collective-permute-start.18) | collective-permute-done | bytes 262176 | tf_op jit(solution)/shard_map/ppermute | solution.py:424
  119.8 0.8 shard_map.103
  120.5 0.9 collective-permute-start.21
  121.5 1.1 constant_dynamic-slice_fusion.cotangent_ref
  122.6 0.5 collective-permute-done.21.got_ref
  123.0 2.3 %shard_map.104 = (bf16[512,512]{1,0:T(8,128)(2,1)}, bf16[512,512]{1,0:T(8,128)(2,1)S(1)}) custom-call(s32[12]{0:T(128)S(1)} %stack.51.meta_ref, f32[512,256]{1,0:T(8,128)S(1)} %get-tuple-element.44.mine_ref, f32[512,256]{1,0:T(8,128)S(1)} %collective-permute-done.21.got_ref, bf16[512,512]{1,0:T(8,128)(2,1)S(1)} %copy-done, ...), custom_call_target="tpu_custom_call" | custom-call | tf_op jit(solution)/shard_map/pallas_call | solution.py:305
  125.3 0.4 collective-permute-start.22
  125.7 1.5 collective-permute-done.22.other_slope_ref
  127.2 0.7 shard_map.105
  128.0 8.5 %all_to_all.20 = bf16[8,32,512]{2,1,0:T(8,128)(2,1)S(1)} all-to-all(bf16[8,32,512]{2,1,0:T(8,128)(2,1)S(1)} %bitcast.39), channel_id=1, replica_groups={{0,16,32,48,64,80,96,112},{8,24,40,56,72,88,104,120},{1,17,33,49,65,81,..., dimensions={0} | all-to-all | bytes 524288 | tf_op jit(solution)/shard_map/all_to_all | solution.py:277
  136.5 0.1 convert_element_type.20
  136.6 12.2 %all_to_all.21 = bf16[8,32,512]{2,1,0:T(8,128)(2,1)S(1)} all-to-all(bf16[8,32,512]{2,1,0:T(8,128)(2,1)S(1)} %broadcast_in_dim.6), channel_id=1, replica_groups=mesh['row'=16,'col'=8] {'col'}, dimensions={0} | all-to-all | bytes 524288 | tf_op jit(solution)/shard_map/all_to_all | solution.py:277
  148.9 0.1 convert_element_type.23
  149.0 9.3 %all_to_all.22 = bf16[8,32,512]{2,1,0:T(8,128)(2,1)S(1)} all-to-all(bf16[8,32,512]{2,1,0:T(8,128)(2,1)S(1)} %broadcast_in_dim.7), channel_id=1, replica_groups={{0,16,32,48,64,80,96,112},{8,24,40,56,72,88,104,120},{1,17,33,49,65,81,..., dimensions={0} | all-to-all | bytes 524288 | tf_op jit(solution)/shard_map/all_to_all | solution.py:277
  158.3 3.6 %collective-permute-start.23 = (bf16[256,512]{1,0:T(8,128)(2,1)S(1)}, bf16[256,512]{1,0:T(8,128)(2,1)S(1)}, u32[]{:S(2)}, u32[]{:S(2)}) collective-permute-start(bf16[256,512]{1,0:T(8,128)(2,1)S(1)} %bitcast.52), channel_id=1, source_target_pairs={{0,8},{8,0},{16,24},{24,16},{32,40},{40,32},{48,56},{56,48},{64,72... | collective-permute-start | bytes 786440 | tf_op jit(solution)/shard_map/ppermute | solution.py:446
  161.9 1.2 collective-permute-done.23
  163.1 0.1 broadcast_select_fusion.1
  163.1 1.1 maximum_convert_fusion
  (23 shorter events, 0.2 us)
Async XLA Ops:
  0.6 0.7 copy-start.3
  3.6 21.2 %collective-permute-start.1 = (bf16[192,128,128]{2,1,0:T(8,128)(2,1)}, bf16[192,128,128]{2,1,0:T(8,128)(2,1)}, u32[]{:S(2)}, u32[]{:S(2)}) collective-permute-start(bf16[192,128,128]{2,1,0:T(8,128)(2,1)} %bitcast.49), channel_id=1, source_target_pairs={{0,8},{8,0},{16,24},{24,16},{32,40},{40,32},{48,56},{56,48},{64,72... | collective-permute-start | bytes 18874376 | tf_op jit(solution)/shard_map/ppermute | solution.py:364
  5.1 19.2 %all-to-all-start = ((bf16[16,64,256]{2,1,0:T(8,128)(2,1)}), bf16[16,64,256]{2,1,0:T(8,128)(2,1)S(1)}, u32[]{:S(2)}, u32[]{:S(2)}) async-start(bf16[16,64,256]{2,1,0:T(8,128)(2,1)} %shard_map.96), calls=%async_computation | async-start | bytes 1048576 | tf_op jit(solution)/shard_map/all_to_all | solution.py:277
  12.9 0.7 copy-start.4
  13.6 0.7 copy-start.5
  14.7 10.1 %collective-permute-start = (s32[8,288]{1,0:T(8,128)S(1)}, s32[8,288]{1,0:T(8,128)S(1)}, u32[]{:S(2)}, u32[]{:S(2)}) collective-permute-start(s32[8,288]{1,0:T(8,128)S(1)} %shard_map.95), channel_id=1, source_target_pairs={{0,8},{8,0},{16,24},{24,16},{32,40},{40,32},{48,56},{56,48},{64,72... | collective-permute-start | bytes 27656 | tf_op jit(solution)/shard_map/ppermute | solution.py:356
  24.8 8.4 %collective-permute-start.2 = (bf16[2,512,256]{2,1,0:T(8,128)(2,1)S(1)}, bf16[2,512,256]{2,1,0:T(8,128)(2,1)S(1)}, u32[]{:S(2)}, u32[]{:S(2)}) collective-permute-start(bf16[2,512,256]{2,1,0:T(8,128)(2,1)S(1)} %shard_map.97), channel_id=1, source_target_pairs={{0,16},{8,72},{16,32},{24,88},{32,48},{40,104},{48,0},{56,120},{64... | collective-permute-start | bytes 1572872 | tf_op jit(solution)/shard_map/ppermute | solution.py:381
  25.3 10.4 %collective-permute-start.5 = (bf16[2,512,256]{2,1,0:T(8,128)(2,1)S(1)}, bf16[2,512,256]{2,1,0:T(8,128)(2,1)S(1)}, u32[]{:S(2)}, u32[]{:S(2)}) collective-permute-start(bf16[2,512,256]{2,1,0:T(8,128)(2,1)S(1)} %shard_map.97), channel_id=1, source_target_pairs={{0,48},{16,0},{32,16},{48,32},{64,112},{80,64},{96,80},{112,96},{1... | collective-permute-start | bytes 1572872 | tf_op jit(solution)/shard_map/ppermute | solution.py:381
  26.0 15.3 %collective-permute-start.3 = (bf16[2,512,256]{2,1,0:T(8,128)(2,1)S(1)}, bf16[2,512,256]{2,1,0:T(8,128)(2,1)S(1)}, u32[]{:S(2)}, u32[]{:S(2)}) collective-permute-start(bf16[2,512,256]{2,1,0:T(8,128)(2,1)S(1)} %shard_map.97), channel_id=1, source_target_pairs={{0,64},{8,24},{16,80},{24,40},{32,96},{40,56},{48,112},{56,8},{64,... | collective-permute-start | bytes 1572872 | tf_op jit(solution)/shard_map/ppermute | solution.py:381
  27.7 17.9 %collective-permute-start.6 = (bf16[2,512,256]{2,1,0:T(8,128)(2,1)S(1)}, bf16[2,512,256]{2,1,0:T(8,128)(2,1)S(1)}, u32[]{:S(2)}, u32[]{:S(2)}) collective-permute-start(bf16[2,512,256]{2,1,0:T(8,128)(2,1)S(1)} %shard_map.97), channel_id=1, source_target_pairs={{0,32},{16,48},{32,0},{48,16},{64,96},{80,112},{96,64},{112,80},{1... | collective-permute-start | bytes 1572872 | tf_op jit(solution)/shard_map/ppermute | solution.py:381
  33.2 18.5 %collective-permute-start.4 = (bf16[2,512,256]{2,1,0:T(8,128)(2,1)S(1)}, bf16[2,512,256]{2,1,0:T(8,128)(2,1)S(1)}, u32[]{:S(2)}, u32[]{:S(2)}) collective-permute-start(bf16[2,512,256]{2,1,0:T(8,128)(2,1)S(1)} %collective-permute-done.2), channel_id=1, source_target_pairs={{0,64},{8,24},{16,80},{24,40},{32,96},{40,56},{48,112},{56,8},{64,... | collective-permute-start | bytes 1572872 | tf_op jit(solution)/shard_map/ppermute | solution.py:381
  35.7 20.5 %collective-permute-start.7 = (bf16[2,512,256]{2,1,0:T(8,128)(2,1)S(1)}, bf16[2,512,256]{2,1,0:T(8,128)(2,1)S(1)}, u32[]{:S(2)}, u32[]{:S(2)}) collective-permute-start(bf16[2,512,256]{2,1,0:T(8,128)(2,1)S(1)} %collective-permute-done.5), channel_id=1, source_target_pairs={{0,64},{16,80},{32,96},{48,112},{64,0},{80,16},{96,32},{112,48},{1... | collective-permute-start | bytes 1572872 | tf_op jit(solution)/shard_map/ppermute | solution.py:381
  36.4 26.5 %collective-permute-start.10 = (bf16[2,512,256]{2,1,0:T(8,128)(2,1)S(1)}, bf16[2,512,256]{2,1,0:T(8,128)(2,1)}, u32[]{:S(2)}, u32[]{:S(2)}) collective-permute-start(bf16[2,512,256]{2,1,0:T(8,128)(2,1)S(1)} %shard_map.97), channel_id=1, source_target_pairs={{8,56},{24,8},{40,24},{56,40},{72,120},{88,72},{104,88},{120,104},... | collective-permute-start | bytes 1572872 | tf_op jit(solution)/shard_map/ppermute | solution.py:381
  41.2 21.7 %collective-permute-start.9 = (bf16[2,512,256]{2,1,0:T(8,128)(2,1)S(1)}, bf16[2,512,256]{2,1,0:T(8,128)(2,1)}, u32[]{:S(2)}, u32[]{:S(2)}) collective-permute-start(bf16[2,512,256]{2,1,0:T(8,128)(2,1)S(1)} %collective-permute-done.2), channel_id=1, source_target_pairs={{8,56},{24,8},{40,24},{56,40},{72,120},{88,72},{104,88},{120,104},... | collective-permute-start | bytes 1572872 | tf_op jit(solution)/shard_map/ppermute | solution.py:381
  45.6 17.3 %collective-permute-start.8 = (bf16[2,512,256]{2,1,0:T(8,128)(2,1)S(1)}, bf16[2,512,256]{2,1,0:T(8,128)(2,1)}, u32[]{:S(2)}, u32[]{:S(2)}) collective-permute-start(bf16[2,512,256]{2,1,0:T(8,128)(2,1)S(1)} %collective-permute-done.6), channel_id=1, source_target_pairs={{0,64},{16,80},{32,96},{48,112},{64,0},{80,16},{96,32},{112,48},{1... | collective-permute-start | bytes 1572872 | tf_op jit(solution)/shard_map/ppermute | solution.py:381
  51.7 11.5 %collective-permute-start.11 = (bf16[2,512,256]{2,1,0:T(8,128)(2,1)S(1)}, bf16[2,512,256]{2,1,0:T(8,128)(2,1)}, u32[]{:S(2)}, u32[]{:S(2)}) collective-permute-start(bf16[2,512,256]{2,1,0:T(8,128)(2,1)S(1)} %shard_map.97), channel_id=1, source_target_pairs={{8,40},{24,56},{40,8},{56,24},{72,104},{88,120},{104,72},{120,88},... | collective-permute-start | bytes 1572872 | tf_op jit(solution)/shard_map/ppermute | solution.py:381
  56.3 0.8 copy-start.1
  57.1 11.8 %collective-permute-start.12 = (bf16[2,512,256]{2,1,0:T(8,128)(2,1)S(1)}, bf16[2,512,256]{2,1,0:T(8,128)(2,1)}, u32[]{:S(2)}, u32[]{:S(2)}) collective-permute-start(bf16[2,512,256]{2,1,0:T(8,128)(2,1)S(1)} %collective-permute-done.2), channel_id=1, source_target_pairs={{8,40},{24,56},{40,8},{56,24},{72,104},{88,120},{104,72},{120,88},... | collective-permute-start | bytes 1572872 | tf_op jit(solution)/shard_map/ppermute | solution.py:381
  59.5 9.3 %copy-start.2 = (bf16[2,512,256]{2,1,0:T(8,128)(2,1)S(1)}, bf16[2,512,256]{2,1,0:T(8,128)(2,1)}, u32[]{:S(2)}) copy-start(bf16[2,512,256]{2,1,0:T(8,128)(2,1)} %copy-done.1) | copy-start | bytes 1572868
  75.7 23.1 %collective-permute-start.13 = (bf16[4,512,256]{2,1,0:T(8,128)(2,1)S(1)}, bf16[4,512,256]{2,1,0:T(8,128)(2,1)S(1)}, u32[]{:S(2)}, u32[]{:S(2)}) collective-permute-start(bf16[4,512,256]{2,1,0:T(8,128)(2,1)S(1)} %get-tuple-element.33), channel_id=1, source_target_pairs={{0,4},{1,5},{2,6},{3,7},{4,0},{5,1},{6,2},{7,3},{8,12},{9,13},{10,... | collective-permute-start | bytes 3145736 | tf_op jit(solution)/shard_map/ppermute | solution.py:415
  79.0 44.0 %copy-start = (bf16[512,512]{1,0:T(8,128)(2,1)S(1)}, bf16[512,512]{1,0:T(8,128)(2,1)}, u32[]{:S(2)}) copy-start(bf16[512,512]{1,0:T(8,128)(2,1)} %weight_ref.1) | copy-start | bytes 1572868
  79.0 30.5 %collective-permute-start.15 = (bf16[2,512,256]{2,1,0:T(8,128)(2,1)S(1)}, bf16[2,512,256]{2,1,0:T(8,128)(2,1)S(1)}, u32[]{:S(2)}, u32[]{:S(2)}) collective-permute-start(bf16[2,512,256]{2,1,0:T(8,128)(2,1)S(1)} %get-tuple-element.36), channel_id=1, source_target_pairs={{0,1},{1,2},{2,3},{3,0},{4,5},{5,6},{6,7},{7,4},{8,9},{9,10},{10,1... | collective-permute-start | bytes 1572872 | tf_op jit(solution)/shard_map/ppermute | solution.py:414
  79.9 29.7 %collective-permute-start.16 = (bf16[2,512,256]{2,1,0:T(8,128)(2,1)S(1)}, bf16[2,512,256]{2,1,0:T(8,128)(2,1)S(1)}, u32[]{:S(2)}, u32[]{:S(2)}) collective-permute-start(bf16[2,512,256]{2,1,0:T(8,128)(2,1)S(1)} %get-tuple-element.37), channel_id=1, source_target_pairs={{0,3},{1,0},{2,1},{3,2},{4,7},{5,4},{6,5},{7,6},{8,11},{9,8},{10,9... | collective-permute-start | bytes 1572872 | tf_op jit(solution)/shard_map/ppermute | solution.py:414
  81.8 27.7 %collective-permute-start.17 = (bf16[2,512,256]{2,1,0:T(8,128)(2,1)S(1)}, bf16[2,512,256]{2,1,0:T(8,128)(2,1)S(1)}, u32[]{:S(2)}, u32[]{:S(2)}) collective-permute-start(bf16[2,512,256]{2,1,0:T(8,128)(2,1)S(1)} %get-tuple-element.38), channel_id=1, source_target_pairs={{0,2},{1,3},{2,0},{3,1},{4,6},{5,7},{6,4},{7,5},{8,10},{9,11},{10,... | collective-permute-start | bytes 1572872 | tf_op jit(solution)/shard_map/ppermute | solution.py:414
  99.7 7.8 %collective-permute-start.14 = (bf16[512,256]{1,0:T(8,128)(2,1)S(1)}, bf16[512,256]{1,0:T(8,128)(2,1)S(1)}, u32[]{:S(2)}, u32[]{:S(2)}) collective-permute-start(bf16[512,256]{1,0:T(8,128)(2,1)S(1)} %get-tuple-element.34), channel_id=1, source_target_pairs={{0,1},{1,2},{2,3},{3,0},{4,5},{5,6},{6,7},{7,4},{8,9},{9,10},{10,1... | collective-permute-start | bytes 786440 | tf_op jit(solution)/shard_map/ppermute | solution.py:420
  99.8 14.0 %collective-permute-start.19 = (bf16[512,256]{1,0:T(8,128)(2,1)S(1)}, bf16[512,256]{1,0:T(8,128)(2,1)S(1)}, u32[]{:S(2)}, u32[]{:S(2)}) collective-permute-start(bf16[512,256]{1,0:T(8,128)(2,1)S(1)} %get-tuple-element.42), channel_id=1, source_target_pairs={{0,3},{1,0},{2,1},{3,2},{4,7},{5,4},{6,5},{7,6},{8,11},{9,8},{10,9... | collective-permute-start | bytes 786440 | tf_op jit(solution)/shard_map/ppermute | solution.py:420
  107.5 9.4 %collective-permute-start.20 = (bf16[512,256]{1,0:T(8,128)(2,1)S(1)}, bf16[512,256]{1,0:T(8,128)(2,1)S(1)}, u32[]{:S(2)}, u32[]{:S(2)}) collective-permute-start(bf16[512,256]{1,0:T(8,128)(2,1)S(1)} %get-tuple-element.43), channel_id=1, source_target_pairs={{0,2},{1,3},{2,0},{3,1},{4,6},{5,7},{6,4},{7,5},{8,10},{9,11},{10,... | collective-permute-start | bytes 786440 | tf_op jit(solution)/shard_map/ppermute | solution.py:420
  110.3 9.5 %collective-permute-start.18 = (bf16[512,256]{1,0:T(8,128)(2,1)S(1)}, bf16[512,256]{1,0:T(8,128)(2,1)S(1)}, u32[]{:S(2)}, u32[]{:S(2)}) collective-permute-start(bf16[512,256]{1,0:T(8,128)(2,1)S(1)} %get-tuple-element.40), channel_id=1, source_target_pairs={{0,4},{1,5},{2,6},{3,7},{4,0},{5,1},{6,2},{7,3},{8,12},{9,13},{10,... | collective-permute-start | bytes 786440 | tf_op jit(solution)/shard_map/ppermute | solution.py:424
  120.5 2.5 %collective-permute-start.21 = (f32[512,256]{1,0:T(8,128)S(1)}, f32[512,256]{1,0:T(8,128)S(1)}, u32[]{:S(2)}, u32[]{:S(2)}) collective-permute-start(f32[512,256]{1,0:T(8,128)S(1)} %get-tuple-element.45.other_ref), channel_id=1, source_target_pairs={{0,8},{8,0},{16,24},{24,16},{32,40},{40,32},{48,56},{56,48},{64,72... | collective-permute-start | bytes 1572872 | tf_op jit(solution)/shard_map/ppermute | solution.py:428
  125.3 1.9 %collective-permute-start.22 = (bf16[512,512]{1,0:T(8,128)(2,1)S(1)}, bf16[512,512]{1,0:T(8,128)(2,1)S(1)}, u32[]{:S(2)}, u32[]{:S(2)}) collective-permute-start(bf16[512,512]{1,0:T(8,128)(2,1)S(1)} %get-tuple-element.47.slope_ref), channel_id=1, source_target_pairs={{0,8},{8,0},{16,24},{24,16},{32,40},{40,32},{48,56},{56,48},{64,72... | collective-permute-start | bytes 1572872 | tf_op jit(solution)/shard_map/ppermute | solution.py:435
  158.3 4.7 %collective-permute-start.23 = (bf16[256,512]{1,0:T(8,128)(2,1)S(1)}, bf16[256,512]{1,0:T(8,128)(2,1)S(1)}, u32[]{:S(2)}, u32[]{:S(2)}) collective-permute-start(bf16[256,512]{1,0:T(8,128)(2,1)S(1)} %bitcast.52), channel_id=1, source_target_pairs={{0,8},{8,0},{16,24},{24,16},{32,40},{40,32},{48,56},{56,48},{64,72... | collective-permute-start | bytes 786440 | tf_op jit(solution)/shard_map/ppermute | solution.py:446

commit v15 on v14

--- a/solution.py
+++ b/solution.py
@@ -228,13 +228,20 @@
     return high, (value - high.astype(F32)).astype(BF16)
 
 
-def layer_kernel(meta_ref, mine_ref, got_ref, weight_ref, cotangent_ref, act_ref, slope_ref):
-    core = meta_ref[0]
-    pre = jnp.zeros((SLOTS, F), F32)
-    for half, mixed in ((core, mine_ref[...]), (1 - core, got_ref[...])):
-        weight = weight_ref[pl.ds(pl.multiple_of(half * HALF, HALF), HALF), :]
-        for piece in two_parts(mixed):
-            pre = pre + jnp.dot(piece, weight, preferred_element_type=F32)
+def half_product(pre, mixed, weight_ref, half):
+    weight = weight_ref[pl.ds(pl.multiple_of(half * HALF, HALF), HALF), :]
+    for piece in two_parts(mixed):
+        pre = pre + jnp.dot(piece, weight, preferred_element_type=F32)
+    return pre
+
+
+def half_layer_kernel(meta_ref, mine_ref, weight_ref, pre_ref):
+    start = jnp.zeros((SLOTS, F), F32)
+    pre_ref[...] = half_product(start, mine_ref[...], weight_ref, meta_ref[0])
+
+
+def layer_kernel(meta_ref, pre_ref, got_ref, weight_ref, cotangent_ref, act_ref, slope_ref):
+    pre = half_product(pre_ref[...], got_ref[...], weight_ref, 1 - meta_ref[0])
     sigmoid = jax.nn.sigmoid(pre)
     act_ref[...] = (pre * sigmoid).astype(BF16)
     slope_ref[...] = (
@@ -401,7 +408,7 @@
     source = held(CHIPS, 2, N_ROW, N_COL * PER_PEER, HALF)
     keep1, send1, source, tiles0 = call(
         tiles_y_kernel,
-        [smem, smem, vmem, pinned, pinned] + [hbm] * BLOCKS,
+        [smem, smem, vmem, pinned, pinned] + [pinned] * BLOCKS,
         [held(4, SLOTS, HALF), held(4, SLOTS, HALF), source, staged],
         [total, pltpu.SemaphoreType.DMA((CHIPS,)), pltpu.SemaphoreType.DMA],
     )(meta, plans[1], tiles1, tiles, other_tiles, *blocks)
@@ -426,11 +433,14 @@
         meta, keep0, got0, keep1, *got1
     )
     theirs = lax.ppermute(others, "row", swap)
+    half = call(half_layer_kernel, [smem] + [vmem] * 2, held(SLOTS, F, dtype=F32))(
+        meta, mine, weight
+    )
     cotangent = lax.dynamic_slice_in_dim(out_cotangent, col * SLOTS, SLOTS, 0)
     activations, slope = call(
         layer_kernel, [smem] + [vmem] * 4, [array(SLOTS, F), held(SLOTS, F)]
     )(
-        meta, mine, theirs, weight, cotangent
+        meta, half, theirs, weight, cotangent
     )
     other_slope = lax.ppermute(slope, "row", swap)
     half = call(gradient_kernel, [vmem] * 4, held(HALF, F))(

time: 165 us -> 166 us (level)
  blocking collectives: 30.1 us -> 31.9 us
    ppermute x1, waiting for transfers between devices: 2.89 us -> 0.87 us  [shards(): got0 = lax.ppermute(send0, 'col', y_moves())]
    all_to_all x3, blocking collectives: 30.1 us -> 31.9 us  [exchange(): lax.all_to_all(parts, axis, split_axis=0, concat_axis=0, axis_index_group...]
    pallas_call x11 -> x12, Pallas kernels: 22 us -> 23.2 us  [run(): return made(*held)]
  transfers between devices with their start and end apart: 25 -> 25, of which waited for: 14 -> 12; matrix products, arithmetic and copies ran while one was open for 1% -> 1% of each run, Pallas kernels for 5% -> 6%
where the time goes in v15:
time: 166 us
  waiting for transfers between devices  58.4 us (35%)
  starting transfers between devices  45.9 us (28%)
  blocking collectives  31.9 us (19%)
  Pallas kernels  23.2 us (14%)
  local copies, waits for them, and re-layouts  3.27 us (2%)
  between operations  1.83 us (1%)
    all_to_all x3, blocking collectives, exchange(): lax.all_to_all(parts, axis, split_axis=0, concat_axis=0, axis_index_group...  31.9 us
    ppermute x11, starting transfers between devices, hop(): return lax.ppermute(block, 'row', row_moves(move))  23.4 us
    pallas_call x12, Pallas kernels, run(): return made(*held)  23.2 us
    ppermute x1, waiting for transfers between devices, shards(): got1 = lax.ppermute(send1, 'col', y_moves())  17.2 us
    ppermute x11, waiting for transfers between devices, hop(): return lax.ppermute(block, 'row', row_moves(move))  16.9 us
    ppermute x3, waiting for transfers between devices, shards(): got1 = [lax.ppermute(send1[k - 1], 'col', x_moves(k)) for k in (1, 3, 2)]  10.8 us
    all_to_all x1, waiting for transfers between devices, exchange(): lax.all_to_all(parts, axis, split_axis=0, concat_axis=0, axis_index_group...  9.51 us
    all_to_all x1, starting transfers between devices, exchange(): lax.all_to_all(parts, axis, split_axis=0, concat_axis=0, axis_index_group...  7.14 us
  transfers between devices with their start and end apart: 25, of which 12 were waited for; matrix products, arithmetic and copies ran while one was open for 1% of the time, Pallas kernels for 6%

profile of v15, /device:TPU:1, one launch (start us, length us, event | category | flops | bytes accessed | tf_op | source)
XLA Modules:
  0.0 165.8 jit_solution(4820224235615765389)
XLA Ops:
  0.6 0.7 copy-done.2
  1.3 2.3 %shard_map.96 = bf16[16,64,256]{2,1,0:T(8,128)(2,1)} custom-call(s32[1,512]{1,0:T(1,128)S(1)} %bitcast.40, bf16[512,512]{1,0:T(8,128)(2,1)} %features_hbm.1), custom_call_target="tpu_custom_call" | custom-call | tf_op jit(solution)/shard_map/pallas_call | solution.py:312
  3.6 1.5 collective-permute-start.1
  5.1 7.1 %all-to-all-start = ((bf16[16,64,256]{2,1,0:T(8,128)(2,1)}), bf16[16,64,256]{2,1,0:T(8,128)(2,1)S(1)}, u32[]{:S(2)}, u32[]{:S(2)}) async-start(bf16[16,64,256]{2,1,0:T(8,128)(2,1)} %shard_map.96), calls=%async_computation | async-start | bytes 1048576 | tf_op jit(solution)/shard_map/all_to_all | solution.py:284
  12.9 0.0 copy-start.3
  12.9 0.7 copy-done.3
  13.6 0.7 copy-done.4
  14.3 0.5 shard_map.95
  14.7 0.1 collective-permute-start
  14.8 9.5 %all-to-all-done.arrived_ref = bf16[16,64,256]{2,1,0:T(8,128)(2,1)S(1)} async-done(((bf16[16,64,256]{2,1,0:T(8,128)(2,1)}), bf16[16,64,256]{2,1,0:T(8,128)(2,1)S(1)}, u32[]{:S(2)}, u32[]{:S(2)}) %all-to-all-start) | async-done | bytes 524320 | tf_op jit(solution)/shard_map/all_to_all | solution.py:284
  24.4 0.4 shard_map.97
  24.8 0.0 copy-start
  24.8 0.5 collective-permute-start.2
  25.3 0.7 collective-permute-start.5
  26.0 1.7 %collective-permute-start.3 = (bf16[2,512,256]{2,1,0:T(8,128)(2,1)S(1)}, bf16[2,512,256]{2,1,0:T(8,128)(2,1)S(1)}, u32[]{:S(2)}, u32[]{:S(2)}) collective-permute-start(bf16[2,512,256]{2,1,0:T(8,128)(2,1)S(1)} %shard_map.97), channel_id=1, source_target_pairs={{0,64},{8,24},{16,80},{24,40},{32,96},{40,56},{48,112},{56,8},{64,... | collective-permute-start | bytes 1572872 | tf_op jit(solution)/shard_map/ppermute | solution.py:388
  27.7 0.7 collective-permute-start.6
  28.4 4.8 %collective-permute-done.2 = bf16[2,512,256]{2,1,0:T(8,128)(2,1)S(1)} collective-permute-done((bf16[2,512,256]{2,1,0:T(8,128)(2,1)S(1)}, bf16[2,512,256]{2,1,0:T(8,128)(2,1)S(1)}, u32[]{:S(2)}, u32[]{:S(2)}) %collective-permute-start.2) | collective-permute-done | bytes 524320 | tf_op jit(solution)/shard_map/ppermute | solution.py:388
  33.2 2.5 %collective-permute-start.4 = (bf16[2,512,256]{2,1,0:T(8,128)(2,1)S(1)}, bf16[2,512,256]{2,1,0:T(8,128)(2,1)S(1)}, u32[]{:S(2)}, u32[]{:S(2)}) collective-permute-start(bf16[2,512,256]{2,1,0:T(8,128)(2,1)S(1)} %collective-permute-done.2), channel_id=1, source_target_pairs={{0,64},{8,24},{16,80},{24,40},{32,96},{40,56},{48,112},{56,8},{64,... | collective-permute-start | bytes 1572872 | tf_op jit(solution)/shard_map/ppermute | solution.py:388
  35.8 0.7 collective-permute-start.7
  36.4 4.1 %collective-permute-start.10 = (bf16[2,512,256]{2,1,0:T(8,128)(2,1)S(1)}, bf16[2,512,256]{2,1,0:T(8,128)(2,1)}, u32[]{:S(2)}, u32[]{:S(2)}) collective-permute-start(bf16[2,512,256]{2,1,0:T(8,128)(2,1)S(1)} %shard_map.97), channel_id=1, source_target_pairs={{8,56},{24,8},{40,24},{56,40},{72,120},{88,72},{104,88},{120,104},... | collective-permute-start | bytes 1572872 | tf_op jit(solution)/shard_map/ppermute | solution.py:388
  40.5 0.7 collective-permute-done.3
  41.2 4.3 %collective-permute-start.9 = (bf16[2,512,256]{2,1,0:T(8,128)(2,1)S(1)}, bf16[2,512,256]{2,1,0:T(8,128)(2,1)}, u32[]{:S(2)}, u32[]{:S(2)}) collective-permute-start(bf16[2,512,256]{2,1,0:T(8,128)(2,1)S(1)} %collective-permute-done.2), channel_id=1, source_target_pairs={{8,56},{24,8},{40,24},{56,40},{72,120},{88,72},{104,88},{120,104},... | collective-permute-start | bytes 1572872 | tf_op jit(solution)/shard_map/ppermute | solution.py:388
  45.6 1.5 collective-permute-start.8
  47.1 4.6 %collective-permute-done.4 = bf16[2,512,256]{2,1,0:T(8,128)(2,1)S(1)} collective-permute-done((bf16[2,512,256]{2,1,0:T(8,128)(2,1)S(1)}, bf16[2,512,256]{2,1,0:T(8,128)(2,1)S(1)}, u32[]{:S(2)}, u32[]{:S(2)}) %collective-permute-start.4) | collective-permute-done | bytes 524320 | tf_op jit(solution)/shard_map/ppermute | solution.py:388
  51.7 4.5 %collective-permute-start.11 = (bf16[2,512,256]{2,1,0:T(8,128)(2,1)S(1)}, bf16[2,512,256]{2,1,0:T(8,128)(2,1)}, u32[]{:S(2)}, u32[]{:S(2)}) collective-permute-start(bf16[2,512,256]{2,1,0:T(8,128)(2,1)S(1)} %shard_map.97), channel_id=1, source_target_pairs={{8,40},{24,56},{40,8},{56,24},{72,104},{88,120},{104,72},{120,88},... | collective-permute-start | bytes 1572872 | tf_op jit(solution)/shard_map/ppermute | solution.py:388
  56.3 2.2 %collective-permute-start.12 = (bf16[2,512,256]{2,1,0:T(8,128)(2,1)S(1)}, bf16[2,512,256]{2,1,0:T(8,128)(2,1)}, u32[]{:S(2)}, u32[]{:S(2)}) collective-permute-start(bf16[2,512,256]{2,1,0:T(8,128)(2,1)S(1)} %collective-permute-done.2), channel_id=1, source_target_pairs={{8,40},{24,56},{40,8},{56,24},{72,104},{88,120},{104,72},{120,88},... | collective-permute-start | bytes 1572872 | tf_op jit(solution)/shard_map/ppermute | solution.py:388
  58.7 0.1 stack.51.meta_ref
  58.8 3.3 %shard_map.98.tiles = bf16[193,128,128]{2,1,0:T(8,128)(2,1)S(1)} custom-call(s32[12]{0:T(128)S(1)} %stack.51.meta_ref, bf16[192,128,128]{2,1,0:T(8,128)(2,1)} %bitcast.44, bf16[192,128,128]{2,1,0:T(8,128)(2,1)} %collective-permute-done.1.other_hbm), custom_call_target="tpu_custom_call" | custom-call | tf_op jit(solution)/shard_map/pallas_call | solution.py:312
  62.2 1.0 collective-permute-done.11
  63.2 5.6 %collective-permute-done.12 = bf16[2,512,256]{2,1,0:T(8,128)(2,1)} collective-permute-done((bf16[2,512,256]{2,1,0:T(8,128)(2,1)S(1)}, bf16[2,512,256]{2,1,0:T(8,128)(2,1)}, u32[]{:S(2)}, u32[]{:S(2)}) %collective-permute-start.12) | collective-permute-done | bytes 524320 | tf_op jit(solution)/shard_map/ppermute | solution.py:388
  68.9 7.4 %shard_map.99 = (bf16[4,512,256]{2,1,0:T(8,128)(2,1)S(1)}, bf16[4,512,256]{2,1,0:T(8,128)(2,1)S(1)}, bf16[8,2,16,32,256]{4,3,2,1,0:T(8,128)(2,1)S(1)}, bf16[193,128,128]{2,1,0:T(8,128)(2,1)S(1)}) custom-call(s32[12]{0:T(128)S(1)} %stack.51.meta_ref, s32[8,288]{1,0:T(8,128)S(1)} %get-tuple-element.50.plan_ref, bf16[193,128,128]{2,1,0:T(8,128)(2,1)S(1)} %shard_map.98.tiles, ...), custom_call_target="tpu_custom_call" | custom-call | tf_op jit(solution)/shard_map/pallas_call | solution.py:312
  76.2 0.1 collective-permute-start.13
  76.3 3.2 %shard_map.100 = (bf16[2,512,256]{2,1,0:T(8,128)(2,1)S(1)}, bf16[2,512,256]{2,1,0:T(8,128)(2,1)S(1)}, bf16[2,512,256]{2,1,0:T(8,128)(2,1)S(1)}, bf16[2,512,256]{2,1,0:T(8,128)(2,1)S(1)}) custom-call(s32[12]{0:T(128)S(1)} %stack.51.meta_ref, s32[8,288]{1,0:T(8,128)S(1)} %get-tuple-element.51.plan_ref, bf16[193,128,128]{2,1,0:T(8,128)(2,1)S(1)} %get-tuple-element.29.tiles, ...), custom_call_target="tpu_custom_call" | custom-call | tf_op jit(solution)/shard_map/pallas_call | solution.py:312
  79.5 0.0 copy-start.1
  79.5 0.1 collective-permute-start.15
  79.6 2.7 %collective-permute-start.16 = (bf16[2,512,256]{2,1,0:T(8,128)(2,1)S(1)}, bf16[2,512,256]{2,1,0:T(8,128)(2,1)S(1)}, u32[]{:S(2)}, u32[]{:S(2)}) collective-permute-start(bf16[2,512,256]{2,1,0:T(8,128)(2,1)S(1)} %get-tuple-element.37), channel_id=1, source_target_pairs={{0,3},{1,0},{2,1},{3,2},{4,7},{5,4},{6,5},{7,6},{8,11},{9,8},{10,9... | collective-permute-start | bytes 1572872 | tf_op jit(solution)/shard_map/ppermute | solution.py:421
  82.3 0.2 collective-permute-start.17
  82.5 17.2 %collective-permute-done.13.got_ref = bf16[4,512,256]{2,1,0:T(8,128)(2,1)S(1)} collective-permute-done((bf16[4,512,256]{2,1,0:T(8,128)(2,1)S(1)}, bf16[4,512,256]{2,1,0:T(8,128)(2,1)S(1)}, u32[]{:S(2)}, u32[]{:S(2)}) %collective-permute-start.13) | collective-permute-done | bytes 1048608 | tf_op jit(solution)/shard_map/ppermute | solution.py:422
  99.7 0.8 shard_map.101
  100.5 0.1 collective-permute-start.14
  100.6 2.7 %collective-permute-start.19 = (bf16[512,256]{1,0:T(8,128)(2,1)S(1)}, bf16[512,256]{1,0:T(8,128)(2,1)S(1)}, u32[]{:S(2)}, u32[]{:S(2)}) collective-permute-start(bf16[512,256]{1,0:T(8,128)(2,1)S(1)} %get-tuple-element.42), channel_id=1, source_target_pairs={{0,3},{1,0},{2,1},{3,2},{4,7},{5,4},{6,5},{7,6},{8,11},{9,8},{10,9... | collective-permute-start | bytes 786440 | tf_op jit(solution)/shard_map/ppermute | solution.py:427
  103.3 5.2 %collective-permute-done.14.a_ref = bf16[512,256]{1,0:T(8,128)(2,1)S(1)} collective-permute-done((bf16[512,256]{1,0:T(8,128)(2,1)S(1)}, bf16[512,256]{1,0:T(8,128)(2,1)S(1)}, u32[]{:S(2)}, u32[]{:S(2)}) %collective-permute-start.14) | collective-permute-done | bytes 262176 | tf_op jit(solution)/shard_map/ppermute | solution.py:427
  108.5 0.7 collective-permute-start.20
  109.2 0.8 shard_map.102
  110.0 2.5 %collective-permute-start.18 = (bf16[512,256]{1,0:T(8,128)(2,1)S(1)}, bf16[512,256]{1,0:T(8,128)(2,1)S(1)}, u32[]{:S(2)}, u32[]{:S(2)}) collective-permute-start(bf16[512,256]{1,0:T(8,128)(2,1)S(1)} %get-tuple-element.40), channel_id=1, source_target_pairs={{0,4},{1,5},{2,6},{3,7},{4,0},{5,1},{6,2},{7,3},{8,12},{9,13},{10,... | collective-permute-start | bytes 786440 | tf_op jit(solution)/shard_map/ppermute | solution.py:431
  112.6 5.6 %collective-permute-done.20.c_ref = bf16[512,256]{1,0:T(8,128)(2,1)S(1)} collective-permute-done((bf16[512,256]{1,0:T(8,128)(2,1)S(1)}, bf16[512,256]{1,0:T(8,128)(2,1)S(1)}, u32[]{:S(2)}, u32[]{:S(2)}) %collective-permute-start.20) | collective-permute-done | bytes 262176 | tf_op jit(solution)/shard_map/ppermute | solution.py:427
  118.1 0.9 collective-permute-done.18.got0
  119.0 0.8 shard_map.103
  119.8 1.4 collective-permute-start.21
  121.2 1.1 constant_dynamic-slice_fusion.cotangent_ref
  122.3 1.0 shard_map.104.pre_ref
  123.3 2.1 %shard_map.105 = (bf16[512,512]{1,0:T(8,128)(2,1)}, bf16[512,512]{1,0:T(8,128)(2,1)S(1)}) custom-call(s32[12]{0:T(128)S(1)} %stack.51.meta_ref, f32[512,512]{1,0:T(8,128)S(1)} %shard_map.104.pre_ref, f32[512,256]{1,0:T(8,128)S(1)} %collective-permute-done.21.got_ref, bf16[512,512]{1,0:T(8,128)(2,1)S(1)} %copy-done.1, ...), custom_call_target="tpu_custom_call" | custom-call | tf_op jit(solution)/shard_map/pallas_call | solution.py:312
  125.4 0.0 collective-permute-start.22
  125.4 1.9 %collective-permute-done.22.other_slope_ref = bf16[512,512]{1,0:T(8,128)(2,1)S(1)} collective-permute-done((bf16[512,512]{1,0:T(8,128)(2,1)S(1)}, bf16[512,512]{1,0:T(8,128)(2,1)S(1)}, u32[]{:S(2)}, u32[]{:S(2)}) %collective-permute-start.22) | collective-permute-done | bytes 524320 | tf_op jit(solution)/shard_map/ppermute | solution.py:445
  127.3 0.7 shard_map.106
  128.0 9.3 %all_to_all.20 = bf16[8,32,512]{2,1,0:T(8,128)(2,1)S(1)} all-to-all(bf16[8,32,512]{2,1,0:T(8,128)(2,1)S(1)} %bitcast.39), channel_id=1, replica_groups={{0,16,32,48,64,80,96,112},{8,24,40,56,72,88,104,120},{1,17,33,49,65,81,..., dimensions={0} | all-to-all | bytes 524288 | tf_op jit(solution)/shard_map/all_to_all | solution.py:284
  137.3 0.1 convert_element_type.20
  137.4 13.2 %all_to_all.21 = bf16[8,32,512]{2,1,0:T(8,128)(2,1)S(1)} all-to-all(bf16[8,32,512]{2,1,0:T(8,128)(2,1)S(1)} %broadcast_in_dim.6), channel_id=1, replica_groups=mesh['row'=16,'col'=8] {'col'}, dimensions={0} | all-to-all | bytes 524288 | tf_op jit(solution)/shard_map/all_to_all | solution.py:284
  150.6 0.1 convert_element_type.23
  150.7 9.5 %all_to_all.22 = bf16[8,32,512]{2,1,0:T(8,128)(2,1)S(1)} all-to-all(bf16[8,32,512]{2,1,0:T(8,128)(2,1)S(1)} %broadcast_in_dim.7), channel_id=1, replica_groups={{0,16,32,48,64,80,96,112},{8,24,40,56,72,88,104,120},{1,17,33,49,65,81,..., dimensions={0} | all-to-all | bytes 524288 | tf_op jit(solution)/shard_map/all_to_all | solution.py:284
  160.2 3.3 %collective-permute-start.23 = (bf16[256,512]{1,0:T(8,128)(2,1)S(1)}, bf16[256,512]{1,0:T(8,128)(2,1)S(1)}, u32[]{:S(2)}, u32[]{:S(2)}) collective-permute-start(bf16[256,512]{1,0:T(8,128)(2,1)S(1)} %bitcast.46), channel_id=1, source_target_pairs={{0,8},{8,0},{16,24},{24,16},{32,40},{40,32},{48,56},{56,48},{64,72... | collective-permute-start | bytes 786440 | tf_op jit(solution)/shard_map/ppermute | solution.py:456
  163.5 1.2 collective-permute-done.23
  164.6 0.1 broadcast_select_fusion.1
  164.7 1.1 maximum_convert_fusion
  (34 shorter events, 0.2 us)
Async XLA Ops:
  0.6 0.7 copy-start.2
  3.6 21.2 %collective-permute-start.1 = (bf16[192,128,128]{2,1,0:T(8,128)(2,1)}, bf16[192,128,128]{2,1,0:T(8,128)(2,1)}, u32[]{:S(2)}, u32[]{:S(2)}) collective-permute-start(bf16[192,128,128]{2,1,0:T(8,128)(2,1)} %bitcast.43), channel_id=1, source_target_pairs={{0,8},{8,0},{16,24},{24,16},{32,40},{40,32},{48,56},{56,48},{64,72... | collective-permute-start | bytes 18874376 | tf_op jit(solution)/shard_map/ppermute | solution.py:371
  5.1 19.2 %all-to-all-start = ((bf16[16,64,256]{2,1,0:T(8,128)(2,1)}), bf16[16,64,256]{2,1,0:T(8,128)(2,1)S(1)}, u32[]{:S(2)}, u32[]{:S(2)}) async-start(bf16[16,64,256]{2,1,0:T(8,128)(2,1)} %shard_map.96), calls=%async_computation | async-start | bytes 1048576 | tf_op jit(solution)/shard_map/all_to_all | solution.py:284
  12.9 0.7 copy-start.3
  13.6 0.7 copy-start.4
  14.7 10.1 %collective-permute-start = (s32[8,288]{1,0:T(8,128)S(1)}, s32[8,288]{1,0:T(8,128)S(1)}, u32[]{:S(2)}, u32[]{:S(2)}) collective-permute-start(s32[8,288]{1,0:T(8,128)S(1)} %shard_map.95), channel_id=1, source_target_pairs={{0,8},{8,0},{16,24},{24,16},{32,40},{40,32},{48,56},{56,48},{64,72... | collective-permute-start | bytes 27656 | tf_op jit(solution)/shard_map/ppermute | solution.py:363
  24.8 37.3 %copy-start = (bf16[2,512,256]{2,1,0:T(8,128)(2,1)}, bf16[2,512,256]{2,1,0:T(8,128)(2,1)S(1)}, u32[]{:S(2)}) copy-start(bf16[2,512,256]{2,1,0:T(8,128)(2,1)S(1)} %shard_map.97) | copy-start | bytes 1572868
  24.8 8.4 %collective-permute-start.2 = (bf16[2,512,256]{2,1,0:T(8,128)(2,1)S(1)}, bf16[2,512,256]{2,1,0:T(8,128)(2,1)S(1)}, u32[]{:S(2)}, u32[]{:S(2)}) collective-permute-start(bf16[2,512,256]{2,1,0:T(8,128)(2,1)S(1)} %shard_map.97), channel_id=1, source_target_pairs={{0,16},{8,72},{16,32},{24,88},{32,48},{40,104},{48,0},{56,120},{64... | collective-permute-start | bytes 1572872 | tf_op jit(solution)/shard_map/ppermute | solution.py:388
  25.3 10.4 %collective-permute-start.5 = (bf16[2,512,256]{2,1,0:T(8,128)(2,1)S(1)}, bf16[2,512,256]{2,1,0:T(8,128)(2,1)S(1)}, u32[]{:S(2)}, u32[]{:S(2)}) collective-permute-start(bf16[2,512,256]{2,1,0:T(8,128)(2,1)S(1)} %shard_map.97), channel_id=1, source_target_pairs={{0,48},{16,0},{32,16},{48,32},{64,112},{80,64},{96,80},{112,96},{1... | collective-permute-start | bytes 1572872 | tf_op jit(solution)/shard_map/ppermute | solution.py:388
  26.0 15.3 %collective-permute-start.3 = (bf16[2,512,256]{2,1,0:T(8,128)(2,1)S(1)}, bf16[2,512,256]{2,1,0:T(8,128)(2,1)S(1)}, u32[]{:S(2)}, u32[]{:S(2)}) collective-permute-start(bf16[2,512,256]{2,1,0:T(8,128)(2,1)S(1)} %shard_map.97), channel_id=1, source_target_pairs={{0,64},{8,24},{16,80},{24,40},{32,96},{40,56},{48,112},{56,8},{64,... | collective-permute-start | bytes 1572872 | tf_op jit(solution)/shard_map/ppermute | solution.py:388
  27.7 17.9 %collective-permute-start.6 = (bf16[2,512,256]{2,1,0:T(8,128)(2,1)S(1)}, bf16[2,512,256]{2,1,0:T(8,128)(2,1)S(1)}, u32[]{:S(2)}, u32[]{:S(2)}) collective-permute-start(bf16[2,512,256]{2,1,0:T(8,128)(2,1)S(1)} %shard_map.97), channel_id=1, source_target_pairs={{0,32},{16,48},{32,0},{48,16},{64,96},{80,112},{96,64},{112,80},{1... | collective-permute-start | bytes 1572872 | tf_op jit(solution)/shard_map/ppermute | solution.py:388
  33.2 28.9 %copy-start.5 = (bf16[2,512,256]{2,1,0:T(8,128)(2,1)}, bf16[2,512,256]{2,1,0:T(8,128)(2,1)S(1)}, u32[]{:S(2)}) copy-start(bf16[2,512,256]{2,1,0:T(8,128)(2,1)S(1)} %collective-permute-done.2) | copy-start | bytes 1572868
  33.2 18.5 %collective-permute-start.4 = (bf16[2,512,256]{2,1,0:T(8,128)(2,1)S(1)}, bf16[2,512,256]{2,1,0:T(8,128)(2,1)S(1)}, u32[]{:S(2)}, u32[]{:S(2)}) collective-permute-start(bf16[2,512,256]{2,1,0:T(8,128)(2,1)S(1)} %collective-permute-done.2), channel_id=1, source_target_pairs={{0,64},{8,24},{16,80},{24,40},{32,96},{40,56},{48,112},{56,8},{64,... | collective-permute-start | bytes 1572872 | tf_op jit(solution)/shard_map/ppermute | solution.py:388
  35.8 26.4 %copy-start.6 = (bf16[2,512,256]{2,1,0:T(8,128)(2,1)}, bf16[2,512,256]{2,1,0:T(8,128)(2,1)S(1)}, u32[]{:S(2)}) copy-start(bf16[2,512,256]{2,1,0:T(8,128)(2,1)S(1)} %collective-permute-done.5) | copy-start | bytes 1572868
  35.8 20.5 %collective-permute-start.7 = (bf16[2,512,256]{2,1,0:T(8,128)(2,1)S(1)}, bf16[2,512,256]{2,1,0:T(8,128)(2,1)S(1)}, u32[]{:S(2)}, u32[]{:S(2)}) collective-permute-start(bf16[2,512,256]{2,1,0:T(8,128)(2,1)S(1)} %collective-permute-done.5), channel_id=1, source_target_pairs={{0,64},{16,80},{32,96},{48,112},{64,0},{80,16},{96,32},{112,48},{1... | collective-permute-start | bytes 1572872 | tf_op jit(solution)/shard_map/ppermute | solution.py:388
  36.4 25.8 %collective-permute-start.10 = (bf16[2,512,256]{2,1,0:T(8,128)(2,1)S(1)}, bf16[2,512,256]{2,1,0:T(8,128)(2,1)}, u32[]{:S(2)}, u32[]{:S(2)}) collective-permute-start(bf16[2,512,256]{2,1,0:T(8,128)(2,1)S(1)} %shard_map.97), channel_id=1, source_target_pairs={{8,56},{24,8},{40,24},{56,40},{72,120},{88,72},{104,88},{120,104},... | collective-permute-start | bytes 1572872 | tf_op jit(solution)/shard_map/ppermute | solution.py:388
  41.2 20.9 %copy-start.7 = (bf16[2,512,256]{2,1,0:T(8,128)(2,1)}, bf16[2,512,256]{2,1,0:T(8,128)(2,1)S(1)}, u32[]{:S(2)}) copy-start(bf16[2,512,256]{2,1,0:T(8,128)(2,1)S(1)} %collective-permute-done.3) | copy-start | bytes 1572868
  41.2 21.0 %collective-permute-start.9 = (bf16[2,512,256]{2,1,0:T(8,128)(2,1)S(1)}, bf16[2,512,256]{2,1,0:T(8,128)(2,1)}, u32[]{:S(2)}, u32[]{:S(2)}) collective-permute-start(bf16[2,512,256]{2,1,0:T(8,128)(2,1)S(1)} %collective-permute-done.2), channel_id=1, source_target_pairs={{8,56},{24,8},{40,24},{56,40},{72,120},{88,72},{104,88},{120,104},... | collective-permute-start | bytes 1572872 | tf_op jit(solution)/shard_map/ppermute | solution.py:388
  45.6 16.6 %copy-start.8 = (bf16[2,512,256]{2,1,0:T(8,128)(2,1)}, bf16[2,512,256]{2,1,0:T(8,128)(2,1)S(1)}, u32[]{:S(2)}) copy-start(bf16[2,512,256]{2,1,0:T(8,128)(2,1)S(1)} %collective-permute-done.6) | copy-start | bytes 1572868
  45.6 16.6 %collective-permute-start.8 = (bf16[2,512,256]{2,1,0:T(8,128)(2,1)S(1)}, bf16[2,512,256]{2,1,0:T(8,128)(2,1)}, u32[]{:S(2)}, u32[]{:S(2)}) collective-permute-start(bf16[2,512,256]{2,1,0:T(8,128)(2,1)S(1)} %collective-permute-done.6), channel_id=1, source_target_pairs={{0,64},{16,80},{32,96},{48,112},{64,0},{80,16},{96,32},{112,48},{1... | collective-permute-start | bytes 1572872 | tf_op jit(solution)/shard_map/ppermute | solution.py:388
  51.7 4.6 %copy-start.9 = (bf16[2,512,256]{2,1,0:T(8,128)(2,1)}, bf16[2,512,256]{2,1,0:T(8,128)(2,1)S(1)}, u32[]{:S(2)}) copy-start(bf16[2,512,256]{2,1,0:T(8,128)(2,1)S(1)} %collective-permute-done.4) | copy-start | bytes 1572868
  51.7 11.5 %collective-permute-start.11 = (bf16[2,512,256]{2,1,0:T(8,128)(2,1)S(1)}, bf16[2,512,256]{2,1,0:T(8,128)(2,1)}, u32[]{:S(2)}, u32[]{:S(2)}) collective-permute-start(bf16[2,512,256]{2,1,0:T(8,128)(2,1)S(1)} %shard_map.97), channel_id=1, source_target_pairs={{8,40},{24,56},{40,8},{56,24},{72,104},{88,120},{104,72},{120,88},... | collective-permute-start | bytes 1572872 | tf_op jit(solution)/shard_map/ppermute | solution.py:388
  56.3 2.3 %copy-start.10 = (bf16[2,512,256]{2,1,0:T(8,128)(2,1)}, bf16[2,512,256]{2,1,0:T(8,128)(2,1)S(1)}, u32[]{:S(2)}) copy-start(bf16[2,512,256]{2,1,0:T(8,128)(2,1)S(1)} %collective-permute-done.7) | copy-start | bytes 1572868
  56.3 12.6 %collective-permute-start.12 = (bf16[2,512,256]{2,1,0:T(8,128)(2,1)S(1)}, bf16[2,512,256]{2,1,0:T(8,128)(2,1)}, u32[]{:S(2)}, u32[]{:S(2)}) collective-permute-start(bf16[2,512,256]{2,1,0:T(8,128)(2,1)S(1)} %collective-permute-done.2), channel_id=1, source_target_pairs={{8,40},{24,56},{40,8},{56,24},{72,104},{88,120},{104,72},{120,88},... | collective-permute-start | bytes 1572872 | tf_op jit(solution)/shard_map/ppermute | solution.py:388
  76.2 23.5 %collective-permute-start.13 = (bf16[4,512,256]{2,1,0:T(8,128)(2,1)S(1)}, bf16[4,512,256]{2,1,0:T(8,128)(2,1)S(1)}, u32[]{:S(2)}, u32[]{:S(2)}) collective-permute-start(bf16[4,512,256]{2,1,0:T(8,128)(2,1)S(1)} %get-tuple-element.33), channel_id=1, source_target_pairs={{0,4},{1,5},{2,6},{3,7},{4,0},{5,1},{6,2},{7,3},{8,12},{9,13},{10,... | collective-permute-start | bytes 3145736 | tf_op jit(solution)/shard_map/ppermute | solution.py:422
  79.5 42.8 %copy-start.1 = (bf16[512,512]{1,0:T(8,128)(2,1)S(1)}, bf16[512,512]{1,0:T(8,128)(2,1)}, u32[]{:S(2)}) copy-start(bf16[512,512]{1,0:T(8,128)(2,1)} %weight_ref.3) | copy-start | bytes 1572868
  79.5 29.7 %collective-permute-start.15 = (bf16[2,512,256]{2,1,0:T(8,128)(2,1)S(1)}, bf16[2,512,256]{2,1,0:T(8,128)(2,1)S(1)}, u32[]{:S(2)}, u32[]{:S(2)}) collective-permute-start(bf16[2,512,256]{2,1,0:T(8,128)(2,1)S(1)} %get-tuple-element.36), channel_id=1, source_target_pairs={{0,1},{1,2},{2,3},{3,0},{4,5},{5,6},{6,7},{7,4},{8,9},{9,10},{10,1... | collective-permute-start | bytes 1572872 | tf_op jit(solution)/shard_map/ppermute | solution.py:421
  79.6 29.6 %collective-permute-start.16 = (bf16[2,512,256]{2,1,0:T(8,128)(2,1)S(1)}, bf16[2,512,256]{2,1,0:T(8,128)(2,1)S(1)}, u32[]{:S(2)}, u32[]{:S(2)}) collective-permute-start(bf16[2,512,256]{2,1,0:T(8,128)(2,1)S(1)} %get-tuple-element.37), channel_id=1, source_target_pairs={{0,3},{1,0},{2,1},{3,2},{4,7},{5,4},{6,5},{7,6},{8,11},{9,8},{10,9... | collective-permute-start | bytes 1572872 | tf_op jit(solution)/shard_map/ppermute | solution.py:421
  82.3 27.0 %collective-permute-start.17 = (bf16[2,512,256]{2,1,0:T(8,128)(2,1)S(1)}, bf16[2,512,256]{2,1,0:T(8,128)(2,1)S(1)}, u32[]{:S(2)}, u32[]{:S(2)}) collective-permute-start(bf16[2,512,256]{2,1,0:T(8,128)(2,1)S(1)} %get-tuple-element.38), channel_id=1, source_target_pairs={{0,2},{1,3},{2,0},{3,1},{4,6},{5,7},{6,4},{7,5},{8,10},{9,11},{10,... | collective-permute-start | bytes 1572872 | tf_op jit(solution)/shard_map/ppermute | solution.py:421
  100.5 8.0 %collective-permute-start.14 = (bf16[512,256]{1,0:T(8,128)(2,1)S(1)}, bf16[512,256]{1,0:T(8,128)(2,1)S(1)}, u32[]{:S(2)}, u32[]{:S(2)}) collective-permute-start(bf16[512,256]{1,0:T(8,128)(2,1)S(1)} %get-tuple-element.34), channel_id=1, source_target_pairs={{0,1},{1,2},{2,3},{3,0},{4,5},{5,6},{6,7},{7,4},{8,9},{9,10},{10,1... | collective-permute-start | bytes 786440 | tf_op jit(solution)/shard_map/ppermute | solution.py:427
  100.6 11.9 %collective-permute-start.19 = (bf16[512,256]{1,0:T(8,128)(2,1)S(1)}, bf16[512,256]{1,0:T(8,128)(2,1)S(1)}, u32[]{:S(2)}, u32[]{:S(2)}) collective-permute-start(bf16[512,256]{1,0:T(8,128)(2,1)S(1)} %get-tuple-element.42), channel_id=1, source_target_pairs={{0,3},{1,0},{2,1},{3,2},{4,7},{5,4},{6,5},{7,6},{8,11},{9,8},{10,9... | collective-permute-start | bytes 786440 | tf_op jit(solution)/shard_map/ppermute | solution.py:427
  108.5 9.6 %collective-permute-start.20 = (bf16[512,256]{1,0:T(8,128)(2,1)S(1)}, bf16[512,256]{1,0:T(8,128)(2,1)S(1)}, u32[]{:S(2)}, u32[]{:S(2)}) collective-permute-start(bf16[512,256]{1,0:T(8,128)(2,1)S(1)} %get-tuple-element.43), channel_id=1, source_target_pairs={{0,2},{1,3},{2,0},{3,1},{4,6},{5,7},{6,4},{7,5},{8,10},{9,11},{10,... | collective-permute-start | bytes 786440 | tf_op jit(solution)/shard_map/ppermute | solution.py:427
  110.0 9.0 %collective-permute-start.18 = (bf16[512,256]{1,0:T(8,128)(2,1)S(1)}, bf16[512,256]{1,0:T(8,128)(2,1)S(1)}, u32[]{:S(2)}, u32[]{:S(2)}) collective-permute-start(bf16[512,256]{1,0:T(8,128)(2,1)S(1)} %get-tuple-element.40), channel_id=1, source_target_pairs={{0,4},{1,5},{2,6},{3,7},{4,0},{5,1},{6,2},{7,3},{8,12},{9,13},{10,... | collective-permute-start | bytes 786440 | tf_op jit(solution)/shard_map/ppermute | solution.py:431
  119.8 3.5 %collective-permute-start.21 = (f32[512,256]{1,0:T(8,128)S(1)}, f32[512,256]{1,0:T(8,128)S(1)}, u32[]{:S(2)}, u32[]{:S(2)}) collective-permute-start(f32[512,256]{1,0:T(8,128)S(1)} %get-tuple-element.45.other_ref), channel_id=1, source_target_pairs={{0,8},{8,0},{16,24},{24,16},{32,40},{40,32},{48,56},{56,48},{64,72... | collective-permute-start | bytes 1572872 | tf_op jit(solution)/shard_map/ppermute | solution.py:435
  125.4 1.9 %collective-permute-start.22 = (bf16[512,512]{1,0:T(8,128)(2,1)S(1)}, bf16[512,512]{1,0:T(8,128)(2,1)S(1)}, u32[]{:S(2)}, u32[]{:S(2)}) collective-permute-start(bf16[512,512]{1,0:T(8,128)(2,1)S(1)} %get-tuple-element.47.slope_ref), channel_id=1, source_target_pairs={{0,8},{8,0},{16,24},{24,16},{32,40},{40,32},{48,56},{56,48},{64,72... | collective-permute-start | bytes 1572872 | tf_op jit(solution)/shard_map/ppermute | solution.py:445
  160.2 4.4 %collective-permute-start.23 = (bf16[256,512]{1,0:T(8,128)(2,1)S(1)}, bf16[256,512]{1,0:T(8,128)(2,1)S(1)}, u32[]{:S(2)}, u32[]{:S(2)}) collective-permute-start(bf16[256,512]{1,0:T(8,128)(2,1)S(1)} %bitcast.46), channel_id=1, source_target_pairs={{0,8},{8,0},{16,24},{24,16},{32,40},{40,32},{48,56},{56,48},{64,72... | collective-permute-start | bytes 786440 | tf_op jit(solution)/shard_map/ppermute | solution.py:456

commit v16 on v15

--- a/solution.py
+++ b/solution.py
@@ -408,7 +408,7 @@
     source = held(CHIPS, 2, N_ROW, N_COL * PER_PEER, HALF)
     keep1, send1, source, tiles0 = call(
         tiles_y_kernel,
-        [smem, smem, vmem, pinned, pinned] + [pinned] * BLOCKS,
+        [smem, smem, vmem, pinned, pinned] + [hbm] * BLOCKS,
         [held(4, SLOTS, HALF), held(4, SLOTS, HALF), source, staged],
         [total, pltpu.SemaphoreType.DMA((CHIPS,)), pltpu.SemaphoreType.DMA],
     )(meta, plans[1], tiles1, tiles, other_tiles, *blocks)

time: 166 us -> 166 us (level)
  blocking collectives: 31.9 us -> 29.9 us
  starting transfers between devices: 45.9 us -> 43.9 us
  waiting for transfers between devices: 58.4 us -> 60.4 us
    ppermute x3, waiting for transfers between devices: 10.8 us -> 17 us  [shards(): got1 = [lax.ppermute(send1[k - 1], 'col', x_moves(k)) for k in (1, 3, 2)]]
    ppermute x1, waiting for transfers between devices: 17.2 us -> 13.4 us  [shards(): got1 = lax.ppermute(send1, 'col', y_moves())]
    ppermute x1, starting transfers between devices: 2.5 us -> 0.09 us  [shards(): got0 = lax.ppermute(send0, 'col', y_moves())]
    ppermute x1, starting transfers between devices: 0.09 us -> 2.18 us  [shards(): got1 = lax.ppermute(send1, 'col', y_moves())]
    all_to_all x3, blocking collectives: 31.9 us -> 29.9 us  [exchange(): lax.all_to_all(parts, axis, split_axis=0, concat_axis=0, axis_index_group...]
  transfers between devices with their start and end apart: 25 -> 25, of which waited for: 12 -> 13; matrix products, arithmetic and copies ran while one was open for 1% -> 1% of each run, Pallas kernels for 6% -> 7%
where the time goes in v16:
time: 166 us; the launch traced here: 164 us
  waiting for transfers between devices  60.4 us (36%)
  starting transfers between devices  43.9 us (26%)
  blocking collectives  29.9 us (18%)
  Pallas kernels  23.1 us (14%)
  local copies, waits for them, and re-layouts  4.03 us (2%)
  between operations  1.75 us (1%)
    all_to_all x3, blocking collectives, exchange(): lax.all_to_all(parts, axis, split_axis=0, concat_axis=0, axis_index_group...  29.9 us
    ppermute x11, starting transfers between devices, hop(): return lax.ppermute(block, 'row', row_moves(move))  23.3 us
    pallas_call x12, Pallas kernels, run(): return made(*held)  23.1 us
    ppermute x3, waiting for transfers between devices, shards(): got1 = [lax.ppermute(send1[k - 1], 'col', x_moves(k)) for k in (1, 3, 2)]  17 us
    ppermute x11, waiting for transfers between devices, hop(): return lax.ppermute(block, 'row', row_moves(move))  16.2 us
    ppermute x1, waiting for transfers between devices, shards(): got1 = lax.ppermute(send1, 'col', y_moves())  13.4 us
    all_to_all x1, waiting for transfers between devices, exchange(): lax.all_to_all(parts, axis, split_axis=0, concat_axis=0, axis_index_group...  9.51 us
    all_to_all x1, starting transfers between devices, exchange(): lax.all_to_all(parts, axis, split_axis=0, concat_axis=0, axis_index_group...  7.14 us
  transfers between devices with their start and end apart: 25, of which 13 were waited for; matrix products, arithmetic and copies ran while one was open for 1% of the time, Pallas kernels for 7%

profile of v16, /device:TPU:1, one launch (start us, length us, event | category | flops | bytes accessed | tf_op | source)
XLA Modules:
  0.0 164.4 jit_solution(8389548165268925246)
XLA Ops:
  0.6 0.7 copy-done.3
  1.3 2.3 %shard_map.96 = bf16[16,64,256]{2,1,0:T(8,128)(2,1)} custom-call(s32[1,512]{1,0:T(1,128)S(1)} %bitcast.46, bf16[512,512]{1,0:T(8,128)(2,1)} %features_hbm.1), custom_call_target="tpu_custom_call" | custom-call | tf_op jit(solution)/shard_map/pallas_call | solution.py:312
  3.6 1.5 collective-permute-start.1
  5.1 7.1 %all-to-all-start = ((bf16[16,64,256]{2,1,0:T(8,128)(2,1)}), bf16[16,64,256]{2,1,0:T(8,128)(2,1)S(1)}, u32[]{:S(2)}, u32[]{:S(2)}) async-start(bf16[16,64,256]{2,1,0:T(8,128)(2,1)} %shard_map.96), calls=%async_computation | async-start | bytes 1048576 | tf_op jit(solution)/shard_map/all_to_all | solution.py:284
  12.9 0.0 copy-start.4
  12.9 0.7 copy-done.4
  13.6 0.7 copy-done.5
  14.3 0.5 shard_map.95
  14.7 0.1 collective-permute-start
  14.8 9.5 %all-to-all-done.arrived_ref = bf16[16,64,256]{2,1,0:T(8,128)(2,1)S(1)} async-done(((bf16[16,64,256]{2,1,0:T(8,128)(2,1)}), bf16[16,64,256]{2,1,0:T(8,128)(2,1)S(1)}, u32[]{:S(2)}, u32[]{:S(2)}) %all-to-all-start) | async-done | bytes 524320 | tf_op jit(solution)/shard_map/all_to_all | solution.py:284
  24.4 0.4 shard_map.97
  24.8 0.5 collective-permute-start.2
  25.3 0.7 collective-permute-start.5
  26.0 1.7 %collective-permute-start.3 = (bf16[2,512,256]{2,1,0:T(8,128)(2,1)S(1)}, bf16[2,512,256]{2,1,0:T(8,128)(2,1)S(1)}, u32[]{:S(2)}, u32[]{:S(2)}) collective-permute-start(bf16[2,512,256]{2,1,0:T(8,128)(2,1)S(1)} %shard_map.97), channel_id=1, source_target_pairs={{0,64},{8,24},{16,80},{24,40},{32,96},{40,56},{48,112},{56,8},{64,... | collective-permute-start | bytes 1572872 | tf_op jit(solution)/shard_map/ppermute | solution.py:388
  27.7 0.7 collective-permute-start.6
  28.4 4.8 %collective-permute-done.2 = bf16[2,512,256]{2,1,0:T(8,128)(2,1)S(1)} collective-permute-done((bf16[2,512,256]{2,1,0:T(8,128)(2,1)S(1)}, bf16[2,512,256]{2,1,0:T(8,128)(2,1)S(1)}, u32[]{:S(2)}, u32[]{:S(2)}) %collective-permute-start.2) | collective-permute-done | bytes 524320 | tf_op jit(solution)/shard_map/ppermute | solution.py:388
  33.2 2.5 %collective-permute-start.4 = (bf16[2,512,256]{2,1,0:T(8,128)(2,1)S(1)}, bf16[2,512,256]{2,1,0:T(8,128)(2,1)S(1)}, u32[]{:S(2)}, u32[]{:S(2)}) collective-permute-start(bf16[2,512,256]{2,1,0:T(8,128)(2,1)S(1)} %collective-permute-done.2), channel_id=1, source_target_pairs={{0,64},{8,24},{16,80},{24,40},{32,96},{40,56},{48,112},{56,8},{64,... | collective-permute-start | bytes 1572872 | tf_op jit(solution)/shard_map/ppermute | solution.py:388
  35.7 0.7 collective-permute-start.7
  36.4 4.0 %collective-permute-start.10 = (bf16[2,512,256]{2,1,0:T(8,128)(2,1)S(1)}, bf16[2,512,256]{2,1,0:T(8,128)(2,1)}, u32[]{:S(2)}, u32[]{:S(2)}) collective-permute-start(bf16[2,512,256]{2,1,0:T(8,128)(2,1)S(1)} %shard_map.97), channel_id=1, source_target_pairs={{8,56},{24,8},{40,24},{56,40},{72,120},{88,72},{104,88},{120,104},... | collective-permute-start | bytes 1572872 | tf_op jit(solution)/shard_map/ppermute | solution.py:388
  40.5 0.8 collective-permute-done.3
  41.2 4.3 %collective-permute-start.9 = (bf16[2,512,256]{2,1,0:T(8,128)(2,1)S(1)}, bf16[2,512,256]{2,1,0:T(8,128)(2,1)}, u32[]{:S(2)}, u32[]{:S(2)}) collective-permute-start(bf16[2,512,256]{2,1,0:T(8,128)(2,1)S(1)} %collective-permute-done.2), channel_id=1, source_target_pairs={{8,56},{24,8},{40,24},{56,40},{72,120},{88,72},{104,88},{120,104},... | collective-permute-start | bytes 1572872 | tf_op jit(solution)/shard_map/ppermute | solution.py:388
  45.6 1.5 collective-permute-start.8
  47.0 4.7 %collective-permute-done.4 = bf16[2,512,256]{2,1,0:T(8,128)(2,1)S(1)} collective-permute-done((bf16[2,512,256]{2,1,0:T(8,128)(2,1)S(1)}, bf16[2,512,256]{2,1,0:T(8,128)(2,1)S(1)}, u32[]{:S(2)}, u32[]{:S(2)}) %collective-permute-start.4) | collective-permute-done | bytes 524320 | tf_op jit(solution)/shard_map/ppermute | solution.py:388
  51.7 4.5 %collective-permute-start.11 = (bf16[2,512,256]{2,1,0:T(8,128)(2,1)S(1)}, bf16[2,512,256]{2,1,0:T(8,128)(2,1)}, u32[]{:S(2)}, u32[]{:S(2)}) collective-permute-start(bf16[2,512,256]{2,1,0:T(8,128)(2,1)S(1)} %shard_map.97), channel_id=1, source_target_pairs={{8,40},{24,56},{40,8},{56,24},{72,104},{88,120},{104,72},{120,88},... | collective-permute-start | bytes 1572872 | tf_op jit(solution)/shard_map/ppermute | solution.py:388
  56.3 0.8 copy-done.1
  57.1 2.2 %collective-permute-start.12 = (bf16[2,512,256]{2,1,0:T(8,128)(2,1)S(1)}, bf16[2,512,256]{2,1,0:T(8,128)(2,1)}, u32[]{:S(2)}, u32[]{:S(2)}) collective-permute-start(bf16[2,512,256]{2,1,0:T(8,128)(2,1)S(1)} %collective-permute-done.2), channel_id=1, source_target_pairs={{8,40},{24,56},{40,8},{56,24},{72,104},{88,120},{104,72},{120,88},... | collective-permute-start | bytes 1572872 | tf_op jit(solution)/shard_map/ppermute | solution.py:388
  59.4 0.1 stack.51.meta_ref
  59.5 0.0 copy-start.2
  59.6 3.3 %shard_map.98.tiles = bf16[193,128,128]{2,1,0:T(8,128)(2,1)S(1)} custom-call(s32[12]{0:T(128)S(1)} %stack.51.meta_ref, bf16[192,128,128]{2,1,0:T(8,128)(2,1)} %bitcast.50, bf16[192,128,128]{2,1,0:T(8,128)(2,1)} %collective-permute-done.1.other_hbm), custom_call_target="tpu_custom_call" | custom-call | tf_op jit(solution)/shard_map/pallas_call | solution.py:312
  62.9 0.3 collective-permute-done.11
  63.2 5.6 %collective-permute-done.12 = bf16[2,512,256]{2,1,0:T(8,128)(2,1)} collective-permute-done((bf16[2,512,256]{2,1,0:T(8,128)(2,1)S(1)}, bf16[2,512,256]{2,1,0:T(8,128)(2,1)}, u32[]{:S(2)}, u32[]{:S(2)}) %collective-permute-start.12) | collective-permute-done | bytes 524320 | tf_op jit(solution)/shard_map/ppermute | solution.py:388
  68.8 5.3 %shard_map.99 = (bf16[4,512,256]{2,1,0:T(8,128)(2,1)S(1)}, bf16[4,512,256]{2,1,0:T(8,128)(2,1)S(1)}, bf16[8,2,16,32,256]{4,3,2,1,0:T(8,128)(2,1)S(1)}, bf16[193,128,128]{2,1,0:T(8,128)(2,1)S(1)}) custom-call(s32[12]{0:T(128)S(1)} %stack.51.meta_ref, s32[8,288]{1,0:T(8,128)S(1)} %get-tuple-element.50.plan_ref, bf16[193,128,128]{2,1,0:T(8,128)(2,1)S(1)} %shard_map.98.tiles, ...), custom_call_target="tpu_custom_call" | custom-call | tf_op jit(solution)/shard_map/pallas_call | solution.py:312
  74.1 2.2 %collective-permute-start.13 = (bf16[4,512,256]{2,1,0:T(8,128)(2,1)S(1)}, bf16[4,512,256]{2,1,0:T(8,128)(2,1)S(1)}, u32[]{:S(2)}, u32[]{:S(2)}) collective-permute-start(bf16[4,512,256]{2,1,0:T(8,128)(2,1)S(1)} %get-tuple-element.33), channel_id=1, source_target_pairs={{0,4},{1,5},{2,6},{3,7},{4,0},{5,1},{6,2},{7,3},{8,12},{9,13},{10,... | collective-permute-start | bytes 3145736 | tf_op jit(solution)/shard_map/ppermute | solution.py:422
  76.3 5.1 %shard_map.100 = (bf16[2,512,256]{2,1,0:T(8,128)(2,1)S(1)}, bf16[2,512,256]{2,1,0:T(8,128)(2,1)S(1)}, bf16[2,512,256]{2,1,0:T(8,128)(2,1)S(1)}, bf16[2,512,256]{2,1,0:T(8,128)(2,1)S(1)}) custom-call(s32[12]{0:T(128)S(1)} %stack.51.meta_ref, s32[8,288]{1,0:T(8,128)S(1)} %get-tuple-element.51.plan_ref, bf16[193,128,128]{2,1,0:T(8,128)(2,1)S(1)} %get-tuple-element.29.tiles, ...), custom_call_target="tpu_custom_call" | custom-call | tf_op jit(solution)/shard_map/pallas_call | solution.py:312
  81.5 0.1 collective-permute-start.15
  81.5 2.7 %collective-permute-start.16 = (bf16[2,512,256]{2,1,0:T(8,128)(2,1)S(1)}, bf16[2,512,256]{2,1,0:T(8,128)(2,1)S(1)}, u32[]{:S(2)}, u32[]{:S(2)}) collective-permute-start(bf16[2,512,256]{2,1,0:T(8,128)(2,1)S(1)} %get-tuple-element.37), channel_id=1, source_target_pairs={{0,3},{1,0},{2,1},{3,2},{4,7},{5,4},{6,5},{7,6},{8,11},{9,8},{10,9... | collective-permute-start | bytes 1572872 | tf_op jit(solution)/shard_map/ppermute | solution.py:421
  84.2 13.4 %collective-permute-done.13.got_ref = bf16[4,512,256]{2,1,0:T(8,128)(2,1)S(1)} collective-permute-done((bf16[4,512,256]{2,1,0:T(8,128)(2,1)S(1)}, bf16[4,512,256]{2,1,0:T(8,128)(2,1)S(1)}, u32[]{:S(2)}, u32[]{:S(2)}) %collective-permute-start.13) | collective-permute-done | bytes 1048608 | tf_op jit(solution)/shard_map/ppermute | solution.py:422
  97.6 0.8 shard_map.101
  98.4 0.2 collective-permute-start.14
  98.6 2.6 %collective-permute-start.19 = (bf16[512,256]{1,0:T(8,128)(2,1)S(1)}, bf16[512,256]{1,0:T(8,128)(2,1)S(1)}, u32[]{:S(2)}, u32[]{:S(2)}) collective-permute-start(bf16[512,256]{1,0:T(8,128)(2,1)S(1)} %get-tuple-element.42), channel_id=1, source_target_pairs={{0,3},{1,0},{2,1},{3,2},{4,7},{5,4},{6,5},{7,6},{8,11},{9,8},{10,9... | collective-permute-start | bytes 786440 | tf_op jit(solution)/shard_map/ppermute | solution.py:427
  101.1 9.6 %collective-permute-done.14.a_ref = bf16[512,256]{1,0:T(8,128)(2,1)S(1)} collective-permute-done((bf16[512,256]{1,0:T(8,128)(2,1)S(1)}, bf16[512,256]{1,0:T(8,128)(2,1)S(1)}, u32[]{:S(2)}, u32[]{:S(2)}) %collective-permute-start.14) | collective-permute-done | bytes 262176 | tf_op jit(solution)/shard_map/ppermute | solution.py:427
  110.7 0.2 collective-permute-start.20
  111.0 0.8 shard_map.102
  111.8 0.1 collective-permute-start.18
  111.9 4.3 %collective-permute-done.19.b_ref = bf16[512,256]{1,0:T(8,128)(2,1)S(1)} collective-permute-done((bf16[512,256]{1,0:T(8,128)(2,1)S(1)}, bf16[512,256]{1,0:T(8,128)(2,1)S(1)}, u32[]{:S(2)}, u32[]{:S(2)}) %collective-permute-start.19) | collective-permute-done | bytes 262176 | tf_op jit(solution)/shard_map/ppermute | solution.py:427
  116.2 3.1 %collective-permute-done.20.c_ref = bf16[512,256]{1,0:T(8,128)(2,1)S(1)} collective-permute-done((bf16[512,256]{1,0:T(8,128)(2,1)S(1)}, bf16[512,256]{1,0:T(8,128)(2,1)S(1)}, u32[]{:S(2)}, u32[]{:S(2)}) %collective-permute-start.20) | collective-permute-done | bytes 262176 | tf_op jit(solution)/shard_map/ppermute | solution.py:427
  119.3 1.2 collective-permute-done.18.got0
  120.5 0.8 shard_map.103
  121.3 1.6 collective-permute-start.21
  122.9 1.1 constant_dynamic-slice_fusion.cotangent_ref
  124.0 1.0 shard_map.104.pre_ref
  125.0 2.1 %shard_map.105 = (bf16[512,512]{1,0:T(8,128)(2,1)}, bf16[512,512]{1,0:T(8,128)(2,1)S(1)}) custom-call(s32[12]{0:T(128)S(1)} %stack.51.meta_ref, f32[512,512]{1,0:T(8,128)S(1)} %shard_map.104.pre_ref, f32[512,256]{1,0:T(8,128)S(1)} %collective-permute-done.21.got_ref, bf16[512,512]{1,0:T(8,128)(2,1)S(1)} %copy-done, ...), custom_call_target="tpu_custom_call" | custom-call | tf_op jit(solution)/shard_map/pallas_call | solution.py:312
  127.1 0.0 collective-permute-start.22
  127.1 1.9 %collective-permute-done.22.other_slope_ref = bf16[512,512]{1,0:T(8,128)(2,1)S(1)} collective-permute-done((bf16[512,512]{1,0:T(8,128)(2,1)S(1)}, bf16[512,512]{1,0:T(8,128)(2,1)S(1)}, u32[]{:S(2)}, u32[]{:S(2)}) %collective-permute-start.22) | collective-permute-done | bytes 524320 | tf_op jit(solution)/shard_map/ppermute | solution.py:445
  129.0 0.7 shard_map.106
  129.7 9.0 %all_to_all.20 = bf16[8,32,512]{2,1,0:T(8,128)(2,1)S(1)} all-to-all(bf16[8,32,512]{2,1,0:T(8,128)(2,1)S(1)} %bitcast.39), channel_id=1, replica_groups={{0,16,32,48,64,80,96,112},{8,24,40,56,72,88,104,120},{1,17,33,49,65,81,..., dimensions={0} | all-to-all | bytes 524288 | tf_op jit(solution)/shard_map/all_to_all | solution.py:284
  138.7 0.1 convert_element_type.20
  138.9 10.1 %all_to_all.21 = bf16[8,32,512]{2,1,0:T(8,128)(2,1)S(1)} all-to-all(bf16[8,32,512]{2,1,0:T(8,128)(2,1)S(1)} %broadcast_in_dim.6), channel_id=1, replica_groups=mesh['row'=16,'col'=8] {'col'}, dimensions={0} | all-to-all | bytes 524288 | tf_op jit(solution)/shard_map/all_to_all | solution.py:284
  148.9 0.1 convert_element_type.23
  149.0 10.8 %all_to_all.22 = bf16[8,32,512]{2,1,0:T(8,128)(2,1)S(1)} all-to-all(bf16[8,32,512]{2,1,0:T(8,128)(2,1)S(1)} %broadcast_in_dim.7), channel_id=1, replica_groups={{0,16,32,48,64,80,96,112},{8,24,40,56,72,88,104,120},{1,17,33,49,65,81,..., dimensions={0} | all-to-all | bytes 524288 | tf_op jit(solution)/shard_map/all_to_all | solution.py:284
  159.9 2.2 %collective-permute-start.23 = (bf16[256,512]{1,0:T(8,128)(2,1)S(1)}, bf16[256,512]{1,0:T(8,128)(2,1)S(1)}, u32[]{:S(2)}, u32[]{:S(2)}) collective-permute-start(bf16[256,512]{1,0:T(8,128)(2,1)S(1)} %bitcast.52), channel_id=1, source_target_pairs={{0,8},{8,0},{16,24},{24,16},{32,40},{40,32},{48,56},{56,48},{64,72... | collective-permute-start | bytes 786440 | tf_op jit(solution)/shard_map/ppermute | solution.py:456
  162.1 1.2 collective-permute-done.23
  163.2 0.1 broadcast_select_fusion.1
  163.3 1.1 maximum_convert_fusion
  (24 shorter events, 0.2 us)
Async XLA Ops:
  0.6 0.7 copy-start.3
  3.6 21.2 %collective-permute-start.1 = (bf16[192,128,128]{2,1,0:T(8,128)(2,1)}, bf16[192,128,128]{2,1,0:T(8,128)(2,1)}, u32[]{:S(2)}, u32[]{:S(2)}) collective-permute-start(bf16[192,128,128]{2,1,0:T(8,128)(2,1)} %bitcast.49), channel_id=1, source_target_pairs={{0,8},{8,0},{16,24},{24,16},{32,40},{40,32},{48,56},{56,48},{64,72... | collective-permute-start | bytes 18874376 | tf_op jit(solution)/shard_map/ppermute | solution.py:371
  5.1 19.2 %all-to-all-start = ((bf16[16,64,256]{2,1,0:T(8,128)(2,1)}), bf16[16,64,256]{2,1,0:T(8,128)(2,1)S(1)}, u32[]{:S(2)}, u32[]{:S(2)}) async-start(bf16[16,64,256]{2,1,0:T(8,128)(2,1)} %shard_map.96), calls=%async_computation | async-start | bytes 1048576 | tf_op jit(solution)/shard_map/all_to_all | solution.py:284
  12.9 0.7 copy-start.4
  13.6 0.7 copy-start.5
  14.7 10.1 %collective-permute-start = (s32[8,288]{1,0:T(8,128)S(1)}, s32[8,288]{1,0:T(8,128)S(1)}, u32[]{:S(2)}, u32[]{:S(2)}) collective-permute-start(s32[8,288]{1,0:T(8,128)S(1)} %shard_map.95), channel_id=1, source_target_pairs={{0,8},{8,0},{16,24},{24,16},{32,40},{40,32},{48,56},{56,48},{64,72... | collective-permute-start | bytes 27656 | tf_op jit(solution)/shard_map/ppermute | solution.py:363
  24.8 8.4 %collective-permute-start.2 = (bf16[2,512,256]{2,1,0:T(8,128)(2,1)S(1)}, bf16[2,512,256]{2,1,0:T(8,128)(2,1)S(1)}, u32[]{:S(2)}, u32[]{:S(2)}) collective-permute-start(bf16[2,512,256]{2,1,0:T(8,128)(2,1)S(1)} %shard_map.97), channel_id=1, source_target_pairs={{0,16},{8,72},{16,32},{24,88},{32,48},{40,104},{48,0},{56,120},{64... | collective-permute-start | bytes 1572872 | tf_op jit(solution)/shard_map/ppermute | solution.py:388
  25.3 10.4 %collective-permute-start.5 = (bf16[2,512,256]{2,1,0:T(8,128)(2,1)S(1)}, bf16[2,512,256]{2,1,0:T(8,128)(2,1)S(1)}, u32[]{:S(2)}, u32[]{:S(2)}) collective-permute-start(bf16[2,512,256]{2,1,0:T(8,128)(2,1)S(1)} %shard_map.97), channel_id=1, source_target_pairs={{0,48},{16,0},{32,16},{48,32},{64,112},{80,64},{96,80},{112,96},{1... | collective-permute-start | bytes 1572872 | tf_op jit(solution)/shard_map/ppermute | solution.py:388
  26.0 15.3 %collective-permute-start.3 = (bf16[2,512,256]{2,1,0:T(8,128)(2,1)S(1)}, bf16[2,512,256]{2,1,0:T(8,128)(2,1)S(1)}, u32[]{:S(2)}, u32[]{:S(2)}) collective-permute-start(bf16[2,512,256]{2,1,0:T(8,128)(2,1)S(1)} %shard_map.97), channel_id=1, source_target_pairs={{0,64},{8,24},{16,80},{24,40},{32,96},{40,56},{48,112},{56,8},{64,... | collective-permute-start | bytes 1572872 | tf_op jit(solution)/shard_map/ppermute | solution.py:388
  27.7 17.9 %collective-permute-start.6 = (bf16[2,512,256]{2,1,0:T(8,128)(2,1)S(1)}, bf16[2,512,256]{2,1,0:T(8,128)(2,1)S(1)}, u32[]{:S(2)}, u32[]{:S(2)}) collective-permute-start(bf16[2,512,256]{2,1,0:T(8,128)(2,1)S(1)} %shard_map.97), channel_id=1, source_target_pairs={{0,32},{16,48},{32,0},{48,16},{64,96},{80,112},{96,64},{112,80},{1... | collective-permute-start | bytes 1572872 | tf_op jit(solution)/shard_map/ppermute | solution.py:388
  33.2 18.5 %collective-permute-start.4 = (bf16[2,512,256]{2,1,0:T(8,128)(2,1)S(1)}, bf16[2,512,256]{2,1,0:T(8,128)(2,1)S(1)}, u32[]{:S(2)}, u32[]{:S(2)}) collective-permute-start(bf16[2,512,256]{2,1,0:T(8,128)(2,1)S(1)} %collective-permute-done.2), channel_id=1, source_target_pairs={{0,64},{8,24},{16,80},{24,40},{32,96},{40,56},{48,112},{56,8},{64,... | collective-permute-start | bytes 1572872 | tf_op jit(solution)/shard_map/ppermute | solution.py:388
  35.7 20.5 %collective-permute-start.7 = (bf16[2,512,256]{2,1,0:T(8,128)(2,1)S(1)}, bf16[2,512,256]{2,1,0:T(8,128)(2,1)S(1)}, u32[]{:S(2)}, u32[]{:S(2)}) collective-permute-start(bf16[2,512,256]{2,1,0:T(8,128)(2,1)S(1)} %collective-permute-done.5), channel_id=1, source_target_pairs={{0,64},{16,80},{32,96},{48,112},{64,0},{80,16},{96,32},{112,48},{1... | collective-permute-start | bytes 1572872 | tf_op jit(solution)/shard_map/ppermute | solution.py:388
  36.4 26.5 %collective-permute-start.10 = (bf16[2,512,256]{2,1,0:T(8,128)(2,1)S(1)}, bf16[2,512,256]{2,1,0:T(8,128)(2,1)}, u32[]{:S(2)}, u32[]{:S(2)}) collective-permute-start(bf16[2,512,256]{2,1,0:T(8,128)(2,1)S(1)} %shard_map.97), channel_id=1, source_target_pairs={{8,56},{24,8},{40,24},{56,40},{72,120},{88,72},{104,88},{120,104},... | collective-permute-start | bytes 1572872 | tf_op jit(solution)/shard_map/ppermute | solution.py:388
  41.2 21.7 %collective-permute-start.9 = (bf16[2,512,256]{2,1,0:T(8,128)(2,1)S(1)}, bf16[2,512,256]{2,1,0:T(8,128)(2,1)}, u32[]{:S(2)}, u32[]{:S(2)}) collective-permute-start(bf16[2,512,256]{2,1,0:T(8,128)(2,1)S(1)} %collective-permute-done.2), channel_id=1, source_target_pairs={{8,56},{24,8},{40,24},{56,40},{72,120},{88,72},{104,88},{120,104},... | collective-permute-start | bytes 1572872 | tf_op jit(solution)/shard_map/ppermute | solution.py:388
  45.6 17.3 %collective-permute-start.8 = (bf16[2,512,256]{2,1,0:T(8,128)(2,1)S(1)}, bf16[2,512,256]{2,1,0:T(8,128)(2,1)}, u32[]{:S(2)}, u32[]{:S(2)}) collective-permute-start(bf16[2,512,256]{2,1,0:T(8,128)(2,1)S(1)} %collective-permute-done.6), channel_id=1, source_target_pairs={{0,64},{16,80},{32,96},{48,112},{64,0},{80,16},{96,32},{112,48},{1... | collective-permute-start | bytes 1572872 | tf_op jit(solution)/shard_map/ppermute | solution.py:388
  51.7 11.5 %collective-permute-start.11 = (bf16[2,512,256]{2,1,0:T(8,128)(2,1)S(1)}, bf16[2,512,256]{2,1,0:T(8,128)(2,1)}, u32[]{:S(2)}, u32[]{:S(2)}) collective-permute-start(bf16[2,512,256]{2,1,0:T(8,128)(2,1)S(1)} %shard_map.97), channel_id=1, source_target_pairs={{8,40},{24,56},{40,8},{56,24},{72,104},{88,120},{104,72},{120,88},... | collective-permute-start | bytes 1572872 | tf_op jit(solution)/shard_map/ppermute | solution.py:388
  56.3 0.8 copy-start.1
  57.1 11.8 %collective-permute-start.12 = (bf16[2,512,256]{2,1,0:T(8,128)(2,1)S(1)}, bf16[2,512,256]{2,1,0:T(8,128)(2,1)}, u32[]{:S(2)}, u32[]{:S(2)}) collective-permute-start(bf16[2,512,256]{2,1,0:T(8,128)(2,1)S(1)} %collective-permute-done.2), channel_id=1, source_target_pairs={{8,40},{24,56},{40,8},{56,24},{72,104},{88,120},{104,72},{120,88},... | collective-permute-start | bytes 1572872 | tf_op jit(solution)/shard_map/ppermute | solution.py:388
  59.5 9.3 %copy-start.2 = (bf16[2,512,256]{2,1,0:T(8,128)(2,1)S(1)}, bf16[2,512,256]{2,1,0:T(8,128)(2,1)}, u32[]{:S(2)}) copy-start(bf16[2,512,256]{2,1,0:T(8,128)(2,1)} %copy-done.1) | copy-start | bytes 1572868
  74.1 23.4 %collective-permute-start.13 = (bf16[4,512,256]{2,1,0:T(8,128)(2,1)S(1)}, bf16[4,512,256]{2,1,0:T(8,128)(2,1)S(1)}, u32[]{:S(2)}, u32[]{:S(2)}) collective-permute-start(bf16[4,512,256]{2,1,0:T(8,128)(2,1)S(1)} %get-tuple-element.33), channel_id=1, source_target_pairs={{0,4},{1,5},{2,6},{3,7},{4,0},{5,1},{6,2},{7,3},{8,12},{9,13},{10,... | collective-permute-start | bytes 3145736 | tf_op jit(solution)/shard_map/ppermute | solution.py:422
  81.4 42.6 %copy-start = (bf16[512,512]{1,0:T(8,128)(2,1)S(1)}, bf16[512,512]{1,0:T(8,128)(2,1)}, u32[]{:S(2)}) copy-start(bf16[512,512]{1,0:T(8,128)(2,1)} %weight_ref.3) | copy-start | bytes 1572868
  81.5 29.5 %collective-permute-start.15 = (bf16[2,512,256]{2,1,0:T(8,128)(2,1)S(1)}, bf16[2,512,256]{2,1,0:T(8,128)(2,1)S(1)}, u32[]{:S(2)}, u32[]{:S(2)}) collective-permute-start(bf16[2,512,256]{2,1,0:T(8,128)(2,1)S(1)} %get-tuple-element.36), channel_id=1, source_target_pairs={{0,1},{1,2},{2,3},{3,0},{4,5},{5,6},{6,7},{7,4},{8,9},{9,10},{10,1... | collective-permute-start | bytes 1572872 | tf_op jit(solution)/shard_map/ppermute | solution.py:421
  81.5 29.4 %collective-permute-start.16 = (bf16[2,512,256]{2,1,0:T(8,128)(2,1)S(1)}, bf16[2,512,256]{2,1,0:T(8,128)(2,1)S(1)}, u32[]{:S(2)}, u32[]{:S(2)}) collective-permute-start(bf16[2,512,256]{2,1,0:T(8,128)(2,1)S(1)} %get-tuple-element.37), channel_id=1, source_target_pairs={{0,3},{1,0},{2,1},{3,2},{4,7},{5,4},{6,5},{7,6},{8,11},{9,8},{10,9... | collective-permute-start | bytes 1572872 | tf_op jit(solution)/shard_map/ppermute | solution.py:421
  84.2 26.8 %collective-permute-start.17 = (bf16[2,512,256]{2,1,0:T(8,128)(2,1)S(1)}, bf16[2,512,256]{2,1,0:T(8,128)(2,1)S(1)}, u32[]{:S(2)}, u32[]{:S(2)}) collective-permute-start(bf16[2,512,256]{2,1,0:T(8,128)(2,1)S(1)} %get-tuple-element.38), channel_id=1, source_target_pairs={{0,2},{1,3},{2,0},{3,1},{4,6},{5,7},{6,4},{7,5},{8,10},{9,11},{10,... | collective-permute-start | bytes 1572872 | tf_op jit(solution)/shard_map/ppermute | solution.py:421
  98.4 12.3 %collective-permute-start.14 = (bf16[512,256]{1,0:T(8,128)(2,1)S(1)}, bf16[512,256]{1,0:T(8,128)(2,1)S(1)}, u32[]{:S(2)}, u32[]{:S(2)}) collective-permute-start(bf16[512,256]{1,0:T(8,128)(2,1)S(1)} %get-tuple-element.34), channel_id=1, source_target_pairs={{0,1},{1,2},{2,3},{3,0},{4,5},{5,6},{6,7},{7,4},{8,9},{9,10},{10,1... | collective-permute-start | bytes 786440 | tf_op jit(solution)/shard_map/ppermute | solution.py:427
  98.6 17.6 %collective-permute-start.19 = (bf16[512,256]{1,0:T(8,128)(2,1)S(1)}, bf16[512,256]{1,0:T(8,128)(2,1)S(1)}, u32[]{:S(2)}, u32[]{:S(2)}) collective-permute-start(bf16[512,256]{1,0:T(8,128)(2,1)S(1)} %get-tuple-element.42), channel_id=1, source_target_pairs={{0,3},{1,0},{2,1},{3,2},{4,7},{5,4},{6,5},{7,6},{8,11},{9,8},{10,9... | collective-permute-start | bytes 786440 | tf_op jit(solution)/shard_map/ppermute | solution.py:427
  110.7 8.6 %collective-permute-start.20 = (bf16[512,256]{1,0:T(8,128)(2,1)S(1)}, bf16[512,256]{1,0:T(8,128)(2,1)S(1)}, u32[]{:S(2)}, u32[]{:S(2)}) collective-permute-start(bf16[512,256]{1,0:T(8,128)(2,1)S(1)} %get-tuple-element.43), channel_id=1, source_target_pairs={{0,2},{1,3},{2,0},{3,1},{4,6},{5,7},{6,4},{7,5},{8,10},{9,11},{10,... | collective-permute-start | bytes 786440 | tf_op jit(solution)/shard_map/ppermute | solution.py:427
  111.8 8.8 %collective-permute-start.18 = (bf16[512,256]{1,0:T(8,128)(2,1)S(1)}, bf16[512,256]{1,0:T(8,128)(2,1)S(1)}, u32[]{:S(2)}, u32[]{:S(2)}) collective-permute-start(bf16[512,256]{1,0:T(8,128)(2,1)S(1)} %get-tuple-element.40), channel_id=1, source_target_pairs={{0,4},{1,5},{2,6},{3,7},{4,0},{5,1},{6,2},{7,3},{8,12},{9,13},{10,... | collective-permute-start | bytes 786440 | tf_op jit(solution)/shard_map/ppermute | solution.py:431
  121.3 3.7 %collective-permute-start.21 = (f32[512,256]{1,0:T(8,128)S(1)}, f32[512,256]{1,0:T(8,128)S(1)}, u32[]{:S(2)}, u32[]{:S(2)}) collective-permute-start(f32[512,256]{1,0:T(8,128)S(1)} %get-tuple-element.45.other_ref), channel_id=1, source_target_pairs={{0,8},{8,0},{16,24},{24,16},{32,40},{40,32},{48,56},{56,48},{64,72... | collective-permute-start | bytes 1572872 | tf_op jit(solution)/shard_map/ppermute | solution.py:435
  127.1 1.9 %collective-permute-start.22 = (bf16[512,512]{1,0:T(8,128)(2,1)S(1)}, bf16[512,512]{1,0:T(8,128)(2,1)S(1)}, u32[]{:S(2)}, u32[]{:S(2)}) collective-permute-start(bf16[512,512]{1,0:T(8,128)(2,1)S(1)} %get-tuple-element.47.slope_ref), channel_id=1, source_target_pairs={{0,8},{8,0},{16,24},{24,16},{32,40},{40,32},{48,56},{56,48},{64,72... | collective-permute-start | bytes 1572872 | tf_op jit(solution)/shard_map/ppermute | solution.py:445
  159.9 3.4 %collective-permute-start.23 = (bf16[256,512]{1,0:T(8,128)(2,1)S(1)}, bf16[256,512]{1,0:T(8,128)(2,1)S(1)}, u32[]{:S(2)}, u32[]{:S(2)}) collective-permute-start(bf16[256,512]{1,0:T(8,128)(2,1)S(1)} %bitcast.52), channel_id=1, source_target_pairs={{0,8},{8,0},{16,24},{24,16},{32,40},{40,32},{48,56},{56,48},{64,72... | collective-permute-start | bytes 786440 | tf_op jit(solution)/shard_map/ppermute | solution.py:456
